TPU v7x, 32 devices: a whole 2x2x4 slice. The times are simulated.
32 devices in a mesh: parts: 1, blk: 4 (over z), dp: 4 (over y, x), chan: 2 (over core).
Axes of the slice: x: 2, y: 2, z: 4, core: 2. Of those that a mesh axis runs over, the one named last changes fastest.
Arguments:
- fields: bfloat16 [4, 4, 1024, 1024], P('dp', 'parts', 'blk'), may hold values from -6 to 6
- lift_weight: bfloat16 [4, 32], P('parts'), may hold values from -3 to 3
- local_weight: bfloat16 [32, 32], P('parts', 'chan'), may hold values from -1 to 1
- spectral_weight: bfloat16 [2, 256, 32, 32, 256], P('parts', ('blk', 'dp'), 'chan'), may hold values from -3 to 3
- cotangent: bfloat16 [4, 32, 1024, 1024], P('dp', 'chan', 'blk', 'parts'), may hold values from -11 to 11
Outputs:
- spectral_grad: bfloat16 [2, 256, 32, 32, 256], P('parts', ('blk', 'dp'), 'chan')
- local_grad: float32 [32, 32], P('parts', 'chan')
- lift_grad: float32 [4, 32], P('parts')
All inputs are finite; a program needn't handle non-finite values.
Results may differ from a plain program's by a relative error of at most 0.017.
Values may be sent and summed in bfloat16 or wider, within the bound.
No kernel may reach another device: no remote copies, remote signals or barrier semaphores. Data moves between devices by JAX's collectives and lax.ppermute only.
A program may use at most 320 MiB of HBM per device.

v0:
```python
import math

import jax
import jax.numpy as jnp
from jax import lax
from jax.sharding import PartitionSpec as P

NX = 1024
NY = 1024
KR = 256
KC = 256


TWO_PI = 2.0 * math.pi
HIGH = lax.Precision.HIGHEST


def phases(freqs, points, length):
    product = (freqs % length)[:, None] * points[None, :] % length
    return TWO_PI / length * product.astype(jnp.float32)


def row_freqs():
    index = jnp.arange(KR, dtype=jnp.int32)
    return jnp.where(index < KR // 2, index, index - KR)


def gelu_slope(value):
    return 0.5 * (1.0 + jax.scipy.special.erf(value / math.sqrt(2.0))) + value * jnp.exp(
        -0.5 * value * value
    ) / math.sqrt(2.0 * math.pi)


def trade_modes(packed):
    return lax.all_to_all(packed, ("blk", "dp"), split_axis=0, concat_axis=0, tiled=True)


def to_modes(field, scale, col_fwd, row_fwd, blocks_count, samples_count, mode_dev):
    chan_dev, rows_dev, cells = field.shape
    width = col_fwd.shape[1]
    half = width // 2
    group = chan_dev // blocks_count
    column_part = jnp.dot(
        field.reshape(chan_dev * rows_dev, cells), col_fwd, preferred_element_type=jnp.float32
    ).astype(jnp.bfloat16)
    column_part = column_part.reshape(blocks_count, group, rows_dev, width)
    columns = lax.all_to_all(column_part, "blk", split_axis=0, concat_axis=2, tiled=True).reshape(
        group, blocks_count * rows_dev, width
    )
    stacked = jnp.concatenate(
        [columns, jnp.concatenate([columns[..., half:], -columns[..., :half]], 2)], 1
    )
    modes = jnp.einsum("mr,crq->mcq", row_fwd, stacked, preferred_element_type=jnp.float32)
    modes = (modes * scale).astype(jnp.bfloat16)
    groups = blocks_count * samples_count
    packed = (
        modes.reshape(groups, mode_dev, group, width)
        .transpose(0, 2, 1, 3)
        .reshape(groups, group * mode_dev * width)
    )
    arrived = trade_modes(packed).reshape(blocks_count, samples_count, group, mode_dev, 2, half)
    return arrived.transpose(1, 3, 4, 0, 2, 5).reshape(samples_count, mode_dev, 2, chan_dev, half)


def to_grid(modes, scale, col_inv, blocks_count, rows_dev):
    samples_count, mode_dev, _, chan_dev, half = modes.shape
    group = chan_dev // blocks_count
    groups = blocks_count * samples_count
    width = 2 * half
    packed = modes.reshape(samples_count, mode_dev, 2, blocks_count, group, half).transpose(
        3, 0, 4, 1, 2, 5
    )
    packed = packed.reshape(groups, group * mode_dev * width)
    arrived = (
        trade_modes(packed)
        .reshape(groups, group, mode_dev, width)
        .transpose(1, 0, 2, 3)
        .reshape(group, groups * mode_dev, width)
    )
    row_angle = phases(row_freqs(), jnp.arange(NX, dtype=jnp.int32), NX)
    row_inv = jnp.concatenate([jnp.cos(row_angle).T, jnp.sin(row_angle).T], 1).astype(jnp.bfloat16)
    rows_all = jnp.einsum(
        "rm,cmq->crq",
        row_inv,
        jnp.concatenate(
            [arrived, jnp.concatenate([-arrived[..., half:], arrived[..., :half]], 2)], 1
        ),
        preferred_element_type=jnp.float32,
    ).astype(jnp.bfloat16)
    rows_part = lax.all_to_all(
        rows_all.reshape(group, blocks_count, rows_dev, width),
        "blk",
        split_axis=1,
        concat_axis=0,
        tiled=True,
    )
    rows_part = rows_part.reshape(chan_dev, rows_dev, width)
    grid = jnp.dot(
        rows_part.reshape(chan_dev * rows_dev, width), col_inv, preferred_element_type=jnp.float32
    )
    return grid.reshape(chan_dev, rows_dev, col_inv.shape[1]) * scale


def contract_inputs(left, weights):

    def term(part_a, part_b):
        return jnp.sum(
            left[:, :, part_a, :, None, :].astype(jnp.float32)
            * weights[part_b][None].astype(jnp.float32),
            axis=2,
        )

    real_part = term(0, 0) - term(1, 1)
    imag_part = term(1, 0) + term(0, 1)
    return jnp.stack([real_part, imag_part], 2)


def contract_outputs(grads, weights):

    def term(part_g, part_b):
        return jnp.sum(
            grads[:, :, part_g, None, :, :].astype(jnp.float32)
            * weights[part_b][None].astype(jnp.float32),
            axis=3,
        )

    real_part = term(0, 0) + term(1, 1)
    imag_part = term(1, 0) - term(0, 1)
    return jnp.stack([real_part, imag_part], 2)


def weight_terms(left, grads):

    def term(part_a, part_g):
        return jnp.sum(
            left[:, :, part_a, :, None, :].astype(jnp.float32)
            * grads[:, :, part_g, None, :, :].astype(jnp.float32),
            axis=0,
        )

    real_part = term(0, 0) + term(1, 1)
    imag_part = term(0, 1) - term(1, 0)
    return jnp.stack([real_part, imag_part], 0)


def per_device(fields, lift_weight, local_weight, spectral_weight, cotangent):
    blocks_count = lax.axis_size("blk")
    samples_count = lax.axis_size("dp")
    sample = fields[0]
    cotan = cotangent[0]
    chan_dev = cotan.shape[0]
    rows_dev = sample.shape[1]
    mode_dev = spectral_weight.shape[1]
    offset = lax.axis_index("chan") * chan_dev
    unit_scale = 1.0 / math.sqrt(NX * NY)
    norm_scale = 1.0 / math.sqrt(samples_count * NX * NY)
    col_angle = phases(jnp.arange(KC, dtype=jnp.int32), jnp.arange(NY, dtype=jnp.int32), NY)
    col_fwd = jnp.concatenate([jnp.cos(col_angle).T, (-jnp.sin(col_angle)).T], 1).astype(
        jnp.bfloat16
    )
    col_inv = jnp.concatenate([jnp.cos(col_angle), -jnp.sin(col_angle)], 0).astype(jnp.bfloat16)
    row_angle = phases(row_freqs(), jnp.arange(NX, dtype=jnp.int32), NX)
    row_fwd = jnp.concatenate([jnp.cos(row_angle), jnp.sin(row_angle)], 1).astype(jnp.bfloat16)
    lifted = jnp.tanh(
        jnp.einsum("jry,jc->cry", sample, lift_weight, preferred_element_type=jnp.float32)
    ).astype(jnp.bfloat16)
    own_lifted = lax.dynamic_slice_in_dim(lifted, offset, chan_dev, 0)
    field_modes = to_modes(
        own_lifted, unit_scale, col_fwd, row_fwd, blocks_count, samples_count, mode_dev
    )
    out_terms = contract_inputs(field_modes, spectral_weight)
    out_modes = lax.psum_scatter(
        out_terms.astype(jnp.bfloat16), "chan", scatter_dimension=3, tiled=True
    )
    spatial = to_grid(out_modes, 2.0 * unit_scale, col_inv, blocks_count, rows_dev)
    pre_act = spatial + jnp.einsum(
        "iry,io->ory", lifted, local_weight, preferred_element_type=jnp.float32
    )
    grad_z = (cotan.astype(jnp.float32) * gelu_slope(pre_act)).astype(jnp.bfloat16)
    local_term = (
        jnp.einsum("iry,ory->io", lifted, grad_z, preferred_element_type=jnp.float32) * norm_scale
    )
    local_grad = lax.psum(local_term, ("blk", "dp"))
    grad_half = to_modes(
        grad_z, 2.0 * unit_scale, col_fwd, row_fwd, blocks_count, samples_count, mode_dev
    )
    grad_modes = lax.all_gather(grad_half, "chan", axis=3, tiled=True)
    spectral_grad = weight_terms(field_modes, grad_modes).astype(jnp.bfloat16)
    back_modes = contract_outputs(grad_modes, spectral_weight).astype(jnp.bfloat16)
    back_grid = to_grid(back_modes, unit_scale, col_inv, blocks_count, rows_dev)
    tanh_value = jnp.tanh(
        jnp.einsum("jry,jc->cry", sample, lift_weight, preferred_element_type=jnp.float32)
    )
    local_back = jnp.einsum("ory,io->iry", grad_z, local_weight, preferred_element_type=jnp.float32)
    sample_wide = sample.astype(jnp.float32)
    lift_all = jnp.einsum(
        "jry,cry->jc", sample_wide, local_back * (1.0 - tanh_value * tanh_value), precision=HIGH
    )
    own_tanh = lax.dynamic_slice_in_dim(tanh_value, offset, chan_dev, 0)
    lift_own = jnp.einsum(
        "jry,cry->jc", sample_wide, back_grid * (1.0 - own_tanh * own_tanh), precision=HIGH
    )
    lift_term = (
        lift_all
        + lax.dynamic_update_slice_in_dim(
            jnp.zeros(lift_all.shape, jnp.float32), lift_own, offset, 1
        )
    ) * norm_scale
    lift_grad = lax.psum(lift_term, ("blk", "dp", "chan"))
    return (spectral_grad, local_grad, lift_grad)


def solution(mesh):
    in_specs = (
        P("dp", "parts", "blk", None),
        P("parts", None),
        P("parts", "chan"),
        P("parts", ("blk", "dp"), "chan", None, None),
        P("dp", "chan", "blk", "parts"),
    )
    out_specs = (
        P("parts", ("blk", "dp"), "chan", None, None),
        P("parts", "chan"),
        P("parts", None),
    )
    return jax.shard_map(
        per_device, mesh=mesh, in_specs=in_specs, out_specs=out_specs, check_vma=False
    )
```

profile of v0, /device:TPU:0, one launch (start us, length us, event | category | flops | bytes accessed | tf_op | source)
XLA Modules:
  0.0 1065.8 jit_solution(9626124495056252605)
XLA Ops:
  11.7 18.4 %fusion.111 = (bf16[32,256,1024]{2,0,1:T(8,128)(2,1)}, f32[32,256,1024]{2,0,1:T(8,128)}) fusion(bf16[4,256,1024]{2,1,0:T(8,128)(2,1)S(1)} %bitcast.169, bf16[4,32]{1,0:T(4,128)(2,1)} %param.6), kind=kOutput, calls=%fused_computation.177 | convolution fusion | flops 75497472 | bytes 52429056 | tf_op jit(solution)/shard_map/jry,jc->cry/dot_general | solution.py:165
  30.1 8.7 constant_dynamic-slice_fusion
  38.8 11.3 %copy.106 = bf16[16,256,1024]{2,1,0:T(8,128)(2,1)} copy(bf16[16,256,1024]{2,0,1:T(8,128)(2,1)} %constant_dynamic-slice_fusion) | data formatting | bytes 16777216 | tf_op jit(solution)/shard_map/dynamic_slice | solution.py:167
  50.1 9.5 convolution_convert_fusion.1
  59.6 6.5 all-to-all-start
  71.0 88.6 %all-to-all-done = bf16[4,4,256,512]{3,2,1,0:T(8,128)(2,1)} async-done(((bf16[4,4,256,512]{3,2,1,0:T(8,128)(2,1)}), bf16[4,4,256,512]{3,2,1,0:T(8,128)(2,1)}, u32[]{:S(2)}, u32[]{:S(2)}) %all-to-all-start) | async-done | bytes 4194336 | tf_op jit(solution)/shard_map/all_to_all | solution.py:47
  168.5 8.4 reduce.4
  183.3 11.6 %bitcast_convert_fusion = (f32[16,16,32,256]{3,2,1,0:T(8,128)}, f32[16,16,32,256]{3,2,1,0:T(8,128)}) fusion(bf16[2,16,16,32,256]{4,3,2,1,0:T(8,128)(2,1)} %param.8), kind=kLoop, calls=%fused_computation.54 | loop fusion | flops 4194304 | bytes 25165824 | tf_op jit(solution)/shard_map/mul | solution.py:108
  194.9 11.8 %all-to-all-done.1 = bf16[16,2,16384]{2,1,0:T(2,128)(2,1)S(1)} async-done(((bf16[16,2,16384]{2,1,0:T(2,128)(2,1)}), bf16[16,2,16384]{2,1,0:T(2,128)(2,1)S(1)}, u32[]{:S(2)}, u32[]{:S(2)}) %all-to-all-start.1) | async-done | bytes 1048608 | tf_op jit(solution)/shard_map/all_to_all | solution.py:35
  210.6 7.7 reduce
  222.9 15.4 %multiply_reduce_fusion.11 = (f32[4,16,32,256]{3,2,1,0:T(8,128)}, f32[4,16,32,256]{3,2,1,0:T(8,128)S(1)}, f32[4,16,32,256]{3,2,1,0:T(8,128)S(1)}, f32[4,16,32,256]{3,2,1,0:T(8,128)}) fusion(f32[16,16,32,256]{3,2,1,0:T(8,128)} %get-tuple-element.20, f32[4,16,16,256]{3,2,1,0:T(8,128)S(1)} %copy.111, f32[4,16,16,256]{3,2,1,0:T(8,128)S(1)} %copy.113, ...), kind=kLoop, calls=%fused_computation.15 | loop fusion | flops 65011712 | bytes 27262976 | tf_op jit(solution)/shard_map/reduce_sum | solution.py:107
  245.4 9.9 reduce-scatter.5.cloned.1.call-done
  258.9 5.7 all_to_all.89
  264.6 9.4 reduce.5
  276.6 7.1 all-to-all-start.2
  288.7 19.5 %all-to-all-done.2 = bf16[16,2,16384]{2,1,0:T(2,128)(2,1)} async-done(((bf16[16,2,16384]{2,1,0:T(2,128)(2,1)}), bf16[16,2,16384]{2,1,0:T(2,128)(2,1)}, u32[]{:S(2)}, u32[]{:S(2)}) %all-to-all-start.2) | async-done | bytes 1048608 | tf_op jit(solution)/shard_map/all_to_all | solution.py:35
  308.2 5.8 reshape.277
  314.0 8.8 reduce.1
  340.8 5.6 cosine_convert_fusion
  346.5 13.8 %fusion.93 = f32[256,1024,16]{1,2,0:T(8,128)} fusion(bf16[32,256,1024]{2,0,1:T(8,128)(2,1)} %get-tuple-element.41, bf16[32,16]{0,1:T(8,128)(2,1)S(1)} %copy-done.11), kind=kOutput, calls=%fused_computation.152 | convolution fusion | flops 268435456 | bytes 33555456 | tf_op jit(solution)/shard_map/iry,io->ory/dot_general | solution.py:176
  360.3 72.9 %all-to-all-done.3 = bf16[4,4,256,512]{2,3,0,1:T(8,128)(2,1)} async-done(((bf16[4,4,256,512]{2,3,0,1:T(8,128)(2,1)}), bf16[4,4,256,512]{2,3,0,1:T(8,128)(2,1)}, u32[]{:S(2)}, u32[]{:S(2)}) %all-to-all-start.3) | async-done | bytes 4194336 | tf_op jit(solution)/shard_map/all_to_all | solution.py:90
  433.2 7.9 copy.143
  441.1 18.2 %fusion.8 = bf16[16,256,1024]{2,0,1:T(8,128)(2,1)} fusion(f32[256,1024,16]{1,2,0:T(8,128)} %fusion.93, bf16[16,256,512]{2,0,1:T(8,128)(2,1)} %copy.143, bf16[1,16,256,1024]{3,2,1,0:T(8,128)(2,1)} %param.9, bf16[256,1024]{1,0:T(8,128)(2,1)} %get-tuple-element.34, bf16[256,1024]{1,0:T(8,128)(2,1)} %get-tuple-element.33), kind=kOutput, calls=%fused_computation.22 | convolution fusion | flops 4351590400 | bytes 38797312 | tf_op jit(solution)/shard_map/dot_general | solution.py:98
  459.3 11.4 %copy.124 = bf16[16,256,1024]{2,1,0:T(8,128)(2,1)} copy(bf16[16,256,1024]{2,0,1:T(8,128)(2,1)} %fusion.8) | data formatting | bytes 16777216 | tf_op jit(solution)/shard_map/convert_element_type | solution.py:179
  470.7 8.4 convolution_convert_fusion
  479.1 96.2 %all_to_all.100 = bf16[4,4,256,512]{3,2,1,0:T(8,128)(2,1)S(1)} all-to-all(bf16[4,4,256,512]{3,2,1,0:T(8,128)(2,1)S(1)} %bitcast.187), channel_id=1, replica_groups=mesh['parts'=1,'blk'=4,'dp'=4,'chan'=2] {'blk'}, dimensions={0} | all-to-all | bytes 8388608 | tf_op jit(solution)/shard_map/all_to_all | solution.py:47
  585.8 9.4 reduce.6
  597.8 30.4 %all_to_all.101 = bf16[16,2,16384]{2,1,0:T(2,128)(2,1)} all-to-all(bf16[16,2,16384]{2,1,0:T(2,128)(2,1)} %reshape.278), channel_id=1, replica_groups=mesh['parts'=1,'blk'=4,'dp'=4,'chan'=2] {'blk','dp'}, dimensions={0} | all-to-all | bytes 2097152 | tf_op jit(solution)/shard_map/all_to_all | solution.py:35
  628.2 5.8 reshape.279
  634.0 8.7 reduce.2
  648.0 9.0 all-gather.2.cloned.1.call-done
  664.3 45.5 %multiply_reduce_fusion.3 = (f32[4,16,16,256]{3,2,1,0:T(8,128)}, f32[4,16,16,256]{3,2,1,0:T(8,128)S(1)}, f32[4,16,16,256]{3,2,1,0:T(8,128)S(1)}, f32[4,16,16,256...) fusion(f32[4,16,32,256]{3,2,1,0:T(8,128)} %copy.129, ...), kind=kLoop, calls=%fused_computation.5 | loop fusion | flops 124780544 | bytes 60817408 | tf_op jit(solution)/shard_map/reduce_sum | solution.py:121
  717.1 8.4 reduce.7
  727.1 33.7 %all_to_all.102 = bf16[16,2,16384]{2,1,0:T(2,128)(2,1)S(1)} all-to-all(bf16[16,2,16384]{2,1,0:T(2,128)(2,1)} %reshape.280), channel_id=1, replica_groups=mesh['parts'=1,'blk'=4,'dp'=4,'chan'=2] {'blk','dp'}, dimensions={0} | all-to-all | bytes 2097152 | tf_op jit(solution)/shard_map/all_to_all | solution.py:35
  764.1 7.7 reduce.3
  774.8 5.6 convert_bitcast_fusion
  780.5 7.9 reshape.252
  788.3 7.5 copy.140
  800.8 12.6 %fusion.48 = f32[32,16]{0,1:T(8,128)S(1)} fusion(bf16[32,256,1024]{2,0,1:T(8,128)(2,1)} %get-tuple-element.41, bf16[16,256,1024]{2,0,1:T(8,128)(2,1)} %fusion.8), kind=kOutput, calls=%fused_computation.90 | convolution fusion | flops 268435968 | bytes 25167872 | tf_op jit(solution)/shard_map/iry,ory->io/dot_general | solution.py:181
  813.4 98.3 %psum.14 = f32[32,16]{0,1:T(8,128)} all-reduce(f32[32,16]{0,1:T(8,128)S(1)} %fusion.48), channel_id=1, replica_groups=mesh['parts'=1,'blk'=4,'dp'=4,'chan'=2] {'blk','dp'}, use_global_device_ids=true, to_apply=%region_9.10 | all-reduce | flops 512 | bytes 4096 | tf_op jit(solution)/shard_map/psum | solution.py:183
  911.7 19.6 %fusion.91 = f32[256,1024,32]{1,2,0:T(8,128)} fusion(bf16[16,256,1024]{2,0,1:T(8,128)(2,1)} %fusion.8, bf16[32,16]{0,1:T(8,128)(2,1)S(1)} %copy-done.11), kind=kOutput, calls=%fused_computation.150 | convolution fusion | flops 268435456 | bytes 41944064 | tf_op jit(solution)/shard_map/ory,io->iry/dot_general | solution.py:194
  931.3 26.7 %fusion = f32[32,4,1]{0,1,2:T(4,128)S(1)} fusion(f32[256,1024,32]{1,2,0:T(8,128)} %fusion.91, f32[32,256,1024]{2,0,1:T(8,128)} %get-tuple-element.42, bf16[4,256,1024]{2,1,0:T(8,128)(2,1)S(1)} %bitcast.171), kind=kOutput, calls=%fused_computation.1 | convolution fusion | flops 427819008 | bytes 69206528 | tf_op jit(solution)/shard_map/jry,cry->jc/dot_general | solution.py:196
  958.0 7.6 fusion.31
  965.6 9.3 fusion.30
  975.0 6.3 pad_maximum_fusion
  981.3 13.7 %fusion.32 = f32[16,256,1024]{2,0,1:T(8,128)} fusion(bf16[16,256,512]{2,1,0:T(8,128)(2,1)} %bitcast.56, bf16[256,1024]{1,0:T(8,128)(2,1)} %get-tuple-element.34, bf16[256,1024]{1,0:T(8,128)(2,1)} %get-tuple-element.33), kind=kOutput, calls=%fused_computation.56 | convolution fusion | flops 4297064448 | bytes 22020096 | tf_op jit(solution)/shard_map/dot_general | solution.py:98
  995.0 18.2 %fusion.55 = f32[4,16]{1,0:T(4,128)S(1)} fusion(f32[32,256,1024]{2,0,1:T(8,128)} %get-tuple-element.42, s32[]{:T(128)S(6)} %select_n.89, f32[16,256,1024]{2,0,1:T(8,128)} %fusion.32, bf16[4,256,1024]{2,1,0:T(8,128)(2,1)S(1)} %bitcast.170, f32[32,4]{0,1:T(4,128)S(1)} %bitcast.203), kind=kOutput, calls=%fused_computation.93 | convolution fusion | flops 218103872 | bytes 35653120 | tf_op jit(solution)/shard_map/jry,cry->jc/dot_general | solution.py:200
  1013.4 45.4 %psum.15 = f32[4,32]{1,0:T(4,128)} all-reduce(f32[4,32]{1,0:T(4,128)S(1)} %broadcast_multiply_fusion), channel_id=1, replica_groups=mesh['parts'=1,'blk'=4,'dp'=4,'chan'=2] {'blk','dp','chan'}, use_global_device_ids=true, to_apply=%region_14.15 | all-reduce | flops 128 | bytes 1024 | tf_op jit(solution)/shard_map/psum | solution.py:209
  (89 shorter events, 115.4 us)
Async XLA Ops:
  7.2 4.5 copy-start
  11.6 38.4 %copy-start.3 = (bf16[1024,256]{1,0:T(8,128)(2,1)}, bf16[1024,256]{1,0:T(8,128)(2,1)S(1)}, u32[]{:S(2)}) copy-start(bf16[1024,256]{1,0:T(8,128)(2,1)S(1)} %get-tuple-element.39) | copy-start | bytes 1572868
  11.7 38.4 %copy-start.5 = (bf16[1024,256]{1,0:T(8,128)(2,1)}, bf16[1024,256]{1,0:T(8,128)(2,1)S(1)}, u32[]{:S(2)}) copy-start(bf16[1024,256]{1,0:T(8,128)(2,1)S(1)} %get-tuple-element.40) | copy-start | bytes 1572868
  59.6 100.0 %all-to-all-start = ((bf16[4,4,256,512]{3,2,1,0:T(8,128)(2,1)}), bf16[4,4,256,512]{3,2,1,0:T(8,128)(2,1)}, u32[]{:S(2)}, u32[]{:S(2)}) async-start(bf16[4,4,256,512]{3,2,1,0:T(8,128)(2,1)} %bitcast.185), calls=%async_computation | async-start | bytes 8388608 | tf_op jit(solution)/shard_map/all_to_all | solution.py:47
  71.0 91.3 %copy-start.7 = (bf16[256,1024]{1,0:T(8,128)(2,1)}, bf16[256,1024]{1,0:T(8,128)(2,1)S(1)}, u32[]{:S(2)}) copy-start(bf16[256,1024]{1,0:T(8,128)(2,1)S(1)} %get-tuple-element.37) | copy-start | bytes 1572868
  71.0 91.3 %copy-start.9 = (bf16[256,1024]{1,0:T(8,128)(2,1)}, bf16[256,1024]{1,0:T(8,128)(2,1)S(1)}, u32[]{:S(2)}) copy-start(bf16[256,1024]{1,0:T(8,128)(2,1)S(1)} %get-tuple-element.38) | copy-start | bytes 1572868
  178.5 28.3 %all-to-all-start.1 = ((bf16[16,2,16384]{2,1,0:T(2,128)(2,1)}), bf16[16,2,16384]{2,1,0:T(2,128)(2,1)S(1)}, u32[]{:S(2)}, u32[]{:S(2)}) async-start(bf16[16,2,16384]{2,1,0:T(2,128)(2,1)} %reshape.274), calls=%async_computation.1 | async-start | bytes 2097152 | tf_op jit(solution)/shard_map/all_to_all | solution.py:35
  183.2 72.1 %reduce-scatter.5.cloned.1.call-start = ((), (), s32[]{:S(2)}) async-start(), calls=%async_computation.10 | async-start | bytes 3145728
  222.9 15.4 %copy-start.1 = (f32[4,16,16,256]{3,2,1,0:T(8,128)}, f32[4,16,16,256]{3,2,1,0:T(8,128)S(1)}, u32[]{:S(2)}) copy-start(f32[4,16,16,256]{3,2,1,0:T(8,128)S(1)} %copy.111) | copy-start | bytes 3145732
  276.6 31.6 %all-to-all-start.2 = ((bf16[16,2,16384]{2,1,0:T(2,128)(2,1)}), bf16[16,2,16384]{2,1,0:T(2,128)(2,1)}, u32[]{:S(2)}, u32[]{:S(2)}) async-start(bf16[16,2,16384]{2,1,0:T(2,128)(2,1)} %reshape.276), calls=%async_computation.2 | async-start | bytes 2097152 | tf_op jit(solution)/shard_map/all_to_all | solution.py:35
  335.3 11.2 %copy-start.11 = (bf16[32,16]{0,1:T(8,128)(2,1)S(1)}, bf16[32,16]{0,1:T(8,128)(2,1)}, u32[]{:S(2)}) copy-start(bf16[32,16]{0,1:T(8,128)(2,1)} %param.7) | copy-start | bytes 3076
  335.3 97.9 %all-to-all-start.3 = ((bf16[4,4,256,512]{2,3,0,1:T(8,128)(2,1)}), bf16[4,4,256,512]{2,3,0,1:T(8,128)(2,1)}, u32[]{:S(2)}, u32[]{:S(2)}) async-start(bf16[4,4,256,512]{2,3,0,1:T(8,128)(2,1)} %bitcast.172), calls=%async_computation.3 | async-start | bytes 8388608 | tf_op jit(solution)/shard_map/all_to_all | solution.py:90
  340.4 316.6 %all-gather.2.cloned.1.call-start = ((), (), s32[]{:S(2)}) async-start(), calls=%async_computation.9 | async-start | bytes 3145728 | tf_op jit(solution)/shard_map/all_gather | solution.py:187
  459.3 11.4 %copy-start.4 = (bf16[1024,256]{1,0:T(8,128)(2,1)S(1)}, bf16[1024,256]{1,0:T(8,128)(2,1)}, u32[]{:S(2)}) copy-start(bf16[1024,256]{1,0:T(8,128)(2,1)} %copy-done.3) | copy-start | bytes 1572868
  459.3 11.4 %copy-start.6 = (bf16[1024,256]{1,0:T(8,128)(2,1)S(1)}, bf16[1024,256]{1,0:T(8,128)(2,1)}, u32[]{:S(2)}) copy-start(bf16[1024,256]{1,0:T(8,128)(2,1)} %copy-done.5) | copy-start | bytes 1572868
  575.7 1.0 copy-start.8
  575.7 1.2 copy-start.10
  659.1 5.1 copy-start.2
  795.8 185.5 %all-to-all-start.7 = ((bf16[4,4,256,512]{3,2,0,1:T(8,128)(2,1)}), bf16[4,4,256,512]{3,2,0,1:T(8,128)(2,1)}, u32[]{:S(2)}, u32[]{:S(2)}) async-start(bf16[4,4,256,512]{3,2,0,1:T(8,128)(2,1)} %copy.140), calls=%async_computation.7 | async-start | bytes 8388608 | tf_op jit(solution)/shard_map/all_to_all | solution.py:90
Sparse Core Ops, SparseCore 0:
  245.5 9.7 reduce-scatter.4
  648.1 8.8 all-gather.1
where the time goes:
time: 1080 us; the launch traced here: 1070 us
  blocking collectives  304 us (28%)
  waiting for transfers between devices  212 us (20%)
  other arithmetic  194 us (18%)
  matrix products  173 us (16%)
  local copies, waits for them, and re-layouts  139 us (13%)
  starting transfers between devices  29 us (3%)
  between operations  14.7 us (1%)
    psum x1, blocking collectives, per_device(): local_grad = lax.psum(local_term, ('blk', 'dp'))  98.3 us
    all_to_all x1, blocking collectives, to_modes(): lax.all_to_all(column_part, 'blk', split_axis=0, concat_axis=2, tiled=True)  96.2 us
    all_to_all x1, waiting for transfers between devices, to_modes(): lax.all_to_all(column_part, 'blk', split_axis=0, concat_axis=2, tiled=True)  88.6 us
    all_to_all x2, waiting for transfers between devices, to_grid(): lax.all_to_all(rows_all.reshape(group, blocks_count, rows_dev, width), 'b...  72.9 us
    all_to_all x8, other arithmetic, trade_modes(): lax.all_to_all(packed, ('blk', 'dp'), split_axis=0, concat_axis=0, tiled=...  68.5 us
    all_to_all x2, blocking collectives, trade_modes(): lax.all_to_all(packed, ('blk', 'dp'), split_axis=0, concat_axis=0, tiled=...  64.1 us
    reduce_sum x1, other arithmetic, term(): jnp.sum(grads[:, :, part_g, None, :, :].astype(jnp.float32) * weights[par...  45.5 us
    psum x1, blocking collectives, per_device(): lift_grad = lax.psum(lift_term, ('blk', 'dp', 'chan'))  45.4 us
  transfers between devices with their start and end apart: 7, of which 6 were waited for; matrix products, arithmetic and copies ran while one was open for 12% of the time, Pallas kernels for 0%

commit v1 on v0

v1 whole, which is shorter than its diff:
```python
import functools
import math

import jax
import jax.numpy as jnp
import ml_dtypes
import numpy as np
from jax import lax
from jax.experimental import pallas as pl
from jax.experimental.pallas import tpu as pltpu
from jax.sharding import PartitionSpec as P

BF = jnp.bfloat16
F32 = jnp.float32
TWO_PI = 2.0 * math.pi
CHUNKS = 1
VMEM = 48 * 1024 * 1024


def table(freqs, points, length):
    product = (freqs % length)[:, None] * points[None, :] % length
    angle = np.float32(TWO_PI / length) * product.astype(np.float32)
    return np.cos(angle), np.sin(angle)


def column_table(cells, modes):
    cos, sin = table(np.arange(modes), np.arange(cells), cells)
    width = modes // CHUNKS
    parts = []
    for c in range(CHUNKS):
        parts += [cos[c * width : (c + 1) * width], -sin[c * width : (c + 1) * width]]
    return np.ascontiguousarray(np.concatenate(parts, 0).T).astype(ml_dtypes.bfloat16)


def row_tables(rows, modes, blocks, samples):
    index = np.arange(modes)
    cos, sin = table(np.where(index < modes // 2, index, index - modes), np.arange(rows), rows)
    both = np.stack([cos, sin]).astype(ml_dtypes.bfloat16)
    sub = modes // (blocks * samples)
    local = rows // blocks
    out = np.empty((blocks, samples, 2 * modes, local), ml_dtypes.bfloat16)
    for z in range(blocks):
        part = both[:, :, z * local : (z + 1) * local]
        for s in range(samples):
            order = np.concatenate(
                [
                    np.arange(sub) + sub * ((s ^ j) + samples * ((z + d) % blocks))
                    for d in range(blocks)
                    for j in range(samples)
                ]
            )
            out[z, s] = part[:, order].reshape(2 * modes, local)
    return out


def gelu_slope(value):
    return 0.5 * (1.0 + lax.erf(value * (1.0 / math.sqrt(2.0)))) + value * jnp.exp(-0.5 * value * value) * (
        1.0 / math.sqrt(2.0 * math.pi)
    )


def row_forward(u, row_tab, scale, outs, at):
    modes = row_tab.shape[0] // 2
    blocks = len(outs[0])
    sub = modes // blocks
    for c, parts in enumerate(outs):
        width = u.shape[1] // (2 * len(outs))
        lo = 2 * width * c
        prod = jnp.dot(row_tab, u[:, lo : lo + 2 * width], preferred_element_type=F32)
        real = (prod[:modes, :width] + prod[modes:, width:]) * scale
        imag = (prod[:modes, width:] - prod[modes:, :width]) * scale
        for d, out in enumerate(parts):
            out[at, :, :width] = real[d * sub : (d + 1) * sub].astype(BF)
            out[at, :, width:] = imag[d * sub : (d + 1) * sub].astype(BF)


def row_inverse(parts, row_inv):
    rows = row_inv.shape[0] // 2
    halves = []
    for own, below, above in parts:
        width = own.shape[-1] // 2
        hops = len(below)
        blocks = [own[0]]
        for s in range(hops - 1, -1, -1):
            blocks.append(below[s][0] + above[hops - 1 - s][0])
        prod = jnp.dot(row_inv, jnp.concatenate(blocks, 0), preferred_element_type=F32)
        halves.append((prod[:rows, :width] - prod[rows:, width:]).astype(BF))
        halves.append((prod[:rows, width:] + prod[rows:, :width]).astype(BF))
    return jnp.concatenate(halves, 1)


def lift_kernel(blocks, scale, lw, fields, col, row_tab, lifted, *outs):
    group, rows, cells = lifted.shape
    inputs = fields.shape[0]
    first = pl.program_id(0) * group
    lanes = min(cells, 256)

    def lift_rows(step, _):
        at = pl.ds(pl.multiple_of(step * 16, 16), 16)
        for lo in range(0, cells, lanes):
            f = [fields[j, at, lo : lo + lanes].astype(F32) for j in range(inputs)]
            for c in range(group):
                total = f[0] * lw[0, first + c]
                for j in range(1, inputs):
                    total = total + f[j] * lw[j, first + c]
                lifted[c, at, lo : lo + lanes] = jnp.tanh(total).astype(BF)
        return 0

    lax.fori_loop(0, rows // 16, lift_rows, 0)
    outs = [outs[i : i + blocks] for i in range(0, len(outs), blocks)]
    for c in range(group):
        u = jnp.dot(lifted[c], col[...], preferred_element_type=F32).astype(BF)
        row_forward(u, row_tab[...], scale, outs, c)


def unpack_parts(refs, hops):
    each = 1 + 2 * hops
    return [
        (refs[i], refs[i + 1 : i + 1 + hops], refs[i + 1 + hops : i + each]) for i in range(0, len(refs), each)
    ]


def middle_kernel(blocks, parts, grid_scale, scale, local, cotan, col, col_inv, row_tab, row_inv, *refs):
    n_in = parts * (2 * blocks - 1)
    modes_in, grad, outs = unpack_parts(refs[:n_in], blocks - 1), refs[n_in], refs[n_in + 1 :]
    outs = [outs[i : i + blocks] for i in range(0, len(outs), blocks)]
    rows = grad.shape[1]
    h = row_inverse(modes_in, row_inv[...])
    step = min(rows, 64)
    pieces = []
    for lo in range(0, rows, step):
        grid = jnp.dot(h[lo : lo + step], col_inv[...], preferred_element_type=F32)
        pre = grid * grid_scale + local[0, lo : lo + step].astype(F32)
        g = (cotan[0, 0, lo : lo + step].astype(F32) * gelu_slope(pre)).astype(BF)
        grad[0, lo : lo + step] = g
        pieces.append(jnp.dot(g, col[...], preferred_element_type=F32).astype(BF))
    row_forward(jnp.concatenate(pieces, 0), row_tab[...], scale, outs, 0)


def final_kernel(blocks, parts, grid_scale, lw, fields, back_a, back_b, col_inv, row_inv, *refs):
    modes_in, out = unpack_parts(refs[:-1], blocks - 1), refs[-1]
    inputs, rows, cells = fields.shape
    chan = pl.program_id(0)
    h = row_inverse(modes_in, row_inv[...])
    step = min(rows, 32)
    sums = [jnp.zeros((8, 128), F32) for _ in range(inputs)]
    for lo in range(0, rows, step):
        grid = jnp.dot(h[lo : lo + step], col_inv[...], preferred_element_type=F32)
        total = (
            grid * grid_scale
            + back_a[0, lo : lo + step].astype(F32)
            + back_b[0, lo : lo + step].astype(F32)
        )
        f = [fields[j, lo : lo + step].astype(F32) for j in range(inputs)]
        pre = f[0] * lw[0, chan]
        for j in range(1, inputs):
            pre = pre + f[j] * lw[j, chan]
        t = jnp.tanh(pre)
        total = total * (1.0 - t * t)
        for j in range(inputs):
            prod = f[j] * total
            for a in range(0, step, 8):
                for b in range(0, cells, 128):
                    sums[j] = sums[j] + prod[a : a + 8, b : b + 128]
    for j in range(inputs):
        out[0, j] = sums[j]


def mix_kernel(samples, core, w_keep, w_send, *refs):
    xs, keep, send = refs[:samples], refs[samples], refs[samples + 1]
    width = w_keep.shape[-1]
    ins, outs = w_keep.shape[2], w_keep.shape[3]
    for lo in range(0, width, 128):
        re, im = pl.ds(lo, 128), pl.ds(width + lo, 128)
        xr = [x[0, :, re].astype(F32) for x in xs]
        xi = [x[0, :, im].astype(F32) for x in xs]
        for w, out in ((w_keep, keep), (w_send, send)):
            real = [jnp.zeros((outs, 128), F32) for _ in range(samples)]
            imag = [jnp.zeros((outs, 128), F32) for _ in range(samples)]
            for i in range(ins):
                wr = w[0, 0, i, :, re].astype(F32)
                wi = w[1, 0, i, :, re].astype(F32)
                for s in range(samples):
                    a, b = xr[s][i : i + 1], xi[s][i : i + 1]
                    real[s] = real[s] + (wr * a - wi * b)
                    imag[s] = imag[s] + (wr * b + wi * a)
            for s in range(samples):
                out[s, 0, :, re] = real[s].astype(BF)
                out[s, 0, :, im] = imag[s].astype(BF)


def back_kernel(samples, core, w_own, w_other, g_other, *refs):
    gs, out = refs[:samples], refs[samples]
    width = w_own.shape[-1]
    ins, outs = w_own.shape[2], w_own.shape[3]
    for lo in range(0, width, 128):
        re, im = pl.ds(lo, 128), pl.ds(width + lo, 128)
        gr = [[g[0, :, re].astype(F32) for g in gs], [g_other[s, 0, :, re].astype(F32) for s in range(samples)]]
        gi = [[g[0, :, im].astype(F32) for g in gs], [g_other[s, 0, :, im].astype(F32) for s in range(samples)]]
        real = [[] for _ in range(samples)]
        imag = [[] for _ in range(samples)]
        for i in range(ins):
            w = [
                (w_own[0, 0, i, :, re].astype(F32), w_own[1, 0, i, :, re].astype(F32)),
                (w_other[0, 0, i, :, re].astype(F32), w_other[1, 0, i, :, re].astype(F32)),
            ]
            for s in range(samples):
                r = m = None
                for half in range(2):
                    wr, wi = w[half]
                    a, b = gr[half][s], gi[half][s]
                    r1 = wr * a + wi * b
                    m1 = wr * b - wi * a
                    r, m = (r1, m1) if r is None else (r + r1, m + m1)
                real[s].append(jnp.sum(r, axis=0, keepdims=True))
                imag[s].append(jnp.sum(m, axis=0, keepdims=True))
        for s in range(samples):
            out[s, 0, :, re] = jnp.concatenate(real[s], 0).astype(BF)
            out[s, 0, :, im] = jnp.concatenate(imag[s], 0).astype(BF)


def weight_kernel(samples, parts, core, g_other, *refs):
    g_others = (g_other,) + refs[: parts - 1]
    refs = refs[parts - 1 :]
    out = refs[-1]
    xs = [refs[c * samples : (c + 1) * samples] for c in range(parts)]
    gs = [refs[(parts + c) * samples : (parts + c + 1) * samples] for c in range(parts)]
    ins, half = xs[0][0].shape[1], gs[0][0].shape[1]
    width = xs[0][0].shape[2] // 2
    own = pl.ds(pl.multiple_of(core[0] * half, half), half)
    other = pl.ds(pl.multiple_of((1 - core[0]) * half, half), half)
    for c in range(parts):
        for lo in range(0, width, 128):
            re, im, to = pl.ds(lo, 128), pl.ds(width + lo, 128), pl.ds(c * width + lo, 128)
            xr = [x[0, :, re].astype(F32) for x in xs[c]]
            xi = [x[0, :, im].astype(F32) for x in xs[c]]
            for where in (own, other):
                if where is own:
                    gr = [g[0, :, re].astype(F32) for g in gs[c]]
                    gi = [g[0, :, im].astype(F32) for g in gs[c]]
                else:
                    gr = [g_others[c][s, 0, :, re].astype(F32) for s in range(samples)]
                    gi = [g_others[c][s, 0, :, im].astype(F32) for s in range(samples)]
                for i in range(ins):
                    real = imag = None
                    for s in range(samples):
                        a, b = xr[s][i : i + 1], xi[s][i : i + 1]
                        r1 = gr[s] * a + gi[s] * b
                        m1 = gi[s] * a - gr[s] * b
                        real, imag = (r1, m1) if real is None else (real + r1, imag + m1)
                    out[0, 0, i, where, to] = real.astype(BF)
                    out[1, 0, i, where, to] = imag.astype(BF)


def call(body, grid, ins, outs, flops, transcendentals=0, prefetch=None):
    scalars = 0 if prefetch is None else 1

    def spec(block, index):
        if block is None:
            return pl.BlockSpec(memory_space=pltpu.SMEM)
        return pl.BlockSpec(block, index)

    moved = sum(a.size * a.dtype.itemsize for a, _, _ in ins) + sum(
        math.prod(s) * jnp.dtype(t).itemsize for s, t, _, _ in outs
    )
    got = pl.pallas_call(
        body,
        grid_spec=pltpu.PrefetchScalarGridSpec(
            num_scalar_prefetch=scalars,
            grid=grid,
            in_specs=[spec(b, i) for _, b, i in ins],
            out_specs=[spec(b, i) for _, _, b, i in outs],
        ),
        out_shape=[jax.ShapeDtypeStruct(s, t) for s, t, _, _ in outs],
        compiler_params=pltpu.CompilerParams(vmem_limit_bytes=VMEM),
        cost_estimate=pl.CostEstimate(flops=int(flops), bytes_accessed=int(moved), transcendentals=int(transcendentals)),
    )(*(() if prefetch is None else (prefetch,)), *[a for a, _, _ in ins])
    return got


def after(value, *earlier):
    return lax.optimization_barrier((value, *earlier))[0]


def chain_sum(parts):
    hops = len(parts) - 1
    blocks = hops + 1
    below = above = None
    for t in range(hops):
        up, down = parts[hops - t], parts[t + 1]
        if t:
            up = (up.astype(F32) + below.astype(F32)).astype(BF)
            down = (down.astype(F32) + above.astype(F32)).astype(BF)
        below = lax.ppermute(up, "blk", [(z, z + 1) for z in range(t + 1)])
        above = lax.ppermute(down, "blk", [(blocks - 1 - z, blocks - 2 - z) for z in range(t + 1)])
    return parts[0], below, above


def chain_gather(own, blocks):
    below, above = [], []
    up = down = own
    for t in range(blocks - 1):
        up = lax.ppermute(up, "blk", [(z, z + 1) for z in range(t, blocks - 1)])
        down = lax.ppermute(down, "blk", [(blocks - 1 - z, blocks - 2 - z) for z in range(t, blocks - 1)])
        below.append(up)
        above.append(down)
    return below, above


def swap_samples(pieces):
    n = len(pieces)
    return [pieces[0]] + [lax.ppermute(pieces[j], "dp", [(i, i ^ j) for i in range(n)]) for j in range(1, n)]


def swap_cores(value):
    return lax.ppermute(value, "chan", [(0, 1), (1, 0)])


def to_modes(parts, samples):
    own, below, above = chain_sum(parts)
    total = (own.astype(F32) + below.astype(F32) + above.astype(F32)).astype(BF)
    total = total.transpose(1, 0, 2)
    sub = total.shape[0] // samples
    return swap_samples([total[j * sub : (j + 1) * sub] for j in range(samples)])


def from_modes(pieces, blocks):
    own = jnp.concatenate(swap_samples(pieces), 0).transpose(1, 0, 2)
    below, above = chain_gather(own, blocks)
    return [own, *below, *above]


def all_sum(value, axes):
    for axis in axes:
        n = lax.axis_size(axis)
        step = 1
        while step < n:
            value = value + lax.ppermute(value, axis, [(i, i ^ step) for i in range(n)])
            step *= 2
    return value


def per_device(fields, lift_weight, local_weight, spectral_weight, cotangent):
    blocks = lax.axis_size("blk")
    samples = lax.axis_size("dp")
    sample = fields[0]
    inputs, rows, cells = sample.shape
    chans = cotangent.shape[1]
    mode_dev = spectral_weight.shape[1]
    half = spectral_weight.shape[3] // 2
    freqs = spectral_weight.shape[4]
    width = freqs // CHUNKS
    modes = mode_dev * blocks * samples
    sub = modes // blocks
    all_rows = rows * blocks
    z, s, core = lax.axis_index("blk"), lax.axis_index("dp"), lax.axis_index("chan")
    core_ref = core.astype(jnp.int32)[None]
    unit_scale = 1.0 / math.sqrt(all_rows * cells)
    norm_scale = 1.0 / math.sqrt(samples * all_rows * cells)

    col = jnp.asarray(column_table(cells, freqs))
    col_inv = jnp.asarray(np.ascontiguousarray(column_table(cells, freqs).T))
    row_tab = lax.dynamic_slice(
        jnp.asarray(row_tables(all_rows, modes, blocks, samples)), (z, s, 0, 0), (1, 1, 2 * modes, rows)
    )[0, 0]
    row_inv = row_tab.reshape(2, modes, rows).transpose(0, 2, 1).reshape(2 * rows, modes)
    own_lw = lax.dynamic_slice_in_dim(lift_weight.astype(F32), core * chans, chans, 1)

    def whole(a):
        return (a, a.shape, lambda i, *_: (0,) * a.ndim)

    def channel(a, n=1):
        return (a, (n, *a.shape[1:]), lambda i, *_: (i,) + (0,) * (a.ndim - 1))

    def part_outs(n):
        return [
            ((chans, sub, 2 * width), BF, (n, sub, 2 * width), lambda i, *_: (i, 0, 0))
            for _ in range(CHUNKS * blocks)
        ]

    matrix = chans * rows * 4 * freqs * (cells + 2 * modes)
    group = 2 if chans % 2 == 0 else 1
    lifted, *shares = call(
        functools.partial(lift_kernel, blocks, unit_scale),
        (chans // group,),
        [(own_lw, None, None), whole(sample), whole(col), whole(row_tab)],
        [(((chans, rows, cells)), BF, (group, rows, cells), lambda i, *_: (i, 0, 0)), *part_outs(group)],
        matrix,
        chans * rows * cells,
    )
    lifted_other = swap_cores(lifted)

    def weight_half(part, other):
        return (
            spectral_weight,
            (2, 1, chans, half, width),
            lambda i, c, part=part, other=other: (0, i, 0, (1 - c[0]) if other else c[0], part),
        )

    def row_mode(a):
        return (a, (1, *a.shape[1:]), lambda i, *_: (i, 0, 0))

    def stacked(a):
        return (a, (samples, 1, *a.shape[2:]), lambda i, *_: (0, i, 0, 0))

    mix_flops = 8 * samples * mode_dev * chans * 2 * half * width
    field_modes, out_parts = [], []
    for part in range(CHUNKS):
        mine = shares[part * blocks : (part + 1) * blocks]
        if part:
            mine = list(lax.optimization_barrier((*mine, *field_modes[-1]))[:blocks])
        xs = to_modes(mine, samples)
        field_modes.append(xs)
        shape = (samples, mode_dev, half, 2 * width)
        keep, send = call(
            functools.partial(mix_kernel, samples),
            (mode_dev,),
            [weight_half(part, False), weight_half(part, True), *[row_mode(x) for x in xs]],
            [(shape, BF, (samples, 1, half, 2 * width), lambda i, *_: (0, i, 0, 0))] * 2,
            mix_flops,
            prefetch=core_ref,
        )
        total = (keep.astype(F32) + swap_cores(send).astype(F32)).astype(BF)
        out_parts += from_modes([total[j] for j in range(samples)], blocks)

    own_rows = lax.dynamic_slice_in_dim(local_weight, core * chans, chans, 0)
    other_rows = lax.dynamic_slice_in_dim(local_weight, (1 - core) * chans, chans, 0)
    local = jnp.einsum("iry,io->ory", lifted, own_rows, preferred_element_type=F32) + jnp.einsum(
        "iry,io->ory", lifted_other, other_rows, preferred_element_type=F32
    )

    grad_z, *shares = call(
        functools.partial(middle_kernel, blocks, CHUNKS, 2.0 * unit_scale, 2.0 * unit_scale),
        (chans,),
        [
            channel(local),
            (cotangent, (1, 1, rows, cells), lambda i, *_: (0, i, 0, 0)),
            whole(col),
            whole(col_inv),
            whole(row_tab),
            whole(row_inv),
            *[channel(a) for a in out_parts],
        ],
        [((chans, rows, cells), BF, (1, rows, cells), lambda i, *_: (i, 0, 0)), *part_outs(1)],
        2 * matrix,
        3 * chans * rows * cells,
    )

    back_a = jnp.einsum("ory,io->iry", grad_z, own_rows, preferred_element_type=F32).astype(BF)
    back_b = swap_cores(
        jnp.einsum("ory,io->iry", grad_z, other_rows, preferred_element_type=F32).astype(BF)
    )
    term_own = jnp.einsum("iry,ory->io", lifted, grad_z, preferred_element_type=F32)
    term_other = jnp.einsum("iry,ory->io", lifted_other, grad_z, preferred_element_type=F32)
    terms = jnp.zeros(local_weight.shape, F32)
    terms = lax.dynamic_update_slice_in_dim(terms, term_own, core * chans, 0)
    terms = lax.dynamic_update_slice_in_dim(terms, term_other, (1 - core) * chans, 0)
    local_grad = all_sum(terms * norm_scale, ("dp", "blk"))

    grad_modes, grad_others, back_parts = [], [], []
    for part in range(CHUNKS):
        mine = shares[part * blocks : (part + 1) * blocks]
        if part:
            mine = list(lax.optimization_barrier((*mine, *grad_modes[-1]))[:blocks])
        gs = to_modes(mine, samples)
        grad_modes.append(gs)
        other = swap_cores(jnp.stack(gs))
        grad_others.append(other)
        shape = (samples, mode_dev, chans, 2 * width)
        (back,) = call(
            functools.partial(back_kernel, samples),
            (mode_dev,),
            [weight_half(part, False), weight_half(part, True), stacked(other), *[row_mode(g) for g in gs]],
            [(shape, BF, (samples, 1, chans, 2 * width), lambda i, *_: (0, i, 0, 0))],
            mix_flops,
            prefetch=core_ref,
        )
        back_parts += from_modes([back[j] for j in range(samples)], blocks)

    (spectral_grad,) = call(
        functools.partial(weight_kernel, samples, CHUNKS),
        (mode_dev,),
        [
            *[stacked(a) for a in grad_others],
            *[row_mode(x) for xs in field_modes for x in xs],
            *[row_mode(g) for gs in grad_modes for g in gs],
        ],
        [
            (
                (2, mode_dev, chans, 2 * half, freqs),
                BF,
                (2, 1, chans, 2 * half, freqs),
                lambda i, *_: (0, i, 0, 0, 0),
            )
        ],
        mix_flops * CHUNKS,
        prefetch=core_ref,
    )

    (sums,) = call(
        functools.partial(final_kernel, blocks, CHUNKS, unit_scale),
        (chans,),
        [
            (own_lw, None, None),
            whole(sample),
            channel(back_a),
            channel(back_b),
            whole(col_inv),
            whole(row_inv),
            *[channel(a) for a in back_parts],
        ],
        [((chans, inputs, 8, 128), F32, (1, inputs, 8, 128), lambda i, *_: (i, 0, 0, 0))],
        matrix,
        chans * rows * cells,
    )
    lift_own = all_sum(jnp.sum(sums, axis=(2, 3)).T * norm_scale, ("dp", "blk"))
    lift_other = swap_cores(lift_own)
    lift_grad = jnp.where(
        core == 0, jnp.concatenate([lift_own, lift_other], 1), jnp.concatenate([lift_other, lift_own], 1)
    )
    return (spectral_grad, local_grad, lift_grad)


def solution(mesh):
    in_specs = (
        P("dp", "parts", "blk", None),
        P("parts", None),
        P("parts", "chan"),
        P("parts", ("blk", "dp"), "chan", None, None),
        P("dp", "chan", "blk", "parts"),
    )
    out_specs = (
        P("parts", ("blk", "dp"), "chan", None, None),
        P("parts", "chan"),
        P("parts", None),
    )
    return jax.shard_map(per_device, mesh=mesh, in_specs=in_specs, out_specs=out_specs, check_vma=False)
```

time: 1080 us -> 635 us (0.59)
  blocking collectives: 304 us -> 0 us
  other arithmetic: 194 us -> 45.4 us
  Pallas kernels: 0 us -> 139 us
  local copies, waits for them, and re-layouts: 139 us -> 36.9 us
  matrix products: 173 us -> 97.5 us
  starting transfers between devices: 29 us -> 86.8 us
  between operations: 14.7 us -> 1.45 us
    ppermute x0 -> x49, waiting for transfers between devices: none -> 219 us  [the longest x6 104 us: chain_sum(): below = lax.ppermute(up, 'blk', [(z, z + 1) for z in range(t + 1)])]
    all_to_all x5 -> x0, waiting for transfers between devices: 193 us -> none  [the longest x1 88.6 us: to_modes(): lax.all_to_all(column_part, 'blk', split_axis=0, concat_axis=2, tiled=True)]
    all_to_all x3 -> x0, blocking collectives: 160 us -> none  [the longest x1 96.2 us: to_modes(): lax.all_to_all(column_part, 'blk', split_axis=0, concat_axis=2, tiled=True)]
    psum x2 -> x0, blocking collectives: 144 us -> none  [the longest x1 98.3 us: per_device(): local_grad = lax.psum(local_term, ('blk', 'dp'))]
    pallas_call x0 -> x6, Pallas kernels: none -> 139 us  [call(): pl.pallas_call(body, grid_spec=pltpu.PrefetchScalarGridSpec(num_scalar_pr...]
    ppermute x0 -> x49, starting transfers between devices: none -> 86.8 us  [the longest x6 31.6 us: chain_sum(): below = lax.ppermute(up, 'blk', [(z, z + 1) for z in range(t + 1)])]
    dot_general x14 -> x6, matrix products: 173 us -> 97.5 us  [the longest x1 23.6 us: per_device(): jnp.einsum('iry,ory->io', lifted_other, grad_z, preferred_element_type=F32)]
    all_to_all x8 -> x0, other arithmetic: 68.5 us -> none  [trade_modes(): lax.all_to_all(packed, ('blk', 'dp'), split_axis=0, concat_axis=0, tiled=...]
  transfers between devices with their start and end apart: 7 -> 49, of which waited for: 6 -> 29; matrix products, arithmetic and copies ran while one was open for 12% -> 27% of each run, Pallas kernels for 0% -> 12%
where the time goes in v1:
time: 635 us; the launch traced here: 626 us
  waiting for transfers between devices  219 us (34%)
  Pallas kernels  139 us (22%)
  matrix products  97.5 us (15%)
  starting transfers between devices  86.8 us (14%)
  other arithmetic  45.4 us (7%)
  local copies, waits for them, and re-layouts  36.9 us (6%)
    pallas_call x6, Pallas kernels, call(): pl.pallas_call(body, grid_spec=pltpu.PrefetchScalarGridSpec(num_scalar_pr...  139 us
    ppermute x6, waiting for transfers between devices, chain_sum(): below = lax.ppermute(up, 'blk', [(z, z + 1) for z in range(t + 1)])  104 us
    ppermute x12, waiting for transfers between devices, swap_samples(): lax.ppermute(pieces[j], 'dp', [(i, i ^ j) for i in range(n)])  41.3 us
    add x1, other arithmetic, per_device(): jnp.einsum('iry,io->ory', lifted, own_rows, preferred_element_type=F32)  34 us
    ppermute x6, starting transfers between devices, chain_sum(): below = lax.ppermute(up, 'blk', [(z, z + 1) for z in range(t + 1)])  31.6 us
    dot_general x1, matrix products, per_device(): jnp.einsum('iry,ory->io', lifted_other, grad_z, preferred_element_type=F32)  23.6 us
    ppermute x6, waiting for transfers between devices, chain_gather(): up = lax.ppermute(up, 'blk', [(z, z + 1) for z in range(t, blocks - 1)])  21.1 us
    dot_general x1, matrix products, per_device(): jnp.einsum('iry,ory->io', lifted, grad_z, preferred_element_type=F32)  20.9 us
  transfers between devices with their start and end apart: 49, of which 29 were waited for; matrix products, arithmetic and copies ran while one was open for 27% of the time, Pallas kernels for 12%

profile of v1, /device:TPU:0, one launch (start us, length us, event | category | flops | bytes accessed | tf_op | source)
XLA Modules:
  0.0 625.7 jit_solution(9882813183469026744)
XLA Ops:
  3.6 20.4 %shard_map.103 = (bf16[16,256,1024]{2,1,0:T(8,128)(2,1)}, bf16[16,64,512]{2,1,0:T(8,128)(2,1)S(1)}, bf16[16,64,512]{2,1,0:T(8,128)(2,1)S(1)}, bf16[16,64,512]{2,1,0:T(8,128)(2,1)S(1)}, bf16[16,64,512]{2,1,0:T(8,128)(2,1)S(1)}) custom-call(f32[4,16]{1,0:T(4,128)S(1)} %constant_dynamic-slice_fusion.1.lw, bf16[4,256,1024]{2,1,0:T(8,128)(2,1)} %bitcast.68, ...), custom_call_target="tpu_custom_call" | custom-call | flops 6442450944 | bytes 15991040 | tf_op jit(solution)/shard_map/pallas_call | solution.py:266
  24.6 5.0 collective-permute-start.1
  31.0 20.9 %collective-permute-done.1 = bf16[16,64,512]{2,0,1:T(8,128)(2,1)S(1)} collective-permute-done((bf16[16,64,512]{2,0,1:T(8,128)(2,1)S(1)}, bf16[16,64,512]{2,0,1:T(8,128)(2,1)S(1)}, u32[]{:S(2)}, u32[]{:S(2)}) %collective-permute-start.1) | collective-permute-done | bytes 1048608 | tf_op jit(solution)/shard_map/ppermute | solution.py:294
  53.7 5.0 collective-permute-start.2
  60.9 19.4 %collective-permute-done.2 = bf16[16,64,512]{2,0,1:T(8,128)(2,1)S(1)} collective-permute-done((bf16[16,64,512]{2,0,1:T(8,128)(2,1)S(1)}, bf16[16,64,512]{2,0,1:T(8,128)(2,1)S(1)}, u32[]{:S(2)}, u32[]{:S(2)}) %collective-permute-start.2) | collective-permute-done | bytes 1048608 | tf_op jit(solution)/shard_map/ppermute | solution.py:294
  81.0 7.0 %collective-permute-start.3 = (bf16[16,64,512]{2,0,1:T(8,128)(2,1)S(1)}, bf16[16,64,512]{2,0,1:T(8,128)(2,1)S(1)}, u32[]{:S(2)}, u32[]{:S(2)}) collective-permute-start(bf16[16,64,512]{2,0,1:T(8,128)(2,1)S(1)} %add_convert_fusion.6), channel_id=1, source_target_pairs={{0,8},{8,16},{16,24},{1,9},{9,17},{17,25},{2,10},{10,18},{18,26},{... | collective-permute-start | bytes 3145736 | tf_op jit(solution)/shard_map/ppermute | solution.py:294
  88.0 18.8 %collective-permute-done.6 = bf16[16,64,512]{2,0,1:T(8,128)(2,1)S(1)} collective-permute-done((bf16[16,64,512]{2,0,1:T(8,128)(2,1)S(1)}, bf16[16,64,512]{2,0,1:T(8,128)(2,1)S(1)}, u32[]{:S(2)}, u32[]{:S(2)}) %collective-permute-start.6) | collective-permute-done | bytes 1048608 | tf_op jit(solution)/shard_map/ppermute | solution.py:295
  113.5 4.9 collective-permute-done.7.refs_1_
  118.4 4.0 collective-permute-done.8.refs_2_
  122.4 14.7 %shard_map.104 = (bf16[4,16,16,512]{3,2,1,0:T(8,128)(2,1)S(1)}, bf16[4,16,16,512]{3,2,1,0:T(8,128)(2,1)S(1)}) custom-call(s32[1]{0:T(128)} %bitcast.core, bf16[2,16,16,32,256]{4,3,2,1,0:T(8,128)(2,1)} %w_other.1, bf16[2,16,16,32,256]{4,3,2,1,0:T(8,128)(2,1)} %w_other.1, bf16[16,16,512]{2,1,0:T(8,128)(2,1)S(1)} %get-tuple-element.50.refs_0_, ...), custom_call_target="tpu_custom_call" | custom-call | flops 67108864 | bytes 19922944 | tf_op jit(solution)/shard_map/pallas_call | solution.py:266
  137.8 2.6 collective-permute-done.10
  145.0 6.6 %collective-permute-done.13 = bf16[16,16,512]{2,0,1:T(8,128)(2,1)S(1)} collective-permute-done((bf16[16,16,512]{2,0,1:T(8,128)(2,1)S(1)}, bf16[16,16,512]{2,0,1:T(8,128)(2,1)S(1)}, u32[]{:S(2)}, u32[]{:S(2)}) %collective-permute-start.13) | collective-permute-done | bytes 262176 | tf_op jit(solution)/shard_map/ppermute | solution.py:312
  151.6 4.8 collective-permute-done.12
  156.6 4.5 collective-permute-start.14
  162.4 21.1 %collective-permute-done.14.refs_1_ = bf16[16,64,512]{2,1,0:T(8,128)(2,1)S(1)} collective-permute-done((bf16[16,64,512]{2,1,0:T(8,128)(2,1)S(1)}, bf16[16,64,512]{2,1,0:T(8,128)(2,1)S(1)}, u32[]{:S(2)}, u32[]{:S(2)}) %collective-permute-start.14) | collective-permute-done | bytes 1048608 | tf_op jit(solution)/shard_map/ppermute | solution.py:303
  185.1 2.7 collective-permute-done.17.refs_4_
  189.4 15.0 %fusion.6 = f32[16,256,1024]{2,0,1:T(8,128)} fusion(bf16[16,256,1024]{2,1,0:T(8,128)(2,1)} %get-tuple-element.15, bf16[32,16]{0,1:T(8,128)(2,1)S(1)} %copy-done, s32[]{:T(128)S(6)} %select_n.23), kind=kOutput, calls=%fused_computation.9 | convolution fusion | flops 134217728 | bytes 25166852 | tf_op jit(solution)/shard_map/iry,io->ory/dot_general | solution.py:428
  205.1 9.6 %collective-permute-done.18.refs_5_ = bf16[16,64,512]{2,1,0:T(8,128)(2,1)} collective-permute-done((bf16[16,64,512]{2,1,0:T(8,128)(2,1)}, bf16[16,64,512]{2,1,0:T(8,128)(2,1)}, u32[]{:S(2)}, u32[]{:S(2)}) %collective-permute-start.18) | collective-permute-done | bytes 1048608 | tf_op jit(solution)/shard_map/ppermute | solution.py:304
  216.0 14.9 %fusion.2 = f32[16,256,1024]{2,0,1:T(8,128)} fusion(bf16[16,256,1024]{2,1,0:T(8,128)(2,1)} %collective-permute-done, bf16[32,16]{0,1:T(8,128)(2,1)S(1)} %copy-done, s32[]{:T(128)S(6)} %select_n.26), kind=kOutput, calls=%fused_computation.5 | convolution fusion | flops 134217728 | bytes 25166852 | tf_op jit(solution)/shard_map/iry,io->ory/dot_general | solution.py:428
  230.9 34.0 %copy_add_fusion.local = f32[16,256,1024]{2,1,0:T(8,128)} fusion(f32[16,256,1024]{2,0,1:T(8,128)} %fusion.2, f32[16,256,1024]{2,0,1:T(8,128)} %fusion.6), kind=kLoop, calls=%fused_computation.2 | loop fusion | flops 4194304 | bytes 50331648 | tf_op jit(solution)/shard_map/add | solution.py:428
  266.2 42.4 %shard_map.105 = (bf16[16,256,1024]{2,1,0:T(8,128)(2,1)}, bf16[16,64,512]{2,1,0:T(8,128)(2,1)S(1)}, bf16[16,64,512]{2,1,0:T(8,128)(2,1)S(1)}, bf16[16,64,512]{2,1,0:T(8,128)(2,1)S(1)}, bf16[16,64,512]{2,1,0:T(8,128)(2,1)S(1)}) custom-call(f32[16,256,1024]{2,1,0:T(8,128)} %copy_add_fusion.local, bf16[1,16,256,1024]{3,2,1,0:T(8,128)(2,1)} %cotan.1, ...), custom_call_target="tpu_custom_call" | custom-call | flops 12884901888 | bytes 47710208 | tf_op jit(solution)/shard_map/pallas_call | solution.py:266
  309.2 4.9 collective-permute-start.20
  315.4 19.1 %collective-permute-done.20 = bf16[16,64,512]{2,0,1:T(8,128)(2,1)S(1)} collective-permute-done((bf16[16,64,512]{2,0,1:T(8,128)(2,1)S(1)}, bf16[16,64,512]{2,0,1:T(8,128)(2,1)S(1)}, u32[]{:S(2)}, u32[]{:S(2)}) %collective-permute-start.20) | collective-permute-done | bytes 1048608 | tf_op jit(solution)/shard_map/ppermute | solution.py:294
  336.8 11.8 %fusion.8 = bf16[16,256,1024]{2,0,1:T(8,128)(2,1)} fusion(bf16[16,256,1024]{2,1,0:T(8,128)(2,1)S(1)} %copy-done.15, bf16[32,16]{0,1:T(8,128)(2,1)S(1)} %copy-done, s32[]{:T(128)S(6)} %select_n.26), kind=kOutput, calls=%fused_computation.11 | convolution fusion | flops 134217728 | bytes 16778244 | tf_op jit(solution)/shard_map/ory,io->iry/dot_general | solution.py:451
  348.6 11.4 %copy.198 = bf16[16,256,1024]{2,1,0:T(8,128)(2,1)} copy(bf16[16,256,1024]{2,0,1:T(8,128)(2,1)} %fusion.8) | data formatting | bytes 16777216 | tf_op jit(solution)/shard_map/ory,io->iry/dot_general | solution.py:451
  360.0 5.0 collective-permute-start.21
  367.1 20.9 %collective-permute-done.21 = bf16[16,64,512]{2,0,1:T(8,128)(2,1)S(1)} collective-permute-done((bf16[16,64,512]{2,0,1:T(8,128)(2,1)S(1)}, bf16[16,64,512]{2,0,1:T(8,128)(2,1)S(1)}, u32[]{:S(2)}, u32[]{:S(2)}) %collective-permute-start.21) | collective-permute-done | bytes 1048608 | tf_op jit(solution)/shard_map/ppermute | solution.py:294
  388.8 4.6 collective-permute-start.22
  393.8 21.8 %collective-permute-done.22 = bf16[16,64,512]{2,0,1:T(8,128)(2,1)S(1)} collective-permute-done((bf16[16,64,512]{2,0,1:T(8,128)(2,1)S(1)}, bf16[16,64,512]{2,0,1:T(8,128)(2,1)S(1)}, u32[]{:S(2)}, u32[]{:S(2)}) %collective-permute-start.22) | collective-permute-done | bytes 1048608 | tf_op jit(solution)/shard_map/ppermute | solution.py:294
  420.2 6.7 %collective-permute-done.28.refs_7_.refs_3_ = bf16[16,16,512]{2,1,0:T(8,128)(2,1)S(1)} collective-permute-done((bf16[16,16,512]{2,1,0:T(8,128)(2,1)S(1)}, bf16[16,16,512]{2,1,0:T(8,128)(2,1)S(1)}, u32[]{:S(2)}, u32[]{:S(2)}) %collective-permute-start.28) | collective-permute-done | bytes 262176 | tf_op jit(solution)/shard_map/ppermute | solution.py:312
  426.9 3.4 collective-permute-done.27.refs_6_.refs_2_
  430.5 2.6 collective-permute-done.29.g_other
  433.2 16.0 %shard_map.107 = bf16[4,16,16,512]{3,2,1,0:T(8,128)(2,1)S(1)} custom-call(s32[1]{0:T(128)} %bitcast.core, bf16[2,16,16,32,256]{4,3,2,1,0:T(8,128)(2,1)} %w_other.1, bf16[2,16,16,32,256]{4,3,2,1,0:T(8,128)(2,1)} %w_other.1, bf16[4,16,16,512]{3,2,1,0:T(8,128)(2,1)S(1)} %collective-permute-done.29.g_other, ...), custom_call_target="tpu_custom_call" | custom-call | flops 67108864 | bytes 19922944 | tf_op jit(solution)/shard_map/pallas_call | solution.py:266
  453.6 6.0 collective-permute-done.37
  459.6 4.8 collective-permute-done.36
  464.5 5.4 collective-permute-start.38
  471.6 20.9 %fusion.18 = f32[16,16]{0,1:T(8,128)S(1)} fusion(bf16[16,256,1024]{2,1,0:T(8,128)(2,1)S(1)} %bitcast.67, bf16[16,256,1024]{2,1,0:T(8,128)(2,1)} %get-tuple-element.15), kind=kOutput, calls=%fused_computation.32 | convolution fusion | flops 134217728 | bytes 16778240 | tf_op jit(solution)/shard_map/iry,ory->io/dot_general | solution.py:453
  494.4 2.3 collective-permute-done.41.refs_4_
  497.9 23.6 %fusion.23 = f32[16,16]{0,1:T(8,128)S(1)} fusion(bf16[16,256,1024]{2,1,0:T(8,128)(2,1)} %get-tuple-element.26, bf16[16,256,1024]{2,1,0:T(8,128)(2,1)} %collective-permute-done), kind=kOutput, calls=%fused_computation.33 | convolution fusion | flops 134217728 | bytes 16778240 | tf_op jit(solution)/shard_map/iry,ory->io/dot_general | solution.py:454
  527.2 2.3 collective-permute-done.30
  530.8 11.2 %fusion.10 = bf16[16,256,1024]{2,0,1:T(8,128)(2,1)} fusion(bf16[16,256,1024]{2,1,0:T(8,128)(2,1)} %get-tuple-element.26, bf16[32,16]{0,1:T(8,128)(2,1)S(1)} %copy-done, s32[]{:T(128)S(6)} %select_n.23), kind=kOutput, calls=%fused_computation.13 | convolution fusion | flops 134217728 | bytes 16778244 | tf_op jit(solution)/shard_map/ory,io->iry/dot_general | solution.py:449
  542.0 11.5 %copy.199.back_a = bf16[16,256,1024]{2,1,0:T(8,128)(2,1)} copy(bf16[16,256,1024]{2,0,1:T(8,128)(2,1)} %fusion.10) | data formatting | bytes 16777216 | tf_op jit(solution)/shard_map/ory,io->iry/dot_general | solution.py:449
  553.5 3.5 collective-permute-start.32
  559.3 33.1 %shard_map.108 = f32[16,4,8,128]{3,2,1,0:T(8,128)S(1)} custom-call(f32[4,16]{1,0:T(4,128)S(1)} %constant_dynamic-slice_fusion.1.lw, bf16[4,256,1024]{2,1,0:T(8,128)(2,1)} %bitcast.69, bf16[16,256,1024]{2,1,0:T(8,128)(2,1)} %copy.199.back_a, bf16[16,256,1024]{2,1,0:T(8,128)(2,1)} %collective-permute-done.34.back_b, bf16[512,1024]{1,0:T(8,128)(2,1)S(1)} %copy-done.10, ...), custom_call_target="tpu_custom_call" | custom-call | flops 6442450944 | bytes 27787520 | tf_op jit(solution)/shard_map/pallas_call | solution.py:266
  598.7 2.9 collective-permute-done.45
  602.5 2.7 collective-permute-done.46
  607.4 2.4 collective-permute-done.47
  612.6 12.1 %shard_map.106 = bf16[2,16,16,32,256]{4,3,2,1,0:T(8,128)(2,1)} custom-call(s32[1]{0:T(128)} %bitcast.core, bf16[4,16,16,512]{3,2,1,0:T(8,128)(2,1)S(1)} %collective-permute-done.29.g_other, bf16[16,16,512]{2,1,0:T(8,128)(2,1)S(1)} %get-tuple-element.50.refs_0_, bf16[16,16,512]{2,1,0:T(8,128)(2,1)S(1)} %copy-done.2, bf16[16,16,512]{2,1,0:T(8,128)(2,1)S(1)} %copy-done.4, ...), custom_call_target="tpu_custom_call" | custom-call | flops 67108864 | bytes 11534336 | tf_op jit(solution)/shard_map/pallas_call | solution.py:266
  (156 shorter events, 72.9 us)
Async XLA Ops:
  24.6 27.3 %collective-permute-start.1 = (bf16[16,64,512]{2,0,1:T(8,128)(2,1)S(1)}, bf16[16,64,512]{2,0,1:T(8,128)(2,1)S(1)}, u32[]{:S(2)}, u32[]{:S(2)}) collective-permute-start(bf16[16,64,512]{2,0,1:T(8,128)(2,1)S(1)} %copy.118), channel_id=1, source_target_pairs={{0,8},{1,9},{2,10},{3,11},{4,12},{5,13},{6,14},{7,15}} | collective-permute-start | bytes 3145736 | tf_op jit(solution)/shard_map/ppermute | solution.py:294
  30.2 21.8 %collective-permute-start.4 = (bf16[16,64,512]{2,0,1:T(8,128)(2,1)S(1)}, bf16[16,64,512]{2,0,1:T(8,128)(2,1)S(1)}, u32[]{:S(2)}, u32[]{:S(2)}) collective-permute-start(bf16[16,64,512]{2,0,1:T(8,128)(2,1)S(1)} %copy.116), channel_id=1, source_target_pairs={{24,16},{25,17},{26,18},{27,19},{28,20},{29,21},{30,22},{31,23}} | collective-permute-start | bytes 3145736 | tf_op jit(solution)/shard_map/ppermute | solution.py:295
  30.9 185.1 %collective-permute-start = (bf16[16,256,1024]{2,1,0:T(8,128)(2,1)}, bf16[16,256,1024]{2,1,0:T(8,128)(2,1)}, u32[]{:S(2)}, u32[]{:S(2)}) collective-permute-start(bf16[16,256,1024]{2,1,0:T(8,128)(2,1)} %get-tuple-element.15), channel_id=1, source_target_pairs={{0,1},{1,0},{2,3},{3,2},{4,5},{5,4},{6,7},{7,6},{8,9},{9,8},{10,11... | collective-permute-start | bytes 25165832 | tf_op jit(solution)/shard_map/ppermute | solution.py:316
  53.0 5.8 collective-permute-start.5
  53.7 26.5 %collective-permute-start.2 = (bf16[16,64,512]{2,0,1:T(8,128)(2,1)S(1)}, bf16[16,64,512]{2,0,1:T(8,128)(2,1)S(1)}, u32[]{:S(2)}, u32[]{:S(2)}) collective-permute-start(bf16[16,64,512]{2,0,1:T(8,128)(2,1)S(1)} %get-tuple-element.51), channel_id=1, source_target_pairs={{0,8},{8,16},{1,9},{9,17},{2,10},{10,18},{3,11},{11,19},{4,12},{12... | collective-permute-start | bytes 3145736 | tf_op jit(solution)/shard_map/ppermute | solution.py:294
  59.6 47.3 %collective-permute-start.6 = (bf16[16,64,512]{2,0,1:T(8,128)(2,1)S(1)}, bf16[16,64,512]{2,0,1:T(8,128)(2,1)S(1)}, u32[]{:S(2)}, u32[]{:S(2)}) collective-permute-start(bf16[16,64,512]{2,0,1:T(8,128)(2,1)S(1)} %add_convert_fusion.5), channel_id=1, source_target_pairs={{24,16},{16,8},{8,0},{25,17},{17,9},{9,1},{26,18},{18,10},{10,2},{... | collective-permute-start | bytes 3145736 | tf_op jit(solution)/shard_map/ppermute | solution.py:295
  81.0 27.9 %collective-permute-start.3 = (bf16[16,64,512]{2,0,1:T(8,128)(2,1)S(1)}, bf16[16,64,512]{2,0,1:T(8,128)(2,1)S(1)}, u32[]{:S(2)}, u32[]{:S(2)}) collective-permute-start(bf16[16,64,512]{2,0,1:T(8,128)(2,1)S(1)} %add_convert_fusion.6), channel_id=1, source_target_pairs={{0,8},{8,16},{16,24},{1,9},{9,17},{17,25},{2,10},{10,18},{18,26},{... | collective-permute-start | bytes 3145736 | tf_op jit(solution)/shard_map/ppermute | solution.py:294
  109.9 8.5 %collective-permute-start.7 = (bf16[16,16,512]{2,1,0:T(8,128)(2,1)S(1)}, bf16[16,16,512]{2,1,0:T(8,128)(2,1)S(1)}, u32[]{:S(2)}, u32[]{:S(2)}) collective-permute-start(bf16[16,16,512]{2,1,0:T(8,128)(2,1)S(1)} %get-tuple-element.49), channel_id=1, source_target_pairs={{0,2},{2,0},{4,6},{6,4},{1,3},{3,1},{5,7},{7,5},{8,10},{10,8},{12,... | collective-permute-start | bytes 786440 | tf_op jit(solution)/shard_map/ppermute | solution.py:312
  111.5 10.9 %collective-permute-start.8 = (bf16[16,16,512]{2,1,0:T(8,128)(2,1)S(1)}, bf16[16,16,512]{2,1,0:T(8,128)(2,1)S(1)}, u32[]{:S(2)}, u32[]{:S(2)}) collective-permute-start(bf16[16,16,512]{2,1,0:T(8,128)(2,1)S(1)} %get-tuple-element.48), channel_id=1, source_target_pairs={{0,4},{2,6},{4,0},{6,2},{1,5},{3,7},{5,1},{7,3},{8,12},{10,14},{12... | collective-permute-start | bytes 786440 | tf_op jit(solution)/shard_map/ppermute | solution.py:312
  113.0 9.4 %collective-permute-start.9 = (bf16[16,16,512]{2,1,0:T(8,128)(2,1)S(1)}, bf16[16,16,512]{2,1,0:T(8,128)(2,1)S(1)}, u32[]{:S(2)}, u32[]{:S(2)}) collective-permute-start(bf16[16,16,512]{2,1,0:T(8,128)(2,1)S(1)} %get-tuple-element.47), channel_id=1, source_target_pairs={{0,6},{2,4},{4,2},{6,0},{1,7},{3,5},{5,3},{7,1},{8,14},{10,12},{12... | collective-permute-start | bytes 786440 | tf_op jit(solution)/shard_map/ppermute | solution.py:312
  137.7 2.7 collective-permute-start.10
  141.5 10.2 %collective-permute-start.13 = (bf16[16,16,512]{2,0,1:T(8,128)(2,1)S(1)}, bf16[16,16,512]{2,0,1:T(8,128)(2,1)S(1)}, u32[]{:S(2)}, u32[]{:S(2)}) collective-permute-start(bf16[16,16,512]{2,0,1:T(8,128)(2,1)S(1)} %get-tuple-element.44), channel_id=1, source_target_pairs={{0,6},{2,4},{4,2},{6,0},{1,7},{3,5},{5,3},{7,1},{8,14},{10,12},{12... | collective-permute-start | bytes 786440 | tf_op jit(solution)/shard_map/ppermute | solution.py:312
  143.0 13.4 %collective-permute-start.12 = (bf16[16,16,512]{2,0,1:T(8,128)(2,1)S(1)}, bf16[16,16,512]{2,0,1:T(8,128)(2,1)S(1)}, u32[]{:S(2)}, u32[]{:S(2)}) collective-permute-start(bf16[16,16,512]{2,0,1:T(8,128)(2,1)S(1)} %get-tuple-element.45), channel_id=1, source_target_pairs={{0,4},{2,6},{4,0},{6,2},{1,5},{3,7},{5,1},{7,3},{8,12},{10,14},{12... | collective-permute-start | bytes 786440 | tf_op jit(solution)/shard_map/ppermute | solution.py:312
  144.1 12.4 %collective-permute-start.11 = (bf16[16,16,512]{2,0,1:T(8,128)(2,1)S(1)}, bf16[16,16,512]{2,0,1:T(8,128)(2,1)S(1)}, u32[]{:S(2)}, u32[]{:S(2)}) collective-permute-start(bf16[16,16,512]{2,0,1:T(8,128)(2,1)S(1)} %get-tuple-element.46), channel_id=1, source_target_pairs={{0,2},{2,0},{4,6},{6,4},{1,3},{3,1},{5,7},{7,5},{8,10},{10,8},{12,... | collective-permute-start | bytes 786440 | tf_op jit(solution)/shard_map/ppermute | solution.py:312
  156.6 26.9 %collective-permute-start.14 = (bf16[16,64,512]{2,1,0:T(8,128)(2,1)S(1)}, bf16[16,64,512]{2,1,0:T(8,128)(2,1)S(1)}, u32[]{:S(2)}, u32[]{:S(2)}) collective-permute-start(bf16[16,64,512]{2,1,0:T(8,128)(2,1)S(1)} %maximum_bitcast_fusion.refs_0_), channel_id=1, source_target_pairs={{0,8},{8,16},{16,24},{1,9},{9,17},{17,25},{2,10},{10,18},{18,26},{... | collective-permute-start | bytes 3145736 | tf_op jit(solution)/shard_map/ppermute | solution.py:303
  161.1 26.7 %collective-permute-start.17 = (bf16[16,64,512]{2,1,0:T(8,128)(2,1)S(1)}, bf16[16,64,512]{2,1,0:T(8,128)(2,1)}, u32[]{:S(2)}, u32[]{:S(2)}) collective-permute-start(bf16[16,64,512]{2,1,0:T(8,128)(2,1)S(1)} %maximum_bitcast_fusion.refs_0_), channel_id=1, source_target_pairs={{24,16},{16,8},{8,0},{25,17},{17,9},{9,1},{26,18},{18,10},{10,2},{... | collective-permute-start | bytes 3145736 | tf_op jit(solution)/shard_map/ppermute | solution.py:304
  183.5 21.0 %collective-permute-start.15 = (bf16[16,64,512]{2,1,0:T(8,128)(2,1)S(1)}, bf16[16,64,512]{2,1,0:T(8,128)(2,1)}, u32[]{:S(2)}, u32[]{:S(2)}) collective-permute-start(bf16[16,64,512]{2,1,0:T(8,128)(2,1)S(1)} %collective-permute-done.14.refs_1_), channel_id=1, source_target_pairs={{8,16},{16,24},{9,17},{17,25},{10,18},{18,26},{11,19},{19,27},{12,... | collective-permute-start | bytes 3145736 | tf_op jit(solution)/shard_map/ppermute | solution.py:303
  187.7 27.0 %collective-permute-start.18 = (bf16[16,64,512]{2,1,0:T(8,128)(2,1)}, bf16[16,64,512]{2,1,0:T(8,128)(2,1)}, u32[]{:S(2)}, u32[]{:S(2)}) collective-permute-start(bf16[16,64,512]{2,1,0:T(8,128)(2,1)} %collective-permute-done.17.refs_4_), channel_id=1, source_target_pairs={{16,8},{8,0},{17,9},{9,1},{18,10},{10,2},{19,11},{11,3},{20,12},{1... | collective-permute-start | bytes 3145736 | tf_op jit(solution)/shard_map/ppermute | solution.py:304
  204.4 60.4 %collective-permute-start.16 = (bf16[16,64,512]{2,1,0:T(8,128)(2,1)}, bf16[16,64,512]{2,1,0:T(8,128)(2,1)S(1)}, u32[]{:S(2)}, u32[]{:S(2)}) collective-permute-start(bf16[16,64,512]{2,1,0:T(8,128)(2,1)} %collective-permute-done.15.refs_2_), channel_id=1, source_target_pairs={{16,24},{17,25},{18,26},{19,27},{20,28},{21,29},{22,30},{23,31}} | collective-permute-start | bytes 3145736 | tf_op jit(solution)/shard_map/ppermute | solution.py:303
  214.7 50.2 %collective-permute-start.19 = (bf16[16,64,512]{2,1,0:T(8,128)(2,1)}, bf16[16,64,512]{2,1,0:T(8,128)(2,1)S(1)}, u32[]{:S(2)}, u32[]{:S(2)}) collective-permute-start(bf16[16,64,512]{2,1,0:T(8,128)(2,1)} %collective-permute-done.18.refs_5_), channel_id=1, source_target_pairs={{8,0},{9,1},{10,2},{11,3},{12,4},{13,5},{14,6},{15,7}} | collective-permute-start | bytes 3145736 | tf_op jit(solution)/shard_map/ppermute | solution.py:304
  309.2 25.4 %collective-permute-start.20 = (bf16[16,64,512]{2,0,1:T(8,128)(2,1)S(1)}, bf16[16,64,512]{2,0,1:T(8,128)(2,1)S(1)}, u32[]{:S(2)}, u32[]{:S(2)}) collective-permute-start(bf16[16,64,512]{2,0,1:T(8,128)(2,1)S(1)} %copy.126), channel_id=1, source_target_pairs={{0,8},{1,9},{2,10},{3,11},{4,12},{5,13},{6,14},{7,15}} | collective-permute-start | bytes 3145736 | tf_op jit(solution)/shard_map/ppermute | solution.py:294
  314.7 19.9 %collective-permute-start.23 = (bf16[16,64,512]{2,0,1:T(8,128)(2,1)S(1)}, bf16[16,64,512]{2,0,1:T(8,128)(2,1)S(1)}, u32[]{:S(2)}, u32[]{:S(2)}) collective-permute-start(bf16[16,64,512]{2,0,1:T(8,128)(2,1)S(1)} %copy.124), channel_id=1, source_target_pairs={{24,16},{25,17},{26,18},{27,19},{28,20},{29,21},{30,22},{31,23}} | collective-permute-start | bytes 3145736 | tf_op jit(solution)/shard_map/ppermute | solution.py:295
  335.8 29.2 %collective-permute-start.24 = (bf16[16,64,512]{2,0,1:T(8,128)(2,1)S(1)}, bf16[16,64,512]{2,0,1:T(8,128)(2,1)S(1)}, u32[]{:S(2)}, u32[]{:S(2)}) collective-permute-start(bf16[16,64,512]{2,0,1:T(8,128)(2,1)S(1)} %get-tuple-element.42), channel_id=1, source_target_pairs={{24,16},{16,8},{25,17},{17,9},{26,18},{18,10},{27,19},{19,11},{28,... | collective-permute-start | bytes 3145736 | tf_op jit(solution)/shard_map/ppermute | solution.py:295
  360.0 198.1 %collective-permute-start.34 = (bf16[16,256,1024]{2,1,0:T(8,128)(2,1)}, bf16[16,256,1024]{2,1,0:T(8,128)(2,1)}, u32[]{:S(2)}, u32[]{:S(2)}) collective-permute-start(bf16[16,256,1024]{2,1,0:T(8,128)(2,1)} %copy.198), channel_id=1, source_target_pairs={{0,1},{1,0},{2,3},{3,2},{4,5},{5,4},{6,7},{7,6},{8,9},{9,8},{10,11... | collective-permute-start | bytes 25165832 | tf_op jit(solution)/shard_map/ppermute | solution.py:316
  360.0 28.0 %collective-permute-start.21 = (bf16[16,64,512]{2,0,1:T(8,128)(2,1)S(1)}, bf16[16,64,512]{2,0,1:T(8,128)(2,1)S(1)}, u32[]{:S(2)}, u32[]{:S(2)}) collective-permute-start(bf16[16,64,512]{2,0,1:T(8,128)(2,1)S(1)} %get-tuple-element.41), channel_id=1, source_target_pairs={{0,8},{8,16},{1,9},{9,17},{2,10},{10,18},{3,11},{11,19},{4,12},{12... | collective-permute-start | bytes 3145736 | tf_op jit(solution)/shard_map/ppermute | solution.py:294
  365.8 28.0 %collective-permute-start.25 = (bf16[16,64,512]{2,0,1:T(8,128)(2,1)S(1)}, bf16[16,64,512]{2,0,1:T(8,128)(2,1)S(1)}, u32[]{:S(2)}, u32[]{:S(2)}) collective-permute-start(bf16[16,64,512]{2,0,1:T(8,128)(2,1)S(1)} %add_convert_fusion.1), channel_id=1, source_target_pairs={{24,16},{16,8},{8,0},{25,17},{17,9},{9,1},{26,18},{18,10},{10,2},{... | collective-permute-start | bytes 3145736 | tf_op jit(solution)/shard_map/ppermute | solution.py:295
  388.8 26.8 %collective-permute-start.22 = (bf16[16,64,512]{2,0,1:T(8,128)(2,1)S(1)}, bf16[16,64,512]{2,0,1:T(8,128)(2,1)S(1)}, u32[]{:S(2)}, u32[]{:S(2)}) collective-permute-start(bf16[16,64,512]{2,0,1:T(8,128)(2,1)S(1)} %add_convert_fusion.2), channel_id=1, source_target_pairs={{0,8},{8,16},{16,24},{1,9},{9,17},{17,25},{2,10},{10,18},{18,26},{... | collective-permute-start | bytes 3145736 | tf_op jit(solution)/shard_map/ppermute | solution.py:294
  416.7 10.2 %collective-permute-start.28 = (bf16[16,16,512]{2,1,0:T(8,128)(2,1)S(1)}, bf16[16,16,512]{2,1,0:T(8,128)(2,1)S(1)}, u32[]{:S(2)}, u32[]{:S(2)}) collective-permute-start(bf16[16,16,512]{2,1,0:T(8,128)(2,1)S(1)} %get-tuple-element.38), channel_id=1, source_target_pairs={{0,6},{2,4},{4,2},{6,0},{1,7},{3,5},{5,3},{7,1},{8,14},{10,12},{12... | collective-permute-start | bytes 786440 | tf_op jit(solution)/shard_map/ppermute | solution.py:312
  418.4 11.9 %collective-permute-start.27 = (bf16[16,16,512]{2,1,0:T(8,128)(2,1)S(1)}, bf16[16,16,512]{2,1,0:T(8,128)(2,1)S(1)}, u32[]{:S(2)}, u32[]{:S(2)}) collective-permute-start(bf16[16,16,512]{2,1,0:T(8,128)(2,1)S(1)} %get-tuple-element.39), channel_id=1, source_target_pairs={{0,4},{2,6},{4,0},{6,2},{1,5},{3,7},{5,1},{7,3},{8,12},{10,14},{12... | collective-permute-start | bytes 786440 | tf_op jit(solution)/shard_map/ppermute | solution.py:312
  419.5 10.8 %collective-permute-start.26 = (bf16[16,16,512]{2,1,0:T(8,128)(2,1)S(1)}, bf16[16,16,512]{2,1,0:T(8,128)(2,1)S(1)}, u32[]{:S(2)}, u32[]{:S(2)}) collective-permute-start(bf16[16,16,512]{2,1,0:T(8,128)(2,1)S(1)} %get-tuple-element.40), channel_id=1, source_target_pairs={{0,2},{2,0},{4,6},{6,4},{1,3},{3,1},{5,7},{7,5},{8,10},{10,8},{12,... | collective-permute-start | bytes 786440 | tf_op jit(solution)/shard_map/ppermute | solution.py:312
  449.5 10.2 %collective-permute-start.37 = (bf16[16,16,512]{2,0,1:T(8,128)(2,1)S(1)}, bf16[16,16,512]{2,0,1:T(8,128)(2,1)S(1)}, u32[]{:S(2)}, u32[]{:S(2)}) collective-permute-start(bf16[16,16,512]{2,0,1:T(8,128)(2,1)S(1)} %bitcast.72), channel_id=1, source_target_pairs={{0,6},{2,4},{4,2},{6,0},{1,7},{3,5},{5,3},{7,1},{8,14},{10,12},{12... | collective-permute-start | bytes 786440 | tf_op jit(solution)/shard_map/ppermute | solution.py:312
  451.4 13.0 %collective-permute-start.36 = (bf16[16,16,512]{2,0,1:T(8,128)(2,1)S(1)}, bf16[16,16,512]{2,0,1:T(8,128)(2,1)S(1)}, u32[]{:S(2)}, u32[]{:S(2)}) collective-permute-start(bf16[16,16,512]{2,0,1:T(8,128)(2,1)S(1)} %bitcast.73), channel_id=1, source_target_pairs={{0,4},{2,6},{4,0},{6,2},{1,5},{3,7},{5,1},{7,3},{8,12},{10,14},{12... | collective-permute-start | bytes 786440 | tf_op jit(solution)/shard_map/ppermute | solution.py:312
  452.7 11.7 %collective-permute-start.35 = (bf16[16,16,512]{2,0,1:T(8,128)(2,1)S(1)}, bf16[16,16,512]{2,0,1:T(8,128)(2,1)S(1)}, u32[]{:S(2)}, u32[]{:S(2)}) collective-permute-start(bf16[16,16,512]{2,0,1:T(8,128)(2,1)S(1)} %bitcast.74), channel_id=1, source_target_pairs={{0,2},{2,0},{4,6},{6,4},{1,3},{3,1},{5,7},{7,5},{8,10},{10,8},{12,... | collective-permute-start | bytes 786440 | tf_op jit(solution)/shard_map/ppermute | solution.py:312
  464.5 28.2 %collective-permute-start.38 = (bf16[16,64,512]{2,1,0:T(8,128)(2,1)S(1)}, bf16[16,64,512]{2,1,0:T(8,128)(2,1)}, u32[]{:S(2)}, u32[]{:S(2)}) collective-permute-start(bf16[16,64,512]{2,1,0:T(8,128)(2,1)S(1)} %maximum_bitcast_fusion.1.refs_0_), channel_id=1, source_target_pairs={{0,8},{8,16},{16,24},{1,9},{9,17},{17,25},{2,10},{10,18},{18,26},{... | collective-permute-start | bytes 3145736 | tf_op jit(solution)/shard_map/ppermute | solution.py:303
  469.9 26.8 %collective-permute-start.41 = (bf16[16,64,512]{2,1,0:T(8,128)(2,1)S(1)}, bf16[16,64,512]{2,1,0:T(8,128)(2,1)}, u32[]{:S(2)}, u32[]{:S(2)}) collective-permute-start(bf16[16,64,512]{2,1,0:T(8,128)(2,1)S(1)} %maximum_bitcast_fusion.1.refs_0_), channel_id=1, source_target_pairs={{24,16},{16,8},{8,0},{25,17},{17,9},{9,1},{26,18},{18,10},{10,2},{... | collective-permute-start | bytes 3145736 | tf_op jit(solution)/shard_map/ppermute | solution.py:304
  492.7 29.0 %collective-permute-start.39 = (bf16[16,64,512]{2,1,0:T(8,128)(2,1)}, bf16[16,64,512]{2,1,0:T(8,128)(2,1)}, u32[]{:S(2)}, u32[]{:S(2)}) collective-permute-start(bf16[16,64,512]{2,1,0:T(8,128)(2,1)} %collective-permute-done.38.refs_1_), channel_id=1, source_target_pairs={{8,16},{16,24},{9,17},{17,25},{10,18},{18,26},{11,19},{19,27},{12,... | collective-permute-start | bytes 3145736 | tf_op jit(solution)/shard_map/ppermute | solution.py:303
  496.7 27.9 %collective-permute-start.42 = (bf16[16,64,512]{2,1,0:T(8,128)(2,1)}, bf16[16,64,512]{2,1,0:T(8,128)(2,1)}, u32[]{:S(2)}, u32[]{:S(2)}) collective-permute-start(bf16[16,64,512]{2,1,0:T(8,128)(2,1)} %collective-permute-done.41.refs_4_), channel_id=1, source_target_pairs={{16,8},{8,0},{17,9},{9,1},{18,10},{10,2},{19,11},{11,3},{20,12},{1... | collective-permute-start | bytes 3145736 | tf_op jit(solution)/shard_map/ppermute | solution.py:304
  521.7 35.3 %collective-permute-start.40 = (bf16[16,64,512]{2,1,0:T(8,128)(2,1)}, bf16[16,64,512]{2,1,0:T(8,128)(2,1)S(1)}, u32[]{:S(2)}, u32[]{:S(2)}) collective-permute-start(bf16[16,64,512]{2,1,0:T(8,128)(2,1)} %collective-permute-done.39.refs_2_), channel_id=1, source_target_pairs={{16,24},{17,25},{18,26},{19,27},{20,28},{21,29},{22,30},{23,31}} | collective-permute-start | bytes 3145736 | tf_op jit(solution)/shard_map/ppermute | solution.py:303
  524.5 33.5 %collective-permute-start.43 = (bf16[16,64,512]{2,1,0:T(8,128)(2,1)}, bf16[16,64,512]{2,1,0:T(8,128)(2,1)}, u32[]{:S(2)}, u32[]{:S(2)}) collective-permute-start(bf16[16,64,512]{2,1,0:T(8,128)(2,1)} %collective-permute-done.42.refs_5_), channel_id=1, source_target_pairs={{8,0},{9,1},{10,2},{11,3},{12,4},{13,5},{14,6},{15,7}} | collective-permute-start | bytes 3145736 | tf_op jit(solution)/shard_map/ppermute | solution.py:304
  525.8 3.7 collective-permute-start.30
  529.5 24.0 %collective-permute-start.31 = (f32[32,16]{0,1:T(8,128)S(1)}, f32[32,16]{0,1:T(8,128)S(1)}, u32[]{:S(2)}, u32[]{:S(2)}) collective-permute-start(f32[32,16]{0,1:T(8,128)S(1)} %fusion.42), channel_id=1, source_target_pairs={{0,4},{2,6},{4,0},{6,2},{1,5},{3,7},{5,1},{7,3},{8,12},{10,14},{12... | collective-permute-start | bytes 6152 | tf_op jit(solution)/shard_map/ppermute | solution.py:338
  553.5 41.7 %collective-permute-start.32 = (f32[32,16]{0,1:T(8,128)S(1)}, f32[32,16]{0,1:T(8,128)S(1)}, u32[]{:S(2)}, u32[]{:S(2)}) collective-permute-start(f32[32,16]{0,1:T(8,128)S(1)} %add.100), channel_id=1, source_target_pairs={{0,8},{8,0},{16,24},{24,16},{1,9},{9,1},{17,25},{25,17},{2,10},{10... | collective-permute-start | bytes 6152 | tf_op jit(solution)/shard_map/ppermute | solution.py:338
  594.2 3.7 collective-permute-start.44
  595.3 11.5 %collective-permute-start.33 = (f32[32,16]{0,1:T(8,128)S(1)}, f32[32,16]{0,1:T(8,128)S(1)}, u32[]{:S(2)}, u32[]{:S(2)}) collective-permute-start(f32[32,16]{0,1:T(8,128)S(1)} %add.101), channel_id=1, source_target_pairs={{0,16},{8,24},{16,0},{24,8},{1,17},{9,25},{17,1},{25,9},{2,18},{10... | collective-permute-start | bytes 6152 | tf_op jit(solution)/shard_map/ppermute | solution.py:338
  597.9 3.7 collective-permute-start.45
  601.6 3.7 collective-permute-start.46
  605.2 4.5 collective-permute-start.47
  609.8 15.0 %collective-permute-start.48 = (f32[4,16]{0,1:T(8,128)S(1)}, f32[4,16]{0,1:T(8,128)S(1)}, u32[]{:S(2)}, u32[]{:S(2)}) collective-permute-start(f32[4,16]{0,1:T(8,128)S(1)} %add.106), channel_id=1, source_target_pairs={{0,1},{1,0},{2,3},{3,2},{4,5},{5,4},{6,7},{7,6},{8,9},{9,8},{10,11... | collective-permute-start | bytes 776 | tf_op jit(solution)/shard_map/ppermute | solution.py:316
  (23 other events, 568.4 us)

commit v2 on v1

v2 whole, which is shorter than its diff:
```python
import functools
import math

import jax
import jax.numpy as jnp
import ml_dtypes
import numpy as np
from jax import lax
from jax.experimental import pallas as pl
from jax.experimental.pallas import tpu as pltpu
from jax.sharding import PartitionSpec as P

BF = jnp.bfloat16
F32 = jnp.float32
TWO_PI = 2.0 * math.pi
CHUNKS = 2
VMEM = 48 * 1024 * 1024


def table(freqs, points, length):
    product = (freqs % length)[:, None] * points[None, :] % length
    angle = np.float32(TWO_PI / length) * product.astype(np.float32)
    return np.cos(angle), np.sin(angle)


def column_table(cells, modes):
    cos, sin = table(np.arange(modes), np.arange(cells), cells)
    return np.ascontiguousarray(np.concatenate([cos, -sin], 0).T).astype(ml_dtypes.bfloat16)


def row_tables(rows, modes, blocks, samples):
    index = np.arange(modes)
    cos, sin = table(np.where(index < modes // 2, index, index - modes), np.arange(rows), rows)
    both = np.stack([cos, sin]).astype(ml_dtypes.bfloat16)
    sub = modes // (blocks * samples)
    piece = sub // CHUNKS
    local = rows // blocks
    out = np.empty((blocks, samples, 2 * modes, local), ml_dtypes.bfloat16)
    for z in range(blocks):
        part = both[:, :, z * local : (z + 1) * local]
        for s in range(samples):
            order = np.concatenate(
                [
                    np.arange(piece) + piece * c + sub * ((s ^ j) + samples * ((z + d) % blocks))
                    for d in range(blocks)
                    for c in range(CHUNKS)
                    for j in range(samples)
                ]
            )
            out[z, s] = part[:, order].reshape(2 * modes, local)
    return out


def gelu_slope(value):
    bell = jnp.exp(-0.5 * value * value)
    t = pl.reciprocal(1.0 + (0.3275911 / math.sqrt(2.0)) * jnp.abs(value))
    poly = 0.5 * 1.061405429
    for a in (-1.453152027, 1.421413741, -0.284496736, 0.254829592):
        poly = poly * t + 0.5 * a
    tail = poly * t * bell
    return jnp.where(value >= 0.0, 1.0 - tail, tail) + value * bell * (1.0 / math.sqrt(2.0 * math.pi))


def lift_rows(fields, lw, chan):
    total = fields[0] * lw[0, chan]
    for j in range(1, len(fields)):
        total = total + fields[j] * lw[j, chan]
    return jnp.tanh(total)


def row_forward(u, row_tab, scale):
    modes, width = row_tab.shape[0] // 2, u.shape[1] // 2
    prod = jnp.dot(row_tab, u, preferred_element_type=F32)
    real = (prod[:modes, :width] + prod[modes:, width:]) * scale
    imag = (prod[:modes, width:] - prod[modes:, :width]) * scale
    return jnp.concatenate([real.astype(BF), imag.astype(BF)], 1)


def split_modes(value, outs, at):
    rows = outs[0][0].shape[1]
    for c, part in enumerate(outs):
        for d, out in enumerate(part):
            lo = (d * len(outs) + c) * rows
            out[at] = value[lo : lo + rows]


def by_part(refs):
    each = len(refs) // CHUNKS
    return [refs[i * each : (i + 1) * each] for i in range(CHUNKS)]


def lift_kernel(scale, lw, fields, col, row_tab, lifted, *outs):
    group, rows, cells = lifted.shape
    first = pl.program_id(0) * group
    step = min(rows, 32)
    us = [[] for _ in range(group)]
    for lo in range(0, rows, step):
        f = [fields[j, lo : lo + step].astype(F32) for j in range(fields.shape[0])]
        for c in range(group):
            v = lift_rows(f, lw, first + c).astype(BF)
            lifted[c, lo : lo + step] = v
            us[c].append(jnp.dot(v, col[...], preferred_element_type=F32).astype(BF))
    for c in range(group):
        split_modes(row_forward(jnp.concatenate(us[c], 0), row_tab[...], scale), by_part(outs), c)


def slope_kernel(scale, first, lw, fields, col, row_tab, *refs):
    out, token = refs[-2:]
    inputs, rows, cells = fields.shape
    blocks, sub = out.shape[0], out.shape[3]
    chan = first + pl.program_id(0)
    step = min(rows, 32)
    us = [[] for _ in range(inputs)]
    for lo in range(0, rows, step):
        f = [fields[j, lo : lo + step].astype(F32) for j in range(inputs)]
        t = lift_rows(f, lw, chan)
        slope = 1.0 - t * t
        for j in range(inputs):
            us[j].append(jnp.dot((f[j] * slope).astype(BF), col[...], preferred_element_type=F32).astype(BF))
    for j in range(inputs):
        v = row_forward(jnp.concatenate(us[j], 0), row_tab[...], scale)
        for d in range(blocks):
            out[d, 0, j] = v[d * sub : (d + 1) * sub]
    token[...] = jnp.zeros(token.shape, F32)


def pair_kernel(low, high, f_low, f_high, out):
    for c in range(out.shape[0]):
        for j in range(out.shape[1]):
            total = None
            for b, f in ((low, f_low), (high, f_high)):
                prod = b[c].astype(F32) * f[0, c, j].astype(F32)
                for r in range(0, prod.shape[0], 8):
                    for k in range(0, prod.shape[1], 128):
                        tile = prod[r : r + 8, k : k + 128]
                        total = tile if total is None else total + tile
            out[c, j] = total


def own_pair_kernel(low, f_low, out):
    for c in range(out.shape[0]):
        for j in range(out.shape[1]):
            total = None
            prod = low[c].astype(F32) * f_low[0, c, j].astype(F32)
            for r in range(0, prod.shape[0], 8):
                for k in range(0, prod.shape[1], 128):
                    tile = prod[r : r + 8, k : k + 128]
                    total = tile if total is None else total + tile
            out[c, j] = total


def local_kernel(mix, own, other, out, token):
    n, rows, cells = own.shape
    for lo in range(0, cells, 256):
        at = pl.ds(lo, 256)
        both = jnp.concatenate([own[:, :, at].reshape(n * rows, 256), other[:, :, at].reshape(n * rows, 256)], 0)
        got = jnp.dot(mix[...], both, preferred_element_type=F32)
        out[:, :, at] = got.reshape(-1, rows, 256)
    token[...] = jnp.zeros(token.shape, F32)


def local_back_kernel(lw, mix, fields, own, other, grad, terms, sums):
    n, rows, cells = own.shape
    inputs = fields.shape[0]

    @pl.when(pl.program_id(0) == 0)
    def _():
        terms[...] = jnp.zeros(terms.shape, F32)
        sums[...] = jnp.zeros(sums.shape, F32)

    g = grad[...].reshape(-1, cells)
    for half, part in enumerate((own, other)):
        terms[half] += lax.dot_general(
            part[...].reshape(n * rows, cells), g, (((1,), (1,)), ((), ())), preferred_element_type=F32
        )

    def lanes(step, _):
        at = pl.ds(pl.multiple_of(step * 256, 256), 256)
        back = jnp.dot(mix[...], grad[:, :, at].reshape(-1, 256), preferred_element_type=F32)
        f = [fields[j, :, at].astype(F32) for j in range(inputs)]
        for c in range(2 * n):
            t = lift_rows(f, lw, c)
            total = back[c * rows : (c + 1) * rows] * (1.0 - t * t)
            for j in range(inputs):
                prod = f[j] * total
                prod = prod[:, :128] + prod[:, 128:]
                tile = prod[:8]
                for r in range(8, rows, 8):
                    tile = tile + prod[r : r + 8]
                sums[c, j] += tile
        return 0

    lax.fori_loop(0, cells // 256, lanes, 0)


def row_inverse(parts, row_inv):
    rows = row_inv.shape[0] // 2
    width = parts[0][0].shape[-1] // 2
    hops = (len(parts[0]) - 1) // 2
    blocks = [part[0][0] for part in parts]
    for s in range(hops - 1, -1, -1):
        blocks += [part[1 + s][0] + part[hops + hops - s][0] for part in parts]
    prod = jnp.dot(row_inv, jnp.concatenate(blocks, 0), preferred_element_type=F32)
    real = prod[:rows, :width] - prod[rows:, width:]
    imag = prod[:rows, width:] + prod[rows:, :width]
    return jnp.concatenate([real.astype(BF), imag.astype(BF)], 1)


def middle_kernel(blocks, grid_scale, scale, local, cotan, col, col_inv, row_tab, row_inv, *refs):
    n_in = CHUNKS * (2 * blocks - 1)
    grad, outs = refs[n_in], refs[n_in + 1 :]
    rows = grad.shape[1]
    h = row_inverse(by_part(refs[:n_in]), row_inv[...])
    step = min(rows, 32)
    pieces = []
    for lo in range(0, rows, step):
        grid = jnp.dot(h[lo : lo + step], col_inv[...], preferred_element_type=F32)
        pre = grid * grid_scale + local[0, lo : lo + step]
        g = (cotan[0, 0, lo : lo + step].astype(F32) * gelu_slope(pre)).astype(BF)
        grad[0, lo : lo + step] = g
        pieces.append(jnp.dot(g, col[...], preferred_element_type=F32).astype(BF))
    split_modes(row_forward(jnp.concatenate(pieces, 0), row_tab[...], scale), by_part(outs), 0)


def mix_kernel(samples, core, w_keep, w_send, *refs):
    xs, keep, send = refs[:samples], refs[samples], refs[samples + 1]
    width = w_keep.shape[-1]
    ins, outs = w_keep.shape[2], w_keep.shape[3]
    for lo in range(0, width, 128):
        re, im = pl.ds(lo, 128), pl.ds(width + lo, 128)
        xr = [x[0, :, re].astype(F32) for x in xs]
        xi = [x[0, :, im].astype(F32) for x in xs]
        for w, out in ((w_keep, keep), (w_send, send)):
            real = [jnp.zeros((outs, 128), F32) for _ in range(samples)]
            imag = [jnp.zeros((outs, 128), F32) for _ in range(samples)]
            for i in range(ins):
                wr = w[0, 0, i, :, re].astype(F32)
                wi = w[1, 0, i, :, re].astype(F32)
                for s in range(samples):
                    a, b = xr[s][i : i + 1], xi[s][i : i + 1]
                    real[s] = real[s] + (wr * a - wi * b)
                    imag[s] = imag[s] + (wr * b + wi * a)
            for s in range(samples):
                out[s, 0, :, re] = real[s].astype(BF)
                out[s, 0, :, im] = imag[s].astype(BF)


def back_kernel(samples, core, w_own, w_other, g_other, *refs):
    gs, out = refs[:samples], refs[samples]
    width = w_own.shape[-1]
    ins, outs = w_own.shape[2], w_own.shape[3]
    for lo in range(0, width, 128):
        re, im = pl.ds(lo, 128), pl.ds(width + lo, 128)
        gr = [[g[0, :, re].astype(F32) for g in gs], [g_other[s, 0, :, re].astype(F32) for s in range(samples)]]
        gi = [[g[0, :, im].astype(F32) for g in gs], [g_other[s, 0, :, im].astype(F32) for s in range(samples)]]
        real = [[] for _ in range(samples)]
        imag = [[] for _ in range(samples)]
        for i in range(ins):
            w = [
                (w_own[0, 0, i, :, re].astype(F32), w_own[1, 0, i, :, re].astype(F32)),
                (w_other[0, 0, i, :, re].astype(F32), w_other[1, 0, i, :, re].astype(F32)),
            ]
            for s in range(samples):
                r = m = None
                for half in range(2):
                    wr, wi = w[half]
                    a, b = gr[half][s], gi[half][s]
                    r1 = wr * a + wi * b
                    m1 = wr * b - wi * a
                    r, m = (r1, m1) if r is None else (r + r1, m + m1)
                real[s].append(jnp.sum(r, axis=0, keepdims=True))
                imag[s].append(jnp.sum(m, axis=0, keepdims=True))
        for s in range(samples):
            out[s, 0, :, re] = jnp.concatenate(real[s], 0).astype(BF)
            out[s, 0, :, im] = jnp.concatenate(imag[s], 0).astype(BF)


def weight_kernel(samples, core, *refs):
    g_other, out, token = refs[0], refs[-2], refs[-1]
    xs, gs = refs[1 : 1 + samples], refs[1 + samples : 1 + 2 * samples]
    ins, half = xs[0].shape[1], gs[0].shape[1]
    width = xs[0].shape[2] // 2
    own = pl.ds(pl.multiple_of(core[0] * half, half), half)
    other = pl.ds(pl.multiple_of((1 - core[0]) * half, half), half)
    for lo in range(0, width, 128):
        re, im = pl.ds(lo, 128), pl.ds(width + lo, 128)
        xr = [x[0, :, re].astype(F32) for x in xs]
        xi = [x[0, :, im].astype(F32) for x in xs]
        for where in (own, other):
            if where is own:
                gr = [g[0, :, re].astype(F32) for g in gs]
                gi = [g[0, :, im].astype(F32) for g in gs]
            else:
                gr = [g_other[s, 0, :, re].astype(F32) for s in range(samples)]
                gi = [g_other[s, 0, :, im].astype(F32) for s in range(samples)]
            for i in range(ins):
                real = imag = None
                for s in range(samples):
                    a, b = xr[s][i : i + 1], xi[s][i : i + 1]
                    r1 = gr[s] * a + gi[s] * b
                    m1 = gi[s] * a - gr[s] * b
                    real, imag = (r1, m1) if real is None else (real + r1, imag + m1)
                out[0, 0, i, where, re] = real.astype(BF)
                out[1, 0, i, where, re] = imag.astype(BF)
    token[...] = jnp.zeros(token.shape, F32)


TOKEN = ((8, 128), F32, (8, 128), lambda i, *_: (0, 0))


def call(body, grid, ins, outs, flops, transcendentals=0, prefetch=None, tokens=(), into=None):
    scalars = 0 if prefetch is None else 1

    def spec(block, index):
        if block is None:
            return pl.BlockSpec(memory_space=pltpu.SMEM)
        return pl.BlockSpec(block, index)

    moved = 0
    for a, block, _ in ins:
        moved += a.size * a.dtype.itemsize if block is None else math.prod(block) * math.prod(grid) * a.dtype.itemsize
    moved += sum(math.prod(b) * math.prod(grid) * jnp.dtype(t).itemsize for _, t, b, _ in outs)
    extra = list(tokens) + ([] if into is None else [into])

    def kernel(*refs):
        n = scalars + len(ins)
        body(*refs[:n], *refs[n + len(extra) :])

    return pl.pallas_call(
        kernel,
        grid_spec=pltpu.PrefetchScalarGridSpec(
            num_scalar_prefetch=scalars,
            grid=grid,
            in_specs=[spec(b, i) for _, b, i in ins] + [pl.BlockSpec(memory_space=pl.ANY)] * len(extra),
            out_specs=[spec(b, i) for _, _, b, i in outs],
        ),
        out_shape=[jax.ShapeDtypeStruct(s, t) for s, t, _, _ in outs],
        input_output_aliases={} if into is None else {scalars + len(ins) + len(extra) - 1: 0},
        compiler_params=pltpu.CompilerParams(vmem_limit_bytes=VMEM),
        cost_estimate=pl.CostEstimate(flops=int(flops), bytes_accessed=int(moved), transcendentals=int(transcendentals)),
    )(*(() if prefetch is None else (prefetch,)), *[a for a, _, _ in ins], *extra)


def hold(value, *tokens):
    if not tokens:
        return value
    anywhere = pl.BlockSpec(memory_space=pl.ANY)
    return pl.pallas_call(
        lambda *refs: None,
        in_specs=[anywhere] * (1 + len(tokens)),
        out_specs=anywhere,
        out_shape=jax.ShapeDtypeStruct(value.shape, value.dtype),
        input_output_aliases={0: 0},
        cost_estimate=pl.CostEstimate(flops=0, bytes_accessed=0, transcendentals=0),
    )(value, *tokens)


def add_kernel(a, b, c, d, up, down):
    up[...] = (a[...].astype(F32) + b[...].astype(F32)).astype(BF)
    down[...] = (c[...].astype(F32) + d[...].astype(F32)).astype(BF)


def add_pairs(a, b, c, d, tokens):
    n = a.shape[0] // 2
    part = ((n, *a.shape[1:]), lambda i, *_: (i, 0, 0))
    return call(
        add_kernel, (2,), [(v, *part) for v in (a, b, c, d)], [(a.shape, BF, *part)] * 2, 4 * a.size, tokens=tokens
    )


def chain_sum(parts, fill, start):
    hops = len(parts) - 1
    blocks = hops + 1
    below = above = None
    tokens = []
    for t in range(hops):
        up, down = parts[hops - t], parts[t + 1]
        if t:
            up, down = add_pairs(up, below, down, above, tokens)
        elif start:
            up, down = hold(up, *start), hold(down, *start)
        below = lax.ppermute(up, "blk", [(z, z + 1) for z in range(t + 1)])
        above = lax.ppermute(down, "blk", [(blocks - 1 - z, blocks - 2 - z) for z in range(t + 1)])
        tokens = [fill.pop(0)()] if fill else []
    return parts[0], below, above


def chain_gather(own, blocks):
    below, above = [], []
    up = down = own
    for t in range(blocks - 1):
        up = lax.ppermute(up, "blk", [(z, z + 1) for z in range(t, blocks - 1)])
        down = lax.ppermute(down, "blk", [(blocks - 1 - z, blocks - 2 - z) for z in range(t, blocks - 1)])
        below.append(up)
        above.append(down)
    return [own, *below, *above]


def swap_samples(pieces):
    n = len(pieces)
    return [pieces[0]] + [lax.ppermute(pieces[j], "dp", [(i, i ^ j) for i in range(n)]) for j in range(1, n)]


def swap_cores(value):
    return lax.ppermute(value, "chan", [(0, 1), (1, 0)])


def to_modes(shares, samples):
    own, below, above = shares
    total = (own.astype(F32) + below.astype(F32) + above.astype(F32)).astype(BF).transpose(1, 0, 2)
    sub = total.shape[0] // samples
    return swap_samples([total[j * sub : (j + 1) * sub] for j in range(samples)])


def from_modes(pieces, blocks):
    return chain_gather(jnp.concatenate(swap_samples(pieces), 0).transpose(1, 0, 2), blocks)


def all_sum(value, axes):
    for axis in axes:
        n = lax.axis_size(axis)
        step = 1
        while step < n:
            value = value + lax.ppermute(value, axis, [(i, i ^ step) for i in range(n)])
            step *= 2
    return value


def per_device(fields, lift_weight, local_weight, spectral_weight, cotangent):
    blocks = lax.axis_size("blk")
    samples = lax.axis_size("dp")
    sample = fields[0]
    inputs, rows, cells = sample.shape
    chans = cotangent.shape[1]
    mode_dev = spectral_weight.shape[1]
    half = spectral_weight.shape[3] // 2
    freqs = spectral_weight.shape[4]
    width = 2 * freqs
    modes = mode_dev * blocks * samples
    sub = modes // blocks
    piece = mode_dev // CHUNKS
    all_rows = rows * blocks
    z, s, core = lax.axis_index("blk"), lax.axis_index("dp"), lax.axis_index("chan")
    core_ref = core.astype(jnp.int32)[None]
    unit_scale = 1.0 / math.sqrt(all_rows * cells)
    norm_scale = 1.0 / math.sqrt(samples * all_rows * cells)

    col = jnp.asarray(column_table(cells, freqs))
    col_inv = jnp.asarray(np.ascontiguousarray(column_table(cells, freqs).T))
    row_tab = lax.dynamic_slice(
        jnp.asarray(row_tables(all_rows, modes, blocks, samples)), (z, s, 0, 0), (1, 1, 2 * modes, rows)
    )[0, 0]
    row_inv = row_tab.reshape(2, modes, rows).transpose(0, 2, 1).reshape(2 * rows, modes)
    lw_wide = lift_weight.astype(F32)
    own_lw = lax.dynamic_slice_in_dim(lw_wide, core * chans, chans, 1)
    both_lw = jnp.concatenate([own_lw, lax.dynamic_slice_in_dim(lw_wide, (1 - core) * chans, chans, 1)], 1)
    lw_rows = jnp.concatenate(
        [
            lax.dynamic_slice_in_dim(local_weight, core * chans, chans, 0),
            lax.dynamic_slice_in_dim(local_weight, (1 - core) * chans, chans, 0),
        ],
        0,
    )
    group_rows = 16
    eye = jnp.eye(group_rows, dtype=BF)
    spread = (lw_rows[:, None, :, None] * eye[None, :, None, :]).reshape(2 * chans * group_rows, chans * group_rows)

    def whole(a):
        return (a, a.shape, lambda i, *_: (0,) * a.ndim)

    def channel(a, n=1):
        return (a, (n, *a.shape[1:]), lambda i, *_: (i,) + (0,) * (a.ndim - 1))

    def part_outs(n):
        shape = (chans, sub // CHUNKS, width)
        return [(shape, BF, (n, *shape[1:]), lambda i, *_: (i, 0, 0)) for _ in range(CHUNKS * blocks)]

    matrix = chans * rows * 4 * freqs * (cells + 2 * modes)
    group = 2
    lifted, *shares = call(
        functools.partial(lift_kernel, unit_scale),
        (chans // group,),
        [(own_lw, None, None), whole(sample), whole(col), whole(row_tab)],
        [((chans, rows, cells), BF, (group, rows, cells), lambda i, *_: (i, 0, 0)), *part_outs(group)],
        matrix,
        chans * rows * cells,
    )
    shares = by_part(shares)
    lifted_other = swap_cores(lifted)

    slopes = [None]

    def slope_piece(first, count):
        def run():
            got, token = call(
                functools.partial(slope_kernel, unit_scale, first),
                (count,),
                [(own_lw, None, None), whole(sample), whole(col), whole(row_tab)],
                [
                    (
                        (blocks, chans, inputs, sub, width),
                        BF,
                        (blocks, 1, inputs, sub, width),
                        lambda i, *_, first=first: (0, first + i, 0, 0, 0),
                    ),
                    TOKEN,
                ],
                matrix * inputs * count // chans,
                count * rows * cells,
                tokens=() if slopes[0] is not None else (shares[0][0],),
                into=slopes[0],
            )
            slopes[0] = got
            return token

        return run

    locals_ = [None]

    def local_piece():
        got, token = call(
            local_kernel,
            (rows // group_rows,),
            [
                whole(spread.T),
                (lifted, (chans, group_rows, cells), lambda i, *_: (0, i, 0)),
                (lifted_other, (chans, group_rows, cells), lambda i, *_: (0, i, 0)),
            ],
            [((chans, rows, cells), F32, (chans, group_rows, cells), lambda i, *_: (0, i, 0)), TOKEN],
            4 * chans * chans * group_rows * rows * cells,
        )
        locals_[0] = got
        return token

    def weight_half(part, other):
        return (
            spectral_weight,
            (2, 1, chans, half, freqs),
            lambda i, c, part=part, other=other: (0, part * piece + i, 0, (1 - c[0]) if other else c[0], 0),
        )

    def row_mode(a):
        return (a, (1, *a.shape[1:]), lambda i, *_: (i, 0, 0))

    def stacked(a):
        return (a, (samples, 1, *a.shape[2:]), lambda i, *_: (0, i, 0, 0))

    def stack_out(n):
        return ((samples, piece, n, width), BF, (samples, 1, n, width), lambda i, *_: (0, i, 0, 0))

    mix_flops = 16 * samples * piece * chans * half * freqs
    count = -(-chans // 5)
    fill = [slope_piece(i, min(count, chans - i)) for i in range(0, chans, count)]
    fill.insert(3, local_piece)
    field_modes, out_parts = [], []
    previous = ()
    for part in range(CHUNKS):
        got = chain_sum(shares[part], fill, previous)
        previous = got[1:]
        xs = to_modes(got, samples)
        field_modes.append(xs)
        keep, send = call(
            functools.partial(mix_kernel, samples),
            (piece,),
            [weight_half(part, False), weight_half(part, True), *[row_mode(x) for x in xs]],
            [stack_out(half)] * 2,
            mix_flops,
            prefetch=core_ref,
        )
        total = (keep.astype(F32) + swap_cores(send).astype(F32)).astype(BF)
        out_parts += from_modes([total[j] for j in range(samples)], blocks)
    while fill:
        fill.pop(0)()
    slopes, local = slopes[0], locals_[0]

    grad_z, *shares = call(
        functools.partial(middle_kernel, blocks, 2.0 * unit_scale, 2.0 * unit_scale),
        (chans,),
        [
            channel(local),
            (cotangent, (1, 1, rows, cells), lambda i, *_: (0, i, 0, 0)),
            whole(col),
            whole(col_inv),
            whole(row_tab),
            whole(row_inv),
            *[channel(a) for a in out_parts],
        ],
        [((chans, rows, cells), BF, (1, rows, cells), lambda i, *_: (i, 0, 0)), *part_outs(1)],
        2 * matrix,
        3 * chans * rows * cells,
    )
    shares = by_part(shares)

    terms, local_sums = [], []

    def back_piece(first, count):
        at = lambda i, *_: (0, first + i, 0)

        def run():
            t, v = call(
                local_back_kernel,
                (count,),
                [
                    (both_lw, None, None),
                    whole(spread),
                    (sample, (inputs, group_rows, cells), at),
                    (lifted, (chans, group_rows, cells), at),
                    (lifted_other, (chans, group_rows, cells), at),
                    (grad_z, (chans, group_rows, cells), at),
                ],
                [
                    (
                        (2, chans * group_rows, chans * group_rows),
                        F32,
                        (2, chans * group_rows, chans * group_rows),
                        lambda i, *_: (0, 0, 0),
                    ),
                    ((2 * chans, inputs, 8, 128), F32, (2 * chans, inputs, 8, 128), lambda i, *_: (0, 0, 0, 0)),
                ],
                8 * chans * chans * group_rows * group_rows * count * cells,
                2 * chans * group_rows * count * cells,
            )
            terms.append(t)
            local_sums.append(v)
            return v

        return run

    steps = rows // group_rows
    count = -(-steps // 4)
    fill = [back_piece(i, min(count, steps - i)) for i in range(0, steps, count)]
    previous = ()
    grad_modes, grad_others, back_parts = [], [], []
    for part in range(CHUNKS):
        got = chain_sum(shares[part], fill, previous)
        previous = got[1:]
        gs = to_modes(got, samples)
        other = swap_cores(jnp.stack(gs))
        grad_modes.append(gs)
        grad_others.append(other)
        (back,) = call(
            functools.partial(back_kernel, samples),
            (piece,),
            [weight_half(part, False), weight_half(part, True), stacked(other), *[row_mode(g) for g in gs]],
            [stack_out(chans)],
            mix_flops,
            prefetch=core_ref,
        )
        back_parts.append(from_modes([back[j] for j in range(samples)], blocks))
    while fill:
        fill.pop(0)()

    term = sum(terms).reshape(2 * chans, group_rows, chans, group_rows)
    term = jnp.sum(term * jnp.eye(group_rows, dtype=F32)[None, :, None, :], axis=(1, 3))
    own_first = jnp.stack([term[:chans], term[chans:]])
    ordered = jnp.where(core == 0, own_first, own_first[::-1]).reshape(2 * chans, chans)
    local_grad = all_sum(ordered * norm_scale, ("dp", "blk"))

    spectral_grad, tokens = None, []
    for part in range(CHUNKS):
        spectral_grad, token = call(
            functools.partial(weight_kernel, samples),
            (piece,),
            [
                stacked(grad_others[part]),
                *[row_mode(x) for x in field_modes[part]],
                *[row_mode(g) for g in grad_modes[part]],
            ],
            [
                (
                    (2, mode_dev, chans, 2 * half, freqs),
                    BF,
                    (2, 1, chans, 2 * half, freqs),
                    lambda i, *_, part=part: (0, part * piece + i, 0, 0, 0),
                ),
                TOKEN,
            ],
            mix_flops,
            prefetch=core_ref,
            into=spectral_grad,
        )
        tokens.append(token)

    sums = []
    bunch = 4
    for part in range(CHUNKS):
        own, arrived = back_parts[part][0], back_parts[part][1:]
        hops = blocks - 1
        out = [((chans, inputs, 8, 128), F32, (bunch, inputs, 8, 128), lambda i, *_: (i, 0, 0, 0))]

        def spectra(d, part=part):
            return (
                slopes,
                (1, bunch, inputs, sub // CHUNKS, width),
                lambda i, *_, d=d, part=part: (d, i, 0, part, 0),
            )

        flops = 4 * chans * inputs * sub * width // CHUNKS
        sums += call(own_pair_kernel, (chans // bunch,), [channel(own, bunch), spectra(0)], out, flops)
        for t in range(hops):
            last = part == CHUNKS - 1 and t == hops - 1
            sums += call(
                pair_kernel,
                (chans // bunch,),
                [
                    channel(arrived[t], bunch),
                    channel(arrived[hops + t], bunch),
                    spectra(blocks - 1 - t),
                    spectra(1 + t),
                ],
                out,
                2 * flops,
                tokens=tokens if last else (),
            )
    lift_own = jnp.sum(sum(sums), axis=(2, 3)).T
    lift_local = jnp.sum(sum(local_sums), axis=(2, 3)).T
    lift_own = jnp.concatenate([lift_own + lift_local[:, :chans], lift_local[:, chans:]], 1) * norm_scale
    lift_own = all_sum(lift_own, ("dp", "blk"))
    theirs = swap_cores(lift_own)
    mine = lift_own[:, :chans] + theirs[:, chans:]
    his = lift_own[:, chans:] + theirs[:, :chans]
    lift_grad = jnp.where(core == 0, jnp.concatenate([mine, his], 1), jnp.concatenate([his, mine], 1))
    return (spectral_grad, local_grad, lift_grad)


def solution(mesh):
    in_specs = (
        P("dp", "parts", "blk", None),
        P("parts", None),
        P("parts", "chan"),
        P("parts", ("blk", "dp"), "chan", None, None),
        P("dp", "chan", "blk", "parts"),
    )
    out_specs = (
        P("parts", ("blk", "dp"), "chan", None, None),
        P("parts", "chan"),
        P("parts", None),
    )
    return jax.shard_map(per_device, mesh=mesh, in_specs=in_specs, out_specs=out_specs, check_vma=False)
```

time: 635 us -> 678 us (1.068)
  Pallas kernels: 139 us -> 347 us
  matrix products: 97.5 us -> 0 us
  waiting for transfers between devices: 219 us -> 122 us
  starting transfers between devices: 86.8 us -> 133 us
  other arithmetic: 45.4 us -> 13.4 us
  local copies, waits for them, and re-layouts: 36.9 us -> 50.1 us
    pallas_call x6 -> x37, Pallas kernels: 139 us -> 347 us  [the longest x33 347 us: call(): pl.pallas_call(kernel, grid_spec=pltpu.PrefetchScalarGridSpec(num_scalar_...]
    dot_general x6 -> x0, matrix products: 97.5 us -> none  [the longest x1 23.6 us: per_device(): jnp.einsum('iry,ory->io', lifted_other, grad_z, preferred_element_type=F32)]
    ppermute x6 -> x12, waiting for transfers between devices: 104 us -> 12.1 us  [chain_sum(): below = lax.ppermute(up, 'blk', [(z, z + 1) for z in range(t + 1)])]
    ppermute x6 -> x12, waiting for transfers between devices: 16.6 us -> 56.2 us  [chain_gather(): lax.ppermute(down, 'blk', [(blocks - 1 - z, blocks - 2 - z) for z in rang...]
    add x1 -> x3, other arithmetic: 34 us -> 1.02 us  [the longest x1 0.94 us: per_device(): term = sum(terms).reshape(2 * chans, group_rows, chans, group_rows)]
    dot_general x2 -> x0, local copies, waits for them, and re-layouts: 22.9 us -> none  [the longest x1 11.5 us: per_device(): jnp.einsum('ory,io->iry', grad_z, own_rows, preferred_element_type=F32)]
    ppermute x12 -> x24, waiting for transfers between devices: 41.3 us -> 19.1 us  [swap_samples(): lax.ppermute(pieces[j], 'dp', [(i, i ^ j) for i in range(n)])]
    unnamed x48 -> x196, local copies, waits for them, and re-layouts: 8.9 us -> 31 us
  transfers between devices with their start and end apart: 49 -> 86, of which waited for: 29 -> 31; matrix products, arithmetic and copies ran while one was open for 27% -> 5% of each run, Pallas kernels for 12% -> 37%
where the time goes in v2:
time: 678 us; the launch traced here: 668 us
  Pallas kernels  347 us (51%)
  starting transfers between devices  133 us (20%)
  waiting for transfers between devices  122 us (18%)
  local copies, waits for them, and re-layouts  50.1 us (7%)
  other arithmetic  13.4 us (2%)
    pallas_call x33, Pallas kernels, call(): pl.pallas_call(kernel, grid_spec=pltpu.PrefetchScalarGridSpec(num_scalar_...  347 us
    ppermute x12, waiting for transfers between devices, chain_gather(): lax.ppermute(down, 'blk', [(blocks - 1 - z, blocks - 2 - z) for z in rang...  56.2 us
    ppermute x12, starting transfers between devices, chain_sum(): below = lax.ppermute(up, 'blk', [(z, z + 1) for z in range(t + 1)])  38.6 us
    unnamed x196, local copies, waits for them, and re-layouts  31 us
    ppermute x24, starting transfers between devices, swap_samples(): lax.ppermute(pieces[j], 'dp', [(i, i ^ j) for i in range(n)])  29.8 us
    ppermute x12, starting transfers between devices, chain_gather(): up = lax.ppermute(up, 'blk', [(z, z + 1) for z in range(t, blocks - 1)])  29.5 us
    ppermute x24, waiting for transfers between devices, swap_samples(): lax.ppermute(pieces[j], 'dp', [(i, i ^ j) for i in range(n)])  19.1 us
    ppermute x8, waiting for transfers between devices, all_sum(): value = value + lax.ppermute(value, axis, [(i, i ^ step) for i in range(n)])  18.8 us
  transfers between devices with their start and end apart: 86, of which 31 were waited for; matrix products, arithmetic and copies ran while one was open for 5% of the time, Pallas kernels for 37%

profile of v2, /device:TPU:0, one launch (start us, length us, event | category | flops | bytes accessed | tf_op | source)
XLA Modules:
  0.0 668.3 jit_solution(1889537200433360779)
XLA Ops:
  4.4 29.5 %shard_map.103 = (bf16[16,256,1024]{2,1,0:T(8,128)(2,1)}, bf16[16,32,512]{2,1,0:T(8,128)(2,1)S(1)}, bf16[16,32,512]{2,1,0:T(8,128)(2,1)}, bf16[16,32,512]{2,1,0:...) custom-call(f32[4,16]{1,0:T(4,128)S(1)} %get-tuple-element.169.refs_, ...), custom_call_target="tpu_custom_call" | custom-call | flops 6442450944 | bytes 39846144 | tf_op jit(solution)/shard_map/pallas_call | solution.py:329
  37.6 5.3 collective-permute-start.1
  48.5 27.4 %shard_map.105 = (bf16[4,16,4,64,512]{4,3,2,1,0:T(8,128)(2,1)}, f32[8,128]{1,0:T(8,128)S(1)}) custom-call(f32[4,16]{1,0:T(4,128)S(1)} %get-tuple-element.169.refs_0_, bf16[4,256,1024]{2,1,0:T(8,128)(2,1)S(1)} %bitcast.86, bf16[1024,512]{1,0:T(8,128)(2,1)S(1)} %copy-done.75, bf16[512,256]{1,0:T(8,128)(2,1)S(1)} %get-tuple-element.125.refs_3_.refs_4_, ...), custom_call_target="tpu_custom_call" | custom-call | flops 6442450944 | bytes 17842432 | tf_op jit(solution)/shard_map/pallas_call | solution.py:329
  80.5 27.4 %shard_map.107 = (bf16[4,16,4,64,512]{4,3,2,1,0:T(8,128)(2,1)}, f32[8,128]{1,0:T(8,128)S(1)}) custom-call(f32[4,16]{1,0:T(4,128)S(1)} %get-tuple-element.169.refs_0_, bf16[4,256,1024]{2,1,0:T(8,128)(2,1)S(1)} %bitcast.87, bf16[1024,512]{1,0:T(8,128)(2,1)S(1)} %copy-done.76, bf16[512,256]{1,0:T(8,128)(2,1)S(1)} %copy-done.67, ...), custom_call_target="tpu_custom_call", output_to_operand_aliasing={{0}: (4, {})} | custom-call | flops 6442450944 | bytes 17842432 | tf_op jit(solution)/shard_map/pallas_call | solution.py:329
  114.5 27.4 %shard_map.113 = (bf16[4,16,4,64,512]{4,3,2,1,0:T(8,128)(2,1)}, f32[8,128]{1,0:T(8,128)}) custom-call(f32[4,16]{1,0:T(4,128)S(1)} %get-tuple-element.169.refs_0_, bf16[4,256,1024]{2,1,0:T(8,128)(2,1)S(1)} %bitcast.88, bf16[1024,512]{1,0:T(8,128)(2,1)S(1)} %copy-done.76, bf16[512,256]{1,0:T(8,128)(2,1)S(1)} %copy-done.68, ...), custom_call_target="tpu_custom_call", output_to_operand_aliasing={{0}: (4, {})} | custom-call | flops 6442450944 | bytes 17842432 | tf_op jit(solution)/shard_map/pallas_call | solution.py:329
  147.1 6.4 collective-permute-start.20
  160.1 20.1 %shard_map.104 = (f32[16,256,1024]{2,1,0:T(8,128)}, f32[8,128]{1,0:T(8,128)S(1)}) custom-call(bf16[256,512]{1,0:T(8,128)(2,1)S(1)} %bitcast.100, bf16[16,256,1024]{2,1,0:T(8,128)(2,1)} %get-tuple-element.62.refs_1_.refs_3_, bf16[16,256,1024]{2,1,0:T(8,128)(2,1)} %collective-permute-done.refs_2_.refs_4_), custom_call_target="tpu_custom_call" | custom-call | flops 4294967296 | bytes 37814272 | tf_op jit(solution)/shard_map/pallas_call | solution.py:329
  183.7 27.4 %shard_map.114 = (bf16[4,16,4,64,512]{4,3,2,1,0:T(8,128)(2,1)}, f32[8,128]{1,0:T(8,128)S(1)}) custom-call(f32[4,16]{1,0:T(4,128)S(1)} %get-tuple-element.169.refs_0_, bf16[4,256,1024]{2,1,0:T(8,128)(2,1)S(1)} %bitcast.89, bf16[1024,512]{1,0:T(8,128)(2,1)S(1)} %copy-done.77, bf16[512,256]{1,0:T(8,128)(2,1)S(1)} %copy-done.69, ...), custom_call_target="tpu_custom_call", output_to_operand_aliasing={{0}: (4, {})} | custom-call | flops 6442450944 | bytes 17842432 | tf_op jit(solution)/shard_map/pallas_call | solution.py:329
  211.8 3.8 collective-permute-start.24
  227.0 7.7 %shard_map.109 = (bf16[4,8,16,512]{3,2,1,0:T(8,128)(2,1)S(1)}, bf16[4,8,16,512]{3,2,1,0:T(8,128)(2,1)S(1)}) custom-call(s32[1]{0:T(128)} %bitcast.refs_0_, bf16[2,16,16,32,256]{4,3,2,1,0:T(8,128)(2,1)} %refs_2_.13, bf16[2,16,16,32,256]{4,3,2,1,0:T(8,128)(2,1)} %refs_2_.13, bf16[8,16,512]{2,1,0:T(8,128)(2,1)S(1)} %get-tuple-element.159.refs_3_.refs_2_, ...), custom_call_target="tpu_custom_call" | custom-call | flops 33554432 | bytes 5767168 | tf_op jit(solution)/shard_map/pallas_call | solution.py:329
  244.9 7.6 %shard_map.116 = (bf16[4,8,16,512]{3,2,1,0:T(8,128)(2,1)S(1)}, bf16[4,8,16,512]{3,2,1,0:T(8,128)(2,1)S(1)}) custom-call(s32[1]{0:T(128)} %bitcast.refs_0_, bf16[2,16,16,32,256]{4,3,2,1,0:T(8,128)(2,1)} %refs_2_.13, bf16[2,16,16,32,256]{4,3,2,1,0:T(8,128)(2,1)} %refs_2_.13, bf16[8,16,512]{2,1,0:T(8,128)(2,1)S(1)} %get-tuple-element.151.refs_3_.refs_2_, ...), custom_call_target="tpu_custom_call" | custom-call | flops 33554432 | bytes 5767168 | tf_op jit(solution)/shard_map/pallas_call | solution.py:329
  263.8 4.9 collective-permute-start.14
  271.0 4.6 collective-permute-start.33
  276.9 4.2 collective-permute-done.14.refs_7_
  291.2 5.6 collective-permute-done.36.refs_17_
  299.5 8.6 %collective-permute-done.18.refs_11_ = bf16[16,32,512]{2,1,0:T(8,128)(2,1)} collective-permute-done((bf16[16,32,512]{2,1,0:T(8,128)(2,1)S(1)}, bf16[16,32,512]{2,1,0:T(8,128)(2,1)}, u32[]{:S(2)}, u32[]{:S(2)}) %collective-permute-start.18) | collective-permute-done | bytes 524320 | tf_op jit(solution)/shard_map/ppermute | solution.py:393
  310.9 8.5 %collective-permute-done.37.refs_18_ = bf16[16,32,512]{2,1,0:T(8,128)(2,1)} collective-permute-done((bf16[16,32,512]{2,1,0:T(8,128)(2,1)S(1)}, bf16[16,32,512]{2,1,0:T(8,128)(2,1)}, u32[]{:S(2)}, u32[]{:S(2)}) %collective-permute-start.37) | collective-permute-done | bytes 524320 | tf_op jit(solution)/shard_map/ppermute | solution.py:393
  321.5 9.1 %collective-permute-done.19.refs_12_ = bf16[16,32,512]{2,1,0:T(8,128)(2,1)} collective-permute-done((bf16[16,32,512]{2,1,0:T(8,128)(2,1)}, bf16[16,32,512]{2,1,0:T(8,128)(2,1)}, u32[]{:S(2)}, u32[]{:S(2)}) %collective-permute-start.19) | collective-permute-done | bytes 524320 | tf_op jit(solution)/shard_map/ppermute | solution.py:393
  330.6 8.7 %collective-permute-done.38.refs_19_ = bf16[16,32,512]{2,1,0:T(8,128)(2,1)} collective-permute-done((bf16[16,32,512]{2,1,0:T(8,128)(2,1)}, bf16[16,32,512]{2,1,0:T(8,128)(2,1)}, u32[]{:S(2)}, u32[]{:S(2)}) %collective-permute-start.38) | collective-permute-done | bytes 524320 | tf_op jit(solution)/shard_map/ppermute | solution.py:393
  343.3 65.5 %shard_map.117 = (bf16[16,256,1024]{2,1,0:T(8,128)(2,1)}, bf16[16,32,512]{2,1,0:T(8,128)(2,1)S(1)}, bf16[16,32,512]{2,1,0:T(8,128)(2,1)S(1)}, bf16[16,32,512]{2,...) custom-call(f32[16,256,1024]{2,1,0:T(8,128)} %get-tuple-element.63.r, ...), custom_call_target="tpu_custom_call" | custom-call | flops 12884901888 | bytes 87031808 | tf_op jit(solution)/shard_map/pallas_call | solution.py:329
  411.9 10.8 %shard_map.118 = (f32[2,256,256]{2,1,0:T(8,128)S(1)}, f32[32,4,8,128]{3,2,1,0:T(8,128)S(1)}) custom-call(f32[4,32]{1,0:T(4,128)S(1)} %pad_maximum_fusion.4.refs_0_, bf16[512,256]{1,0:T(8,128)(2,1)S(1)} %mul.53.refs_1_, bf16[4,256,1024]{2,1,0:T(8,128)(2,1)S(1)} %bitcast.90, bf16[16,256,1024]{2,1,0:T(8,128)(2,1)} %get-tuple-element.62.refs_1_.refs_3_, ...), custom_call_target="tpu_custom_call" | custom-call | flops 2147483648 | bytes 12059136 | tf_op jit(solution)/shard_map/pallas_call | solution.py:329
  425.7 10.8 %shard_map.120 = (f32[2,256,256]{2,1,0:T(8,128)S(1)}, f32[32,4,8,128]{3,2,1,0:T(8,128)S(1)}) custom-call(f32[4,32]{1,0:T(4,128)S(1)} %pad_maximum_fusion.4.refs_0_, bf16[512,256]{1,0:T(8,128)(2,1)S(1)} %mul.53.refs_1_, bf16[4,256,1024]{2,1,0:T(8,128)(2,1)S(1)} %bitcast.91, bf16[16,256,1024]{2,1,0:T(8,128)(2,1)} %get-tuple-element.62.refs_1_.refs_3_, ...), custom_call_target="tpu_custom_call" | custom-call | flops 2147483648 | bytes 12059136 | tf_op jit(solution)/shard_map/pallas_call | solution.py:329
  444.5 5.2 collective-permute-done.43
  458.1 3.8 collective-permute-start.45
  461.9 10.8 %shard_map.124 = (f32[2,256,256]{2,1,0:T(8,128)S(1)}, f32[32,4,8,128]{3,2,1,0:T(8,128)S(1)}) custom-call(f32[4,32]{1,0:T(4,128)S(1)} %pad_maximum_fusion.4.refs_0_, bf16[512,256]{1,0:T(8,128)(2,1)S(1)} %mul.53.refs_1_, bf16[4,256,1024]{2,1,0:T(8,128)(2,1)S(1)} %bitcast.92, bf16[16,256,1024]{2,1,0:T(8,128)(2,1)} %get-tuple-element.62.refs_1_.refs_3_, ...), custom_call_target="tpu_custom_call" | custom-call | flops 2147483648 | bytes 12059136 | tf_op jit(solution)/shard_map/pallas_call | solution.py:329
  477.1 6.2 collective-permute-done.47.refs_1_
  483.9 6.3 collective-permute-start.49
  496.8 4.7 collective-permute-done.50
  511.9 8.6 %shard_map.130 = bf16[4,8,16,512]{3,2,1,0:T(8,128)(2,1)S(1)} custom-call(s32[1]{0:T(128)} %bitcast.refs_0_, bf16[2,16,16,32,256]{4,3,2,1,0:T(8,128)(2,1)} %refs_2_.13, bf16[2,16,16,32,256]{4,3,2,1,0:T(8,128)(2,1)} %refs_2_.13, bf16[4,8,16,512]{3,2,1,0:T(8,128)(2,1)S(1)} %collective-permute-done.58.refs_1_.refs_3_, ...), custom_call_target="tpu_custom_call" | custom-call | flops 33554432 | bytes 5767168 | tf_op jit(solution)/shard_map/pallas_call | solution.py:329
  524.6 8.6 %shard_map.135 = bf16[4,8,16,512]{3,2,1,0:T(8,128)(2,1)S(1)} custom-call(s32[1]{0:T(128)} %bitcast.refs_0_, bf16[2,16,16,32,256]{4,3,2,1,0:T(8,128)(2,1)} %refs_2_.13, bf16[2,16,16,32,256]{4,3,2,1,0:T(8,128)(2,1)} %refs_2_.13, bf16[4,8,16,512]{3,2,1,0:T(8,128)(2,1)S(1)} %collective-permute-done.54.refs_1_.refs_3_, ...), custom_call_target="tpu_custom_call" | custom-call | flops 33554432 | bytes 5767168 | tf_op jit(solution)/shard_map/pallas_call | solution.py:329
  541.4 5.4 collective-permute-start.75
  548.2 10.9 %shard_map.129 = (f32[2,256,256]{2,1,0:T(8,128)S(1)}, f32[32,4,8,128]{3,2,1,0:T(8,128)S(1)}) custom-call(f32[4,32]{1,0:T(4,128)S(1)} %pad_maximum_fusion.4.refs_0_, bf16[512,256]{1,0:T(8,128)(2,1)S(1)} %mul.53.refs_1_, bf16[4,256,1024]{2,1,0:T(8,128)(2,1)S(1)} %bitcast.93, bf16[16,256,1024]{2,1,0:T(8,128)(2,1)} %get-tuple-element.62.refs_1_.refs_3_, ...), custom_call_target="tpu_custom_call" | custom-call | flops 2147483648 | bytes 12059136 | tf_op jit(solution)/shard_map/pallas_call | solution.py:329
  568.1 3.7 reshape.34
  575.9 4.0 collective-permute-done.69.refs_1_
  582.6 8.5 %collective-permute-done.78.refs_1_ = bf16[16,32,512]{2,1,0:T(8,128)(2,1)} collective-permute-done((bf16[16,32,512]{2,1,0:T(8,128)(2,1)}, bf16[16,32,512]{2,1,0:T(8,128)(2,1)}, u32[]{:S(2)}, u32[]{:S(2)}) %collective-permute-start.78) | collective-permute-done | bytes 524320 | tf_op jit(solution)/shard_map/ppermute | solution.py:393
  593.9 3.6 collective-permute-done.59
  601.1 3.4 collective-permute-start.61
  610.0 6.4 shard_map.127
  618.9 3.6 shard_map.132
  622.6 3.8 shard_map.133
  626.5 6.4 shard_map.128
  635.5 3.6 shard_map.134
  639.1 3.6 shard_map.137
  642.8 3.8 shard_map.138
  646.6 3.6 shard_map.139
  650.8 3.5 collective-permute-done.81
  657.9 3.6 collective-permute-done.83
  662.0 3.9 collective-permute-done.84
  (427 shorter events, 194.8 us)
Async XLA Ops:
  37.2 122.0 %collective-permute-start = (bf16[16,256,1024]{2,1,0:T(8,128)(2,1)}, bf16[16,256,1024]{2,1,0:T(8,128)(2,1)}, u32[]{:S(2)}, u32[]{:S(2)}) collective-permute-start(bf16[16,256,1024]{2,1,0:T(8,128)(2,1)} %get-tuple-element.62.refs_1_.refs_3_), channel_id=1, source_target_pairs={{0,1},{1,0},{2,3},{3,2},{4,5},{5,4},{6,7},{7,6},{8,9},{9,8},{10,11... | collective-permute-start | bytes 25165832 | tf_op jit(solution)/shard_map/ppermute | solution.py:405
  37.6 38.2 %collective-permute-start.1 = (bf16[16,32,512]{2,1,0:T(8,128)(2,1)}, bf16[16,32,512]{2,1,0:T(8,128)(2,1)}, u32[]{:S(2)}, u32[]{:S(2)}) collective-permute-start(bf16[16,32,512]{2,1,0:T(8,128)(2,1)} %get-tuple-element.67.refs_2_), channel_id=1, source_target_pairs={{0,8},{1,9},{2,10},{3,11},{4,12},{5,13},{6,14},{7,15}} | collective-permute-start | bytes 1572872 | tf_op jit(solution)/shard_map/ppermute | solution.py:382
  42.9 33.0 %collective-permute-start.2 = (bf16[16,32,512]{2,1,0:T(8,128)(2,1)}, bf16[16,32,512]{2,1,0:T(8,128)(2,1)}, u32[]{:S(2)}, u32[]{:S(2)}) collective-permute-start(bf16[16,32,512]{2,1,0:T(8,128)(2,1)} %get-tuple-element.65.refs_0_), channel_id=1, source_target_pairs={{24,16},{25,17},{26,18},{27,19},{28,20},{29,21},{30,22},{31,23}} | collective-permute-start | bytes 1572872 | tf_op jit(solution)/shard_map/ppermute | solution.py:383
  77.3 30.6 %collective-permute-start.3 = (bf16[16,32,512]{2,1,0:T(8,128)(2,1)S(1)}, bf16[16,32,512]{2,1,0:T(8,128)(2,1)S(1)}, u32[]{:S(2)}, u32[]{:S(2)}) collective-permute-start(bf16[16,32,512]{2,1,0:T(8,128)(2,1)S(1)} %get-tuple-element.69), channel_id=1, source_target_pairs={{0,8},{8,16},{1,9},{9,17},{2,10},{10,18},{3,11},{11,19},{4,12},{12... | collective-permute-start | bytes 1572872 | tf_op jit(solution)/shard_map/ppermute | solution.py:382
  78.6 29.3 %collective-permute-start.4 = (bf16[16,32,512]{2,1,0:T(8,128)(2,1)S(1)}, bf16[16,32,512]{2,1,0:T(8,128)(2,1)S(1)}, u32[]{:S(2)}, u32[]{:S(2)}) collective-permute-start(bf16[16,32,512]{2,1,0:T(8,128)(2,1)S(1)} %get-tuple-element.70), channel_id=1, source_target_pairs={{24,16},{16,8},{25,17},{17,9},{26,18},{18,10},{27,19},{19,11},{28,... | collective-permute-start | bytes 1572872 | tf_op jit(solution)/shard_map/ppermute | solution.py:383
  109.6 32.3 %collective-permute-start.5 = (bf16[16,32,512]{2,0,1:T(8,128)(2,1)S(1)}, bf16[16,32,512]{2,0,1:T(8,128)(2,1)S(1)}, u32[]{:S(2)}, u32[]{:S(2)}) collective-permute-start(bf16[16,32,512]{2,0,1:T(8,128)(2,1)S(1)} %copy.132), channel_id=1, source_target_pairs={{0,8},{8,16},{16,24},{1,9},{9,17},{17,25},{2,10},{10,18},{18,26},{... | collective-permute-start | bytes 1572872 | tf_op jit(solution)/shard_map/ppermute | solution.py:382
  113.2 30.6 %collective-permute-start.6 = (bf16[16,32,512]{2,0,1:T(8,128)(2,1)S(1)}, bf16[16,32,512]{2,0,1:T(8,128)(2,1)S(1)}, u32[]{:S(2)}, u32[]{:S(2)}) collective-permute-start(bf16[16,32,512]{2,0,1:T(8,128)(2,1)S(1)} %copy.133), channel_id=1, source_target_pairs={{24,16},{16,8},{8,0},{25,17},{17,9},{9,1},{26,18},{18,10},{10,2},{... | collective-permute-start | bytes 1572872 | tf_op jit(solution)/shard_map/ppermute | solution.py:383
  145.7 34.5 %collective-permute-start.21 = (bf16[16,32,512]{2,1,0:T(8,128)(2,1)}, bf16[16,32,512]{2,1,0:T(8,128)(2,1)}, u32[]{:S(2)}, u32[]{:S(2)}) collective-permute-start(bf16[16,32,512]{2,1,0:T(8,128)(2,1)} %shard_map.111), channel_id=1, source_target_pairs={{24,16},{25,17},{26,18},{27,19},{28,20},{29,21},{30,22},{31,23}} | collective-permute-start | bytes 1572872 | tf_op jit(solution)/shard_map/ppermute | solution.py:383
  147.1 33.1 %collective-permute-start.20 = (bf16[16,32,512]{2,1,0:T(8,128)(2,1)}, bf16[16,32,512]{2,1,0:T(8,128)(2,1)}, u32[]{:S(2)}, u32[]{:S(2)}) collective-permute-start(bf16[16,32,512]{2,1,0:T(8,128)(2,1)} %shard_map.110), channel_id=1, source_target_pairs={{0,8},{1,9},{2,10},{3,11},{4,12},{5,13},{6,14},{7,15}} | collective-permute-start | bytes 1572872 | tf_op jit(solution)/shard_map/ppermute | solution.py:382
  181.7 29.5 %collective-permute-start.22 = (bf16[16,32,512]{2,1,0:T(8,128)(2,1)S(1)}, bf16[16,32,512]{2,1,0:T(8,128)(2,1)S(1)}, u32[]{:S(2)}, u32[]{:S(2)}) collective-permute-start(bf16[16,32,512]{2,1,0:T(8,128)(2,1)S(1)} %get-tuple-element.82), channel_id=1, source_target_pairs={{0,8},{8,16},{1,9},{9,17},{2,10},{10,18},{3,11},{11,19},{4,12},{12... | collective-permute-start | bytes 1572872 | tf_op jit(solution)/shard_map/ppermute | solution.py:382
  183.0 28.2 %collective-permute-start.23 = (bf16[16,32,512]{2,1,0:T(8,128)(2,1)S(1)}, bf16[16,32,512]{2,1,0:T(8,128)(2,1)S(1)}, u32[]{:S(2)}, u32[]{:S(2)}) collective-permute-start(bf16[16,32,512]{2,1,0:T(8,128)(2,1)S(1)} %get-tuple-element.83), channel_id=1, source_target_pairs={{24,16},{16,8},{25,17},{17,9},{26,18},{18,10},{27,19},{19,11},{28,... | collective-permute-start | bytes 1572872 | tf_op jit(solution)/shard_map/ppermute | solution.py:383
  211.8 23.4 %collective-permute-start.24 = (bf16[16,32,512]{2,0,1:T(8,128)(2,1)S(1)}, bf16[16,32,512]{2,0,1:T(8,128)(2,1)S(1)}, u32[]{:S(2)}, u32[]{:S(2)}) collective-permute-start(bf16[16,32,512]{2,0,1:T(8,128)(2,1)S(1)} %copy.141), channel_id=1, source_target_pairs={{0,8},{8,16},{16,24},{1,9},{9,17},{17,25},{2,10},{10,18},{18,26},{... | collective-permute-start | bytes 1572872 | tf_op jit(solution)/shard_map/ppermute | solution.py:382
  215.8 19.4 %collective-permute-start.25 = (bf16[16,32,512]{2,0,1:T(8,128)(2,1)S(1)}, bf16[16,32,512]{2,0,1:T(8,128)(2,1)S(1)}, u32[]{:S(2)}, u32[]{:S(2)}) collective-permute-start(bf16[16,32,512]{2,0,1:T(8,128)(2,1)S(1)} %copy.142), channel_id=1, source_target_pairs={{24,16},{16,8},{8,0},{25,17},{17,9},{9,1},{26,18},{18,10},{10,2},{... | collective-permute-start | bytes 1572872 | tf_op jit(solution)/shard_map/ppermute | solution.py:383
  235.1 17.9 %collective-permute-start.10 = (bf16[4,8,16,512]{3,1,2,0:T(8,128)(2,1)S(1)}, bf16[4,8,16,512]{3,1,2,0:T(8,128)(2,1)S(1)}, u32[]{:S(2)}, u32[]{:S(2)}) collective-permute-start(bf16[4,8,16,512]{3,1,2,0:T(8,128)(2,1)S(1)} %copy.135), channel_id=1, source_target_pairs={{0,1},{1,0},{2,3},{3,2},{4,5},{5,4},{6,7},{7,6},{8,9},{9,8},{10,11... | collective-permute-start | bytes 1572872 | tf_op jit(solution)/shard_map/ppermute | solution.py:405
  257.5 13.4 %collective-permute-start.30 = (bf16[8,16,512]{2,0,1:T(8,128)(2,1)S(1)}, bf16[8,16,512]{2,0,1:T(8,128)(2,1)S(1)}, u32[]{:S(2)}, u32[]{:S(2)}) collective-permute-start(bf16[8,16,512]{2,0,1:T(8,128)(2,1)S(1)} %get-tuple-element.147), channel_id=1, source_target_pairs={{0,2},{2,0},{4,6},{6,4},{1,3},{3,1},{5,7},{7,5},{8,10},{10,8},{12,... | collective-permute-start | bytes 393224 | tf_op jit(solution)/shard_map/ppermute | solution.py:401
  263.8 17.3 %collective-permute-start.14 = (bf16[16,32,512]{2,1,0:T(8,128)(2,1)S(1)}, bf16[16,32,512]{2,1,0:T(8,128)(2,1)S(1)}, u32[]{:S(2)}, u32[]{:S(2)}) collective-permute-start(bf16[16,32,512]{2,1,0:T(8,128)(2,1)S(1)} %maximum_bitcast_fusion.refs_6_), channel_id=1, source_target_pairs={{0,8},{8,16},{16,24},{1,9},{9,17},{17,25},{2,10},{10,18},{18,26},{... | collective-permute-start | bytes 1572872 | tf_op jit(solution)/shard_map/ppermute | solution.py:392
  268.8 16.8 %collective-permute-start.17 = (bf16[16,32,512]{2,1,0:T(8,128)(2,1)S(1)}, bf16[16,32,512]{2,1,0:T(8,128)(2,1)S(1)}, u32[]{:S(2)}, u32[]{:S(2)}) collective-permute-start(bf16[16,32,512]{2,1,0:T(8,128)(2,1)S(1)} %maximum_bitcast_fusion.refs_6_), channel_id=1, source_target_pairs={{24,16},{16,8},{8,0},{25,17},{17,9},{9,1},{26,18},{18,10},{10,2},{... | collective-permute-start | bytes 1572872 | tf_op jit(solution)/shard_map/ppermute | solution.py:393
  271.0 18.7 %collective-permute-start.33 = (bf16[16,32,512]{2,1,0:T(8,128)(2,1)S(1)}, bf16[16,32,512]{2,1,0:T(8,128)(2,1)S(1)}, u32[]{:S(2)}, u32[]{:S(2)}) collective-permute-start(bf16[16,32,512]{2,1,0:T(8,128)(2,1)S(1)} %maximum_bitcast_fusion.1.refs_13_), channel_id=1, source_target_pairs={{0,8},{8,16},{16,24},{1,9},{9,17},{17,25},{2,10},{10,18},{18,26},{... | collective-permute-start | bytes 1572872 | tf_op jit(solution)/shard_map/ppermute | solution.py:392
  275.6 21.2 %collective-permute-start.36 = (bf16[16,32,512]{2,1,0:T(8,128)(2,1)S(1)}, bf16[16,32,512]{2,1,0:T(8,128)(2,1)S(1)}, u32[]{:S(2)}, u32[]{:S(2)}) collective-permute-start(bf16[16,32,512]{2,1,0:T(8,128)(2,1)S(1)} %maximum_bitcast_fusion.1.refs_13_), channel_id=1, source_target_pairs={{24,16},{16,8},{8,0},{25,17},{17,9},{9,1},{26,18},{18,10},{10,2},{... | collective-permute-start | bytes 1572872 | tf_op jit(solution)/shard_map/ppermute | solution.py:393
  281.1 17.0 %collective-permute-start.15 = (bf16[16,32,512]{2,1,0:T(8,128)(2,1)S(1)}, bf16[16,32,512]{2,1,0:T(8,128)(2,1)}, u32[]{:S(2)}, u32[]{:S(2)}) collective-permute-start(bf16[16,32,512]{2,1,0:T(8,128)(2,1)S(1)} %collective-permute-done.14.refs_7_), channel_id=1, source_target_pairs={{8,16},{16,24},{9,17},{17,25},{10,18},{18,26},{11,19},{19,27},{12,... | collective-permute-start | bytes 1572872 | tf_op jit(solution)/shard_map/ppermute | solution.py:392
  285.5 22.6 %collective-permute-start.18 = (bf16[16,32,512]{2,1,0:T(8,128)(2,1)S(1)}, bf16[16,32,512]{2,1,0:T(8,128)(2,1)}, u32[]{:S(2)}, u32[]{:S(2)}) collective-permute-start(bf16[16,32,512]{2,1,0:T(8,128)(2,1)S(1)} %collective-permute-done.17.refs_10_), channel_id=1, source_target_pairs={{16,8},{8,0},{17,9},{9,1},{18,10},{10,2},{19,11},{11,3},{20,12},{1... | collective-permute-start | bytes 1572872 | tf_op jit(solution)/shard_map/ppermute | solution.py:393
  289.7 19.7 %collective-permute-start.34 = (bf16[16,32,512]{2,1,0:T(8,128)(2,1)S(1)}, bf16[16,32,512]{2,1,0:T(8,128)(2,1)}, u32[]{:S(2)}, u32[]{:S(2)}) collective-permute-start(bf16[16,32,512]{2,1,0:T(8,128)(2,1)S(1)} %collective-permute-done.33.refs_14_), channel_id=1, source_target_pairs={{8,16},{16,24},{9,17},{17,25},{10,18},{18,26},{11,19},{19,27},{12,... | collective-permute-start | bytes 1572872 | tf_op jit(solution)/shard_map/ppermute | solution.py:392
  296.8 22.6 %collective-permute-start.37 = (bf16[16,32,512]{2,1,0:T(8,128)(2,1)S(1)}, bf16[16,32,512]{2,1,0:T(8,128)(2,1)}, u32[]{:S(2)}, u32[]{:S(2)}) collective-permute-start(bf16[16,32,512]{2,1,0:T(8,128)(2,1)S(1)} %collective-permute-done.36.refs_17_), channel_id=1, source_target_pairs={{16,8},{8,0},{17,9},{9,1},{18,10},{10,2},{19,11},{11,3},{20,12},{1... | collective-permute-start | bytes 1572872 | tf_op jit(solution)/shard_map/ppermute | solution.py:393
  298.1 23.4 %collective-permute-start.16 = (bf16[16,32,512]{2,1,0:T(8,128)(2,1)}, bf16[16,32,512]{2,1,0:T(8,128)(2,1)}, u32[]{:S(2)}, u32[]{:S(2)}) collective-permute-start(bf16[16,32,512]{2,1,0:T(8,128)(2,1)} %collective-permute-done.15.refs_8_), channel_id=1, source_target_pairs={{16,24},{17,25},{18,26},{19,27},{20,28},{21,29},{22,30},{23,31}} | collective-permute-start | bytes 1572872 | tf_op jit(solution)/shard_map/ppermute | solution.py:392
  308.1 22.5 %collective-permute-start.19 = (bf16[16,32,512]{2,1,0:T(8,128)(2,1)}, bf16[16,32,512]{2,1,0:T(8,128)(2,1)}, u32[]{:S(2)}, u32[]{:S(2)}) collective-permute-start(bf16[16,32,512]{2,1,0:T(8,128)(2,1)} %collective-permute-done.18.refs_11_), channel_id=1, source_target_pairs={{8,0},{9,1},{10,2},{11,3},{12,4},{13,5},{14,6},{15,7}} | collective-permute-start | bytes 1572872 | tf_op jit(solution)/shard_map/ppermute | solution.py:393
  309.4 21.2 %collective-permute-start.35 = (bf16[16,32,512]{2,1,0:T(8,128)(2,1)}, bf16[16,32,512]{2,1,0:T(8,128)(2,1)}, u32[]{:S(2)}, u32[]{:S(2)}) collective-permute-start(bf16[16,32,512]{2,1,0:T(8,128)(2,1)} %collective-permute-done.34.refs_15_), channel_id=1, source_target_pairs={{16,24},{17,25},{18,26},{19,27},{20,28},{21,29},{22,30},{23,31}} | collective-permute-start | bytes 1572872 | tf_op jit(solution)/shard_map/ppermute | solution.py:392
  319.4 20.0 %collective-permute-start.38 = (bf16[16,32,512]{2,1,0:T(8,128)(2,1)}, bf16[16,32,512]{2,1,0:T(8,128)(2,1)}, u32[]{:S(2)}, u32[]{:S(2)}) collective-permute-start(bf16[16,32,512]{2,1,0:T(8,128)(2,1)} %collective-permute-done.37.refs_18_), channel_id=1, source_target_pairs={{8,0},{9,1},{10,2},{11,3},{12,4},{13,5},{14,6},{15,7}} | collective-permute-start | bytes 1572872 | tf_op jit(solution)/shard_map/ppermute | solution.py:393
  423.0 14.3 %collective-permute-start.41 = (bf16[16,32,512]{2,1,0:T(8,128)(2,1)S(1)}, bf16[16,32,512]{2,1,0:T(8,128)(2,1)S(1)}, u32[]{:S(2)}, u32[]{:S(2)}) collective-permute-start(bf16[16,32,512]{2,1,0:T(8,128)(2,1)S(1)} %get-tuple-element.100), channel_id=1, source_target_pairs={{0,8},{8,16},{1,9},{9,17},{2,10},{10,18},{3,11},{11,19},{4,12},{12... | collective-permute-start | bytes 1572872 | tf_op jit(solution)/shard_map/ppermute | solution.py:382
  441.6 13.1 %collective-permute-start.44 = (bf16[16,32,512]{2,0,1:T(8,128)(2,1)S(1)}, bf16[16,32,512]{2,0,1:T(8,128)(2,1)S(1)}, u32[]{:S(2)}, u32[]{:S(2)}) collective-permute-start(bf16[16,32,512]{2,0,1:T(8,128)(2,1)S(1)} %copy.147), channel_id=1, source_target_pairs={{24,16},{16,8},{8,0},{25,17},{17,9},{9,1},{26,18},{18,10},{10,2},{... | collective-permute-start | bytes 1572872 | tf_op jit(solution)/shard_map/ppermute | solution.py:383
  456.6 16.9 %collective-permute-start.46 = (bf16[16,32,512]{2,1,0:T(8,128)(2,1)}, bf16[16,32,512]{2,1,0:T(8,128)(2,1)}, u32[]{:S(2)}, u32[]{:S(2)}) collective-permute-start(bf16[16,32,512]{2,1,0:T(8,128)(2,1)} %shard_map.123), channel_id=1, source_target_pairs={{24,16},{25,17},{26,18},{27,19},{28,20},{29,21},{30,22},{31,23}} | collective-permute-start | bytes 1572872 | tf_op jit(solution)/shard_map/ppermute | solution.py:383
  458.1 15.4 %collective-permute-start.45 = (bf16[16,32,512]{2,1,0:T(8,128)(2,1)}, bf16[16,32,512]{2,1,0:T(8,128)(2,1)S(1)}, u32[]{:S(2)}, u32[]{:S(2)}) collective-permute-start(bf16[16,32,512]{2,1,0:T(8,128)(2,1)} %shard_map.122), channel_id=1, source_target_pairs={{0,8},{1,9},{2,10},{3,11},{4,12},{5,13},{6,14},{7,15}} | collective-permute-start | bytes 1572872 | tf_op jit(solution)/shard_map/ppermute | solution.py:382
  492.3 13.6 %collective-permute-start.55 = (bf16[8,16,512]{2,1,0:T(8,128)(2,1)S(1)}, bf16[8,16,512]{2,1,0:T(8,128)(2,1)S(1)}, u32[]{:S(2)}, u32[]{:S(2)}) collective-permute-start(bf16[8,16,512]{2,1,0:T(8,128)(2,1)S(1)} %get-tuple-element.138), channel_id=1, source_target_pairs={{0,2},{2,0},{4,6},{6,4},{1,3},{3,1},{5,7},{7,5},{8,10},{10,8},{12,... | collective-permute-start | bytes 393224 | tf_op jit(solution)/shard_map/ppermute | solution.py:401
  520.7 13.5 %collective-permute-start.63 = (bf16[8,16,512]{2,0,1:T(8,128)(2,1)S(1)}, bf16[8,16,512]{2,0,1:T(8,128)(2,1)S(1)}, u32[]{:S(2)}, u32[]{:S(2)}) collective-permute-start(bf16[8,16,512]{2,0,1:T(8,128)(2,1)S(1)} %bitcast.110), channel_id=1, source_target_pairs={{0,2},{2,0},{4,6},{6,4},{1,3},{3,1},{5,7},{7,5},{8,10},{10,8},{12,... | collective-permute-start | bytes 393224 | tf_op jit(solution)/shard_map/ppermute | solution.py:401
  520.9 16.3 %collective-permute-start.64 = (bf16[8,16,512]{2,0,1:T(8,128)(2,1)S(1)}, bf16[8,16,512]{2,0,1:T(8,128)(2,1)S(1)}, u32[]{:S(2)}, u32[]{:S(2)}) collective-permute-start(bf16[8,16,512]{2,0,1:T(8,128)(2,1)S(1)} %bitcast.105), channel_id=1, source_target_pairs={{0,4},{2,6},{4,0},{6,2},{1,5},{3,7},{5,1},{7,3},{8,12},{10,14},{12... | collective-permute-start | bytes 393224 | tf_op jit(solution)/shard_map/ppermute | solution.py:401
  521.6 15.7 %collective-permute-start.65 = (bf16[8,16,512]{2,0,1:T(8,128)(2,1)S(1)}, bf16[8,16,512]{2,0,1:T(8,128)(2,1)S(1)}, u32[]{:S(2)}, u32[]{:S(2)}) collective-permute-start(bf16[8,16,512]{2,0,1:T(8,128)(2,1)S(1)} %bitcast.107), channel_id=1, source_target_pairs={{0,6},{2,4},{4,2},{6,0},{1,7},{3,5},{5,3},{7,1},{8,14},{10,12},{12... | collective-permute-start | bytes 393224 | tf_op jit(solution)/shard_map/ppermute | solution.py:401
  537.3 22.6 %collective-permute-start.66 = (bf16[16,32,512]{2,1,0:T(8,128)(2,1)S(1)}, bf16[16,32,512]{2,1,0:T(8,128)(2,1)}, u32[]{:S(2)}, u32[]{:S(2)}) collective-permute-start(bf16[16,32,512]{2,1,0:T(8,128)(2,1)S(1)} %maximum_bitcast_fusion.2.refs_0_), channel_id=1, source_target_pairs={{0,8},{8,16},{16,24},{1,9},{9,17},{17,25},{2,10},{10,18},{18,26},{... | collective-permute-start | bytes 1572872 | tf_op jit(solution)/shard_map/ppermute | solution.py:392
  540.0 21.6 %collective-permute-start.67 = (bf16[16,32,512]{2,1,0:T(8,128)(2,1)S(1)}, bf16[16,32,512]{2,1,0:T(8,128)(2,1)}, u32[]{:S(2)}, u32[]{:S(2)}) collective-permute-start(bf16[16,32,512]{2,1,0:T(8,128)(2,1)S(1)} %maximum_bitcast_fusion.2.refs_0_), channel_id=1, source_target_pairs={{24,16},{16,8},{8,0},{25,17},{17,9},{9,1},{26,18},{18,10},{10,2},{... | collective-permute-start | bytes 1572872 | tf_op jit(solution)/shard_map/ppermute | solution.py:393
  541.4 21.4 %collective-permute-start.75 = (bf16[16,32,512]{2,1,0:T(8,128)(2,1)S(1)}, bf16[16,32,512]{2,1,0:T(8,128)(2,1)}, u32[]{:S(2)}, u32[]{:S(2)}) collective-permute-start(bf16[16,32,512]{2,1,0:T(8,128)(2,1)S(1)} %maximum_bitcast_fusion.3.refs_0_), channel_id=1, source_target_pairs={{0,8},{8,16},{16,24},{1,9},{9,17},{17,25},{2,10},{10,18},{18,26},{... | collective-permute-start | bytes 1572872 | tf_op jit(solution)/shard_map/ppermute | solution.py:392
  546.8 18.7 %collective-permute-start.76 = (bf16[16,32,512]{2,1,0:T(8,128)(2,1)S(1)}, bf16[16,32,512]{2,1,0:T(8,128)(2,1)}, u32[]{:S(2)}, u32[]{:S(2)}) collective-permute-start(bf16[16,32,512]{2,1,0:T(8,128)(2,1)S(1)} %maximum_bitcast_fusion.3.refs_0_), channel_id=1, source_target_pairs={{24,16},{16,8},{8,0},{25,17},{17,9},{9,1},{26,18},{18,10},{10,2},{... | collective-permute-start | bytes 1572872 | tf_op jit(solution)/shard_map/ppermute | solution.py:393
  559.9 14.5 %collective-permute-start.68 = (bf16[16,32,512]{2,1,0:T(8,128)(2,1)}, bf16[16,32,512]{2,1,0:T(8,128)(2,1)}, u32[]{:S(2)}, u32[]{:S(2)}) collective-permute-start(bf16[16,32,512]{2,1,0:T(8,128)(2,1)} %collective-permute-done.66.refs_0_), channel_id=1, source_target_pairs={{8,16},{16,24},{9,17},{17,25},{10,18},{18,26},{11,19},{19,27},{12,... | collective-permute-start | bytes 1572872 | tf_op jit(solution)/shard_map/ppermute | solution.py:392
  561.5 18.3 %collective-permute-start.69 = (bf16[16,32,512]{2,1,0:T(8,128)(2,1)}, bf16[16,32,512]{2,1,0:T(8,128)(2,1)}, u32[]{:S(2)}, u32[]{:S(2)}) collective-permute-start(bf16[16,32,512]{2,1,0:T(8,128)(2,1)} %collective-permute-done.67.refs_1_), channel_id=1, source_target_pairs={{16,8},{8,0},{17,9},{9,1},{18,10},{10,2},{19,11},{11,3},{20,12},{1... | collective-permute-start | bytes 1572872 | tf_op jit(solution)/shard_map/ppermute | solution.py:393
  562.8 18.3 %collective-permute-start.77 = (bf16[16,32,512]{2,1,0:T(8,128)(2,1)}, bf16[16,32,512]{2,1,0:T(8,128)(2,1)}, u32[]{:S(2)}, u32[]{:S(2)}) collective-permute-start(bf16[16,32,512]{2,1,0:T(8,128)(2,1)} %collective-permute-done.75.refs_0_), channel_id=1, source_target_pairs={{8,16},{16,24},{9,17},{17,25},{10,18},{18,26},{11,19},{19,27},{12,... | collective-permute-start | bytes 1572872 | tf_op jit(solution)/shard_map/ppermute | solution.py:392
  565.5 25.5 %collective-permute-start.78 = (bf16[16,32,512]{2,1,0:T(8,128)(2,1)}, bf16[16,32,512]{2,1,0:T(8,128)(2,1)}, u32[]{:S(2)}, u32[]{:S(2)}) collective-permute-start(bf16[16,32,512]{2,1,0:T(8,128)(2,1)} %collective-permute-done.76.refs_1_), channel_id=1, source_target_pairs={{16,8},{8,0},{17,9},{9,1},{18,10},{10,2},{19,11},{11,3},{20,12},{1... | collective-permute-start | bytes 1572872 | tf_op jit(solution)/shard_map/ppermute | solution.py:393
  574.4 61.1 %collective-permute-start.70 = (bf16[16,32,512]{2,1,0:T(8,128)(2,1)}, bf16[16,32,512]{2,1,0:T(8,128)(2,1)}, u32[]{:S(2)}, u32[]{:S(2)}) collective-permute-start(bf16[16,32,512]{2,1,0:T(8,128)(2,1)} %collective-permute-done.68.refs_0_), channel_id=1, source_target_pairs={{16,24},{17,25},{18,26},{19,27},{20,28},{21,29},{22,30},{23,31}} | collective-permute-start | bytes 1572872 | tf_op jit(solution)/shard_map/ppermute | solution.py:392
  579.9 55.7 %collective-permute-start.71 = (bf16[16,32,512]{2,1,0:T(8,128)(2,1)}, bf16[16,32,512]{2,1,0:T(8,128)(2,1)}, u32[]{:S(2)}, u32[]{:S(2)}) collective-permute-start(bf16[16,32,512]{2,1,0:T(8,128)(2,1)} %collective-permute-done.69.refs_1_), channel_id=1, source_target_pairs={{8,0},{9,1},{10,2},{11,3},{12,4},{13,5},{14,6},{15,7}} | collective-permute-start | bytes 1572872 | tf_op jit(solution)/shard_map/ppermute | solution.py:393
  581.2 65.4 %collective-permute-start.79 = (bf16[16,32,512]{2,1,0:T(8,128)(2,1)}, bf16[16,32,512]{2,1,0:T(8,128)(2,1)}, u32[]{:S(2)}, u32[]{:S(2)}) collective-permute-start(bf16[16,32,512]{2,1,0:T(8,128)(2,1)} %collective-permute-done.77.refs_0_), channel_id=1, source_target_pairs={{16,24},{17,25},{18,26},{19,27},{20,28},{21,29},{22,30},{23,31}} | collective-permute-start | bytes 1572872 | tf_op jit(solution)/shard_map/ppermute | solution.py:392
  591.1 55.5 %collective-permute-start.80 = (bf16[16,32,512]{2,1,0:T(8,128)(2,1)}, bf16[16,32,512]{2,1,0:T(8,128)(2,1)}, u32[]{:S(2)}, u32[]{:S(2)}) collective-permute-start(bf16[16,32,512]{2,1,0:T(8,128)(2,1)} %collective-permute-done.78.refs_1_), channel_id=1, source_target_pairs={{8,0},{9,1},{10,2},{11,3},{12,4},{13,5},{14,6},{15,7}} | collective-permute-start | bytes 1572872 | tf_op jit(solution)/shard_map/ppermute | solution.py:393
  601.1 53.7 %collective-permute-start.61 = (f32[32,16]{0,1:T(8,128)S(1)}, f32[32,16]{0,1:T(8,128)}, u32[]{:S(2)}, u32[]{:S(2)}) collective-permute-start(f32[32,16]{0,1:T(8,128)S(1)} %add.134), channel_id=1, source_target_pairs={{0,8},{8,0},{16,24},{24,16},{1,9},{9,1},{17,25},{25,17},{2,10},{10... | collective-permute-start | bytes 6152 | tf_op jit(solution)/shard_map/ppermute | solution.py:424
  (130 other events, 1683.3 us)

commit v3 on v2

--- a/solution.py
+++ b/solution.py
@@ -13,7 +13,7 @@
 BF = jnp.bfloat16
 F32 = jnp.float32
 TWO_PI = 2.0 * math.pi
-CHUNKS = 2
+CHUNKS = 1
 VMEM = 48 * 1024 * 1024
 
 
@@ -52,13 +52,9 @@
 
 
 def gelu_slope(value):
-    bell = jnp.exp(-0.5 * value * value)
-    t = pl.reciprocal(1.0 + (0.3275911 / math.sqrt(2.0)) * jnp.abs(value))
-    poly = 0.5 * 1.061405429
-    for a in (-1.453152027, 1.421413741, -0.284496736, 0.254829592):
-        poly = poly * t + 0.5 * a
-    tail = poly * t * bell
-    return jnp.where(value >= 0.0, 1.0 - tail, tail) + value * bell * (1.0 / math.sqrt(2.0 * math.pi))
+    return 0.5 * (1.0 + lax.erf(value * (1.0 / math.sqrt(2.0)))) + value * jnp.exp(-0.5 * value * value) * (
+        1.0 / math.sqrt(2.0 * math.pi)
+    )
 
 
 def lift_rows(fields, lw, chan):
@@ -89,64 +85,57 @@
     return [refs[i * each : (i + 1) * each] for i in range(CHUNKS)]
 
 
-def lift_kernel(scale, lw, fields, col, row_tab, lifted, *outs):
+def lift_kernel(bunch, scale, lw, fields, col, row_tab, lifted, *outs):
     group, rows, cells = lifted.shape
     first = pl.program_id(0) * group
-    step = min(rows, 32)
-    us = [[] for _ in range(group)]
-    for lo in range(0, rows, step):
-        f = [fields[j, lo : lo + step].astype(F32) for j in range(fields.shape[0])]
-        for c in range(group):
-            v = lift_rows(f, lw, first + c).astype(BF)
-            lifted[c, lo : lo + step] = v
-            us[c].append(jnp.dot(v, col[...], preferred_element_type=F32).astype(BF))
-    for c in range(group):
-        split_modes(row_forward(jnp.concatenate(us[c], 0), row_tab[...], scale), by_part(outs), c)
+    lanes = min(cells, 512)
+    for b in range(0, group, bunch):
+        for lo in range(0, rows, 16):
+            for at in range(0, cells, lanes):
+                f = [fields[j, lo : lo + 16, at : at + lanes].astype(F32) for j in range(fields.shape[0])]
+                for c in range(b, b + bunch):
+                    lifted[c, lo : lo + 16, at : at + lanes] = lift_rows(f, lw, first + c).astype(BF)
+        u = jnp.dot(lifted[b : b + bunch].reshape(bunch * rows, cells), col[...], preferred_element_type=F32).astype(BF)
+        for c in range(bunch):
+            split_modes(row_forward(u[c * rows : (c + 1) * rows], row_tab[...], scale), by_part(outs), b + c)
 
 
 def slope_kernel(scale, first, lw, fields, col, row_tab, *refs):
     out, token = refs[-2:]
     inputs, rows, cells = fields.shape
-    blocks, sub = out.shape[0], out.shape[3]
-    chan = first + pl.program_id(0)
-    step = min(rows, 32)
-    us = [[] for _ in range(inputs)]
-    for lo in range(0, rows, step):
-        f = [fields[j, lo : lo + step].astype(F32) for j in range(inputs)]
-        t = lift_rows(f, lw, chan)
-        slope = 1.0 - t * t
+    blocks, group, sub = out.shape[0], out.shape[1], out.shape[3]
+    for c in range(group):
+        chan = first + pl.program_id(0) * group + c
+        w = [[] for _ in range(inputs)]
+        for lo in range(0, rows, 16):
+            f = [fields[j, lo : lo + 16].astype(F32) for j in range(inputs)]
+            t = lift_rows(f, lw, chan)
+            slope = 1.0 - t * t
+            for j in range(inputs):
+                w[j].append((f[j] * slope).astype(BF))
+        u = jnp.dot(jnp.concatenate(sum(w, []), 0), col[...], preferred_element_type=F32).astype(BF)
         for j in range(inputs):
-            us[j].append(jnp.dot((f[j] * slope).astype(BF), col[...], preferred_element_type=F32).astype(BF))
-    for j in range(inputs):
-        v = row_forward(jnp.concatenate(us[j], 0), row_tab[...], scale)
-        for d in range(blocks):
-            out[d, 0, j] = v[d * sub : (d + 1) * sub]
+            v = row_forward(u[j * rows : (j + 1) * rows], row_tab[...], scale)
+            for d in range(blocks):
+                out[d, c, j] = v[d * sub : (d + 1) * sub]
     token[...] = jnp.zeros(token.shape, F32)
 
 
-def pair_kernel(low, high, f_low, f_high, out):
+def pair_kernel(n, *refs):
+    out, token = refs[-2:]
     for c in range(out.shape[0]):
+        back = [b[c].astype(F32) for b in refs[:n]]
         for j in range(out.shape[1]):
             total = None
-            for b, f in ((low, f_low), (high, f_high)):
-                prod = b[c].astype(F32) * f[0, c, j].astype(F32)
-                for r in range(0, prod.shape[0], 8):
-                    for k in range(0, prod.shape[1], 128):
-                        tile = prod[r : r + 8, k : k + 128]
-                        total = tile if total is None else total + tile
-            out[c, j] = total
-
-
-def own_pair_kernel(low, f_low, out):
-    for c in range(out.shape[0]):
-        for j in range(out.shape[1]):
-            total = None
-            prod = low[c].astype(F32) * f_low[0, c, j].astype(F32)
-            for r in range(0, prod.shape[0], 8):
-                for k in range(0, prod.shape[1], 128):
-                    tile = prod[r : r + 8, k : k + 128]
-                    total = tile if total is None else total + tile
-            out[c, j] = total
+            for b, f in zip(back, refs[n : 2 * n], strict=True):
+                for r in range(0, b.shape[0], 8):
+                    prod = b[r : r + 8] * f[0, c, j, r : r + 8].astype(F32)
+                    total = prod if total is None else total + prod
+            tile = total[:, :128]
+            for k in range(128, total.shape[1], 128):
+                tile = tile + total[:, k : k + 128]
+            out[c, j] = tile
+    token[...] = jnp.zeros(token.shape, F32)
 
 
 def local_kernel(mix, own, other, out, token):
@@ -193,33 +182,34 @@
     lax.fori_loop(0, cells // 256, lanes, 0)
 
 
-def row_inverse(parts, row_inv):
+def row_inverse(parts, chan, row_inv):
     rows = row_inv.shape[0] // 2
     width = parts[0][0].shape[-1] // 2
     hops = (len(parts[0]) - 1) // 2
-    blocks = [part[0][0] for part in parts]
+    blocks = [part[0][chan] for part in parts]
     for s in range(hops - 1, -1, -1):
-        blocks += [part[1 + s][0] + part[hops + hops - s][0] for part in parts]
+        blocks += [part[1 + s][chan] + part[hops + hops - s][chan] for part in parts]
     prod = jnp.dot(row_inv, jnp.concatenate(blocks, 0), preferred_element_type=F32)
     real = prod[:rows, :width] - prod[rows:, width:]
     imag = prod[:rows, width:] + prod[rows:, :width]
     return jnp.concatenate([real.astype(BF), imag.astype(BF)], 1)
 
 
-def middle_kernel(blocks, grid_scale, scale, local, cotan, col, col_inv, row_tab, row_inv, *refs):
+def middle_kernel(blocks, bunch, grid_scale, scale, local, cotan, col, col_inv, row_tab, row_inv, *refs):
     n_in = CHUNKS * (2 * blocks - 1)
-    grad, outs = refs[n_in], refs[n_in + 1 :]
-    rows = grad.shape[1]
-    h = row_inverse(by_part(refs[:n_in]), row_inv[...])
-    step = min(rows, 32)
-    pieces = []
-    for lo in range(0, rows, step):
-        grid = jnp.dot(h[lo : lo + step], col_inv[...], preferred_element_type=F32)
-        pre = grid * grid_scale + local[0, lo : lo + step]
-        g = (cotan[0, 0, lo : lo + step].astype(F32) * gelu_slope(pre)).astype(BF)
-        grad[0, lo : lo + step] = g
-        pieces.append(jnp.dot(g, col[...], preferred_element_type=F32).astype(BF))
-    split_modes(row_forward(jnp.concatenate(pieces, 0), row_tab[...], scale), by_part(outs), 0)
+    parts, grad, outs = by_part(refs[:n_in]), refs[n_in], refs[n_in + 1 :]
+    group, rows, cells = grad.shape
+    for b in range(0, group, bunch):
+        h = jnp.concatenate([row_inverse(parts, c, row_inv[...]) for c in range(b, b + bunch)], 0)
+        grid = jnp.dot(h, col_inv[...], preferred_element_type=F32)
+        for c in range(bunch):
+            for lo in range(0, rows, 16):
+                pre = grid[c * rows + lo : c * rows + lo + 16] * grid_scale + local[b + c, lo : lo + 16]
+                slope = cotan[0, b + c, lo : lo + 16].astype(F32) * gelu_slope(pre)
+                grad[b + c, lo : lo + 16] = slope.astype(BF)
+        u = jnp.dot(grad[b : b + bunch].reshape(bunch * rows, cells), col[...], preferred_element_type=F32).astype(BF)
+        for c in range(bunch):
+            split_modes(row_forward(u[c * rows : (c + 1) * rows], row_tab[...], scale), by_part(outs), b + c)
 
 
 def mix_kernel(samples, core, w_keep, w_send, *refs):
@@ -368,32 +358,45 @@
     )
 
 
-def chain_sum(parts, fill, start):
-    hops = len(parts) - 1
+def run_next(fill, source):
+    return fill.pop(0)(source) if fill else None
+
+
+def chain_sums(shares, fill):
+    hops = len(shares[0]) - 1
     blocks = hops + 1
-    below = above = None
-    tokens = []
+    got = [None] * len(shares)
+    token = None
     for t in range(hops):
-        up, down = parts[hops - t], parts[t + 1]
-        if t:
-            up, down = add_pairs(up, below, down, above, tokens)
-        elif start:
-            up, down = hold(up, *start), hold(down, *start)
-        below = lax.ppermute(up, "blk", [(z, z + 1) for z in range(t + 1)])
-        above = lax.ppermute(down, "blk", [(blocks - 1 - z, blocks - 2 - z) for z in range(t + 1)])
-        tokens = [fill.pop(0)()] if fill else []
-    return parts[0], below, above
-
-
-def chain_gather(own, blocks):
-    below, above = [], []
-    up = down = own
+        for p, part in enumerate(shares):
+            up, down = part[hops - t], part[t + 1]
+            if t:
+                up, down = add_pairs(up, got[p][1], down, got[p][2], [] if token is None else [token])
+            elif token is not None:
+                up, down = hold(up, token), hold(down, token)
+            below = lax.ppermute(up, "blk", [(z, z + 1) for z in range(t + 1)])
+            above = lax.ppermute(down, "blk", [(blocks - 1 - z, blocks - 2 - z) for z in range(t + 1)])
+            got[p] = (part[0], below, above)
+            token = run_next(fill, up)
+    return got, token
+
+
+def chain_gathers(owns, blocks, below, above, fill):
+    token = None
     for t in range(blocks - 1):
-        up = lax.ppermute(up, "blk", [(z, z + 1) for z in range(t, blocks - 1)])
-        down = lax.ppermute(down, "blk", [(blocks - 1 - z, blocks - 2 - z) for z in range(t, blocks - 1)])
-        below.append(up)
-        above.append(down)
-    return [own, *below, *above]
+        for p, own in enumerate(owns):
+            if t and token is not None:
+                below[p][-1], above[p][-1] = hold(below[p][-1], token), hold(above[p][-1], token)
+            elif token is not None:
+                own = hold(own, token)
+                owns[p] = own
+            up, down = (below[p][-1], above[p][-1]) if t else (own, own)
+            below[p].append(lax.ppermute(up, "blk", [(z, z + 1) for z in range(t, blocks - 1)]))
+            above[p].append(
+                lax.ppermute(down, "blk", [(blocks - 1 - z, blocks - 2 - z) for z in range(t, blocks - 1)])
+            )
+            token = run_next(fill, up)
+    return token
 
 
 def swap_samples(pieces):
@@ -405,15 +408,17 @@
     return lax.ppermute(value, "chan", [(0, 1), (1, 0)])
 
 
-def to_modes(shares, samples):
+def to_modes(shares, samples, token):
     own, below, above = shares
+    if token is not None:
+        own = hold(own, token)
     total = (own.astype(F32) + below.astype(F32) + above.astype(F32)).astype(BF).transpose(1, 0, 2)
     sub = total.shape[0] // samples
     return swap_samples([total[j * sub : (j + 1) * sub] for j in range(samples)])
 
 
-def from_modes(pieces, blocks):
-    return chain_gather(jnp.concatenate(swap_samples(pieces), 0).transpose(1, 0, 2), blocks)
+def from_modes(pieces):
+    return jnp.concatenate(swap_samples(pieces), 0).transpose(1, 0, 2)
 
 
 def all_sum(value, axes):
@@ -476,9 +481,9 @@
         return [(shape, BF, (n, *shape[1:]), lambda i, *_: (i, 0, 0)) for _ in range(CHUNKS * blocks)]
 
     matrix = chans * rows * 4 * freqs * (cells + 2 * modes)
-    group = 2
+    group, bunch = math.gcd(chans, 8), math.gcd(chans, 4)
     lifted, *shares = call(
-        functools.partial(lift_kernel, unit_scale),
+        functools.partial(lift_kernel, bunch, unit_scale),
         (chans // group,),
         [(own_lw, None, None), whole(sample), whole(col), whole(row_tab)],
         [((chans, rows, cells), BF, (group, rows, cells), lambda i, *_: (i, 0, 0)), *part_outs(group)],
@@ -491,23 +496,23 @@
     slopes = [None]
 
     def slope_piece(first, count):
-        def run():
+        def run(source):
             got, token = call(
                 functools.partial(slope_kernel, unit_scale, first),
-                (count,),
+                (count // 2,),
                 [(own_lw, None, None), whole(sample), whole(col), whole(row_tab)],
                 [
                     (
                         (blocks, chans, inputs, sub, width),
                         BF,
-                        (blocks, 1, inputs, sub, width),
-                        lambda i, *_, first=first: (0, first + i, 0, 0, 0),
+                        (blocks, 2, inputs, sub, width),
+                        lambda i, *_, first=first: (0, first // 2 + i, 0, 0, 0),
                     ),
                     TOKEN,
                 ],
                 matrix * inputs * count // chans,
                 count * rows * cells,
-                tokens=() if slopes[0] is not None else (shares[0][0],),
+                tokens=(source,),
                 into=slopes[0],
             )
             slopes[0] = got
@@ -517,20 +522,25 @@
 
     locals_ = [None]
 
-    def local_piece():
-        got, token = call(
-            local_kernel,
-            (rows // group_rows,),
-            [
-                whole(spread.T),
-                (lifted, (chans, group_rows, cells), lambda i, *_: (0, i, 0)),
-                (lifted_other, (chans, group_rows, cells), lambda i, *_: (0, i, 0)),
-            ],
-            [((chans, rows, cells), F32, (chans, group_rows, cells), lambda i, *_: (0, i, 0)), TOKEN],
-            4 * chans * chans * group_rows * rows * cells,
-        )
-        locals_[0] = got
-        return token
+    def local_piece(first, count):
+        def run(source):
+            at = lambda i, *_: (0, first + i, 0)
+            locals_[0], token = call(
+                local_kernel,
+                (count,),
+                [
+                    whole(spread.T),
+                    (lifted, (chans, group_rows, cells), at),
+                    (lifted_other, (chans, group_rows, cells), at),
+                ],
+                [((chans, rows, cells), F32, (chans, group_rows, cells), at), TOKEN],
+                4 * chans * chans * group_rows * group_rows * count * cells,
+                tokens=(source,),
+                into=locals_[0],
+            )
+            return token
+
+        return run
 
     def weight_half(part, other):
         return (
@@ -549,15 +559,15 @@
         return ((samples, piece, n, width), BF, (samples, 1, n, width), lambda i, *_: (0, i, 0, 0))
 
     mix_flops = 16 * samples * piece * chans * half * freqs
-    count = -(-chans // 5)
-    fill = [slope_piece(i, min(count, chans - i)) for i in range(0, chans, count)]
-    fill.insert(3, local_piece)
-    field_modes, out_parts = [], []
-    previous = ()
+    count = chans // 2
+    fill = [slope_piece(i, count) for i in range(0, chans, count)]
+    field_modes, out_parts, sent = [], [], []
+
+    got, token = chain_sums(shares, fill)
+    for run in fill:
+        token = run(shares[0][0])
     for part in range(CHUNKS):
-        got = chain_sum(shares[part], fill, previous)
-        previous = got[1:]
-        xs = to_modes(got, samples)
+        xs = to_modes(got[part], samples, token)
         field_modes.append(xs)
         keep, send = call(
             functools.partial(mix_kernel, samples),
@@ -566,26 +576,35 @@
             [stack_out(half)] * 2,
             mix_flops,
             prefetch=core_ref,
+            tokens=sent[-1:],
         )
+        token = keep
         total = (keep.astype(F32) + swap_cores(send).astype(F32)).astype(BF)
-        out_parts += from_modes([total[j] for j in range(samples)], blocks)
-    while fill:
-        fill.pop(0)()
+        sent.append(from_modes([total[j] for j in range(samples)]))
+    steps = rows // group_rows
+    count = -(-steps // 2)
+    fill = [local_piece(i, min(count, steps - i)) for i in range(0, steps, count)]
+    below, above = [[] for _ in range(CHUNKS)], [[] for _ in range(CHUNKS)]
+    chain_gathers(sent, blocks, below, above, fill)
+    for part in range(CHUNKS):
+        out_parts += [sent[part], *below[part], *above[part]]
+    for run in fill:
+        run(sent[-1])
     slopes, local = slopes[0], locals_[0]
 
     grad_z, *shares = call(
-        functools.partial(middle_kernel, blocks, 2.0 * unit_scale, 2.0 * unit_scale),
-        (chans,),
+        functools.partial(middle_kernel, blocks, math.gcd(chans, 2), 2.0 * unit_scale, 2.0 * unit_scale),
+        (chans // bunch,),
         [
-            channel(local),
-            (cotangent, (1, 1, rows, cells), lambda i, *_: (0, i, 0, 0)),
+            channel(local, bunch),
+            (cotangent, (1, bunch, rows, cells), lambda i, *_: (0, i, 0, 0)),
             whole(col),
             whole(col_inv),
             whole(row_tab),
             whole(row_inv),
-            *[channel(a) for a in out_parts],
+            *[channel(a, bunch) for a in out_parts],
         ],
-        [((chans, rows, cells), BF, (1, rows, cells), lambda i, *_: (i, 0, 0)), *part_outs(1)],
+        [((chans, rows, cells), BF, (bunch, rows, cells), lambda i, *_: (i, 0, 0)), *part_outs(bunch)],
         2 * matrix,
         3 * chans * rows * cells,
     )
@@ -596,7 +615,7 @@
     def back_piece(first, count):
         at = lambda i, *_: (0, first + i, 0)
 
-        def run():
+        def run(source):
             t, v = call(
                 local_back_kernel,
                 (count,),
@@ -619,6 +638,7 @@
                 ],
                 8 * chans * chans * group_rows * group_rows * count * cells,
                 2 * chans * group_rows * count * cells,
+                tokens=(source,),
             )
             terms.append(t)
             local_sums.append(v)
@@ -627,14 +647,15 @@
         return run
 
     steps = rows // group_rows
-    count = -(-steps // 4)
+    count = -(-steps // 2)
     fill = [back_piece(i, min(count, steps - i)) for i in range(0, steps, count)]
-    previous = ()
-    grad_modes, grad_others, back_parts = [], [], []
+    grad_modes, grad_others, sent = [], [], []
+
+    got, token = chain_sums(shares, fill)
+    for run in fill:
+        token = run(grad_z)
     for part in range(CHUNKS):
-        got = chain_sum(shares[part], fill, previous)
-        previous = got[1:]
-        gs = to_modes(got, samples)
+        gs = to_modes(got[part], samples, token)
         other = swap_cores(jnp.stack(gs))
         grad_modes.append(gs)
         grad_others.append(other)
@@ -645,77 +666,90 @@
             [stack_out(chans)],
             mix_flops,
             prefetch=core_ref,
+            tokens=sent[-1:],
         )
-        back_parts.append(from_modes([back[j] for j in range(samples)], blocks))
-    while fill:
-        fill.pop(0)()
+        token = back
+        sent.append(from_modes([back[j] for j in range(samples)]))
 
     term = sum(terms).reshape(2 * chans, group_rows, chans, group_rows)
     term = jnp.sum(term * jnp.eye(group_rows, dtype=F32)[None, :, None, :], axis=(1, 3))
     own_first = jnp.stack([term[:chans], term[chans:]])
     ordered = jnp.where(core == 0, own_first, own_first[::-1]).reshape(2 * chans, chans)
-    local_grad = all_sum(ordered * norm_scale, ("dp", "blk"))
-
-    spectral_grad, tokens = None, []
-    for part in range(CHUNKS):
-        spectral_grad, token = call(
-            functools.partial(weight_kernel, samples),
-            (piece,),
-            [
-                stacked(grad_others[part]),
-                *[row_mode(x) for x in field_modes[part]],
-                *[row_mode(g) for g in grad_modes[part]],
-            ],
-            [
-                (
-                    (2, mode_dev, chans, 2 * half, freqs),
-                    BF,
-                    (2, 1, chans, 2 * half, freqs),
-                    lambda i, *_, part=part: (0, part * piece + i, 0, 0, 0),
-                ),
-                TOKEN,
-            ],
-            mix_flops,
-            prefetch=core_ref,
-            into=spectral_grad,
-        )
-        tokens.append(token)
+    ordered = ordered * norm_scale
+
+    gradient = [None]
+
+    def weight_piece(part):
+        def run(source):
+            gradient[0], token = call(
+                functools.partial(weight_kernel, samples),
+                (piece,),
+                [
+                    stacked(grad_others[part]),
+                    *[row_mode(x) for x in field_modes[part]],
+                    *[row_mode(g) for g in grad_modes[part]],
+                ],
+                [
+                    (
+                        (2, mode_dev, chans, 2 * half, freqs),
+                        BF,
+                        (2, 1, chans, 2 * half, freqs),
+                        lambda i, *_: (0, part * piece + i, 0, 0, 0),
+                    ),
+                    TOKEN,
+                ],
+                mix_flops,
+                prefetch=core_ref,
+                tokens=(source,),
+                into=gradient[0],
+            )
+            return token
+
+        return run
 
     sums = []
-    bunch = 4
-    for part in range(CHUNKS):
-        own, arrived = back_parts[part][0], back_parts[part][1:]
-        hops = blocks - 1
-        out = [((chans, inputs, 8, 128), F32, (bunch, inputs, 8, 128), lambda i, *_: (i, 0, 0, 0))]
-
-        def spectra(d, part=part):
+    at_once = 4
+
+    def pairs(modes_of, tokens=()):
+        def spectra(part, d):
             return (
                 slopes,
-                (1, bunch, inputs, sub // CHUNKS, width),
-                lambda i, *_, d=d, part=part: (d, i, 0, part, 0),
+                (1, at_once, inputs, sub // CHUNKS, width),
+                lambda i, *_: (d, i, 0, part, 0),
             )
 
-        flops = 4 * chans * inputs * sub * width // CHUNKS
-        sums += call(own_pair_kernel, (chans // bunch,), [channel(own, bunch), spectra(0)], out, flops)
-        for t in range(hops):
-            last = part == CHUNKS - 1 and t == hops - 1
-            sums += call(
-                pair_kernel,
-                (chans // bunch,),
-                [
-                    channel(arrived[t], bunch),
-                    channel(arrived[hops + t], bunch),
-                    spectra(blocks - 1 - t),
-                    spectra(1 + t),
-                ],
-                out,
-                2 * flops,
-                tokens=tokens if last else (),
-            )
+        got, token = call(
+            functools.partial(pair_kernel, len(modes_of)),
+            (chans // at_once,),
+            [channel(a, at_once) for *_, a in modes_of] + [spectra(p, d) for p, d, _ in modes_of],
+            [((chans, inputs, 8, 128), F32, (at_once, inputs, 8, 128), lambda i, *_: (i, 0, 0, 0)), TOKEN],
+            4 * len(modes_of) * chans * inputs * sub * width // CHUNKS,
+            tokens=tokens,
+        )
+        sums.append(got)
+        return token
+
+    below, above = [[] for _ in range(CHUNKS)], [[] for _ in range(CHUNKS)]
+
+    def arrived(part, t):
+        return [(part, blocks - 1 - t, below[part][t]), (part, 1 + t, above[part][t])]
+
+    def pair_piece(part, t):
+        return lambda source: pairs(([(part, 0, sent[part])] if t == 0 else []) + arrived(part, t), [source])
+
+    fill = [weight_piece(part) for part in range(CHUNKS)]
+    fill += [pair_piece(part, t) for t in range(blocks - 2) for part in range(CHUNKS)]
+    token = chain_gathers(sent, blocks, below, above, fill)
+    for run in fill:
+        token = run(sent[-1])
+    pairs(sum([arrived(part, blocks - 2) for part in range(CHUNKS)], []), [ordered] + ([] if token is None else [token]))
+    spectral_grad = gradient[0]
     lift_own = jnp.sum(sum(sums), axis=(2, 3)).T
     lift_local = jnp.sum(sum(local_sums), axis=(2, 3)).T
     lift_own = jnp.concatenate([lift_own + lift_local[:, :chans], lift_local[:, chans:]], 1) * norm_scale
-    lift_own = all_sum(lift_own, ("dp", "blk"))
+    packed = all_sum(jnp.concatenate([ordered.reshape(-1), lift_own.reshape(-1)]), ("dp", "blk"))
+    local_grad = packed[: ordered.size].reshape(ordered.shape)
+    lift_own = packed[ordered.size :].reshape(lift_own.shape)
     theirs = swap_cores(lift_own)
     mine = lift_own[:, :chans] + theirs[:, chans:]
     his = lift_own[:, chans:] + theirs[:, :chans]

time: 678 us -> 503 us (0.74)
  Pallas kernels: 347 us -> 197 us
  waiting for transfers between devices: 122 us -> 187 us
  starting transfers between devices: 133 us -> 72.8 us
  local copies, waits for them, and re-layouts: 50.1 us -> 26 us
    pallas_call x33 -> x18, Pallas kernels: 347 us -> 197 us  [call(): pl.pallas_call(kernel, grid_spec=pltpu.PrefetchScalarGridSpec(num_scalar_...]
    ppermute x48 -> x24, waiting for transfers between devices: 83.4 us -> 130 us  [the longest x6 70.8 us: chain_gathers(): lax.ppermute(down, 'blk', [(blocks - 1 - z, blocks - 2 - z) for z in rang...]
    ppermute x48 -> x24, starting transfers between devices: 97.3 us -> 55.2 us  [the longest x6 26.5 us: chain_sums(): below = lax.ppermute(up, 'blk', [(z, z + 1) for z in range(t + 1)])]
    ppermute x24 -> x12, waiting for transfers between devices: 19.1 us -> 38 us  [swap_samples(): lax.ppermute(pieces[j], 'dp', [(i, i ^ j) for i in range(n)])]
    unnamed x196 -> x80, local copies, waits for them, and re-layouts: 31 us -> 12.4 us
    ppermute x24 -> x12, starting transfers between devices: 29.8 us -> 14.3 us  [swap_samples(): lax.ppermute(pieces[j], 'dp', [(i, i ^ j) for i in range(n)])]
    ppermute x8 -> x4, waiting for transfers between devices: 18.8 us -> 12.7 us  [all_sum(): value = value + lax.ppermute(value, axis, [(i, i ^ step) for i in range(n)])]
  transfers between devices with their start and end apart: 86 -> 44, of which waited for: 31 -> 30; matrix products, arithmetic and copies ran while one was open for 5% -> 4% of each run, Pallas kernels for 37% -> 27%
where the time goes in v3:
time: 503 us; the launch traced here: 495 us
  Pallas kernels  197 us (39%)
  waiting for transfers between devices  187 us (37%)
  starting transfers between devices  72.8 us (14%)
  local copies, waits for them, and re-layouts  26 us (5%)
  other arithmetic  10.1 us (2%)
    pallas_call x18, Pallas kernels, call(): pl.pallas_call(kernel, grid_spec=pltpu.PrefetchScalarGridSpec(num_scalar_...  197 us
    ppermute x6, waiting for transfers between devices, chain_gathers(): lax.ppermute(down, 'blk', [(blocks - 1 - z, blocks - 2 - z) for z in rang...  70.8 us
    ppermute x12, waiting for transfers between devices, swap_samples(): lax.ppermute(pieces[j], 'dp', [(i, i ^ j) for i in range(n)])  38 us
    ppermute x6, waiting for transfers between devices, chain_sums(): lax.ppermute(down, 'blk', [(blocks - 1 - z, blocks - 2 - z) for z in rang...  35.5 us
    ppermute x6, starting transfers between devices, chain_sums(): below = lax.ppermute(up, 'blk', [(z, z + 1) for z in range(t + 1)])  26.5 us
    ppermute x6, starting transfers between devices, chain_gathers(): lax.ppermute(up, 'blk', [(z, z + 1) for z in range(t, blocks - 1)])  15 us
    ppermute x12, starting transfers between devices, swap_samples(): lax.ppermute(pieces[j], 'dp', [(i, i ^ j) for i in range(n)])  14.3 us
    ppermute x6, waiting for transfers between devices, chain_sums(): below = lax.ppermute(up, 'blk', [(z, z + 1) for z in range(t + 1)])  12.9 us
  transfers between devices with their start and end apart: 44, of which 30 were waited for; matrix products, arithmetic and copies ran while one was open for 4% of the time, Pallas kernels for 27%

profile of v3, /device:TPU:0, one launch (start us, length us, event | category | flops | bytes accessed | tf_op | source)
XLA Modules:
  0.0 494.6 jit_solution(15262348095536877004)
XLA Ops:
  4.4 11.8 %shard_map.103 = (bf16[16,256,1024]{2,1,0:T(8,128)(2,1)}, bf16[16,64,512]{2,1,0:T(8,128)(2,1)S(1)}, bf16[16,64,512]{2,1,0:T(8,128)(2,1)S(1)}, bf16[16,64,512]{2,1,0:T(8,128)(2,1)S(1)}, bf16[16,64,512]{2,1,0:T(8,128)(2,1)S(1)}) custom-call(f32[4,16]{1,0:T(4,128)S(1)} %get-tuple-element.118.refs_0_, bf16[4,256,1024]{2,1,0:T(8,128)(2,1)} %bitcast.52, ...), custom_call_target="tpu_custom_call" | custom-call | flops 6442450944 | bytes 19398912 | tf_op jit(solution)/shard_map/pallas_call | solution.py:319
  16.7 4.5 collective-permute-start.1
  21.9 17.1 %shard_map.104 = (bf16[4,16,4,64,512]{4,3,2,1,0:T(8,128)(2,1)}, f32[8,128]{1,0:T(8,128)S(1)}) custom-call(f32[4,16]{1,0:T(4,128)S(1)} %get-tuple-element.118.refs_0_, bf16[4,256,1024]{2,1,0:T(8,128)(2,1)S(1)} %bitcast.53, bf16[1024,512]{1,0:T(8,128)(2,1)S(1)} %copy-done.30, bf16[512,256]{1,0:T(8,128)(2,1)S(1)} %get-tuple-element.91.refs_3_.refs_4_, ...), custom_call_target="tpu_custom_call" | custom-call | flops 12884901888 | bytes 22036736 | tf_op jit(solution)/shard_map/pallas_call | solution.py:319
  39.0 5.2 %collective-permute-done.1.refs_1_ = bf16[16,64,512]{2,1,0:T(8,128)(2,1)S(1)} collective-permute-done((bf16[16,64,512]{2,1,0:T(8,128)(2,1)S(1)}, bf16[16,64,512]{2,1,0:T(8,128)(2,1)S(1)}, u32[]{:S(2)}, u32[]{:S(2)}) %collective-permute-start.1) | collective-permute-done | bytes 1048608 | tf_op jit(solution)/shard_map/ppermute | solution.py:377
  44.7 4.5 collective-permute-start.3
  50.1 17.1 %shard_map.106 = (bf16[4,16,4,64,512]{4,3,2,1,0:T(8,128)(2,1)}, f32[8,128]{1,0:T(8,128)S(1)}) custom-call(f32[4,16]{1,0:T(4,128)S(1)} %get-tuple-element.118.refs_0_, bf16[4,256,1024]{2,1,0:T(8,128)(2,1)S(1)} %bitcast.54, bf16[1024,512]{1,0:T(8,128)(2,1)S(1)} %copy-done.31, ...), custom_call_target="tpu_custom_call", output_to_operand_aliasing={{0}: (5, {})} | custom-call | flops 12884901888 | bytes 22036736 | tf_op jit(solution)/shard_map/pallas_call | solution.py:319
  67.2 4.2 collective-permute-done.3.refs_1_
  76.4 9.0 %collective-permute-start.5 = (bf16[16,64,512]{2,0,1:T(8,128)(2,1)S(1)}, bf16[16,64,512]{2,0,1:T(8,128)(2,1)S(1)}, u32[]{:S(2)}, u32[]{:S(2)}) collective-permute-start(bf16[16,64,512]{2,0,1:T(8,128)(2,1)S(1)} %copy.72), channel_id=1, source_target_pairs={{0,8},{8,16},{16,24},{1,9},{9,17},{17,25},{2,10},{10,18},{18,26},{... | collective-permute-start | bytes 3145736 | tf_op jit(solution)/shard_map/ppermute | solution.py:377
  85.4 19.3 %collective-permute-done.6 = bf16[16,64,512]{2,0,1:T(8,128)(2,1)S(1)} collective-permute-done((bf16[16,64,512]{2,0,1:T(8,128)(2,1)S(1)}, bf16[16,64,512]{2,0,1:T(8,128)(2,1)S(1)}, u32[]{:S(2)}, u32[]{:S(2)}) %collective-permute-start.6) | collective-permute-done | bytes 1048608 | tf_op jit(solution)/shard_map/ppermute | solution.py:378
  111.0 5.1 %collective-permute-done.7.refs_4_.refs_3_ = bf16[16,16,512]{2,1,0:T(8,128)(2,1)S(1)} collective-permute-done((bf16[16,16,512]{2,1,0:T(8,128)(2,1)S(1)}, bf16[16,16,512]{2,1,0:T(8,128)(2,1)S(1)}, u32[]{:S(2)}, u32[]{:S(2)}) %collective-permute-start.7) | collective-permute-done | bytes 262176 | tf_op jit(solution)/shard_map/ppermute | solution.py:404
  116.1 4.0 collective-permute-done.8.refs_5_.refs_4_
  120.2 14.7 %shard_map.108 = (bf16[4,16,16,512]{3,2,1,0:T(8,128)(2,1)S(1)}, bf16[4,16,16,512]{3,2,1,0:T(8,128)(2,1)S(1)}) custom-call(s32[1]{0:T(128)} %bitcast.refs_0_, bf16[2,16,16,32,256]{4,3,2,1,0:T(8,128)(2,1)} %refs_2_.7, bf16[2,16,16,32,256]{4,3,2,1,0:T(8,128)(2,1)} %refs_2_.7, bf16[16,16,512]{2,1,0:T(8,128)(2,1)S(1)} %get-tuple-element.108.refs_3_.refs_2_, ...), custom_call_target="tpu_custom_call" | custom-call | flops 67108864 | bytes 11534336 | tf_op jit(solution)/shard_map/pallas_call | solution.py:319
  135.6 2.6 collective-permute-done.10
  142.8 6.6 %collective-permute-done.13 = bf16[16,16,512]{2,0,1:T(8,128)(2,1)S(1)} collective-permute-done((bf16[16,16,512]{2,0,1:T(8,128)(2,1)S(1)}, bf16[16,16,512]{2,0,1:T(8,128)(2,1)S(1)}, u32[]{:S(2)}, u32[]{:S(2)}) %collective-permute-start.13) | collective-permute-done | bytes 262176 | tf_op jit(solution)/shard_map/ppermute | solution.py:404
  149.4 4.8 collective-permute-done.12
  154.3 5.4 %collective-permute-start.14 = (bf16[16,64,512]{2,1,0:T(8,128)(2,1)S(1)}, bf16[16,64,512]{2,1,0:T(8,128)(2,1)}, u32[]{:S(2)}, u32[]{:S(2)}) collective-permute-start(bf16[16,64,512]{2,1,0:T(8,128)(2,1)S(1)} %maximum_bitcast_fusion.refs_3_.refs_6_), channel_id=1, source_target_pairs={{0,8},{8,16},{16,24},{1,9},{9,17},{17,25},{2,10},{10,18},{18,26},{... | collective-permute-start | bytes 3145736 | tf_op jit(solution)/shard_map/ppermute | solution.py:394
  162.8 3.2 mul.58.refs_1_
  167.8 10.3 %shard_map.109 = (f32[16,256,1024]{2,1,0:T(8,128)}, f32[8,128]{1,0:T(8,128)S(1)}) custom-call(bf16[256,512]{1,0:T(8,128)(2,1)S(1)} %bitcast.57, bf16[16,256,1024]{2,1,0:T(8,128)(2,1)} %get-tuple-element.42.refs_1_.refs_3_, bf16[16,256,1024]{2,1,0:T(8,128)(2,1)} %collective-permute-done.refs_2_.refs_4_, ...), custom_call_target="tpu_custom_call" | custom-call | flops 2147483648 | bytes 18907136 | tf_op jit(solution)/shard_map/pallas_call | solution.py:319
  178.7 2.5 collective-permute-done.14.refs_0_
  182.8 3.6 collective-permute-done.17.refs_0_
  187.9 10.3 %shard_map.111 = (f32[16,256,1024]{2,1,0:T(8,128)}, f32[8,128]{1,0:T(8,128)S(1)}) custom-call(bf16[256,512]{1,0:T(8,128)(2,1)S(1)} %bitcast.58, bf16[16,256,1024]{2,1,0:T(8,128)(2,1)} %get-tuple-element.42.refs_1_.refs_3_, bf16[16,256,1024]{2,1,0:T(8,128)(2,1)} %collective-permute-done.refs_2_.refs_4_, ...), custom_call_target="tpu_custom_call", output_to_operand_aliasing={{0}: (4, {})} | custom-call | flops 2147483648 | bytes 18907136 | tf_op jit(solution)/shard_map/pallas_call | solution.py:319
  200.8 11.8 %collective-permute-done.18.refs_0_ = bf16[16,64,512]{2,1,0:T(8,128)(2,1)} collective-permute-done((bf16[16,64,512]{2,1,0:T(8,128)(2,1)}, bf16[16,64,512]{2,1,0:T(8,128)(2,1)}, u32[]{:S(2)}, u32[]{:S(2)}) %collective-permute-start.18) | collective-permute-done | bytes 1048608 | tf_op jit(solution)/shard_map/ppermute | solution.py:396
  214.0 23.7 %collective-permute-done.19.refs_12_ = bf16[16,64,512]{2,1,0:T(8,128)(2,1)} collective-permute-done((bf16[16,64,512]{2,1,0:T(8,128)(2,1)}, bf16[16,64,512]{2,1,0:T(8,128)(2,1)}, u32[]{:S(2)}, u32[]{:S(2)}) %collective-permute-start.19) | collective-permute-done | bytes 1048608 | tf_op jit(solution)/shard_map/ppermute | solution.py:396
  238.9 27.7 %shard_map.115 = (bf16[16,256,1024]{2,1,0:T(8,128)(2,1)}, bf16[16,64,512]{2,1,0:T(8,128)(2,1)S(1)}, bf16[16,64,512]{2,1,0:T(8,128)(2,1)S(1)}, bf16[16,64,512]{2,1,0:T(8,128)(2,1)S(1)}, bf16[16,64,512]{2,1,0:T(8,128)(2,1)S(1)}) custom-call(f32[16,256,1024]{2,1,0:T(8,128)} %get-tuple-element.58.refs_0_, bf16[1,16,256,1024]{3,2,1,0:T(8,128)(2,1)} %refs_1_.4, ...), custom_call_target="tpu_custom_call" | custom-call | flops 12884901888 | bytes 55574528 | tf_op jit(solution)/shard_map/pallas_call | solution.py:319
  268.9 20.2 %shard_map.116 = (f32[2,256,256]{2,1,0:T(8,128)S(1)}, f32[32,4,8,128]{3,2,1,0:T(8,128)S(1)}) custom-call(f32[4,32]{1,0:T(4,128)S(1)} %pad_maximum_fusion.3.refs_0_, bf16[512,256]{1,0:T(8,128)(2,1)S(1)} %mul.58.refs_1_, bf16[4,256,1024]{2,1,0:T(8,128)(2,1)S(1)} %bitcast.55, bf16[16,256,1024]{2,1,0:T(8,128)(2,1)} %get-tuple-element.42.refs_1_.refs_3_, ...), custom_call_target="tpu_custom_call" | custom-call | flops 4294967296 | bytes 24117760 | tf_op jit(solution)/shard_map/pallas_call | solution.py:319
  293.4 20.2 %shard_map.118 = (f32[2,256,256]{2,1,0:T(8,128)S(1)}, f32[32,4,8,128]{3,2,1,0:T(8,128)S(1)}) custom-call(f32[4,32]{1,0:T(4,128)S(1)} %pad_maximum_fusion.3.refs_0_, bf16[512,256]{1,0:T(8,128)(2,1)S(1)} %mul.58.refs_1_, bf16[4,256,1024]{2,1,0:T(8,128)(2,1)S(1)} %bitcast.56, bf16[16,256,1024]{2,1,0:T(8,128)(2,1)} %get-tuple-element.42.refs_1_.refs_3_, ...), custom_call_target="tpu_custom_call" | custom-call | flops 4294967296 | bytes 24117760 | tf_op jit(solution)/shard_map/pallas_call | solution.py:319
  318.7 5.1 %collective-permute-start.24 = (bf16[16,64,512]{2,0,1:T(8,128)(2,1)S(1)}, bf16[16,64,512]{2,0,1:T(8,128)(2,1)S(1)}, u32[]{:S(2)}, u32[]{:S(2)}) collective-permute-start(bf16[16,64,512]{2,0,1:T(8,128)(2,1)S(1)} %copy.78), channel_id=1, source_target_pairs={{0,8},{8,16},{16,24},{1,9},{9,17},{17,25},{2,10},{10,18},{18,26},{... | collective-permute-start | bytes 3145736 | tf_op jit(solution)/shard_map/ppermute | solution.py:377
  323.8 16.2 %collective-permute-done.25 = bf16[16,64,512]{2,0,1:T(8,128)(2,1)S(1)} collective-permute-done((bf16[16,64,512]{2,0,1:T(8,128)(2,1)S(1)}, bf16[16,64,512]{2,0,1:T(8,128)(2,1)S(1)}, u32[]{:S(2)}, u32[]{:S(2)}) %collective-permute-start.25) | collective-permute-done | bytes 1048608 | tf_op jit(solution)/shard_map/ppermute | solution.py:378
  346.3 3.9 collective-permute-done.28.refs_7_.refs_9_
  350.2 2.7 collective-permute-done.27.refs_6_.refs_8_
  353.1 2.6 collective-permute-done.29.refs_3_.refs_1_
  355.8 15.9 %shard_map.120 = bf16[4,16,16,512]{3,2,1,0:T(8,128)(2,1)S(1)} custom-call(s32[1]{0:T(128)} %bitcast.refs_0_, bf16[2,16,16,32,256]{4,3,2,1,0:T(8,128)(2,1)} %refs_2_.7, bf16[2,16,16,32,256]{4,3,2,1,0:T(8,128)(2,1)} %refs_2_.7, bf16[4,16,16,512]{3,2,1,0:T(8,128)(2,1)S(1)} %collective-permute-done.29.refs_3_.refs_1_, ...), custom_call_target="tpu_custom_call" | custom-call | flops 67108864 | bytes 11534336 | tf_op jit(solution)/shard_map/pallas_call | solution.py:319
  376.1 6.0 %collective-permute-done.32 = bf16[16,16,512]{2,0,1:T(8,128)(2,1)S(1)} collective-permute-done((bf16[16,16,512]{2,0,1:T(8,128)(2,1)S(1)}, bf16[16,16,512]{2,0,1:T(8,128)(2,1)S(1)}, u32[]{:S(2)}, u32[]{:S(2)}) %collective-permute-start.32) | collective-permute-done | bytes 262176 | tf_op jit(solution)/shard_map/ppermute | solution.py:404
  382.1 4.8 collective-permute-done.31
  387.0 4.5 collective-permute-start.33
  392.8 12.1 %shard_map.121 = (bf16[2,16,16,32,256]{4,3,2,1,0:T(8,128)(2,1)}, f32[8,128]{1,0:T(8,128)S(1)}) custom-call(s32[1]{0:T(128)} %bitcast.refs_0_, bf16[4,16,16,512]{3,2,1,0:T(8,128)(2,1)S(1)} %collective-permute-done.29.refs_3_.refs_1_, bf16[16,16,512]{2,1,0:T(8,128)(2,1)S(1)} %copy-done.9, bf16[16,16,512]{2,1,0:T(8,128)(2,1)S(1)} %copy-done.15, ...), custom_call_target="tpu_custom_call" | custom-call | flops 67108864 | bytes 11599872 | tf_op jit(solution)/shard_map/pallas_call | solution.py:319
  405.5 8.4 %collective-permute-done.33.refs_0_ = bf16[16,64,512]{2,1,0:T(8,128)(2,1)S(1)} collective-permute-done((bf16[16,64,512]{2,1,0:T(8,128)(2,1)S(1)}, bf16[16,64,512]{2,1,0:T(8,128)(2,1)S(1)}, u32[]{:S(2)}, u32[]{:S(2)}) %collective-permute-start.33) | collective-permute-done | bytes 1048608 | tf_op jit(solution)/shard_map/ppermute | solution.py:394
  415.9 2.4 collective-permute-done.34.refs_0_
  420.4 3.8 reshape.60
  424.2 5.5 %shard_map.124 = (f32[16,4,8,128]{3,2,1,0:T(8,128)S(1)}, f32[8,128]{1,0:T(8,128)S(1)}) custom-call(bf16[16,64,512]{2,1,0:T(8,128)(2,1)S(1)} %maximum_bitcast_fusion.1.refs_10_.refs_0_, bf16[16,64,512]{2,1,0:T(8,128)(2,1)S(1)} %copy-done.3, bf16[16,64,512]{2,1,0:T(8,128)(2,1)} %shard_map.123.refs_2_, ...), custom_call_target="tpu_custom_call" | custom-call | flops 25165824 | bytes 16007168 | tf_op jit(solution)/shard_map/pallas_call | solution.py:319
  432.1 13.4 %collective-permute-done.36.refs_0_ = bf16[16,64,512]{2,1,0:T(8,128)(2,1)} collective-permute-done((bf16[16,64,512]{2,1,0:T(8,128)(2,1)}, bf16[16,64,512]{2,1,0:T(8,128)(2,1)}, u32[]{:S(2)}, u32[]{:S(2)}) %collective-permute-start.36) | collective-permute-done | bytes 1048608 | tf_op jit(solution)/shard_map/ppermute | solution.py:396
  447.0 2.7 multiply_reduce_fusion
  450.1 5.3 %shard_map.127 = (f32[16,4,8,128]{3,2,1,0:T(8,128)S(1)}, f32[8,128]{1,0:T(8,128)S(1)}) custom-call(bf16[16,64,512]{2,1,0:T(8,128)(2,1)S(1)} %copy-done.1, bf16[16,64,512]{2,1,0:T(8,128)(2,1)} %shard_map.126.refs_1_, bf16[4,16,4,64,512]{4,3,2,1,0:T(8,128)(2,1)} %get-tuple-element.75.refs_3_.refs_4_.refs_5_.refs_2_, ...), custom_call_target="tpu_custom_call" | custom-call | flops 16777216 | bytes 10764288 | tf_op jit(solution)/shard_map/pallas_call | solution.py:319
  455.4 16.0 %collective-permute-done.38.refs_1_ = bf16[16,64,512]{2,1,0:T(8,128)(2,1)} collective-permute-done((bf16[16,64,512]{2,1,0:T(8,128)(2,1)}, bf16[16,64,512]{2,1,0:T(8,128)(2,1)}, u32[]{:S(2)}, u32[]{:S(2)}) %collective-permute-start.38) | collective-permute-done | bytes 1048608 | tf_op jit(solution)/shard_map/ppermute | solution.py:396
  471.3 4.9 shard_map.128
  481.6 2.4 collective-permute-done.40
  484.0 3.6 collective-permute-done.41
  487.6 4.5 collective-permute-done.42
  (200 shorter events, 76.7 us)
Async XLA Ops:
  3.1 47.0 %copy-start.24 = (bf16[512,256]{1,0:T(8,128)(2,1)}, bf16[512,256]{1,0:T(8,128)(2,1)S(1)}, u32[]{:S(2)}) copy-start(bf16[512,256]{1,0:T(8,128)(2,1)S(1)} %get-tuple-element.91.refs_3_.refs_4_) | copy-start | bytes 786436
  16.2 150.7 %collective-permute-start = (bf16[16,256,1024]{2,1,0:T(8,128)(2,1)}, bf16[16,256,1024]{2,1,0:T(8,128)(2,1)}, u32[]{:S(2)}, u32[]{:S(2)}) collective-permute-start(bf16[16,256,1024]{2,1,0:T(8,128)(2,1)} %get-tuple-element.42.refs_1_.refs_3_), channel_id=1, source_target_pairs={{0,1},{1,0},{2,3},{3,2},{4,5},{5,4},{6,7},{7,6},{8,9},{9,8},{10,11... | collective-permute-start | bytes 25165832 | tf_op jit(solution)/shard_map/ppermute | solution.py:408
  16.7 27.6 %collective-permute-start.1 = (bf16[16,64,512]{2,1,0:T(8,128)(2,1)S(1)}, bf16[16,64,512]{2,1,0:T(8,128)(2,1)S(1)}, u32[]{:S(2)}, u32[]{:S(2)}) collective-permute-start(bf16[16,64,512]{2,1,0:T(8,128)(2,1)S(1)} %get-tuple-element.46.refs_4_.refs_2_), channel_id=1, source_target_pairs={{0,8},{1,9},{2,10},{3,11},{4,12},{5,13},{6,14},{7,15}} | collective-permute-start | bytes 3145736 | tf_op jit(solution)/shard_map/ppermute | solution.py:377
  21.2 23.0 %collective-permute-start.2 = (bf16[16,64,512]{2,1,0:T(8,128)(2,1)S(1)}, bf16[16,64,512]{2,1,0:T(8,128)(2,1)S(1)}, u32[]{:S(2)}, u32[]{:S(2)}) collective-permute-start(bf16[16,64,512]{2,1,0:T(8,128)(2,1)S(1)} %get-tuple-element.44.refs_0_), channel_id=1, source_target_pairs={{24,16},{25,17},{26,18},{27,19},{28,20},{29,21},{30,22},{31,23}} | collective-permute-start | bytes 3145736 | tf_op jit(solution)/shard_map/ppermute | solution.py:378
  44.7 26.7 %collective-permute-start.3 = (bf16[16,64,512]{2,1,0:T(8,128)(2,1)S(1)}, bf16[16,64,512]{2,1,0:T(8,128)(2,1)S(1)}, u32[]{:S(2)}, u32[]{:S(2)}) collective-permute-start(bf16[16,64,512]{2,1,0:T(8,128)(2,1)S(1)} %get-tuple-element.48.refs_4_), channel_id=1, source_target_pairs={{0,8},{8,16},{1,9},{9,17},{2,10},{10,18},{3,11},{11,19},{4,12},{12... | collective-permute-start | bytes 3145736 | tf_op jit(solution)/shard_map/ppermute | solution.py:377
  49.2 22.2 %collective-permute-start.4 = (bf16[16,64,512]{2,1,0:T(8,128)(2,1)S(1)}, bf16[16,64,512]{2,1,0:T(8,128)(2,1)S(1)}, u32[]{:S(2)}, u32[]{:S(2)}) collective-permute-start(bf16[16,64,512]{2,1,0:T(8,128)(2,1)S(1)} %get-tuple-element.49), channel_id=1, source_target_pairs={{24,16},{16,8},{25,17},{17,9},{26,18},{18,10},{27,19},{19,11},{28,... | collective-permute-start | bytes 3145736 | tf_op jit(solution)/shard_map/ppermute | solution.py:378
  74.5 30.2 %collective-permute-start.6 = (bf16[16,64,512]{2,0,1:T(8,128)(2,1)S(1)}, bf16[16,64,512]{2,0,1:T(8,128)(2,1)S(1)}, u32[]{:S(2)}, u32[]{:S(2)}) collective-permute-start(bf16[16,64,512]{2,0,1:T(8,128)(2,1)S(1)} %copy.73), channel_id=1, source_target_pairs={{24,16},{16,8},{8,0},{25,17},{17,9},{9,1},{26,18},{18,10},{10,2},{... | collective-permute-start | bytes 3145736 | tf_op jit(solution)/shard_map/ppermute | solution.py:378
  76.4 30.0 %collective-permute-start.5 = (bf16[16,64,512]{2,0,1:T(8,128)(2,1)S(1)}, bf16[16,64,512]{2,0,1:T(8,128)(2,1)S(1)}, u32[]{:S(2)}, u32[]{:S(2)}) collective-permute-start(bf16[16,64,512]{2,0,1:T(8,128)(2,1)S(1)} %copy.72), channel_id=1, source_target_pairs={{0,8},{8,16},{16,24},{1,9},{9,17},{17,25},{2,10},{10,18},{18,26},{... | collective-permute-start | bytes 3145736 | tf_op jit(solution)/shard_map/ppermute | solution.py:377
  107.4 27.4 %copy-start.8 = (bf16[16,16,512]{2,1,0:T(8,128)(2,1)}, bf16[16,16,512]{2,1,0:T(8,128)(2,1)S(1)}, u32[]{:S(2)}) copy-start(bf16[16,16,512]{2,1,0:T(8,128)(2,1)S(1)} %get-tuple-element.108.refs_3_.refs_2_) | copy-start | bytes 786436
  107.4 8.7 %collective-permute-start.7 = (bf16[16,16,512]{2,1,0:T(8,128)(2,1)S(1)}, bf16[16,16,512]{2,1,0:T(8,128)(2,1)S(1)}, u32[]{:S(2)}, u32[]{:S(2)}) collective-permute-start(bf16[16,16,512]{2,1,0:T(8,128)(2,1)S(1)} %get-tuple-element.107), channel_id=1, source_target_pairs={{0,2},{2,0},{4,6},{6,4},{1,3},{3,1},{5,7},{7,5},{8,10},{10,8},{12,... | collective-permute-start | bytes 786440 | tf_op jit(solution)/shard_map/ppermute | solution.py:404
  109.0 11.2 %collective-permute-start.8 = (bf16[16,16,512]{2,1,0:T(8,128)(2,1)S(1)}, bf16[16,16,512]{2,1,0:T(8,128)(2,1)S(1)}, u32[]{:S(2)}, u32[]{:S(2)}) collective-permute-start(bf16[16,16,512]{2,1,0:T(8,128)(2,1)S(1)} %get-tuple-element.106), channel_id=1, source_target_pairs={{0,4},{2,6},{4,0},{6,2},{1,5},{3,7},{5,1},{7,3},{8,12},{10,14},{12... | collective-permute-start | bytes 786440 | tf_op jit(solution)/shard_map/ppermute | solution.py:404
  110.5 9.6 %collective-permute-start.9 = (bf16[16,16,512]{2,1,0:T(8,128)(2,1)S(1)}, bf16[16,16,512]{2,1,0:T(8,128)(2,1)S(1)}, u32[]{:S(2)}, u32[]{:S(2)}) collective-permute-start(bf16[16,16,512]{2,1,0:T(8,128)(2,1)S(1)} %get-tuple-element.105), channel_id=1, source_target_pairs={{0,6},{2,4},{4,2},{6,0},{1,7},{3,5},{5,3},{7,1},{8,14},{10,12},{12... | collective-permute-start | bytes 786440 | tf_op jit(solution)/shard_map/ppermute | solution.py:404
  135.5 2.7 collective-permute-start.10
  139.1 21.9 %copy-start.36 = (bf16[32,16]{0,1:T(8,128)(2,1)S(1)}, bf16[32,16]{0,1:T(8,128)(2,1)}, u32[]{:S(2)}) copy-start(bf16[32,16]{0,1:T(8,128)(2,1)} %param.10) | copy-start | bytes 3076
  139.2 10.2 %collective-permute-start.13 = (bf16[16,16,512]{2,0,1:T(8,128)(2,1)S(1)}, bf16[16,16,512]{2,0,1:T(8,128)(2,1)S(1)}, u32[]{:S(2)}, u32[]{:S(2)}) collective-permute-start(bf16[16,16,512]{2,0,1:T(8,128)(2,1)S(1)} %get-tuple-element.102), channel_id=1, source_target_pairs={{0,6},{2,4},{4,2},{6,0},{1,7},{3,5},{5,3},{7,1},{8,14},{10,12},{12... | collective-permute-start | bytes 786440 | tf_op jit(solution)/shard_map/ppermute | solution.py:404
  140.8 13.4 %collective-permute-start.12 = (bf16[16,16,512]{2,0,1:T(8,128)(2,1)S(1)}, bf16[16,16,512]{2,0,1:T(8,128)(2,1)S(1)}, u32[]{:S(2)}, u32[]{:S(2)}) collective-permute-start(bf16[16,16,512]{2,0,1:T(8,128)(2,1)S(1)} %get-tuple-element.103), channel_id=1, source_target_pairs={{0,4},{2,6},{4,0},{6,2},{1,5},{3,7},{5,1},{7,3},{8,12},{10,14},{12... | collective-permute-start | bytes 786440 | tf_op jit(solution)/shard_map/ppermute | solution.py:404
  141.8 12.4 %collective-permute-start.11 = (bf16[16,16,512]{2,0,1:T(8,128)(2,1)S(1)}, bf16[16,16,512]{2,0,1:T(8,128)(2,1)S(1)}, u32[]{:S(2)}, u32[]{:S(2)}) collective-permute-start(bf16[16,16,512]{2,0,1:T(8,128)(2,1)S(1)} %get-tuple-element.104), channel_id=1, source_target_pairs={{0,2},{2,0},{4,6},{6,4},{1,3},{3,1},{5,7},{7,5},{8,10},{10,8},{12,... | collective-permute-start | bytes 786440 | tf_op jit(solution)/shard_map/ppermute | solution.py:404
  154.3 26.9 %collective-permute-start.14 = (bf16[16,64,512]{2,1,0:T(8,128)(2,1)S(1)}, bf16[16,64,512]{2,1,0:T(8,128)(2,1)}, u32[]{:S(2)}, u32[]{:S(2)}) collective-permute-start(bf16[16,64,512]{2,1,0:T(8,128)(2,1)S(1)} %maximum_bitcast_fusion.refs_3_.refs_6_), channel_id=1, source_target_pairs={{0,8},{8,16},{16,24},{1,9},{9,17},{17,25},{2,10},{10,18},{18,26},{... | collective-permute-start | bytes 3145736 | tf_op jit(solution)/shard_map/ppermute | solution.py:394
  159.7 26.7 %collective-permute-start.17 = (bf16[16,64,512]{2,1,0:T(8,128)(2,1)S(1)}, bf16[16,64,512]{2,1,0:T(8,128)(2,1)}, u32[]{:S(2)}, u32[]{:S(2)}) collective-permute-start(bf16[16,64,512]{2,1,0:T(8,128)(2,1)S(1)} %maximum_bitcast_fusion.refs_3_.refs_6_), channel_id=1, source_target_pairs={{24,16},{16,8},{8,0},{25,17},{17,9},{9,1},{26,18},{18,10},{10,2},{... | collective-permute-start | bytes 3145736 | tf_op jit(solution)/shard_map/ppermute | solution.py:396
  181.2 17.6 %collective-permute-start.15 = (bf16[16,64,512]{2,1,0:T(8,128)(2,1)}, bf16[16,64,512]{2,1,0:T(8,128)(2,1)}, u32[]{:S(2)}, u32[]{:S(2)}) collective-permute-start(bf16[16,64,512]{2,1,0:T(8,128)(2,1)} %shard_map.110.refs_3_.refs_7_), channel_id=1, source_target_pairs={{8,16},{16,24},{9,17},{17,25},{10,18},{18,26},{11,19},{19,27},{12,... | collective-permute-start | bytes 3145736 | tf_op jit(solution)/shard_map/ppermute | solution.py:394
  186.4 26.2 %collective-permute-start.18 = (bf16[16,64,512]{2,1,0:T(8,128)(2,1)}, bf16[16,64,512]{2,1,0:T(8,128)(2,1)}, u32[]{:S(2)}, u32[]{:S(2)}) collective-permute-start(bf16[16,64,512]{2,1,0:T(8,128)(2,1)} %shard_map.113.refs_10_), channel_id=1, source_target_pairs={{16,8},{8,0},{17,9},{9,1},{18,10},{10,2},{19,11},{11,3},{20,12},{1... | collective-permute-start | bytes 3145736 | tf_op jit(solution)/shard_map/ppermute | solution.py:396
  198.8 38.9 %copy-start.25 = (bf16[512,256]{1,0:T(8,128)(2,1)S(1)}, bf16[512,256]{1,0:T(8,128)(2,1)}, u32[]{:S(2)}) copy-start(bf16[512,256]{1,0:T(8,128)(2,1)} %copy-done.24) | copy-start | bytes 786436
  198.8 15.2 %collective-permute-start.16 = (bf16[16,64,512]{2,1,0:T(8,128)(2,1)}, bf16[16,64,512]{2,1,0:T(8,128)(2,1)}, u32[]{:S(2)}, u32[]{:S(2)}) collective-permute-start(bf16[16,64,512]{2,1,0:T(8,128)(2,1)} %shard_map.112.refs_8_), channel_id=1, source_target_pairs={{16,24},{17,25},{18,26},{19,27},{20,28},{21,29},{22,30},{23,31}} | collective-permute-start | bytes 3145736 | tf_op jit(solution)/shard_map/ppermute | solution.py:394
  212.6 25.1 %collective-permute-start.19 = (bf16[16,64,512]{2,1,0:T(8,128)(2,1)}, bf16[16,64,512]{2,1,0:T(8,128)(2,1)}, u32[]{:S(2)}, u32[]{:S(2)}) collective-permute-start(bf16[16,64,512]{2,1,0:T(8,128)(2,1)} %shard_map.114.refs_11_), channel_id=1, source_target_pairs={{8,0},{9,1},{10,2},{11,3},{12,4},{13,5},{14,6},{15,7}} | collective-permute-start | bytes 3145736 | tf_op jit(solution)/shard_map/ppermute | solution.py:396
  266.6 23.3 %collective-permute-start.20 = (bf16[16,64,512]{2,1,0:T(8,128)(2,1)S(1)}, bf16[16,64,512]{2,1,0:T(8,128)(2,1)S(1)}, u32[]{:S(2)}, u32[]{:S(2)}) collective-permute-start(bf16[16,64,512]{2,1,0:T(8,128)(2,1)S(1)} %get-tuple-element.63.refs_6_.refs_2_), channel_id=1, source_target_pairs={{0,8},{1,9},{2,10},{3,11},{4,12},{5,13},{6,14},{7,15}} | collective-permute-start | bytes 3145736 | tf_op jit(solution)/shard_map/ppermute | solution.py:377
  268.1 21.8 %collective-permute-start.21 = (bf16[16,64,512]{2,1,0:T(8,128)(2,1)S(1)}, bf16[16,64,512]{2,1,0:T(8,128)(2,1)S(1)}, u32[]{:S(2)}, u32[]{:S(2)}) collective-permute-start(bf16[16,64,512]{2,1,0:T(8,128)(2,1)S(1)} %get-tuple-element.61.refs_0_), channel_id=1, source_target_pairs={{24,16},{25,17},{26,18},{27,19},{28,20},{29,21},{30,22},{31,23}} | collective-permute-start | bytes 3145736 | tf_op jit(solution)/shard_map/ppermute | solution.py:378
  290.8 22.8 %collective-permute-start.22 = (bf16[16,64,512]{2,1,0:T(8,128)(2,1)S(1)}, bf16[16,64,512]{2,1,0:T(8,128)(2,1)S(1)}, u32[]{:S(2)}, u32[]{:S(2)}) collective-permute-start(bf16[16,64,512]{2,1,0:T(8,128)(2,1)S(1)} %get-tuple-element.66.refs_6_), channel_id=1, source_target_pairs={{0,8},{8,16},{1,9},{9,17},{2,10},{10,18},{3,11},{11,19},{4,12},{12... | collective-permute-start | bytes 3145736 | tf_op jit(solution)/shard_map/ppermute | solution.py:377
  292.7 20.9 %collective-permute-start.23 = (bf16[16,64,512]{2,1,0:T(8,128)(2,1)S(1)}, bf16[16,64,512]{2,1,0:T(8,128)(2,1)S(1)}, u32[]{:S(2)}, u32[]{:S(2)}) collective-permute-start(bf16[16,64,512]{2,1,0:T(8,128)(2,1)S(1)} %get-tuple-element.67), channel_id=1, source_target_pairs={{24,16},{16,8},{25,17},{17,9},{26,18},{18,10},{27,19},{19,11},{28,... | collective-permute-start | bytes 3145736 | tf_op jit(solution)/shard_map/ppermute | solution.py:378
  316.8 23.2 %collective-permute-start.25 = (bf16[16,64,512]{2,0,1:T(8,128)(2,1)S(1)}, bf16[16,64,512]{2,0,1:T(8,128)(2,1)S(1)}, u32[]{:S(2)}, u32[]{:S(2)}) collective-permute-start(bf16[16,64,512]{2,0,1:T(8,128)(2,1)S(1)} %copy.79), channel_id=1, source_target_pairs={{24,16},{16,8},{8,0},{25,17},{17,9},{9,1},{26,18},{18,10},{10,2},{... | collective-permute-start | bytes 3145736 | tf_op jit(solution)/shard_map/ppermute | solution.py:378
  318.7 23.0 %collective-permute-start.24 = (bf16[16,64,512]{2,0,1:T(8,128)(2,1)S(1)}, bf16[16,64,512]{2,0,1:T(8,128)(2,1)S(1)}, u32[]{:S(2)}, u32[]{:S(2)}) collective-permute-start(bf16[16,64,512]{2,0,1:T(8,128)(2,1)S(1)} %copy.78), channel_id=1, source_target_pairs={{0,8},{8,16},{16,24},{1,9},{9,17},{17,25},{2,10},{10,18},{18,26},{... | collective-permute-start | bytes 3145736 | tf_op jit(solution)/shard_map/ppermute | solution.py:377
  342.8 7.4 %collective-permute-start.28 = (bf16[16,16,512]{2,1,0:T(8,128)(2,1)S(1)}, bf16[16,16,512]{2,1,0:T(8,128)(2,1)S(1)}, u32[]{:S(2)}, u32[]{:S(2)}) collective-permute-start(bf16[16,16,512]{2,1,0:T(8,128)(2,1)S(1)} %get-tuple-element.98), channel_id=1, source_target_pairs={{0,6},{2,4},{4,2},{6,0},{1,7},{3,5},{5,3},{7,1},{8,14},{10,12},{12... | collective-permute-start | bytes 786440 | tf_op jit(solution)/shard_map/ppermute | solution.py:404
  344.7 8.2 %collective-permute-start.27 = (bf16[16,16,512]{2,1,0:T(8,128)(2,1)S(1)}, bf16[16,16,512]{2,1,0:T(8,128)(2,1)S(1)}, u32[]{:S(2)}, u32[]{:S(2)}) collective-permute-start(bf16[16,16,512]{2,1,0:T(8,128)(2,1)S(1)} %get-tuple-element.99), channel_id=1, source_target_pairs={{0,4},{2,6},{4,0},{6,2},{1,5},{3,7},{5,1},{7,3},{8,12},{10,14},{12... | collective-permute-start | bytes 786440 | tf_op jit(solution)/shard_map/ppermute | solution.py:404
  345.8 7.2 %collective-permute-start.26 = (bf16[16,16,512]{2,1,0:T(8,128)(2,1)S(1)}, bf16[16,16,512]{2,1,0:T(8,128)(2,1)S(1)}, u32[]{:S(2)}, u32[]{:S(2)}) collective-permute-start(bf16[16,16,512]{2,1,0:T(8,128)(2,1)S(1)} %get-tuple-element.100), channel_id=1, source_target_pairs={{0,2},{2,0},{4,6},{6,4},{1,3},{3,1},{5,7},{7,5},{8,10},{10,8},{12,... | collective-permute-start | bytes 786440 | tf_op jit(solution)/shard_map/ppermute | solution.py:404
  353.1 2.7 collective-permute-start.29
  372.0 10.2 %collective-permute-start.32 = (bf16[16,16,512]{2,0,1:T(8,128)(2,1)S(1)}, bf16[16,16,512]{2,0,1:T(8,128)(2,1)S(1)}, u32[]{:S(2)}, u32[]{:S(2)}) collective-permute-start(bf16[16,16,512]{2,0,1:T(8,128)(2,1)S(1)} %bitcast.66), channel_id=1, source_target_pairs={{0,6},{2,4},{4,2},{6,0},{1,7},{3,5},{5,3},{7,1},{8,14},{10,12},{12... | collective-permute-start | bytes 786440 | tf_op jit(solution)/shard_map/ppermute | solution.py:404
  374.0 12.9 %collective-permute-start.31 = (bf16[16,16,512]{2,0,1:T(8,128)(2,1)S(1)}, bf16[16,16,512]{2,0,1:T(8,128)(2,1)S(1)}, u32[]{:S(2)}, u32[]{:S(2)}) collective-permute-start(bf16[16,16,512]{2,0,1:T(8,128)(2,1)S(1)} %bitcast.67), channel_id=1, source_target_pairs={{0,4},{2,6},{4,0},{6,2},{1,5},{3,7},{5,1},{7,3},{8,12},{10,14},{12... | collective-permute-start | bytes 786440 | tf_op jit(solution)/shard_map/ppermute | solution.py:404
  375.3 11.6 %collective-permute-start.30 = (bf16[16,16,512]{2,0,1:T(8,128)(2,1)S(1)}, bf16[16,16,512]{2,0,1:T(8,128)(2,1)S(1)}, u32[]{:S(2)}, u32[]{:S(2)}) collective-permute-start(bf16[16,16,512]{2,0,1:T(8,128)(2,1)S(1)} %bitcast.68), channel_id=1, source_target_pairs={{0,2},{2,0},{4,6},{6,4},{1,3},{3,1},{5,7},{7,5},{8,10},{10,8},{12,... | collective-permute-start | bytes 786440 | tf_op jit(solution)/shard_map/ppermute | solution.py:404
  387.0 27.0 %collective-permute-start.33 = (bf16[16,64,512]{2,1,0:T(8,128)(2,1)S(1)}, bf16[16,64,512]{2,1,0:T(8,128)(2,1)S(1)}, u32[]{:S(2)}, u32[]{:S(2)}) collective-permute-start(bf16[16,64,512]{2,1,0:T(8,128)(2,1)S(1)} %maximum_bitcast_fusion.1.refs_10_.refs_0_), channel_id=1, source_target_pairs={{0,8},{8,16},{16,24},{1,9},{9,17},{17,25},{2,10},{10,18},{18,26},{... | collective-permute-start | bytes 3145736 | tf_op jit(solution)/shard_map/ppermute | solution.py:394
  391.5 26.8 %collective-permute-start.34 = (bf16[16,64,512]{2,1,0:T(8,128)(2,1)S(1)}, bf16[16,64,512]{2,1,0:T(8,128)(2,1)}, u32[]{:S(2)}, u32[]{:S(2)}) collective-permute-start(bf16[16,64,512]{2,1,0:T(8,128)(2,1)S(1)} %maximum_bitcast_fusion.1.refs_10_.refs_0_), channel_id=1, source_target_pairs={{24,16},{16,8},{8,0},{25,17},{17,9},{9,1},{26,18},{18,10},{10,2},{... | collective-permute-start | bytes 3145736 | tf_op jit(solution)/shard_map/ppermute | solution.py:396
  415.0 15.3 %collective-permute-start.35 = (bf16[16,64,512]{2,1,0:T(8,128)(2,1)}, bf16[16,64,512]{2,1,0:T(8,128)(2,1)S(1)}, u32[]{:S(2)}, u32[]{:S(2)}) collective-permute-start(bf16[16,64,512]{2,1,0:T(8,128)(2,1)} %shard_map.122.refs_1_.refs_6_), channel_id=1, source_target_pairs={{8,16},{16,24},{9,17},{17,25},{10,18},{18,26},{11,19},{19,27},{12,... | collective-permute-start | bytes 3145736 | tf_op jit(solution)/shard_map/ppermute | solution.py:394
  418.3 27.3 %collective-permute-start.36 = (bf16[16,64,512]{2,1,0:T(8,128)(2,1)}, bf16[16,64,512]{2,1,0:T(8,128)(2,1)}, u32[]{:S(2)}, u32[]{:S(2)}) collective-permute-start(bf16[16,64,512]{2,1,0:T(8,128)(2,1)} %shard_map.123.refs_2_), channel_id=1, source_target_pairs={{16,8},{8,0},{17,9},{9,1},{18,10},{10,2},{19,11},{11,3},{20,12},{1... | collective-permute-start | bytes 3145736 | tf_op jit(solution)/shard_map/ppermute | solution.py:396
  431.4 24.0 %collective-permute-start.37 = (bf16[16,64,512]{2,1,0:T(8,128)(2,1)}, bf16[16,64,512]{2,1,0:T(8,128)(2,1)S(1)}, u32[]{:S(2)}, u32[]{:S(2)}) collective-permute-start(bf16[16,64,512]{2,1,0:T(8,128)(2,1)} %shard_map.125.refs_0_.refs_4_), channel_id=1, source_target_pairs={{16,24},{17,25},{18,26},{19,27},{20,28},{21,29},{22,30},{23,31}} | collective-permute-start | bytes 3145736 | tf_op jit(solution)/shard_map/ppermute | solution.py:394
  445.6 25.8 %collective-permute-start.38 = (bf16[16,64,512]{2,1,0:T(8,128)(2,1)}, bf16[16,64,512]{2,1,0:T(8,128)(2,1)}, u32[]{:S(2)}, u32[]{:S(2)}) collective-permute-start(bf16[16,64,512]{2,1,0:T(8,128)(2,1)} %shard_map.126.refs_1_), channel_id=1, source_target_pairs={{8,0},{9,1},{10,2},{11,3},{12,4},{13,5},{14,6},{15,7}} | collective-permute-start | bytes 3145736 | tf_op jit(solution)/shard_map/ppermute | solution.py:396
  476.7 3.6 collective-permute-start.39
  480.4 3.6 collective-permute-start.40
  484.0 3.6 collective-permute-start.41
  487.6 4.5 collective-permute-start.42
  492.2 1.2 collective-permute-start.43
  (33 other events, 227.3 us)

commit v4 on v3

--- a/solution.py
+++ b/solution.py
@@ -13,7 +13,7 @@
 BF = jnp.bfloat16
 F32 = jnp.float32
 TWO_PI = 2.0 * math.pi
-CHUNKS = 1
+CHUNKS = 2
 VMEM = 48 * 1024 * 1024
 
 
@@ -182,13 +182,13 @@
     lax.fori_loop(0, cells // 256, lanes, 0)
 
 
-def row_inverse(parts, chan, row_inv):
+def row_inverse(refs, chan, row_inv):
     rows = row_inv.shape[0] // 2
-    width = parts[0][0].shape[-1] // 2
-    hops = (len(parts[0]) - 1) // 2
-    blocks = [part[0][chan] for part in parts]
+    width = refs[0].shape[-1] // 2
+    hops = (len(refs) - 1) // 2
+    blocks = [refs[0][chan]]
     for s in range(hops - 1, -1, -1):
-        blocks += [part[1 + s][chan] + part[hops + hops - s][chan] for part in parts]
+        blocks.append(refs[1 + s][chan] + refs[hops + hops - s][chan])
     prod = jnp.dot(row_inv, jnp.concatenate(blocks, 0), preferred_element_type=F32)
     real = prod[:rows, :width] - prod[rows:, width:]
     imag = prod[:rows, width:] + prod[rows:, :width]
@@ -196,11 +196,11 @@
 
 
 def middle_kernel(blocks, bunch, grid_scale, scale, local, cotan, col, col_inv, row_tab, row_inv, *refs):
-    n_in = CHUNKS * (2 * blocks - 1)
-    parts, grad, outs = by_part(refs[:n_in]), refs[n_in], refs[n_in + 1 :]
+    n_in = 2 * blocks - 1
+    grad, outs = refs[n_in], refs[n_in + 1 :]
     group, rows, cells = grad.shape
     for b in range(0, group, bunch):
-        h = jnp.concatenate([row_inverse(parts, c, row_inv[...]) for c in range(b, b + bunch)], 0)
+        h = jnp.concatenate([row_inverse(refs[:n_in], c, row_inv[...]) for c in range(b, b + bunch)], 0)
         grid = jnp.dot(h, col_inv[...], preferred_element_type=F32)
         for c in range(bunch):
             for lo in range(0, rows, 16):
@@ -298,7 +298,7 @@
 TOKEN = ((8, 128), F32, (8, 128), lambda i, *_: (0, 0))
 
 
-def call(body, grid, ins, outs, flops, transcendentals=0, prefetch=None, tokens=(), into=None):
+def call(body, grid, ins, outs, flops, transcendentals=0, prefetch=None, tokens=(), into=None, vmem=VMEM):
     scalars = 0 if prefetch is None else 1
 
     def spec(block, index):
@@ -308,7 +308,7 @@
 
     moved = 0
     for a, block, _ in ins:
-        moved += a.size * a.dtype.itemsize if block is None else math.prod(block) * math.prod(grid) * a.dtype.itemsize
+        moved += a.size * a.dtype.itemsize if block is None else math.prod(n for n in block if isinstance(n, int)) * math.prod(grid) * a.dtype.itemsize
     moved += sum(math.prod(b) * math.prod(grid) * jnp.dtype(t).itemsize for _, t, b, _ in outs)
     extra = list(tokens) + ([] if into is None else [into])
 
@@ -326,7 +326,7 @@
         ),
         out_shape=[jax.ShapeDtypeStruct(s, t) for s, t, _, _ in outs],
         input_output_aliases={} if into is None else {scalars + len(ins) + len(extra) - 1: 0},
-        compiler_params=pltpu.CompilerParams(vmem_limit_bytes=VMEM),
+        compiler_params=pltpu.CompilerParams(vmem_limit_bytes=vmem),
         cost_estimate=pl.CostEstimate(flops=int(flops), bytes_accessed=int(moved), transcendentals=int(transcendentals)),
     )(*(() if prefetch is None else (prefetch,)), *[a for a, _, _ in ins], *extra)
 
@@ -334,6 +334,7 @@
 def hold(value, *tokens):
     if not tokens:
         return value
+    tokens = list(tokens)
     anywhere = pl.BlockSpec(memory_space=pl.ANY)
     return pl.pallas_call(
         lambda *refs: None,
@@ -358,45 +359,45 @@
     )
 
 
+def spaced(fill):
+    return [run for f in fill for run in [f] + [None] * (CHUNKS - 1)]
+
+
 def run_next(fill, source):
-    return fill.pop(0)(source) if fill else None
+    run = fill.pop(0) if fill else None
+    got = [] if run is None else run(source)
+    return got if isinstance(got, list) else [got]
 
 
 def chain_sums(shares, fill):
     hops = len(shares[0]) - 1
     blocks = hops + 1
     got = [None] * len(shares)
-    token = None
+    tokens = []
     for t in range(hops):
         for p, part in enumerate(shares):
             up, down = part[hops - t], part[t + 1]
             if t:
-                up, down = add_pairs(up, got[p][1], down, got[p][2], [] if token is None else [token])
-            elif token is not None:
-                up, down = hold(up, token), hold(down, token)
+                up, down = add_pairs(up, got[p][1], down, got[p][2], tokens)
+            else:
+                up, down = hold(up, *tokens), hold(down, *tokens)
             below = lax.ppermute(up, "blk", [(z, z + 1) for z in range(t + 1)])
             above = lax.ppermute(down, "blk", [(blocks - 1 - z, blocks - 2 - z) for z in range(t + 1)])
             got[p] = (part[0], below, above)
-            token = run_next(fill, up)
-    return got, token
-
-
-def chain_gathers(owns, blocks, below, above, fill):
-    token = None
+            tokens = run_next(fill, up)
+    return got
+
+
+def chain_gather(own, blocks, below, above, fill):
+    tokens = []
     for t in range(blocks - 1):
-        for p, own in enumerate(owns):
-            if t and token is not None:
-                below[p][-1], above[p][-1] = hold(below[p][-1], token), hold(above[p][-1], token)
-            elif token is not None:
-                own = hold(own, token)
-                owns[p] = own
-            up, down = (below[p][-1], above[p][-1]) if t else (own, own)
-            below[p].append(lax.ppermute(up, "blk", [(z, z + 1) for z in range(t, blocks - 1)]))
-            above[p].append(
-                lax.ppermute(down, "blk", [(blocks - 1 - z, blocks - 2 - z) for z in range(t, blocks - 1)])
-            )
-            token = run_next(fill, up)
-    return token
+        if tokens:
+            below[-1], above[-1] = hold(below[-1], *tokens), hold(above[-1], *tokens)
+        up, down = (below[-1], above[-1]) if t else (own, own)
+        below.append(lax.ppermute(up, "blk", [(z, z + 1) for z in range(t, blocks - 1)]))
+        above.append(lax.ppermute(down, "blk", [(blocks - 1 - z, blocks - 2 - z) for z in range(t, blocks - 1)]))
+        tokens = run_next(fill, up)
+    return tokens
 
 
 def swap_samples(pieces):
@@ -408,26 +409,26 @@
     return lax.ppermute(value, "chan", [(0, 1), (1, 0)])
 
 
-def to_modes(shares, samples, token):
-    own, below, above = shares
-    if token is not None:
-        own = hold(own, token)
-    total = (own.astype(F32) + below.astype(F32) + above.astype(F32)).astype(BF).transpose(1, 0, 2)
-    sub = total.shape[0] // samples
-    return swap_samples([total[j * sub : (j + 1) * sub] for j in range(samples)])
-
-
-def from_modes(pieces):
-    return jnp.concatenate(swap_samples(pieces), 0).transpose(1, 0, 2)
+def to_modes(parts, samples):
+    got = []
+    for own, below, above in parts:
+        total = (own.astype(F32) + below.astype(F32) + above.astype(F32)).astype(BF).transpose(1, 0, 2)
+        sub = total.shape[0] // samples
+        got.append((total, swap_samples([total[j * sub : (j + 1) * sub] for j in range(samples)])))
+    return got
+
+
+def from_modes(parts):
+    return jnp.concatenate([a for pieces in parts for a in pieces], 0).transpose(1, 0, 2)
 
 
 def all_sum(value, axes):
     for axis in axes:
         n = lax.axis_size(axis)
-        step = 1
-        while step < n:
-            value = value + lax.ppermute(value, axis, [(i, i ^ step) for i in range(n)])
-            step *= 2
+        values = [value] + [lax.ppermute(value, axis, [(i, i ^ j) for i in range(n)]) for j in range(1, n)]
+        while len(values) > 1:
+            values = [a + b for a, b in zip(values[::2], values[1::2], strict=True)]
+        value = values[0]
     return value
 
 
@@ -452,9 +453,8 @@
 
     col = jnp.asarray(column_table(cells, freqs))
     col_inv = jnp.asarray(np.ascontiguousarray(column_table(cells, freqs).T))
-    row_tab = lax.dynamic_slice(
-        jnp.asarray(row_tables(all_rows, modes, blocks, samples)), (z, s, 0, 0), (1, 1, 2 * modes, rows)
-    )[0, 0]
+    row_all = jnp.asarray(row_tables(all_rows, modes, blocks, samples))
+    row_tab = lax.dynamic_slice(row_all, (z, s, 0, 0), (1, 1, 2 * modes, rows))[0, 0]
     row_inv = row_tab.reshape(2, modes, rows).transpose(0, 2, 1).reshape(2 * rows, modes)
     lw_wide = lift_weight.astype(F32)
     own_lw = lax.dynamic_slice_in_dim(lw_wide, core * chans, chans, 1)
@@ -483,12 +483,18 @@
     matrix = chans * rows * 4 * freqs * (cells + 2 * modes)
     group, bunch = math.gcd(chans, 8), math.gcd(chans, 4)
     lifted, *shares = call(
-        functools.partial(lift_kernel, bunch, unit_scale),
+        lambda place, *refs: lift_kernel(bunch, unit_scale, *refs),
         (chans // group,),
-        [(own_lw, None, None), whole(sample), whole(col), whole(row_tab)],
+        [
+            (own_lw, None, None),
+            whole(sample),
+            whole(col),
+            (row_all, (pl.squeezed, pl.squeezed, 2 * modes, rows), lambda i, place: (place[0], place[1], 0, 0)),
+        ],
         [((chans, rows, cells), BF, (group, rows, cells), lambda i, *_: (i, 0, 0)), *part_outs(group)],
         matrix,
         chans * rows * cells,
+        prefetch=jnp.stack([z, s]).astype(jnp.int32),
     )
     shares = by_part(shares)
     lifted_other = swap_cores(lifted)
@@ -559,15 +565,14 @@
         return ((samples, piece, n, width), BF, (samples, 1, n, width), lambda i, *_: (0, i, 0, 0))
 
     mix_flops = 16 * samples * piece * chans * half * freqs
-    count = chans // 2
-    fill = [slope_piece(i, count) for i in range(0, chans, count)]
-    field_modes, out_parts, sent = [], [], []
-
-    got, token = chain_sums(shares, fill)
-    for run in fill:
-        token = run(shares[0][0])
+    count = math.gcd(chans, 4)
+    slope_fill = [slope_piece(i, count) for i in range(0, chans, count)]
+    field_modes = []
+
+    arrivals = to_modes(chain_sums(shares, spaced(slope_fill[:-1])), samples)
+    parts = []
     for part in range(CHUNKS):
-        xs = to_modes(got[part], samples, token)
+        xs = arrivals[part][1]
         field_modes.append(xs)
         keep, send = call(
             functools.partial(mix_kernel, samples),
@@ -576,21 +581,20 @@
             [stack_out(half)] * 2,
             mix_flops,
             prefetch=core_ref,
-            tokens=sent[-1:],
+            tokens=[total for total, _ in arrivals[part + 1 :]],
         )
-        token = keep
+        send = hold(send, *[x for _, later in arrivals[part + 1 :] for x in later[1:]])
         total = (keep.astype(F32) + swap_cores(send).astype(F32)).astype(BF)
-        sent.append(from_modes([total[j] for j in range(samples)]))
+        parts.append(swap_samples([total[j] for j in range(samples)]))
+    out_modes = from_modes(parts)
     steps = rows // group_rows
     count = -(-steps // 2)
     fill = [local_piece(i, min(count, steps - i)) for i in range(0, steps, count)]
-    below, above = [[] for _ in range(CHUNKS)], [[] for _ in range(CHUNKS)]
-    chain_gathers(sent, blocks, below, above, fill)
-    for part in range(CHUNKS):
-        out_parts += [sent[part], *below[part], *above[part]]
+    below, above = [], []
+    chain_gather(out_modes, blocks, below, above, fill)
     for run in fill:
-        run(sent[-1])
-    slopes, local = slopes[0], locals_[0]
+        run(out_modes)
+    local = locals_[0]
 
     grad_z, *shares = call(
         functools.partial(middle_kernel, blocks, math.gcd(chans, 2), 2.0 * unit_scale, 2.0 * unit_scale),
@@ -602,11 +606,12 @@
             whole(col_inv),
             whole(row_tab),
             whole(row_inv),
-            *[channel(a, bunch) for a in out_parts],
+            *[channel(a, bunch) for a in (out_modes, *below, *above)],
         ],
         [((chans, rows, cells), BF, (bunch, rows, cells), lambda i, *_: (i, 0, 0)), *part_outs(bunch)],
         2 * matrix,
         3 * chans * rows * cells,
+        vmem=60 * 1024 * 1024,
     )
     shares = by_part(shares)
 
@@ -647,15 +652,14 @@
         return run
 
     steps = rows // group_rows
-    count = -(-steps // 2)
-    fill = [back_piece(i, min(count, steps - i)) for i in range(0, steps, count)]
-    grad_modes, grad_others, sent = [], [], []
-
-    got, token = chain_sums(shares, fill)
-    for run in fill:
-        token = run(grad_z)
+    count = -(-steps // 4)
+    back_fill = [back_piece(i, min(count, steps - i)) for i in range(0, steps, count)]
+    grad_modes, grad_others = [], []
+
+    arrivals = to_modes(chain_sums(shares, spaced(back_fill[:-1])), samples)
+    parts = []
     for part in range(CHUNKS):
-        gs = to_modes(got[part], samples, token)
+        gs = arrivals[part][1]
         other = swap_cores(jnp.stack(gs))
         grad_modes.append(gs)
         grad_others.append(other)
@@ -666,16 +670,11 @@
             [stack_out(chans)],
             mix_flops,
             prefetch=core_ref,
-            tokens=sent[-1:],
+            tokens=[total for total, _ in arrivals[part + 1 :]],
         )
-        token = back
-        sent.append(from_modes([back[j] for j in range(samples)]))
-
-    term = sum(terms).reshape(2 * chans, group_rows, chans, group_rows)
-    term = jnp.sum(term * jnp.eye(group_rows, dtype=F32)[None, :, None, :], axis=(1, 3))
-    own_first = jnp.stack([term[:chans], term[chans:]])
-    ordered = jnp.where(core == 0, own_first, own_first[::-1]).reshape(2 * chans, chans)
-    ordered = ordered * norm_scale
+        parts.append(swap_samples([back[j] for j in range(samples)]))
+    back_modes = from_modes(parts)
+    below, above = [], []
 
     gradient = [None]
 
@@ -711,38 +710,47 @@
     at_once = 4
 
     def pairs(modes_of, tokens=()):
-        def spectra(part, d):
-            return (
-                slopes,
-                (1, at_once, inputs, sub // CHUNKS, width),
-                lambda i, *_: (d, i, 0, part, 0),
-            )
+        def spectra(d):
+            return (slopes[0], (1, at_once, inputs, sub, width), lambda i, *_: (d, i, 0, 0, 0))
 
         got, token = call(
             functools.partial(pair_kernel, len(modes_of)),
             (chans // at_once,),
-            [channel(a, at_once) for *_, a in modes_of] + [spectra(p, d) for p, d, _ in modes_of],
+            [channel(a, at_once) for _, a in modes_of] + [spectra(d) for d, _ in modes_of],
             [((chans, inputs, 8, 128), F32, (at_once, inputs, 8, 128), lambda i, *_: (i, 0, 0, 0)), TOKEN],
-            4 * len(modes_of) * chans * inputs * sub * width // CHUNKS,
+            4 * len(modes_of) * chans * inputs * sub * width,
             tokens=tokens,
         )
         sums.append(got)
         return token
 
-    below, above = [[] for _ in range(CHUNKS)], [[] for _ in range(CHUNKS)]
-
-    def arrived(part, t):
-        return [(part, blocks - 1 - t, below[part][t]), (part, 1 + t, above[part][t])]
-
-    def pair_piece(part, t):
-        return lambda source: pairs(([(part, 0, sent[part])] if t == 0 else []) + arrived(part, t), [source])
-
-    fill = [weight_piece(part) for part in range(CHUNKS)]
-    fill += [pair_piece(part, t) for t in range(blocks - 2) for part in range(CHUNKS)]
-    token = chain_gathers(sent, blocks, below, above, fill)
-    for run in fill:
-        token = run(sent[-1])
-    pairs(sum([arrived(part, blocks - 2) for part in range(CHUNKS)], []), [ordered] + ([] if token is None else [token]))
+    def arrived(t):
+        return [(blocks - 1 - t, below[t]), (1 + t, above[t])]
+
+    def pair_piece(t):
+        return lambda source: pairs(([(0, back_modes)] if t == 0 else []) + arrived(t), [source])
+
+    def together(*runs):
+        def run(source):
+            return [r(source) for r in runs]
+
+        return run
+
+    fill = [
+        together(*[weight_piece(part) for part in range(CHUNKS)], *slope_fill[-1:]),
+        together(*back_fill[-1:], pair_piece(0)),
+    ]
+    fill += [pair_piece(t) for t in range(1, blocks - 2)]
+    tokens = chain_gather(back_modes, blocks, below, above, fill)
+    while fill:
+        tokens = tokens + run_next(fill, back_modes)
+    term = sum(terms).reshape(2 * chans, group_rows, chans, group_rows)
+    term = jnp.sum(term * jnp.eye(group_rows, dtype=F32)[None, :, None, :], axis=(1, 3))
+    own_first = jnp.stack([term[:chans], term[chans:]])
+    ordered = jnp.where(core == 0, own_first, own_first[::-1]).reshape(2 * chans, chans)
+    ordered = ordered * norm_scale
+
+    pairs(arrived(blocks - 2), [ordered, *tokens])
     spectral_grad = gradient[0]
     lift_own = jnp.sum(sum(sums), axis=(2, 3)).T
     lift_local = jnp.sum(sum(local_sums), axis=(2, 3)).T

time: 503 us -> 486 us (0.966)
  waiting for transfers between devices: 187 us -> 67.7 us
  starting transfers between devices: 72.8 us -> 125 us
  local copies, waits for them, and re-layouts: 26 us -> 62.7 us
  Pallas kernels: 197 us -> 210 us
    ppermute x16 -> x18, waiting for transfers between devices: 94.4 us -> 50.8 us  [the longest x6 46.6 us: chain_gather(): lax.ppermute(down, 'blk', [(blocks - 1 - z, blocks - 2 - z) for z in rang...]
    unnamed x80 -> x180, local copies, waits for them, and re-layouts: 12.4 us -> 46 us
    ppermute x6 -> x12, waiting for transfers between devices: 35.5 us -> 6.01 us  [chain_sums(): lax.ppermute(down, 'blk', [(blocks - 1 - z, blocks - 2 - z) for z in rang...]
    ppermute x12 -> x24, waiting for transfers between devices: 38 us -> 9.04 us  [swap_samples(): lax.ppermute(pieces[j], 'dp', [(i, i ^ j) for i in range(n)])]
    ppermute x6 -> x12, starting transfers between devices: 26.5 us -> 49.2 us  [chain_sums(): below = lax.ppermute(up, 'blk', [(z, z + 1) for z in range(t + 1)])]
    ppermute x12 -> x24, starting transfers between devices: 14.3 us -> 31 us  [swap_samples(): lax.ppermute(pieces[j], 'dp', [(i, i ^ j) for i in range(n)])]
    pallas_call x18 -> x29, Pallas kernels: 197 us -> 210 us  [call(): pl.pallas_call(kernel, grid_spec=pltpu.PrefetchScalarGridSpec(num_scalar_...]
    ppermute x6 -> x12, waiting for transfers between devices: 12.9 us -> 1.49 us  [chain_sums(): below = lax.ppermute(up, 'blk', [(z, z + 1) for z in range(t + 1)])]
  transfers between devices with their start and end apart: 44 -> 72, of which waited for: 30 -> 21; matrix products, arithmetic and copies ran while one was open for 4% -> 8% of each run, Pallas kernels for 27% -> 35%
where the time goes in v4:
time: 486 us; the launch traced here: 477 us
  Pallas kernels  210 us (43%)
  starting transfers between devices  125 us (26%)
  waiting for transfers between devices  67.7 us (14%)
  local copies, waits for them, and re-layouts  62.7 us (13%)
  other arithmetic  9.27 us (2%)
    pallas_call x29, Pallas kernels, call(): pl.pallas_call(kernel, grid_spec=pltpu.PrefetchScalarGridSpec(num_scalar_...  210 us
    ppermute x12, starting transfers between devices, chain_sums(): below = lax.ppermute(up, 'blk', [(z, z + 1) for z in range(t + 1)])  49.2 us
    ppermute x6, waiting for transfers between devices, chain_gather(): lax.ppermute(down, 'blk', [(blocks - 1 - z, blocks - 2 - z) for z in rang...  46.6 us
    unnamed x180, local copies, waits for them, and re-layouts  46 us
    ppermute x24, starting transfers between devices, swap_samples(): lax.ppermute(pieces[j], 'dp', [(i, i ^ j) for i in range(n)])  31 us
    ppermute x6, starting transfers between devices, chain_gather(): lax.ppermute(up, 'blk', [(z, z + 1) for z in range(t, blocks - 1)])  15.7 us
    ppermute x12, starting transfers between devices, chain_sums(): lax.ppermute(down, 'blk', [(blocks - 1 - z, blocks - 2 - z) for z in rang...  12.3 us
  transfers between devices with their start and end apart: 72, of which 21 were waited for; matrix products, arithmetic and copies ran while one was open for 8% of the time, Pallas kernels for 35%

profile of v4, /device:TPU:0, one launch (start us, length us, event | category | flops | bytes accessed | tf_op | source)
XLA Modules:
  0.0 477.3 jit_solution(14221952115415734385)
XLA Ops:
  2.7 12.6 %shard_map.103 = (bf16[16,256,1024]{2,1,0:T(8,128)(2,1)}, bf16[16,32,512]{2,1,0:T(8,128)(2,1)S(1)}, bf16[16,32,512]{2,1,0:T(8,128)(2,1)}, bf16[16,32,512]{2,1,0:...) custom-call(s32[2]{0:T(128)S(1)} %pad_add_fusion.refs_0_, ...), custom_call_target="tpu_custom_call" | custom-call | flops 6442450944 | bytes 19398912 | tf_op jit(solution)/shard_map/pallas_call | solution.py:319
  20.4 5.3 %collective-permute-start.1 = (bf16[16,32,512]{2,1,0:T(8,128)(2,1)}, bf16[16,32,512]{2,1,0:T(8,128)(2,1)}, u32[]{:S(2)}, u32[]{:S(2)}) collective-permute-start(bf16[16,32,512]{2,1,0:T(8,128)(2,1)} %get-tuple-element.74.refs_2_.refs_4_), channel_id=1, source_target_pairs={{0,8},{1,9},{2,10},{3,11},{4,12},{5,13},{6,14},{7,15}} | collective-permute-start | bytes 1572872 | tf_op jit(solution)/shard_map/ppermute | solution.py:384
  29.5 9.5 %shard_map.106 = (bf16[4,16,4,64,512]{4,3,2,1,0:T(8,128)(2,1)}, f32[8,128]{1,0:T(8,128)S(1)}) custom-call(f32[4,16]{1,0:T(4,128)S(1)} %get-tuple-element.189.refs_1_.refs_0_, bf16[4,256,1024]{2,1,0:T(8,128)(2,1)S(1)} %bitcast.88, bf16[1024,512]{1,0:T(8,128)(2,1)S(1)} %copy-done.67, bf16[512,256]{1,0:T(8,128)(2,1)S(1)} %get-tuple-element.147.refs_3_.refs_4_, ...), custom_call_target="tpu_custom_call" | custom-call | flops 6442450944 | bytes 11018496 | tf_op jit(solution)/shard_map/pallas_call | solution.py:319
  39.5 2.1 collective-permute-start.10
  49.3 9.7 %shard_map.109 = (bf16[4,16,4,64,512]{4,3,2,1,0:T(8,128)(2,1)}, f32[8,128]{1,0:T(8,128)S(1)}) custom-call(f32[4,16]{1,0:T(4,128)S(1)} %get-tuple-element.189.refs_1_.refs_0_, bf16[4,256,1024]{2,1,0:T(8,128)(2,1)S(1)} %bitcast.89, bf16[1024,512]{1,0:T(8,128)(2,1)S(1)} %copy-done.68, ...), custom_call_target="tpu_custom_call", output_to_operand_aliasing={{0}: (5, {})} | custom-call | flops 6442450944 | bytes 11018496 | tf_op jit(solution)/shard_map/pallas_call | solution.py:319
  60.3 3.9 collective-permute-start.12
  66.8 3.7 collective-permute-start.5
  71.8 9.6 %shard_map.111 = (bf16[4,16,4,64,512]{4,3,2,1,0:T(8,128)(2,1)}, f32[8,128]{1,0:T(8,128)S(1)}) custom-call(f32[4,16]{1,0:T(4,128)S(1)} %get-tuple-element.189.refs_1_.refs_0_, bf16[4,256,1024]{2,1,0:T(8,128)(2,1)S(1)} %bitcast.90, bf16[1024,512]{1,0:T(8,128)(2,1)S(1)} %copy-done.69, ...), custom_call_target="tpu_custom_call", output_to_operand_aliasing={{0}: (5, {})} | custom-call | flops 6442450944 | bytes 11018496 | tf_op jit(solution)/shard_map/pallas_call | solution.py:319
  83.6 7.6 %collective-permute-start.14 = (bf16[16,32,512]{2,0,1:T(8,128)(2,1)S(1)}, bf16[16,32,512]{2,0,1:T(8,128)(2,1)S(1)}, u32[]{:S(2)}, u32[]{:S(2)}) collective-permute-start(bf16[16,32,512]{2,0,1:T(8,128)(2,1)S(1)} %copy.119), channel_id=1, source_target_pairs={{0,8},{8,16},{16,24},{1,9},{9,17},{17,25},{2,10},{10,18},{18,26},{... | collective-permute-start | bytes 1572872 | tf_op jit(solution)/shard_map/ppermute | solution.py:384
  91.7 2.5 collective-permute-start.9
  94.7 5.1 %collective-permute-done.15 = bf16[16,32,512]{2,0,1:T(8,128)(2,1)S(1)} collective-permute-done((bf16[16,32,512]{2,0,1:T(8,128)(2,1)S(1)}, bf16[16,32,512]{2,0,1:T(8,128)(2,1)S(1)}, u32[]{:S(2)}, u32[]{:S(2)}) %collective-permute-start.15) | collective-permute-done | bytes 524320 | tf_op jit(solution)/shard_map/ppermute | solution.py:385
  101.8 2.5 collective-permute-start.18
  106.1 7.6 %shard_map.113 = (bf16[4,8,16,512]{3,2,1,0:T(8,128)(2,1)S(1)}, bf16[4,8,16,512]{3,2,1,0:T(8,128)(2,1)S(1)}) custom-call(s32[1]{0:T(128)} %bitcast.refs_0_, bf16[2,16,16,32,256]{4,3,2,1,0:T(8,128)(2,1)} %refs_2_.12, bf16[2,16,16,32,256]{4,3,2,1,0:T(8,128)(2,1)} %refs_2_.12, bf16[8,16,512]{2,1,0:T(8,128)(2,1)S(1)} %get-tuple-element.179.refs_3_.refs_2_, ...), custom_call_target="tpu_custom_call" | custom-call | flops 33554432 | bytes 5767168 | tf_op jit(solution)/shard_map/pallas_call | solution.py:319
  119.4 7.6 %shard_map.115 = (bf16[4,8,16,512]{3,2,1,0:T(8,128)(2,1)S(1)}, bf16[4,8,16,512]{3,2,1,0:T(8,128)(2,1)S(1)}) custom-call(s32[1]{0:T(128)} %bitcast.refs_0_, bf16[2,16,16,32,256]{4,3,2,1,0:T(8,128)(2,1)} %refs_2_.12, bf16[2,16,16,32,256]{4,3,2,1,0:T(8,128)(2,1)} %refs_2_.12, bf16[8,16,512]{2,1,0:T(8,128)(2,1)S(1)} %get-tuple-element.169.refs_3_.refs_2_, ...), custom_call_target="tpu_custom_call" | custom-call | flops 33554432 | bytes 5767168 | tf_op jit(solution)/shard_map/pallas_call | solution.py:319
  128.3 2.6 collective-permute-start.22
  133.0 2.6 collective-permute-start.26
  135.6 2.5 collective-permute-done.20
  148.5 5.4 %collective-permute-start.27 = (bf16[16,64,512]{2,1,0:T(8,128)(2,1)}, bf16[16,64,512]{2,1,0:T(8,128)(2,1)S(1)}, u32[]{:S(2)}, u32[]{:S(2)}) collective-permute-start(bf16[16,64,512]{2,1,0:T(8,128)(2,1)} %bitcast.16.refs_3_.refs_6_), channel_id=1, source_target_pairs={{0,8},{8,16},{16,24},{1,9},{9,17},{17,25},{2,10},{10,18},{18,26},{... | collective-permute-start | bytes 3145736 | tf_op jit(solution)/shard_map/ppermute | solution.py:397
  155.7 3.2 mul.58.refs_1_
  160.7 10.3 %shard_map.116 = (f32[16,256,1024]{2,1,0:T(8,128)}, f32[8,128]{1,0:T(8,128)S(1)}) custom-call(bf16[256,512]{1,0:T(8,128)(2,1)S(1)} %bitcast.96, bf16[16,256,1024]{2,1,0:T(8,128)(2,1)} %get-tuple-element.70.refs_1_.refs_3_, bf16[16,256,1024]{2,1,0:T(8,128)(2,1)} %collective-permute-done.refs_2_.refs_4_, bf16[16,64,512]{2,1,0:T(8,128)(2,1)} %bitcast.16.refs_3_.refs_6_), custom_call_target="tpu_custom_call" | custom-call | flops 2147483648 | bytes 18907136 | tf_op jit(solution)/shard_map/pallas_call | solution.py:319
  178.5 10.3 %shard_map.118 = (f32[16,256,1024]{2,1,0:T(8,128)}, f32[8,128]{1,0:T(8,128)S(1)}) custom-call(bf16[256,512]{1,0:T(8,128)(2,1)S(1)} %bitcast.97, bf16[16,256,1024]{2,1,0:T(8,128)(2,1)} %get-tuple-element.70.refs_1_.refs_3_, bf16[16,256,1024]{2,1,0:T(8,128)(2,1)} %collective-permute-done.refs_2_.refs_4_, ...), custom_call_target="tpu_custom_call", output_to_operand_aliasing={{0}: (4, {})} | custom-call | flops 2147483648 | bytes 18907136 | tf_op jit(solution)/shard_map/pallas_call | solution.py:319
  189.5 8.3 %collective-permute-done.31.refs_0_ = bf16[16,64,512]{2,1,0:T(8,128)(2,1)} collective-permute-done((bf16[16,64,512]{2,1,0:T(8,128)(2,1)}, bf16[16,64,512]{2,1,0:T(8,128)(2,1)}, u32[]{:S(2)}, u32[]{:S(2)}) %collective-permute-start.31) | collective-permute-done | bytes 1048608 | tf_op jit(solution)/shard_map/ppermute | solution.py:398
  202.8 18.5 %collective-permute-done.32.refs_12_ = bf16[16,64,512]{2,1,0:T(8,128)(2,1)} collective-permute-done((bf16[16,64,512]{2,1,0:T(8,128)(2,1)}, bf16[16,64,512]{2,1,0:T(8,128)(2,1)}, u32[]{:S(2)}, u32[]{:S(2)}) %collective-permute-start.32) | collective-permute-done | bytes 1048608 | tf_op jit(solution)/shard_map/ppermute | solution.py:398
  222.3 27.5 %shard_map.122 = (bf16[16,256,1024]{2,1,0:T(8,128)(2,1)}, bf16[16,32,512]{2,1,0:T(8,128)(2,1)}, bf16[16,32,512]{2,1,0:T(8,128)(2,1)}, bf16[16,32,512]{2,1,0:T(8,...) custom-call(f32[16,256,1024]{2,1,0:T(8,128)} %get-tuple-element.98.r, ...), custom_call_target="tpu_custom_call" | custom-call | flops 12884901888 | bytes 55574528 | tf_op jit(solution)/shard_map/pallas_call | solution.py:319
  251.3 2.2 collective-permute-start.35
  258.5 10.8 %shard_map.123 = (f32[2,256,256]{2,1,0:T(8,128)S(1)}, f32[32,4,8,128]{3,2,1,0:T(8,128)S(1)}) custom-call(f32[4,32]{1,0:T(4,128)S(1)} %pad_maximum_fusion.4.refs_0_, bf16[512,256]{1,0:T(8,128)(2,1)S(1)} %mul.58.refs_1_, bf16[4,256,1024]{2,1,0:T(8,128)(2,1)S(1)} %bitcast.91, bf16[16,256,1024]{2,1,0:T(8,128)(2,1)} %get-tuple-element.70.refs_1_.refs_3_, ...), custom_call_target="tpu_custom_call" | custom-call | flops 2147483648 | bytes 12059136 | tf_op jit(solution)/shard_map/pallas_call | solution.py:319
  276.5 10.8 %shard_map.127 = (f32[2,256,256]{2,1,0:T(8,128)S(1)}, f32[32,4,8,128]{3,2,1,0:T(8,128)S(1)}) custom-call(f32[4,32]{1,0:T(4,128)S(1)} %pad_maximum_fusion.4.refs_0_, bf16[512,256]{1,0:T(8,128)(2,1)S(1)} %mul.58.refs_1_, bf16[4,256,1024]{2,1,0:T(8,128)(2,1)S(1)} %bitcast.92, bf16[16,256,1024]{2,1,0:T(8,128)(2,1)} %get-tuple-element.70.refs_1_.refs_3_, ...), custom_call_target="tpu_custom_call" | custom-call | flops 2147483648 | bytes 12059136 | tf_op jit(solution)/shard_map/pallas_call | solution.py:319
  288.4 8.8 %collective-permute-start.37 = (bf16[16,32,512]{2,1,0:T(8,128)(2,1)S(1)}, bf16[16,32,512]{2,1,0:T(8,128)(2,1)S(1)}, u32[]{:S(2)}, u32[]{:S(2)}) collective-permute-start(bf16[16,32,512]{2,1,0:T(8,128)(2,1)S(1)} %get-tuple-element.111), channel_id=1, source_target_pairs={{0,8},{8,16},{1,9},{9,17},{2,10},{10,18},{3,11},{11,19},{4,12},{12... | collective-permute-start | bytes 1572872 | tf_op jit(solution)/shard_map/ppermute | solution.py:384
  298.9 2.6 collective-permute-start.47
  302.8 10.8 %shard_map.130 = (f32[2,256,256]{2,1,0:T(8,128)S(1)}, f32[32,4,8,128]{3,2,1,0:T(8,128)S(1)}) custom-call(f32[4,32]{1,0:T(4,128)S(1)} %pad_maximum_fusion.4.refs_0_, bf16[512,256]{1,0:T(8,128)(2,1)S(1)} %mul.58.refs_1_, bf16[4,256,1024]{2,1,0:T(8,128)(2,1)S(1)} %bitcast.93, bf16[16,256,1024]{2,1,0:T(8,128)(2,1)} %get-tuple-element.70.refs_1_.refs_3_, ...), custom_call_target="tpu_custom_call" | custom-call | flops 2147483648 | bytes 12059136 | tf_op jit(solution)/shard_map/pallas_call | solution.py:319
  316.6 8.5 %collective-permute-start.41 = (bf16[16,32,512]{2,0,1:T(8,128)(2,1)S(1)}, bf16[16,32,512]{2,0,1:T(8,128)(2,1)S(1)}, u32[]{:S(2)}, u32[]{:S(2)}) collective-permute-start(bf16[16,32,512]{2,0,1:T(8,128)(2,1)S(1)} %copy.127), channel_id=1, source_target_pairs={{0,8},{8,16},{16,24},{1,9},{9,17},{17,25},{2,10},{10,18},{18,26},{... | collective-permute-start | bytes 1572872 | tf_op jit(solution)/shard_map/ppermute | solution.py:384
  325.7 2.5 collective-permute-start.50
  332.1 2.5 collective-permute-start.44
  335.7 2.3 collective-permute-done.45.refs_7_.refs_9_
  339.8 8.4 %shard_map.132 = bf16[4,8,16,512]{3,2,1,0:T(8,128)(2,1)S(1)} custom-call(s32[1]{0:T(128)} %bitcast.refs_0_, bf16[2,16,16,32,256]{4,3,2,1,0:T(8,128)(2,1)} %refs_2_.12, bf16[2,16,16,32,256]{4,3,2,1,0:T(8,128)(2,1)} %refs_2_.12, bf16[4,8,16,512]{3,2,1,0:T(8,128)(2,1)S(1)} %collective-permute-done.52.refs_3_.refs_1_, ...), custom_call_target="tpu_custom_call" | custom-call | flops 33554432 | bytes 5767168 | tf_op jit(solution)/shard_map/pallas_call | solution.py:319
  352.1 8.5 %shard_map.133 = bf16[4,8,16,512]{3,2,1,0:T(8,128)(2,1)S(1)} custom-call(s32[1]{0:T(128)} %bitcast.refs_0_, bf16[2,16,16,32,256]{4,3,2,1,0:T(8,128)(2,1)} %refs_2_.12, bf16[2,16,16,32,256]{4,3,2,1,0:T(8,128)(2,1)} %refs_2_.12, bf16[4,8,16,512]{3,2,1,0:T(8,128)(2,1)S(1)} %collective-permute-done.46.refs_3_.refs_1_, ...), custom_call_target="tpu_custom_call" | custom-call | flops 33554432 | bytes 5767168 | tf_op jit(solution)/shard_map/pallas_call | solution.py:319
  371.7 5.1 %collective-permute-start.59 = (bf16[16,64,512]{2,1,0:T(8,128)(2,1)}, bf16[16,64,512]{2,1,0:T(8,128)(2,1)S(1)}, u32[]{:S(2)}, u32[]{:S(2)}) collective-permute-start(bf16[16,64,512]{2,1,0:T(8,128)(2,1)} %bitcast.38.refs_10_.refs_4_.refs_0_), channel_id=1, source_target_pairs={{0,8},{8,16},{16,24},{1,9},{9,17},{17,25},{2,10},{10,18},{18,26},{... | collective-permute-start | bytes 3145736 | tf_op jit(solution)/shard_map/ppermute | solution.py:397
  376.8 6.4 %shard_map.134 = (bf16[2,16,16,32,256]{4,3,2,1,0:T(8,128)(2,1)}, f32[8,128]{1,0:T(8,128)S(1)}) custom-call(s32[1]{0:T(128)} %bitcast.refs_0_, bf16[4,8,16,512]{3,2,1,0:T(8,128)(2,1)S(1)} %collective-permute-done.52.refs_3_.refs_1_, bf16[8,16,512]{2,1,0:T(8,128)(2,1)S(1)} %copy-done.37, bf16[8,16,512]{2,1,0:T(8,128)(2,1)S(1)} %copy-done.43, ...), custom_call_target="tpu_custom_call" | custom-call | flops 33554432 | bytes 5799936 | tf_op jit(solution)/shard_map/pallas_call | solution.py:319
  383.2 6.4 %shard_map.135 = (bf16[2,16,16,32,256]{4,3,2,1,0:T(8,128)(2,1)}, f32[8,128]{1,0:T(8,128)S(1)}) custom-call(s32[1]{0:T(128)} %bitcast.refs_0_, bf16[4,8,16,512]{3,2,1,0:T(8,128)(2,1)S(1)} %collective-permute-done.46.refs_3_.refs_1_, bf16[8,16,512]{2,1,0:T(8,128)(2,1)S(1)} %get-tuple-element.169.refs_3_.refs_2_, ...), custom_call_target="tpu_custom_call", output_to_operand_aliasing={{0}: (11, {})} | custom-call | flops 33554432 | bytes 5799936 | tf_op jit(solution)/shard_map/pallas_call | solution.py:319
  390.3 9.5 %shard_map.136 = (bf16[4,16,4,64,512]{4,3,2,1,0:T(8,128)(2,1)}, f32[8,128]{1,0:T(8,128)S(1)}) custom-call(f32[4,16]{1,0:T(4,128)S(1)} %get-tuple-element.189.refs_1_.refs_0_, bf16[4,256,1024]{2,1,0:T(8,128)(2,1)S(1)} %bitcast.94, bf16[1024,512]{1,0:T(8,128)(2,1)S(1)} %copy-done.70, bf16[512,256]{1,0:T(8,128)(2,1)S(1)} %copy-done.58, ...), custom_call_target="tpu_custom_call", output_to_operand_aliasing={{0}: (5, {})} | custom-call | flops 6442450944 | bytes 11018496 | tf_op jit(solution)/shard_map/pallas_call | solution.py:319
  405.8 10.9 %shard_map.138 = (f32[2,256,256]{2,1,0:T(8,128)S(1)}, f32[32,4,8,128]{3,2,1,0:T(8,128)S(1)}) custom-call(f32[4,32]{1,0:T(4,128)S(1)} %pad_maximum_fusion.4.refs_0_, bf16[512,256]{1,0:T(8,128)(2,1)S(1)} %mul.58.refs_1_, bf16[4,256,1024]{2,1,0:T(8,128)(2,1)S(1)} %bitcast.95, bf16[16,256,1024]{2,1,0:T(8,128)(2,1)} %get-tuple-element.70.refs_1_.refs_3_, ...), custom_call_target="tpu_custom_call" | custom-call | flops 2147483648 | bytes 12059136 | tf_op jit(solution)/shard_map/pallas_call | solution.py:319
  417.7 2.7 reshape.60
  420.4 5.8 %shard_map.140 = (f32[16,4,8,128]{3,2,1,0:T(8,128)S(1)}, f32[8,128]{1,0:T(8,128)S(1)}) custom-call(bf16[16,64,512]{2,1,0:T(8,128)(2,1)} %bitcast.38.refs_10_.refs_4_.refs_0_, bf16[16,64,512]{2,1,0:T(8,128)(2,1)S(1)} %copy-done.3, bf16[16,64,512]{2,1,0:T(8,128)(2,1)} %shard_map.139.refs_2_, ...), custom_call_target="tpu_custom_call" | custom-call | flops 25165824 | bytes 16007168 | tf_op jit(solution)/shard_map/pallas_call | solution.py:319
  430.7 2.7 multiply_reduce_fusion
  433.8 5.5 %shard_map.143 = (f32[16,4,8,128]{3,2,1,0:T(8,128)S(1)}, f32[8,128]{1,0:T(8,128)S(1)}) custom-call(bf16[16,64,512]{2,1,0:T(8,128)(2,1)} %shard_map.141.refs_0_.refs_4_, bf16[16,64,512]{2,1,0:T(8,128)(2,1)} %shard_map.142.refs_1_, bf16[4,16,4,64,512]{4,3,2,1,0:T(8,128)(2,1)} %get-tuple-element.130.refs_3_.refs_4_.refs_5_.refs_2_, ...), custom_call_target="tpu_custom_call" | custom-call | flops 16777216 | bytes 10764288 | tf_op jit(solution)/shard_map/pallas_call | solution.py:319
  439.4 18.0 %collective-permute-done.64.refs_1_ = bf16[16,64,512]{2,1,0:T(8,128)(2,1)S(1)} collective-permute-done((bf16[16,64,512]{2,1,0:T(8,128)(2,1)}, bf16[16,64,512]{2,1,0:T(8,128)(2,1)S(1)}, u32[]{:S(2)}, u32[]{:S(2)}) %collective-permute-start.64) | collective-permute-done | bytes 1048608 | tf_op jit(solution)/shard_map/ppermute | solution.py:398
  457.3 4.9 %shard_map.144 = (f32[16,4,8,128]{3,2,1,0:T(8,128)S(1)}, f32[8,128]{1,0:T(8,128)}) custom-call(bf16[16,64,512]{2,1,0:T(8,128)(2,1)} %collective-permute-done.63.refs_0_, bf16[16,64,512]{2,1,0:T(8,128)(2,1)S(1)} %collective-permute-done.64.refs_1_, bf16[4,16,4,64,512]{4,3,2,1,0:T(8,128)(2,1)} %get-tuple-element.130.refs_3_.refs_4_.refs_5_.refs_2_, ...), custom_call_target="tpu_custom_call" | custom-call | flops 16777216 | bytes 10764288 | tf_op jit(solution)/shard_map/pallas_call | solution.py:319
  470.0 3.3 collective-permute-start.68
  (384 shorter events, 134.1 us)
Async XLA Ops:
  18.5 141.3 %collective-permute-start = (bf16[16,256,1024]{2,1,0:T(8,128)(2,1)}, bf16[16,256,1024]{2,1,0:T(8,128)(2,1)}, u32[]{:S(2)}, u32[]{:S(2)}) collective-permute-start(bf16[16,256,1024]{2,1,0:T(8,128)(2,1)} %get-tuple-element.70.refs_1_.refs_3_), channel_id=1, source_target_pairs={{0,1},{1,0},{2,3},{3,2},{4,5},{5,4},{6,7},{7,6},{8,9},{9,8},{10,11... | collective-permute-start | bytes 25165832 | tf_op jit(solution)/shard_map/ppermute | solution.py:409
  18.9 24.2 %collective-permute-start.2 = (bf16[16,32,512]{2,1,0:T(8,128)(2,1)}, bf16[16,32,512]{2,1,0:T(8,128)(2,1)}, u32[]{:S(2)}, u32[]{:S(2)}) collective-permute-start(bf16[16,32,512]{2,1,0:T(8,128)(2,1)} %get-tuple-element.72.refs_0_), channel_id=1, source_target_pairs={{24,16},{25,17},{26,18},{27,19},{28,20},{29,21},{30,22},{31,23}} | collective-permute-start | bytes 1572872 | tf_op jit(solution)/shard_map/ppermute | solution.py:385
  20.4 22.7 %collective-permute-start.1 = (bf16[16,32,512]{2,1,0:T(8,128)(2,1)}, bf16[16,32,512]{2,1,0:T(8,128)(2,1)}, u32[]{:S(2)}, u32[]{:S(2)}) collective-permute-start(bf16[16,32,512]{2,1,0:T(8,128)(2,1)} %get-tuple-element.74.refs_2_.refs_4_), channel_id=1, source_target_pairs={{0,8},{1,9},{2,10},{3,11},{4,12},{5,13},{6,14},{7,15}} | collective-permute-start | bytes 1572872 | tf_op jit(solution)/shard_map/ppermute | solution.py:384
  39.5 19.5 %collective-permute-start.10 = (bf16[16,32,512]{2,1,0:T(8,128)(2,1)}, bf16[16,32,512]{2,1,0:T(8,128)(2,1)}, u32[]{:S(2)}, u32[]{:S(2)}) collective-permute-start(bf16[16,32,512]{2,1,0:T(8,128)(2,1)} %shard_map.107), channel_id=1, source_target_pairs={{0,8},{1,9},{2,10},{3,11},{4,12},{5,13},{6,14},{7,15}} | collective-permute-start | bytes 1572872 | tf_op jit(solution)/shard_map/ppermute | solution.py:384
  42.4 16.6 %collective-permute-start.11 = (bf16[16,32,512]{2,1,0:T(8,128)(2,1)}, bf16[16,32,512]{2,1,0:T(8,128)(2,1)S(1)}, u32[]{:S(2)}, u32[]{:S(2)}) collective-permute-start(bf16[16,32,512]{2,1,0:T(8,128)(2,1)} %shard_map.108), channel_id=1, source_target_pairs={{24,16},{25,17},{26,18},{27,19},{28,20},{29,21},{30,22},{31,23}} | collective-permute-start | bytes 1572872 | tf_op jit(solution)/shard_map/ppermute | solution.py:385
  45.5 19.3 %collective-permute-start.4 = (bf16[16,32,512]{2,1,0:T(8,128)(2,1)S(1)}, bf16[16,32,512]{2,1,0:T(8,128)(2,1)S(1)}, u32[]{:S(2)}, u32[]{:S(2)}) collective-permute-start(bf16[16,32,512]{2,1,0:T(8,128)(2,1)S(1)} %get-tuple-element.76), channel_id=1, source_target_pairs={{24,16},{16,8},{25,17},{17,9},{26,18},{18,10},{27,19},{19,11},{28,... | collective-permute-start | bytes 1572872 | tf_op jit(solution)/shard_map/ppermute | solution.py:385
  46.2 18.6 %collective-permute-start.3 = (bf16[16,32,512]{2,1,0:T(8,128)(2,1)S(1)}, bf16[16,32,512]{2,1,0:T(8,128)(2,1)S(1)}, u32[]{:S(2)}, u32[]{:S(2)}) collective-permute-start(bf16[16,32,512]{2,1,0:T(8,128)(2,1)S(1)} %get-tuple-element.75.refs_4_), channel_id=1, source_target_pairs={{0,8},{8,16},{1,9},{9,17},{2,10},{10,18},{3,11},{11,19},{4,12},{12... | collective-permute-start | bytes 1572872 | tf_op jit(solution)/shard_map/ppermute | solution.py:384
  60.3 21.1 %collective-permute-start.12 = (bf16[16,32,512]{2,1,0:T(8,128)(2,1)S(1)}, bf16[16,32,512]{2,1,0:T(8,128)(2,1)S(1)}, u32[]{:S(2)}, u32[]{:S(2)}) collective-permute-start(bf16[16,32,512]{2,1,0:T(8,128)(2,1)S(1)} %get-tuple-element.86), channel_id=1, source_target_pairs={{0,8},{8,16},{1,9},{9,17},{2,10},{10,18},{3,11},{11,19},{4,12},{12... | collective-permute-start | bytes 1572872 | tf_op jit(solution)/shard_map/ppermute | solution.py:384
  64.1 17.3 %collective-permute-start.13 = (bf16[16,32,512]{2,1,0:T(8,128)(2,1)S(1)}, bf16[16,32,512]{2,1,0:T(8,128)(2,1)S(1)}, u32[]{:S(2)}, u32[]{:S(2)}) collective-permute-start(bf16[16,32,512]{2,1,0:T(8,128)(2,1)S(1)} %get-tuple-element.87), channel_id=1, source_target_pairs={{24,16},{16,8},{25,17},{17,9},{26,18},{18,10},{27,19},{19,11},{28,... | collective-permute-start | bytes 1572872 | tf_op jit(solution)/shard_map/ppermute | solution.py:385
  66.8 24.3 %collective-permute-start.5 = (bf16[16,32,512]{2,0,1:T(8,128)(2,1)S(1)}, bf16[16,32,512]{2,0,1:T(8,128)(2,1)S(1)}, u32[]{:S(2)}, u32[]{:S(2)}) collective-permute-start(bf16[16,32,512]{2,0,1:T(8,128)(2,1)S(1)} %copy.116), channel_id=1, source_target_pairs={{0,8},{8,16},{16,24},{1,9},{9,17},{17,25},{2,10},{10,18},{18,26},{... | collective-permute-start | bytes 1572872 | tf_op jit(solution)/shard_map/ppermute | solution.py:384
  70.5 20.7 %collective-permute-start.6 = (bf16[16,32,512]{2,0,1:T(8,128)(2,1)S(1)}, bf16[16,32,512]{2,0,1:T(8,128)(2,1)S(1)}, u32[]{:S(2)}, u32[]{:S(2)}) collective-permute-start(bf16[16,32,512]{2,0,1:T(8,128)(2,1)S(1)} %copy.117), channel_id=1, source_target_pairs={{24,16},{16,8},{8,0},{25,17},{17,9},{9,1},{26,18},{18,10},{10,2},{... | collective-permute-start | bytes 1572872 | tf_op jit(solution)/shard_map/ppermute | solution.py:385
  82.0 17.9 %collective-permute-start.15 = (bf16[16,32,512]{2,0,1:T(8,128)(2,1)S(1)}, bf16[16,32,512]{2,0,1:T(8,128)(2,1)S(1)}, u32[]{:S(2)}, u32[]{:S(2)}) collective-permute-start(bf16[16,32,512]{2,0,1:T(8,128)(2,1)S(1)} %copy.120), channel_id=1, source_target_pairs={{24,16},{16,8},{8,0},{25,17},{17,9},{9,1},{26,18},{18,10},{10,2},{... | collective-permute-start | bytes 1572872 | tf_op jit(solution)/shard_map/ppermute | solution.py:385
  83.6 17.8 %collective-permute-start.14 = (bf16[16,32,512]{2,0,1:T(8,128)(2,1)S(1)}, bf16[16,32,512]{2,0,1:T(8,128)(2,1)S(1)}, u32[]{:S(2)}, u32[]{:S(2)}) collective-permute-start(bf16[16,32,512]{2,0,1:T(8,128)(2,1)S(1)} %copy.119), channel_id=1, source_target_pairs={{0,8},{8,16},{16,24},{1,9},{9,17},{17,25},{2,10},{10,18},{18,26},{... | collective-permute-start | bytes 1572872 | tf_op jit(solution)/shard_map/ppermute | solution.py:384
  91.7 12.6 %collective-permute-start.9 = (bf16[8,16,512]{2,1,0:T(8,128)(2,1)S(1)}, bf16[8,16,512]{2,1,0:T(8,128)(2,1)S(1)}, u32[]{:S(2)}, u32[]{:S(2)}) collective-permute-start(bf16[8,16,512]{2,1,0:T(8,128)(2,1)S(1)} %get-tuple-element.176), channel_id=1, source_target_pairs={{0,6},{2,4},{4,2},{6,0},{1,7},{3,5},{5,3},{7,1},{8,14},{10,12},{12... | collective-permute-start | bytes 393224 | tf_op jit(solution)/shard_map/ppermute | solution.py:405
  94.2 10.6 %collective-permute-start.8 = (bf16[8,16,512]{2,1,0:T(8,128)(2,1)S(1)}, bf16[8,16,512]{2,1,0:T(8,128)(2,1)S(1)}, u32[]{:S(2)}, u32[]{:S(2)}) collective-permute-start(bf16[8,16,512]{2,1,0:T(8,128)(2,1)S(1)} %get-tuple-element.177), channel_id=1, source_target_pairs={{0,4},{2,6},{4,0},{6,2},{1,5},{3,7},{5,1},{7,3},{8,12},{10,14},{12... | collective-permute-start | bytes 393224 | tf_op jit(solution)/shard_map/ppermute | solution.py:405
  101.8 12.7 %collective-permute-start.18 = (bf16[8,16,512]{2,1,0:T(8,128)(2,1)S(1)}, bf16[8,16,512]{2,1,0:T(8,128)(2,1)S(1)}, u32[]{:S(2)}, u32[]{:S(2)}) collective-permute-start(bf16[8,16,512]{2,1,0:T(8,128)(2,1)S(1)} %get-tuple-element.170), channel_id=1, source_target_pairs={{0,6},{2,4},{4,2},{6,0},{1,7},{3,5},{5,3},{7,1},{8,14},{10,12},{12... | collective-permute-start | bytes 393224 | tf_op jit(solution)/shard_map/ppermute | solution.py:405
  104.3 10.2 %collective-permute-start.17 = (bf16[8,16,512]{2,1,0:T(8,128)(2,1)S(1)}, bf16[8,16,512]{2,1,0:T(8,128)(2,1)S(1)}, u32[]{:S(2)}, u32[]{:S(2)}) collective-permute-start(bf16[8,16,512]{2,1,0:T(8,128)(2,1)S(1)} %get-tuple-element.171), channel_id=1, source_target_pairs={{0,4},{2,6},{4,0},{6,2},{1,5},{3,7},{5,1},{7,3},{8,12},{10,14},{12... | collective-permute-start | bytes 393224 | tf_op jit(solution)/shard_map/ppermute | solution.py:405
  116.6 11.3 %collective-permute-start.19 = (bf16[4,8,16,512]{3,1,2,0:T(8,128)(2,1)S(1)}, bf16[4,8,16,512]{3,1,2,0:T(8,128)(2,1)S(1)}, u32[]{:S(2)}, u32[]{:S(2)}) collective-permute-start(bf16[4,8,16,512]{3,1,2,0:T(8,128)(2,1)S(1)} %copy.122), channel_id=1, source_target_pairs={{0,1},{1,0},{2,3},{3,2},{4,5},{5,4},{6,7},{7,6},{8,9},{9,8},{10,11... | collective-permute-start | bytes 1572872 | tf_op jit(solution)/shard_map/ppermute | solution.py:409
  128.3 13.6 %collective-permute-start.22 = (bf16[8,16,512]{2,0,1:T(8,128)(2,1)S(1)}, bf16[8,16,512]{2,0,1:T(8,128)(2,1)S(1)}, u32[]{:S(2)}, u32[]{:S(2)}) collective-permute-start(bf16[8,16,512]{2,0,1:T(8,128)(2,1)S(1)} %get-tuple-element.173), channel_id=1, source_target_pairs={{0,6},{2,4},{4,2},{6,0},{1,7},{3,5},{5,3},{7,1},{8,14},{10,12},{12... | collective-permute-start | bytes 393224 | tf_op jit(solution)/shard_map/ppermute | solution.py:405
  133.0 13.5 %collective-permute-start.26 = (bf16[8,16,512]{2,0,1:T(8,128)(2,1)S(1)}, bf16[8,16,512]{2,0,1:T(8,128)(2,1)S(1)}, u32[]{:S(2)}, u32[]{:S(2)}) collective-permute-start(bf16[8,16,512]{2,0,1:T(8,128)(2,1)S(1)} %get-tuple-element.166), channel_id=1, source_target_pairs={{0,6},{2,4},{4,2},{6,0},{1,7},{3,5},{5,3},{7,1},{8,14},{10,12},{12... | collective-permute-start | bytes 393224 | tf_op jit(solution)/shard_map/ppermute | solution.py:405
  147.2 26.2 %collective-permute-start.30 = (bf16[16,64,512]{2,1,0:T(8,128)(2,1)}, bf16[16,64,512]{2,1,0:T(8,128)(2,1)}, u32[]{:S(2)}, u32[]{:S(2)}) collective-permute-start(bf16[16,64,512]{2,1,0:T(8,128)(2,1)} %bitcast.16.refs_3_.refs_6_), channel_id=1, source_target_pairs={{24,16},{16,8},{8,0},{25,17},{17,9},{9,1},{26,18},{18,10},{10,2},{... | collective-permute-start | bytes 3145736 | tf_op jit(solution)/shard_map/ppermute | solution.py:398
  148.5 26.2 %collective-permute-start.27 = (bf16[16,64,512]{2,1,0:T(8,128)(2,1)}, bf16[16,64,512]{2,1,0:T(8,128)(2,1)S(1)}, u32[]{:S(2)}, u32[]{:S(2)}) collective-permute-start(bf16[16,64,512]{2,1,0:T(8,128)(2,1)} %bitcast.16.refs_3_.refs_6_), channel_id=1, source_target_pairs={{0,8},{8,16},{16,24},{1,9},{9,17},{17,25},{2,10},{10,18},{18,26},{... | collective-permute-start | bytes 3145736 | tf_op jit(solution)/shard_map/ppermute | solution.py:397
  173.4 24.4 %collective-permute-start.31 = (bf16[16,64,512]{2,1,0:T(8,128)(2,1)}, bf16[16,64,512]{2,1,0:T(8,128)(2,1)}, u32[]{:S(2)}, u32[]{:S(2)}) collective-permute-start(bf16[16,64,512]{2,1,0:T(8,128)(2,1)} %shard_map.120.refs_10_), channel_id=1, source_target_pairs={{16,8},{8,0},{17,9},{9,1},{18,10},{10,2},{19,11},{11,3},{20,12},{1... | collective-permute-start | bytes 3145736 | tf_op jit(solution)/shard_map/ppermute | solution.py:398
  175.6 23.5 %collective-permute-start.28 = (bf16[16,64,512]{2,1,0:T(8,128)(2,1)}, bf16[16,64,512]{2,1,0:T(8,128)(2,1)S(1)}, u32[]{:S(2)}, u32[]{:S(2)}) collective-permute-start(bf16[16,64,512]{2,1,0:T(8,128)(2,1)} %shard_map.117.refs_3_.refs_7_), channel_id=1, source_target_pairs={{8,16},{16,24},{9,17},{17,25},{10,18},{18,26},{11,19},{19,27},{12,... | collective-permute-start | bytes 3145736 | tf_op jit(solution)/shard_map/ppermute | solution.py:397
  197.8 23.5 %collective-permute-start.32 = (bf16[16,64,512]{2,1,0:T(8,128)(2,1)}, bf16[16,64,512]{2,1,0:T(8,128)(2,1)}, u32[]{:S(2)}, u32[]{:S(2)}) collective-permute-start(bf16[16,64,512]{2,1,0:T(8,128)(2,1)} %shard_map.121.refs_11_), channel_id=1, source_target_pairs={{8,0},{9,1},{10,2},{11,3},{12,4},{13,5},{14,6},{15,7}} | collective-permute-start | bytes 3145736 | tf_op jit(solution)/shard_map/ppermute | solution.py:398
  200.1 21.3 %collective-permute-start.29 = (bf16[16,64,512]{2,1,0:T(8,128)(2,1)}, bf16[16,64,512]{2,1,0:T(8,128)(2,1)S(1)}, u32[]{:S(2)}, u32[]{:S(2)}) collective-permute-start(bf16[16,64,512]{2,1,0:T(8,128)(2,1)} %shard_map.119.refs_8_), channel_id=1, source_target_pairs={{16,24},{17,25},{18,26},{19,27},{20,28},{21,29},{22,30},{23,31}} | collective-permute-start | bytes 3145736 | tf_op jit(solution)/shard_map/ppermute | solution.py:397
  249.8 23.1 %collective-permute-start.36 = (bf16[16,32,512]{2,1,0:T(8,128)(2,1)}, bf16[16,32,512]{2,1,0:T(8,128)(2,1)}, u32[]{:S(2)}, u32[]{:S(2)}) collective-permute-start(bf16[16,32,512]{2,1,0:T(8,128)(2,1)} %get-tuple-element.108.refs_0_), channel_id=1, source_target_pairs={{24,16},{25,17},{26,18},{27,19},{28,20},{29,21},{30,22},{31,23}} | collective-permute-start | bytes 1572872 | tf_op jit(solution)/shard_map/ppermute | solution.py:385
  251.3 21.6 %collective-permute-start.35 = (bf16[16,32,512]{2,1,0:T(8,128)(2,1)}, bf16[16,32,512]{2,1,0:T(8,128)(2,1)}, u32[]{:S(2)}, u32[]{:S(2)}) collective-permute-start(bf16[16,32,512]{2,1,0:T(8,128)(2,1)} %get-tuple-element.105.refs_6_.refs_2_), channel_id=1, source_target_pairs={{0,8},{1,9},{2,10},{3,11},{4,12},{5,13},{6,14},{7,15}} | collective-permute-start | bytes 1572872 | tf_op jit(solution)/shard_map/ppermute | solution.py:384
  270.9 17.2 %collective-permute-start.33 = (bf16[16,32,512]{2,1,0:T(8,128)(2,1)}, bf16[16,32,512]{2,1,0:T(8,128)(2,1)S(1)}, u32[]{:S(2)}, u32[]{:S(2)}) collective-permute-start(bf16[16,32,512]{2,1,0:T(8,128)(2,1)} %shard_map.124), channel_id=1, source_target_pairs={{0,8},{1,9},{2,10},{3,11},{4,12},{5,13},{6,14},{7,15}} | collective-permute-start | bytes 1572872 | tf_op jit(solution)/shard_map/ppermute | solution.py:384
  272.2 15.9 %collective-permute-start.34 = (bf16[16,32,512]{2,1,0:T(8,128)(2,1)}, bf16[16,32,512]{2,1,0:T(8,128)(2,1)S(1)}, u32[]{:S(2)}, u32[]{:S(2)}) collective-permute-start(bf16[16,32,512]{2,1,0:T(8,128)(2,1)} %shard_map.125), channel_id=1, source_target_pairs={{24,16},{25,17},{26,18},{27,19},{28,20},{29,21},{30,22},{31,23}} | collective-permute-start | bytes 1572872 | tf_op jit(solution)/shard_map/ppermute | solution.py:385
  274.3 23.6 %collective-permute-start.40 = (bf16[16,32,512]{2,1,0:T(8,128)(2,1)S(1)}, bf16[16,32,512]{2,1,0:T(8,128)(2,1)S(1)}, u32[]{:S(2)}, u32[]{:S(2)}) collective-permute-start(bf16[16,32,512]{2,1,0:T(8,128)(2,1)S(1)} %get-tuple-element.113), channel_id=1, source_target_pairs={{24,16},{16,8},{25,17},{17,9},{26,18},{18,10},{27,19},{19,11},{28,... | collective-permute-start | bytes 1572872 | tf_op jit(solution)/shard_map/ppermute | solution.py:385
  275.0 22.9 %collective-permute-start.39 = (bf16[16,32,512]{2,1,0:T(8,128)(2,1)S(1)}, bf16[16,32,512]{2,1,0:T(8,128)(2,1)S(1)}, u32[]{:S(2)}, u32[]{:S(2)}) collective-permute-start(bf16[16,32,512]{2,1,0:T(8,128)(2,1)S(1)} %get-tuple-element.109.refs_6_), channel_id=1, source_target_pairs={{0,8},{8,16},{1,9},{9,17},{2,10},{10,18},{3,11},{11,19},{4,12},{12... | collective-permute-start | bytes 1572872 | tf_op jit(solution)/shard_map/ppermute | solution.py:384
  288.4 26.0 %collective-permute-start.37 = (bf16[16,32,512]{2,1,0:T(8,128)(2,1)S(1)}, bf16[16,32,512]{2,1,0:T(8,128)(2,1)S(1)}, u32[]{:S(2)}, u32[]{:S(2)}) collective-permute-start(bf16[16,32,512]{2,1,0:T(8,128)(2,1)S(1)} %get-tuple-element.111), channel_id=1, source_target_pairs={{0,8},{8,16},{1,9},{9,17},{2,10},{10,18},{3,11},{11,19},{4,12},{12... | collective-permute-start | bytes 1572872 | tf_op jit(solution)/shard_map/ppermute | solution.py:384
  297.2 17.2 %collective-permute-start.38 = (bf16[16,32,512]{2,1,0:T(8,128)(2,1)S(1)}, bf16[16,32,512]{2,1,0:T(8,128)(2,1)S(1)}, u32[]{:S(2)}, u32[]{:S(2)}) collective-permute-start(bf16[16,32,512]{2,1,0:T(8,128)(2,1)S(1)} %get-tuple-element.112), channel_id=1, source_target_pairs={{24,16},{16,8},{25,17},{17,9},{26,18},{18,10},{27,19},{19,11},{28,... | collective-permute-start | bytes 1572872 | tf_op jit(solution)/shard_map/ppermute | solution.py:385
  298.9 26.2 %collective-permute-start.47 = (bf16[16,32,512]{2,0,1:T(8,128)(2,1)S(1)}, bf16[16,32,512]{2,0,1:T(8,128)(2,1)S(1)}, u32[]{:S(2)}, u32[]{:S(2)}) collective-permute-start(bf16[16,32,512]{2,0,1:T(8,128)(2,1)S(1)} %copy.130), channel_id=1, source_target_pairs={{0,8},{8,16},{16,24},{1,9},{9,17},{17,25},{2,10},{10,18},{18,26},{... | collective-permute-start | bytes 1572872 | tf_op jit(solution)/shard_map/ppermute | solution.py:384
  301.5 23.6 %collective-permute-start.48 = (bf16[16,32,512]{2,0,1:T(8,128)(2,1)S(1)}, bf16[16,32,512]{2,0,1:T(8,128)(2,1)S(1)}, u32[]{:S(2)}, u32[]{:S(2)}) collective-permute-start(bf16[16,32,512]{2,0,1:T(8,128)(2,1)S(1)} %copy.131), channel_id=1, source_target_pairs={{24,16},{16,8},{8,0},{25,17},{17,9},{9,1},{26,18},{18,10},{10,2},{... | collective-permute-start | bytes 1572872 | tf_op jit(solution)/shard_map/ppermute | solution.py:385
  315.3 14.7 %collective-permute-start.42 = (bf16[16,32,512]{2,0,1:T(8,128)(2,1)S(1)}, bf16[16,32,512]{2,0,1:T(8,128)(2,1)S(1)}, u32[]{:S(2)}, u32[]{:S(2)}) collective-permute-start(bf16[16,32,512]{2,0,1:T(8,128)(2,1)S(1)} %copy.128), channel_id=1, source_target_pairs={{24,16},{16,8},{8,0},{25,17},{17,9},{9,1},{26,18},{18,10},{10,2},{... | collective-permute-start | bytes 1572872 | tf_op jit(solution)/shard_map/ppermute | solution.py:385
  316.6 14.9 %collective-permute-start.41 = (bf16[16,32,512]{2,0,1:T(8,128)(2,1)S(1)}, bf16[16,32,512]{2,0,1:T(8,128)(2,1)S(1)}, u32[]{:S(2)}, u32[]{:S(2)}) collective-permute-start(bf16[16,32,512]{2,0,1:T(8,128)(2,1)S(1)} %copy.127), channel_id=1, source_target_pairs={{0,8},{8,16},{16,24},{1,9},{9,17},{17,25},{2,10},{10,18},{18,26},{... | collective-permute-start | bytes 1572872 | tf_op jit(solution)/shard_map/ppermute | solution.py:384
  339.7 12.4 %collective-permute-start.46 = (bf16[4,8,16,512]{3,2,1,0:T(8,128)(2,1)S(1)}, bf16[4,8,16,512]{3,2,1,0:T(8,128)(2,1)S(1)}, u32[]{:S(2)}, u32[]{:S(2)}) collective-permute-start(bf16[4,8,16,512]{3,2,1,0:T(8,128)(2,1)S(1)} %pad_maximum_fusion), channel_id=1, source_target_pairs={{0,1},{1,0},{2,3},{3,2},{4,5},{5,4},{6,7},{7,6},{8,9},{9,8},{10,11... | collective-permute-start | bytes 1572872 | tf_op jit(solution)/shard_map/ppermute | solution.py:409
  348.5 15.3 %collective-permute-start.53 = (bf16[8,16,512]{2,0,1:T(8,128)(2,1)S(1)}, bf16[8,16,512]{2,0,1:T(8,128)(2,1)S(1)}, u32[]{:S(2)}, u32[]{:S(2)}) collective-permute-start(bf16[8,16,512]{2,0,1:T(8,128)(2,1)S(1)} %bitcast.112), channel_id=1, source_target_pairs={{0,2},{2,0},{4,6},{6,4},{1,3},{3,1},{5,7},{7,5},{8,10},{10,8},{12,... | collective-permute-start | bytes 393224 | tf_op jit(solution)/shard_map/ppermute | solution.py:405
  349.5 16.5 %collective-permute-start.54 = (bf16[8,16,512]{2,0,1:T(8,128)(2,1)S(1)}, bf16[8,16,512]{2,0,1:T(8,128)(2,1)S(1)}, u32[]{:S(2)}, u32[]{:S(2)}) collective-permute-start(bf16[8,16,512]{2,0,1:T(8,128)(2,1)S(1)} %bitcast.108), channel_id=1, source_target_pairs={{0,4},{2,6},{4,0},{6,2},{1,5},{3,7},{5,1},{7,3},{8,12},{10,14},{12... | collective-permute-start | bytes 393224 | tf_op jit(solution)/shard_map/ppermute | solution.py:405
  350.6 16.1 %collective-permute-start.55 = (bf16[8,16,512]{2,0,1:T(8,128)(2,1)S(1)}, bf16[8,16,512]{2,0,1:T(8,128)(2,1)S(1)}, u32[]{:S(2)}, u32[]{:S(2)}) collective-permute-start(bf16[8,16,512]{2,0,1:T(8,128)(2,1)S(1)} %bitcast.107), channel_id=1, source_target_pairs={{0,6},{2,4},{4,2},{6,0},{1,7},{3,5},{5,3},{7,1},{8,14},{10,12},{12... | collective-permute-start | bytes 393224 | tf_op jit(solution)/shard_map/ppermute | solution.py:405
  370.4 30.0 %collective-permute-start.60 = (bf16[16,64,512]{2,1,0:T(8,128)(2,1)}, bf16[16,64,512]{2,1,0:T(8,128)(2,1)}, u32[]{:S(2)}, u32[]{:S(2)}) collective-permute-start(bf16[16,64,512]{2,1,0:T(8,128)(2,1)} %bitcast.38.refs_10_.refs_4_.refs_0_), channel_id=1, source_target_pairs={{24,16},{16,8},{8,0},{25,17},{17,9},{9,1},{26,18},{18,10},{10,2},{... | collective-permute-start | bytes 3145736 | tf_op jit(solution)/shard_map/ppermute | solution.py:398
  371.7 30.0 %collective-permute-start.59 = (bf16[16,64,512]{2,1,0:T(8,128)(2,1)}, bf16[16,64,512]{2,1,0:T(8,128)(2,1)S(1)}, u32[]{:S(2)}, u32[]{:S(2)}) collective-permute-start(bf16[16,64,512]{2,1,0:T(8,128)(2,1)} %bitcast.38.refs_10_.refs_4_.refs_0_), channel_id=1, source_target_pairs={{0,8},{8,16},{16,24},{1,9},{9,17},{17,25},{2,10},{10,18},{18,26},{... | collective-permute-start | bytes 3145736 | tf_op jit(solution)/shard_map/ppermute | solution.py:397
  400.3 27.2 %collective-permute-start.62 = (bf16[16,64,512]{2,1,0:T(8,128)(2,1)}, bf16[16,64,512]{2,1,0:T(8,128)(2,1)}, u32[]{:S(2)}, u32[]{:S(2)}) collective-permute-start(bf16[16,64,512]{2,1,0:T(8,128)(2,1)} %shard_map.139.refs_2_), channel_id=1, source_target_pairs={{16,8},{8,0},{17,9},{9,1},{18,10},{10,2},{19,11},{11,3},{20,12},{1... | collective-permute-start | bytes 3145736 | tf_op jit(solution)/shard_map/ppermute | solution.py:398
  402.6 26.4 %collective-permute-start.61 = (bf16[16,64,512]{2,1,0:T(8,128)(2,1)}, bf16[16,64,512]{2,1,0:T(8,128)(2,1)}, u32[]{:S(2)}, u32[]{:S(2)}) collective-permute-start(bf16[16,64,512]{2,1,0:T(8,128)(2,1)} %shard_map.137.refs_6_.refs_1_), channel_id=1, source_target_pairs={{8,16},{16,24},{9,17},{17,25},{10,18},{18,26},{11,19},{19,27},{12,... | collective-permute-start | bytes 3145736 | tf_op jit(solution)/shard_map/ppermute | solution.py:397
  427.6 29.7 %collective-permute-start.64 = (bf16[16,64,512]{2,1,0:T(8,128)(2,1)}, bf16[16,64,512]{2,1,0:T(8,128)(2,1)S(1)}, u32[]{:S(2)}, u32[]{:S(2)}) collective-permute-start(bf16[16,64,512]{2,1,0:T(8,128)(2,1)} %shard_map.142.refs_1_), channel_id=1, source_target_pairs={{8,0},{9,1},{10,2},{11,3},{12,4},{13,5},{14,6},{15,7}} | collective-permute-start | bytes 3145736 | tf_op jit(solution)/shard_map/ppermute | solution.py:398
  429.1 28.3 %collective-permute-start.63 = (bf16[16,64,512]{2,1,0:T(8,128)(2,1)}, bf16[16,64,512]{2,1,0:T(8,128)(2,1)}, u32[]{:S(2)}, u32[]{:S(2)}) collective-permute-start(bf16[16,64,512]{2,1,0:T(8,128)(2,1)} %shard_map.141.refs_0_.refs_4_), channel_id=1, source_target_pairs={{16,24},{17,25},{18,26},{19,27},{20,28},{21,29},{22,30},{23,31}} | collective-permute-start | bytes 3145736 | tf_op jit(solution)/shard_map/ppermute | solution.py:397
  (101 other events, 943.1 us)

commit v5 on v4

--- a/solution.py
+++ b/solution.py
@@ -148,14 +148,15 @@
     token[...] = jnp.zeros(token.shape, F32)
 
 
-def local_back_kernel(lw, mix, fields, own, other, grad, terms, sums):
+def local_back_kernel(lw, mix, fields, own, other, grad, *refs):
+    earlier, (terms, sums) = refs[:-2], refs[-2:]
     n, rows, cells = own.shape
     inputs = fields.shape[0]
 
     @pl.when(pl.program_id(0) == 0)
     def _():
-        terms[...] = jnp.zeros(terms.shape, F32)
-        sums[...] = jnp.zeros(sums.shape, F32)
+        for i, total in enumerate((terms, sums)):
+            total[...] = earlier[i][...] if earlier else jnp.zeros(total.shape, F32)
 
     g = grad[...].reshape(-1, cells)
     for half, part in enumerate((own, other)):
@@ -163,8 +164,8 @@
             part[...].reshape(n * rows, cells), g, (((1,), (1,)), ((), ())), preferred_element_type=F32
         )
 
-    def lanes(step, _):
-        at = pl.ds(pl.multiple_of(step * 256, 256), 256)
+    for lo in range(0, cells, 256):
+        at = pl.ds(lo, 256)
         back = jnp.dot(mix[...], grad[:, :, at].reshape(-1, 256), preferred_element_type=F32)
         f = [fields[j, :, at].astype(F32) for j in range(inputs)]
         for c in range(2 * n):
@@ -177,9 +178,6 @@
                 for r in range(8, rows, 8):
                     tile = tile + prod[r : r + 8]
                 sums[c, j] += tile
-        return 0
-
-    lax.fori_loop(0, cells // 256, lanes, 0)
 
 
 def row_inverse(refs, chan, row_inv):
@@ -360,7 +358,7 @@
 
 
 def spaced(fill):
-    return [run for f in fill for run in [f] + [None] * (CHUNKS - 1)]
+    return [None, *fill]
 
 
 def run_next(fill, source):
@@ -379,12 +377,11 @@
             up, down = part[hops - t], part[t + 1]
             if t:
                 up, down = add_pairs(up, got[p][1], down, got[p][2], tokens)
-            else:
-                up, down = hold(up, *tokens), hold(down, *tokens)
+                tokens = []
             below = lax.ppermute(up, "blk", [(z, z + 1) for z in range(t + 1)])
             above = lax.ppermute(down, "blk", [(blocks - 1 - z, blocks - 2 - z) for z in range(t + 1)])
             got[p] = (part[0], below, above)
-            tokens = run_next(fill, up)
+            tokens = tokens + run_next(fill, up)
     return got
 
 
@@ -526,6 +523,12 @@
 
         return run
 
+    def together(*runs):
+        def run(source):
+            return [r(source) for r in runs]
+
+        return run
+
     locals_ = [None]
 
     def local_piece(first, count):
@@ -565,11 +568,12 @@
         return ((samples, piece, n, width), BF, (samples, 1, n, width), lambda i, *_: (0, i, 0, 0))
 
     mix_flops = 16 * samples * piece * chans * half * freqs
-    count = math.gcd(chans, 4)
+    count = math.gcd(chans, 2)
     slope_fill = [slope_piece(i, count) for i in range(0, chans, count)]
+    turns = CHUNKS * (blocks - 1) - 2
     field_modes = []
 
-    arrivals = to_modes(chain_sums(shares, spaced(slope_fill[:-1])), samples)
+    arrivals = to_modes(chain_sums(shares, spaced(slope_fill[:turns])), samples)
     parts = []
     for part in range(CHUNKS):
         xs = arrivals[part][1]
@@ -591,9 +595,13 @@
     count = -(-steps // 2)
     fill = [local_piece(i, min(count, steps - i)) for i in range(0, steps, count)]
     below, above = [], []
-    chain_gather(out_modes, blocks, below, above, fill)
-    for run in fill:
-        run(out_modes)
+    later = slope_fill[turns:]
+    fill = [together(a, *later[i : i + 1]) for i, a in enumerate(fill)]
+    fill.append(together(*later[len(fill) : len(fill) + 1]))
+    later = later[len(fill) :]
+    tokens = chain_gather(out_modes, blocks, below, above, fill)
+    while fill:
+        tokens = tokens + run_next(fill, out_modes)
     local = locals_[0]
 
     grad_z, *shares = call(
@@ -611,6 +619,7 @@
         [((chans, rows, cells), BF, (bunch, rows, cells), lambda i, *_: (i, 0, 0)), *part_outs(bunch)],
         2 * matrix,
         3 * chans * rows * cells,
+        tokens=tokens,
         vmem=60 * 1024 * 1024,
     )
     shares = by_part(shares)
@@ -631,6 +640,7 @@
                     (lifted, (chans, group_rows, cells), at),
                     (lifted_other, (chans, group_rows, cells), at),
                     (grad_z, (chans, group_rows, cells), at),
+                    *[whole(a) for a in (*terms[-1:], *local_sums[-1:])],
                 ],
                 [
                     (
@@ -652,11 +662,11 @@
         return run
 
     steps = rows // group_rows
-    count = -(-steps // 4)
+    count = -(-steps // 8)
     back_fill = [back_piece(i, min(count, steps - i)) for i in range(0, steps, count)]
     grad_modes, grad_others = [], []
 
-    arrivals = to_modes(chain_sums(shares, spaced(back_fill[:-1])), samples)
+    arrivals = to_modes(chain_sums(shares, spaced([together(*back_fill[:3]), *back_fill[3 : turns + 2]])), samples)
     parts = []
     for part in range(CHUNKS):
         gs = arrivals[part][1]
@@ -730,21 +740,16 @@
     def pair_piece(t):
         return lambda source: pairs(([(0, back_modes)] if t == 0 else []) + arrived(t), [source])
 
-    def together(*runs):
-        def run(source):
-            return [r(source) for r in runs]
-
-        return run
-
     fill = [
-        together(*[weight_piece(part) for part in range(CHUNKS)], *slope_fill[-1:]),
-        together(*back_fill[-1:], pair_piece(0)),
+        together(*[weight_piece(part) for part in range(CHUNKS)], *later),
+        together(*back_fill[turns + 2 :]),
+        together(*[pair_piece(t) for t in range(min(2, blocks - 2))]),
     ]
-    fill += [pair_piece(t) for t in range(1, blocks - 2)]
+    fill += [pair_piece(t) for t in range(2, blocks - 2)]
     tokens = chain_gather(back_modes, blocks, below, above, fill)
     while fill:
         tokens = tokens + run_next(fill, back_modes)
-    term = sum(terms).reshape(2 * chans, group_rows, chans, group_rows)
+    term = terms[-1].reshape(2 * chans, group_rows, chans, group_rows)
     term = jnp.sum(term * jnp.eye(group_rows, dtype=F32)[None, :, None, :], axis=(1, 3))
     own_first = jnp.stack([term[:chans], term[chans:]])
     ordered = jnp.where(core == 0, own_first, own_first[::-1]).reshape(2 * chans, chans)
@@ -753,7 +758,7 @@
     pairs(arrived(blocks - 2), [ordered, *tokens])
     spectral_grad = gradient[0]
     lift_own = jnp.sum(sum(sums), axis=(2, 3)).T
-    lift_local = jnp.sum(sum(local_sums), axis=(2, 3)).T
+    lift_local = jnp.sum(local_sums[-1], axis=(2, 3)).T
     lift_own = jnp.concatenate([lift_own + lift_local[:, :chans], lift_local[:, chans:]], 1) * norm_scale
     packed = all_sum(jnp.concatenate([ordered.reshape(-1), lift_own.reshape(-1)]), ("dp", "blk"))
     local_grad = packed[: ordered.size].reshape(ordered.shape)

time: 486 us -> 480 us (0.988)
  local copies, waits for them, and re-layouts: 62.7 us -> 43.7 us
  Pallas kernels: 210 us -> 218 us
    unnamed x180 -> x148, local copies, waits for them, and re-layouts: 46 us -> 26.7 us
    ppermute x6, waiting for transfers between devices: 46.6 us -> 31.2 us  [chain_gather(): lax.ppermute(down, 'blk', [(blocks - 1 - z, blocks - 2 - z) for z in rang...]
    pallas_call x29 -> x37, Pallas kernels: 210 us -> 218 us  [call(): pl.pallas_call(kernel, grid_spec=pltpu.PrefetchScalarGridSpec(num_scalar_...]
    ppermute x12, waiting for transfers between devices: 1.49 us -> 7.2 us  [chain_sums(): below = lax.ppermute(up, 'blk', [(z, z + 1) for z in range(t + 1)])]
  transfers between devices with their start and end apart: 72 -> 72, of which waited for: 21 -> 27; matrix products, arithmetic and copies ran while one was open for 8% -> 6% of each run, Pallas kernels for 35% -> 35%
where the time goes in v5:
time: 480 us; the launch traced here: 471 us
  Pallas kernels  218 us (45%)
  starting transfers between devices  129 us (27%)
  waiting for transfers between devices  69.4 us (14%)
  local copies, waits for them, and re-layouts  43.7 us (9%)
  other arithmetic  9.15 us (2%)
    pallas_call x37, Pallas kernels, call(): pl.pallas_call(kernel, grid_spec=pltpu.PrefetchScalarGridSpec(num_scalar_...  218 us
    ppermute x12, starting transfers between devices, chain_sums(): below = lax.ppermute(up, 'blk', [(z, z + 1) for z in range(t + 1)])  48 us
    ppermute x24, starting transfers between devices, swap_samples(): lax.ppermute(pieces[j], 'dp', [(i, i ^ j) for i in range(n)])  31.5 us
    ppermute x6, waiting for transfers between devices, chain_gather(): lax.ppermute(down, 'blk', [(blocks - 1 - z, blocks - 2 - z) for z in rang...  31.2 us
    unnamed x148, local copies, waits for them, and re-layouts  26.7 us
    ppermute x6, starting transfers between devices, chain_gather(): lax.ppermute(up, 'blk', [(z, z + 1) for z in range(t, blocks - 1)])  17.6 us
    ppermute x12, starting transfers between devices, chain_sums(): lax.ppermute(down, 'blk', [(blocks - 1 - z, blocks - 2 - z) for z in rang...  13.4 us
    ppermute x24, waiting for transfers between devices, swap_samples(): lax.ppermute(pieces[j], 'dp', [(i, i ^ j) for i in range(n)])  11.9 us
  transfers between devices with their start and end apart: 72, of which 27 were waited for; matrix products, arithmetic and copies ran while one was open for 6% of the time, Pallas kernels for 35%

profile of v5, /device:TPU:0, one launch (start us, length us, event | category | flops | bytes accessed | tf_op | source)
XLA Modules:
  0.0 471.1 jit_solution(4772291868366523786)
XLA Ops:
  2.7 13.1 %shard_map.103 = (bf16[16,256,1024]{2,1,0:T(8,128)(2,1)}, bf16[16,32,512]{2,1,0:T(8,128)(2,1)S(1)}, bf16[16,32,512]{2,1,0:T(8,128)(2,1)}, bf16[16,32,512]{2,1,0:...) custom-call(s32[2]{0:T(128)S(1)} %pad_add_fusion.refs_0_, ...), custom_call_target="tpu_custom_call" | custom-call | flops 6442450944 | bytes 19398912 | tf_op jit(solution)/shard_map/pallas_call | solution.py:317
  19.4 5.3 %collective-permute-start.1 = (bf16[16,32,512]{2,1,0:T(8,128)(2,1)}, bf16[16,32,512]{2,1,0:T(8,128)(2,1)}, u32[]{:S(2)}, u32[]{:S(2)}) collective-permute-start(bf16[16,32,512]{2,1,0:T(8,128)(2,1)} %get-tuple-element.90.refs_2_), channel_id=1, source_target_pairs={{0,8},{1,9},{2,10},{3,11},{4,12},{5,13},{6,14},{7,15}} | collective-permute-start | bytes 1572872 | tf_op jit(solution)/shard_map/ppermute | solution.py:381
  31.5 5.8 %shard_map.104 = (bf16[4,16,4,64,512]{4,3,2,1,0:T(8,128)(2,1)}, f32[8,128]{1,0:T(8,128)S(1)}) custom-call(f32[4,16]{1,0:T(4,128)S(1)} %get-tuple-element.221.refs_1_.refs_0_, bf16[4,256,1024]{2,1,0:T(8,128)(2,1)S(1)} %bitcast.88, bf16[1024,512]{1,0:T(8,128)(2,1)S(1)} %copy-done.2, bf16[512,256]{1,0:T(8,128)(2,1)S(1)} %get-tuple-element.179.refs_3_.refs_4_, ...), custom_call_target="tpu_custom_call" | custom-call | flops 3221225472 | bytes 5509376 | tf_op jit(solution)/shard_map/pallas_call | solution.py:317
  38.7 3.6 collective-permute-start.3
  43.5 5.8 %shard_map.106 = (bf16[4,16,4,64,512]{4,3,2,1,0:T(8,128)(2,1)}, f32[8,128]{1,0:T(8,128)S(1)}) custom-call(f32[4,16]{1,0:T(4,128)S(1)} %get-tuple-element.221.refs_1_.refs_0_, bf16[4,256,1024]{2,1,0:T(8,128)(2,1)S(1)} %bitcast.89, bf16[1024,512]{1,0:T(8,128)(2,1)S(1)} %copy-done.2, ...), custom_call_target="tpu_custom_call", output_to_operand_aliasing={{0}: (5, {})} | custom-call | flops 3221225472 | bytes 5509376 | tf_op jit(solution)/shard_map/pallas_call | solution.py:317
  50.7 5.5 %collective-permute-start.12 = (bf16[16,32,512]{2,1,0:T(8,128)(2,1)S(1)}, bf16[16,32,512]{2,1,0:T(8,128)(2,1)S(1)}, u32[]{:S(2)}, u32[]{:S(2)}) collective-permute-start(bf16[16,32,512]{2,1,0:T(8,128)(2,1)S(1)} %get-tuple-element.99.refs_4_), channel_id=1, source_target_pairs={{0,8},{8,16},{1,9},{9,17},{2,10},{10,18},{3,11},{11,19},{4,12},{12... | collective-permute-start | bytes 1572872 | tf_op jit(solution)/shard_map/ppermute | solution.py:381
  57.0 5.8 %shard_map.108 = (bf16[4,16,4,64,512]{4,3,2,1,0:T(8,128)(2,1)}, f32[8,128]{1,0:T(8,128)S(1)}) custom-call(f32[4,16]{1,0:T(4,128)S(1)} %get-tuple-element.221.refs_1_.refs_0_, bf16[4,256,1024]{2,1,0:T(8,128)(2,1)S(1)} %bitcast.90, bf16[1024,512]{1,0:T(8,128)(2,1)S(1)} %copy-done.2, ...), custom_call_target="tpu_custom_call", output_to_operand_aliasing={{0}: (5, {})} | custom-call | flops 3221225472 | bytes 5509376 | tf_op jit(solution)/shard_map/pallas_call | solution.py:317
  64.5 5.1 %collective-permute-start.7 = (bf16[16,32,512]{2,0,1:T(8,128)(2,1)S(1)}, bf16[16,32,512]{2,0,1:T(8,128)(2,1)S(1)}, u32[]{:S(2)}, u32[]{:S(2)}) collective-permute-start(bf16[16,32,512]{2,0,1:T(8,128)(2,1)S(1)} %copy.116), channel_id=1, source_target_pairs={{0,8},{8,16},{16,24},{1,9},{9,17},{17,25},{2,10},{10,18},{18,26},{... | collective-permute-start | bytes 1572872 | tf_op jit(solution)/shard_map/ppermute | solution.py:381
  71.4 5.8 %shard_map.110 = (bf16[4,16,4,64,512]{4,3,2,1,0:T(8,128)(2,1)}, f32[8,128]{1,0:T(8,128)S(1)}) custom-call(f32[4,16]{1,0:T(4,128)S(1)} %get-tuple-element.221.refs_1_.refs_0_, bf16[4,256,1024]{2,1,0:T(8,128)(2,1)S(1)} %bitcast.91, bf16[1024,512]{1,0:T(8,128)(2,1)S(1)} %copy-done.2, ...), custom_call_target="tpu_custom_call", output_to_operand_aliasing={{0}: (5, {})} | custom-call | flops 3221225472 | bytes 5509376 | tf_op jit(solution)/shard_map/pallas_call | solution.py:317
  78.9 5.2 %collective-permute-start.14 = (bf16[16,32,512]{2,0,1:T(8,128)(2,1)S(1)}, bf16[16,32,512]{2,0,1:T(8,128)(2,1)S(1)}, u32[]{:S(2)}, u32[]{:S(2)}) collective-permute-start(bf16[16,32,512]{2,0,1:T(8,128)(2,1)S(1)} %copy.119), channel_id=1, source_target_pairs={{0,8},{8,16},{16,24},{1,9},{9,17},{17,25},{2,10},{10,18},{18,26},{... | collective-permute-start | bytes 1572872 | tf_op jit(solution)/shard_map/ppermute | solution.py:381
  89.3 4.1 collective-permute-done.14
  101.9 7.6 %shard_map.112 = (bf16[4,8,16,512]{3,2,1,0:T(8,128)(2,1)S(1)}, bf16[4,8,16,512]{3,2,1,0:T(8,128)(2,1)S(1)}) custom-call(s32[1]{0:T(128)} %bitcast.refs_0_, bf16[2,16,16,32,256]{4,3,2,1,0:T(8,128)(2,1)} %refs_2_.16, bf16[2,16,16,32,256]{4,3,2,1,0:T(8,128)(2,1)} %refs_2_.16, bf16[8,16,512]{2,1,0:T(8,128)(2,1)S(1)} %get-tuple-element.211.refs_3_.refs_2_, ...), custom_call_target="tpu_custom_call" | custom-call | flops 33554432 | bytes 5767168 | tf_op jit(solution)/shard_map/pallas_call | solution.py:317
  115.1 7.7 %shard_map.114 = (bf16[4,8,16,512]{3,2,1,0:T(8,128)(2,1)S(1)}, bf16[4,8,16,512]{3,2,1,0:T(8,128)(2,1)S(1)}) custom-call(s32[1]{0:T(128)} %bitcast.refs_0_, bf16[2,16,16,32,256]{4,3,2,1,0:T(8,128)(2,1)} %refs_2_.16, bf16[2,16,16,32,256]{4,3,2,1,0:T(8,128)(2,1)} %refs_2_.16, bf16[8,16,512]{2,1,0:T(8,128)(2,1)S(1)} %get-tuple-element.201.refs_3_.refs_2_, ...), custom_call_target="tpu_custom_call" | custom-call | flops 33554432 | bytes 5767168 | tf_op jit(solution)/shard_map/pallas_call | solution.py:317
  140.0 4.6 collective-permute-start.27
  152.9 5.8 %shard_map.116 = (bf16[4,16,4,64,512]{4,3,2,1,0:T(8,128)(2,1)}, f32[8,128]{1,0:T(8,128)S(1)}) custom-call(f32[4,16]{1,0:T(4,128)S(1)} %get-tuple-element.221.refs_1_.refs_0_, bf16[4,256,1024]{2,1,0:T(8,128)(2,1)S(1)} %bitcast.92, bf16[1024,512]{1,0:T(8,128)(2,1)S(1)} %copy-done.2, bf16[512,256]{1,0:T(8,128)(2,1)S(1)} %copy-done.5, ...), custom_call_target="tpu_custom_call", output_to_operand_aliasing={{0}: (5, {})} | custom-call | flops 3221225472 | bytes 5509376 | tf_op jit(solution)/shard_map/pallas_call | solution.py:317
  158.7 10.3 %shard_map.115 = (f32[16,256,1024]{2,1,0:T(8,128)}, f32[8,128]{1,0:T(8,128)S(1)}) custom-call(bf16[256,512]{1,0:T(8,128)(2,1)S(1)} %bitcast.110, bf16[16,256,1024]{2,1,0:T(8,128)(2,1)} %get-tuple-element.86.refs_1_.refs_3_, bf16[16,256,1024]{2,1,0:T(8,128)(2,1)} %collective-permute-done.refs_2_.refs_4_, bf16[16,64,512]{2,1,0:T(8,128)(2,1)} %bitcast.16.refs_3_.refs_4_.refs_6_), custom_call_target="tpu_custom_call" | custom-call | flops 2147483648 | bytes 18907136 | tf_op jit(solution)/shard_map/pallas_call | solution.py:317
  173.8 10.4 %shard_map.118 = (f32[16,256,1024]{2,1,0:T(8,128)}, f32[8,128]{1,0:T(8,128)S(1)}) custom-call(bf16[256,512]{1,0:T(8,128)(2,1)S(1)} %bitcast.111, bf16[16,256,1024]{2,1,0:T(8,128)(2,1)} %get-tuple-element.86.refs_1_.refs_3_, bf16[16,256,1024]{2,1,0:T(8,128)(2,1)} %collective-permute-done.refs_2_.refs_4_, ...), custom_call_target="tpu_custom_call", output_to_operand_aliasing={{0}: (4, {})} | custom-call | flops 2147483648 | bytes 18907136 | tf_op jit(solution)/shard_map/pallas_call | solution.py:317
  184.1 5.8 %shard_map.119 = (bf16[4,16,4,64,512]{4,3,2,1,0:T(8,128)(2,1)}, f32[8,128]{1,0:T(8,128)S(1)}) custom-call(f32[4,16]{1,0:T(4,128)S(1)} %get-tuple-element.221.refs_1_.refs_0_, bf16[4,256,1024]{2,1,0:T(8,128)(2,1)S(1)} %bitcast.93, bf16[1024,512]{1,0:T(8,128)(2,1)S(1)} %copy-done.2, bf16[512,256]{1,0:T(8,128)(2,1)S(1)} %copy-done.6, ...), custom_call_target="tpu_custom_call", output_to_operand_aliasing={{0}: (5, {})} | custom-call | flops 3221225472 | bytes 5509376 | tf_op jit(solution)/shard_map/pallas_call | solution.py:317
  190.5 5.0 %collective-permute-done.31.refs_0_ = bf16[16,64,512]{2,1,0:T(8,128)(2,1)} collective-permute-done((bf16[16,64,512]{2,1,0:T(8,128)(2,1)}, bf16[16,64,512]{2,1,0:T(8,128)(2,1)}, u32[]{:S(2)}, u32[]{:S(2)}) %collective-permute-start.31) | collective-permute-done | bytes 1048608 | tf_op jit(solution)/shard_map/ppermute | solution.py:395
  201.7 5.8 %shard_map.123 = (bf16[4,16,4,64,512]{4,3,2,1,0:T(8,128)(2,1)}, f32[8,128]{1,0:T(8,128)S(1)}) custom-call(f32[4,16]{1,0:T(4,128)S(1)} %get-tuple-element.221.refs_1_.refs_0_, bf16[4,256,1024]{2,1,0:T(8,128)(2,1)S(1)} %bitcast.94, bf16[1024,512]{1,0:T(8,128)(2,1)S(1)} %copy-done.2, bf16[512,256]{1,0:T(8,128)(2,1)S(1)} %copy-done.7, ...), custom_call_target="tpu_custom_call", output_to_operand_aliasing={{0}: (5, {})} | custom-call | flops 3221225472 | bytes 5509376 | tf_op jit(solution)/shard_map/pallas_call | solution.py:317
  208.0 11.8 %collective-permute-done.32.refs_12_ = bf16[16,64,512]{2,1,0:T(8,128)(2,1)} collective-permute-done((bf16[16,64,512]{2,1,0:T(8,128)(2,1)}, bf16[16,64,512]{2,1,0:T(8,128)(2,1)}, u32[]{:S(2)}, u32[]{:S(2)}) %collective-permute-start.32) | collective-permute-done | bytes 1048608 | tf_op jit(solution)/shard_map/ppermute | solution.py:395
  219.9 27.6 %shard_map.124 = (bf16[16,256,1024]{2,1,0:T(8,128)(2,1)}, bf16[16,32,512]{2,1,0:T(8,128)(2,1)}, bf16[16,32,512]{2,1,0:T(8,128)(2,1)}, bf16[16,32,512]{2,1,0:T(8,...) custom-call(f32[16,256,1024]{2,1,0:T(8,128)} %get-tuple-element.118., ...), custom_call_target="tpu_custom_call" | custom-call | flops 12884901888 | bytes 55574528 | tf_op jit(solution)/shard_map/pallas_call | solution.py:317
  252.9 5.1 %shard_map.125 = (f32[2,256,256]{2,1,0:T(8,128)S(1)}, f32[32,4,8,128]{3,2,1,0:T(8,128)S(1)}) custom-call(f32[4,32]{1,0:T(4,128)S(1)} %pad_maximum_fusion.4.refs_0_, bf16[512,256]{1,0:T(8,128)(2,1)S(1)} %mul.58.refs_1_, bf16[4,256,1024]{2,1,0:T(8,128)(2,1)S(1)} %bitcast.95, bf16[16,256,1024]{2,1,0:T(8,128)(2,1)} %get-tuple-element.86.refs_1_.refs_3_, ...), custom_call_target="tpu_custom_call" | custom-call | flops 1073741824 | bytes 6029824 | tf_op jit(solution)/shard_map/pallas_call | solution.py:317
  258.0 5.1 %shard_map.126 = (f32[2,256,256]{2,1,0:T(8,128)S(1)}, f32[32,4,8,128]{3,2,1,0:T(8,128)S(1)}) custom-call(f32[4,32]{1,0:T(4,128)S(1)} %pad_maximum_fusion.4.refs_0_, bf16[512,256]{1,0:T(8,128)(2,1)S(1)} %mul.58.refs_1_, bf16[4,256,1024]{2,1,0:T(8,128)(2,1)S(1)} %bitcast.96, bf16[16,256,1024]{2,1,0:T(8,128)(2,1)} %get-tuple-element.86.refs_1_.refs_3_, ...), custom_call_target="tpu_custom_call" | custom-call | flops 1073741824 | bytes 8126976 | tf_op jit(solution)/shard_map/pallas_call | solution.py:317
  263.2 5.2 %shard_map.127 = (f32[2,256,256]{2,1,0:T(8,128)S(1)}, f32[32,4,8,128]{3,2,1,0:T(8,128)S(1)}) custom-call(f32[4,32]{1,0:T(4,128)S(1)} %pad_maximum_fusion.4.refs_0_, bf16[512,256]{1,0:T(8,128)(2,1)S(1)} %mul.58.refs_1_, bf16[4,256,1024]{2,1,0:T(8,128)(2,1)S(1)} %bitcast.97, bf16[16,256,1024]{2,1,0:T(8,128)(2,1)} %get-tuple-element.86.refs_1_.refs_3_, ...), custom_call_target="tpu_custom_call" | custom-call | flops 1073741824 | bytes 8126976 | tf_op jit(solution)/shard_map/pallas_call | solution.py:317
  270.7 5.2 %shard_map.129 = (f32[2,256,256]{2,1,0:T(8,128)S(1)}, f32[32,4,8,128]{3,2,1,0:T(8,128)S(1)}) custom-call(f32[4,32]{1,0:T(4,128)S(1)} %pad_maximum_fusion.4.refs_0_, bf16[512,256]{1,0:T(8,128)(2,1)S(1)} %mul.58.refs_1_, bf16[4,256,1024]{2,1,0:T(8,128)(2,1)S(1)} %bitcast.98, bf16[16,256,1024]{2,1,0:T(8,128)(2,1)} %get-tuple-element.86.refs_1_.refs_3_, ...), custom_call_target="tpu_custom_call" | custom-call | flops 1073741824 | bytes 8126976 | tf_op jit(solution)/shard_map/pallas_call | solution.py:317
  276.2 6.8 %collective-permute-start.37 = (bf16[16,32,512]{2,1,0:T(8,128)(2,1)S(1)}, bf16[16,32,512]{2,1,0:T(8,128)(2,1)S(1)}, u32[]{:S(2)}, u32[]{:S(2)}) collective-permute-start(bf16[16,32,512]{2,1,0:T(8,128)(2,1)S(1)} %get-tuple-element.140.refs_8_), channel_id=1, source_target_pairs={{0,8},{8,16},{1,9},{9,17},{2,10},{10,18},{3,11},{11,19},{4,12},{12... | collective-permute-start | bytes 1572872 | tf_op jit(solution)/shard_map/ppermute | solution.py:381
  283.9 5.2 %shard_map.131 = (f32[2,256,256]{2,1,0:T(8,128)S(1)}, f32[32,4,8,128]{3,2,1,0:T(8,128)S(1)}) custom-call(f32[4,32]{1,0:T(4,128)S(1)} %pad_maximum_fusion.4.refs_0_, bf16[512,256]{1,0:T(8,128)(2,1)S(1)} %mul.58.refs_1_, bf16[4,256,1024]{2,1,0:T(8,128)(2,1)S(1)} %bitcast.99, bf16[16,256,1024]{2,1,0:T(8,128)(2,1)} %get-tuple-element.86.refs_1_.refs_3_, ...), custom_call_target="tpu_custom_call" | custom-call | flops 1073741824 | bytes 8126976 | tf_op jit(solution)/shard_map/pallas_call | solution.py:317
  289.5 5.2 %shard_map.133 = (f32[2,256,256]{2,1,0:T(8,128)S(1)}, f32[32,4,8,128]{3,2,1,0:T(8,128)S(1)}) custom-call(f32[4,32]{1,0:T(4,128)S(1)} %pad_maximum_fusion.4.refs_0_, bf16[512,256]{1,0:T(8,128)(2,1)S(1)} %mul.58.refs_1_, bf16[4,256,1024]{2,1,0:T(8,128)(2,1)S(1)} %bitcast.100, bf16[16,256,1024]{2,1,0:T(8,128)(2,1)} %get-tuple-element.86.refs_1_.refs_3_, ...), custom_call_target="tpu_custom_call" | custom-call | flops 1073741824 | bytes 8126976 | tf_op jit(solution)/shard_map/pallas_call | solution.py:317
  296.1 5.1 %collective-permute-start.41 = (bf16[16,32,512]{2,0,1:T(8,128)(2,1)S(1)}, bf16[16,32,512]{2,0,1:T(8,128)(2,1)S(1)}, u32[]{:S(2)}, u32[]{:S(2)}) collective-permute-start(bf16[16,32,512]{2,0,1:T(8,128)(2,1)S(1)} %copy.127), channel_id=1, source_target_pairs={{0,8},{8,16},{16,24},{1,9},{9,17},{17,25},{2,10},{10,18},{18,26},{... | collective-permute-start | bytes 1572872 | tf_op jit(solution)/shard_map/ppermute | solution.py:381
  303.2 5.2 %collective-permute-start.47 = (bf16[16,32,512]{2,0,1:T(8,128)(2,1)S(1)}, bf16[16,32,512]{2,0,1:T(8,128)(2,1)S(1)}, u32[]{:S(2)}, u32[]{:S(2)}) collective-permute-start(bf16[16,32,512]{2,0,1:T(8,128)(2,1)S(1)} %copy.130), channel_id=1, source_target_pairs={{0,8},{8,16},{16,24},{1,9},{9,17},{17,25},{2,10},{10,18},{18,26},{... | collective-permute-start | bytes 1572872 | tf_op jit(solution)/shard_map/ppermute | solution.py:381
  313.0 5.5 %collective-permute-done.42 = bf16[16,32,512]{2,0,1:T(8,128)(2,1)S(1)} collective-permute-done((bf16[16,32,512]{2,0,1:T(8,128)(2,1)S(1)}, bf16[16,32,512]{2,0,1:T(8,128)(2,1)S(1)}, u32[]{:S(2)}, u32[]{:S(2)}) %collective-permute-start.42) | collective-permute-done | bytes 524320 | tf_op jit(solution)/shard_map/ppermute | solution.py:382
  331.6 8.4 %shard_map.136 = bf16[4,8,16,512]{3,2,1,0:T(8,128)(2,1)S(1)} custom-call(s32[1]{0:T(128)} %bitcast.refs_0_, bf16[2,16,16,32,256]{4,3,2,1,0:T(8,128)(2,1)} %refs_2_.16, bf16[2,16,16,32,256]{4,3,2,1,0:T(8,128)(2,1)} %refs_2_.16, bf16[4,8,16,512]{3,2,1,0:T(8,128)(2,1)S(1)} %collective-permute-done.46.refs_3_.refs_1_, ...), custom_call_target="tpu_custom_call" | custom-call | flops 33554432 | bytes 5767168 | tf_op jit(solution)/shard_map/pallas_call | solution.py:317
  340.1 8.5 %shard_map.135 = bf16[4,8,16,512]{3,2,1,0:T(8,128)(2,1)S(1)} custom-call(s32[1]{0:T(128)} %bitcast.refs_0_, bf16[2,16,16,32,256]{4,3,2,1,0:T(8,128)(2,1)} %refs_2_.16, bf16[2,16,16,32,256]{4,3,2,1,0:T(8,128)(2,1)} %refs_2_.16, bf16[4,8,16,512]{3,2,1,0:T(8,128)(2,1)S(1)} %collective-permute-done.52.refs_3_.refs_1_, ...), custom_call_target="tpu_custom_call" | custom-call | flops 33554432 | bytes 5767168 | tf_op jit(solution)/shard_map/pallas_call | solution.py:317
  366.1 5.7 %collective-permute-start.59 = (bf16[16,64,512]{2,1,0:T(8,128)(2,1)S(1)}, bf16[16,64,512]{2,1,0:T(8,128)(2,1)}, u32[]{:S(2)}, u32[]{:S(2)}) collective-permute-start(bf16[16,64,512]{2,1,0:T(8,128)(2,1)S(1)} %bitcast.105), channel_id=1, source_target_pairs={{0,8},{8,16},{16,24},{1,9},{9,17},{17,25},{2,10},{10,18},{18,26},{... | collective-permute-start | bytes 3145736 | tf_op jit(solution)/shard_map/ppermute | solution.py:394
  371.9 6.4 %shard_map.137 = (bf16[2,16,16,32,256]{4,3,2,1,0:T(8,128)(2,1)}, f32[8,128]{1,0:T(8,128)S(1)}) custom-call(s32[1]{0:T(128)} %bitcast.refs_0_, bf16[4,8,16,512]{3,2,1,0:T(8,128)(2,1)S(1)} %collective-permute-done.52.refs_3_.refs_1_, bf16[8,16,512]{2,1,0:T(8,128)(2,1)S(1)} %copy-done.33, bf16[8,16,512]{2,1,0:T(8,128)(2,1)S(1)} %copy-done.39, ...), custom_call_target="tpu_custom_call" | custom-call | flops 33554432 | bytes 5799936 | tf_op jit(solution)/shard_map/pallas_call | solution.py:317
  378.4 7.2 %shard_map.138 = (bf16[2,16,16,32,256]{4,3,2,1,0:T(8,128)(2,1)}, f32[8,128]{1,0:T(8,128)S(1)}) custom-call(s32[1]{0:T(128)} %bitcast.refs_0_, bf16[4,8,16,512]{3,2,1,0:T(8,128)(2,1)S(1)} %collective-permute-done.46.refs_3_.refs_1_, bf16[8,16,512]{2,1,0:T(8,128)(2,1)S(1)} %get-tuple-element.201.refs_3_.refs_2_, ...), custom_call_target="tpu_custom_call", output_to_operand_aliasing={{0}: (11, {})} | custom-call | flops 33554432 | bytes 5799936 | tf_op jit(solution)/shard_map/pallas_call | solution.py:317
  385.6 5.8 %shard_map.139 = (bf16[4,16,4,64,512]{4,3,2,1,0:T(8,128)(2,1)}, f32[8,128]{1,0:T(8,128)S(1)}) custom-call(f32[4,16]{1,0:T(4,128)S(1)} %get-tuple-element.221.refs_1_.refs_0_, bf16[4,256,1024]{2,1,0:T(8,128)(2,1)S(1)} %bitcast.101, bf16[1024,512]{1,0:T(8,128)(2,1)S(1)} %copy-done.3, bf16[512,256]{1,0:T(8,128)(2,1)S(1)} %copy-done.8, ...), custom_call_target="tpu_custom_call", output_to_operand_aliasing={{0}: (5, {})} | custom-call | flops 3221225472 | bytes 5509376 | tf_op jit(solution)/shard_map/pallas_call | solution.py:317
  398.0 5.1 %shard_map.141 = (f32[2,256,256]{2,1,0:T(8,128)S(1)}, f32[32,4,8,128]{3,2,1,0:T(8,128)S(1)}) custom-call(f32[4,32]{1,0:T(4,128)S(1)} %pad_maximum_fusion.4.refs_0_, bf16[512,256]{1,0:T(8,128)(2,1)S(1)} %mul.58.refs_1_, bf16[4,256,1024]{2,1,0:T(8,128)(2,1)S(1)} %bitcast.102, bf16[16,256,1024]{2,1,0:T(8,128)(2,1)} %get-tuple-element.86.refs_1_.refs_3_, ...), custom_call_target="tpu_custom_call" | custom-call | flops 1073741824 | bytes 8126976 | tf_op jit(solution)/shard_map/pallas_call | solution.py:317
  403.1 5.3 %shard_map.142 = (f32[2,256,256]{2,1,0:T(8,128)S(1)}, f32[32,4,8,128]{3,2,1,0:T(8,128)S(1)}) custom-call(f32[4,32]{1,0:T(4,128)S(1)} %pad_maximum_fusion.4.refs_0_, bf16[512,256]{1,0:T(8,128)(2,1)S(1)} %mul.58.refs_1_, bf16[4,256,1024]{2,1,0:T(8,128)(2,1)S(1)} %bitcast.103, bf16[16,256,1024]{2,1,0:T(8,128)(2,1)} %get-tuple-element.86.refs_1_.refs_3_, ...), custom_call_target="tpu_custom_call" | custom-call | flops 1073741824 | bytes 8126976 | tf_op jit(solution)/shard_map/pallas_call | solution.py:317
  410.0 9.5 %collective-permute-done.62.refs_0_ = bf16[16,64,512]{2,1,0:T(8,128)(2,1)} collective-permute-done((bf16[16,64,512]{2,1,0:T(8,128)(2,1)}, bf16[16,64,512]{2,1,0:T(8,128)(2,1)}, u32[]{:S(2)}, u32[]{:S(2)}) %collective-permute-start.62) | collective-permute-done | bytes 1048608 | tf_op jit(solution)/shard_map/ppermute | solution.py:395
  422.9 3.7 reshape.60
  429.7 5.4 %shard_map.147 = (f32[16,4,8,128]{3,2,1,0:T(8,128)S(1)}, f32[8,128]{1,0:T(8,128)S(1)}) custom-call(bf16[16,64,512]{2,1,0:T(8,128)(2,1)} %shard_map.144.refs_6_.refs_0_.refs_4_, bf16[16,64,512]{2,1,0:T(8,128)(2,1)} %shard_map.146.refs_1_, bf16[4,16,4,64,512]{4,3,2,1,0:T(8,128)(2,1)} %get-tuple-element.162.refs_3_.refs_4_.refs_5_.refs_2_, ...), custom_call_target="tpu_custom_call" | custom-call | flops 16777216 | bytes 10764288 | tf_op jit(solution)/shard_map/pallas_call | solution.py:317
  435.1 5.6 %shard_map.145 = (f32[16,4,8,128]{3,2,1,0:T(8,128)S(1)}, f32[8,128]{1,0:T(8,128)S(1)}) custom-call(bf16[16,64,512]{2,1,0:T(8,128)(2,1)S(1)} %bitcast.109, bf16[16,64,512]{2,1,0:T(8,128)(2,1)} %shard_map.140.refs_8_.refs_1_, bf16[16,64,512]{2,1,0:T(8,128)(2,1)S(1)} %copy-done.14, ...), custom_call_target="tpu_custom_call" | custom-call | flops 25165824 | bytes 16007168 | tf_op jit(solution)/shard_map/pallas_call | solution.py:317
  440.7 4.6 collective-permute-done.64.refs_1_
  445.3 5.2 %shard_map.148 = (f32[16,4,8,128]{3,2,1,0:T(8,128)S(1)}, f32[8,128]{1,0:T(8,128)}) custom-call(bf16[16,64,512]{2,1,0:T(8,128)(2,1)} %collective-permute-done.63.refs_0_, bf16[16,64,512]{2,1,0:T(8,128)(2,1)} %collective-permute-done.64.refs_1_, bf16[4,16,4,64,512]{4,3,2,1,0:T(8,128)(2,1)} %get-tuple-element.162.refs_3_.refs_4_.refs_5_.refs_2_, ...), custom_call_target="tpu_custom_call" | custom-call | flops 16777216 | bytes 10764288 | tf_op jit(solution)/shard_map/pallas_call | solution.py:317
  457.8 5.4 %collective-permute-start.69 = (f32[640]{0:T(1024)S(1)}, f32[640]{0:T(1024)S(1)}, u32[]{:S(2)}, u32[]{:S(2)}) collective-permute-start(f32[640]{0:T(1024)S(1)} %add_add_fusion.1), channel_id=1, source_target_pairs={{0,16},{8,24},{16,0},{24,8},{1,17},{9,25},{17,1},{25,9},{2,18},{10... | collective-permute-start | bytes 7688 | tf_op jit(solution)/shard_map/ppermute | solution.py:425
  464.8 3.8 collective-permute-done.70
  (355 shorter events, 151.9 us)
Async XLA Ops:
  19.0 139.8 %collective-permute-start = (bf16[16,256,1024]{2,1,0:T(8,128)(2,1)}, bf16[16,256,1024]{2,1,0:T(8,128)(2,1)}, u32[]{:S(2)}, u32[]{:S(2)}) collective-permute-start(bf16[16,256,1024]{2,1,0:T(8,128)(2,1)} %get-tuple-element.86.refs_1_.refs_3_), channel_id=1, source_target_pairs={{0,1},{1,0},{2,3},{3,2},{4,5},{5,4},{6,7},{7,6},{8,9},{9,8},{10,11... | collective-permute-start | bytes 25165832 | tf_op jit(solution)/shard_map/ppermute | solution.py:406
  19.4 17.8 %collective-permute-start.1 = (bf16[16,32,512]{2,1,0:T(8,128)(2,1)}, bf16[16,32,512]{2,1,0:T(8,128)(2,1)}, u32[]{:S(2)}, u32[]{:S(2)}) collective-permute-start(bf16[16,32,512]{2,1,0:T(8,128)(2,1)} %get-tuple-element.90.refs_2_), channel_id=1, source_target_pairs={{0,8},{1,9},{2,10},{3,11},{4,12},{5,13},{6,14},{7,15}} | collective-permute-start | bytes 1572872 | tf_op jit(solution)/shard_map/ppermute | solution.py:381
  24.7 12.6 %collective-permute-start.2 = (bf16[16,32,512]{2,1,0:T(8,128)(2,1)}, bf16[16,32,512]{2,1,0:T(8,128)(2,1)}, u32[]{:S(2)}, u32[]{:S(2)}) collective-permute-start(bf16[16,32,512]{2,1,0:T(8,128)(2,1)} %get-tuple-element.88.refs_0_), channel_id=1, source_target_pairs={{24,16},{25,17},{26,18},{27,19},{28,20},{29,21},{30,22},{31,23}} | collective-permute-start | bytes 1572872 | tf_op jit(solution)/shard_map/ppermute | solution.py:382
  26.2 23.1 %collective-permute-start.5 = (bf16[16,32,512]{2,1,0:T(8,128)(2,1)}, bf16[16,32,512]{2,1,0:T(8,128)(2,1)}, u32[]{:S(2)}, u32[]{:S(2)}) collective-permute-start(bf16[16,32,512]{2,1,0:T(8,128)(2,1)} %get-tuple-element.91.refs_4_.refs_2_), channel_id=1, source_target_pairs={{0,8},{1,9},{2,10},{3,11},{4,12},{5,13},{6,14},{7,15}} | collective-permute-start | bytes 1572872 | tf_op jit(solution)/shard_map/ppermute | solution.py:381
  28.3 21.0 %collective-permute-start.6 = (bf16[16,32,512]{2,1,0:T(8,128)(2,1)}, bf16[16,32,512]{2,1,0:T(8,128)(2,1)}, u32[]{:S(2)}, u32[]{:S(2)}) collective-permute-start(bf16[16,32,512]{2,1,0:T(8,128)(2,1)} %get-tuple-element.96.refs_0_), channel_id=1, source_target_pairs={{24,16},{25,17},{26,18},{27,19},{28,20},{29,21},{30,22},{31,23}} | collective-permute-start | bytes 1572872 | tf_op jit(solution)/shard_map/ppermute | solution.py:382
  38.7 24.0 %collective-permute-start.3 = (bf16[16,32,512]{2,1,0:T(8,128)(2,1)S(1)}, bf16[16,32,512]{2,1,0:T(8,128)(2,1)S(1)}, u32[]{:S(2)}, u32[]{:S(2)}) collective-permute-start(bf16[16,32,512]{2,1,0:T(8,128)(2,1)S(1)} %get-tuple-element.93.refs_4_), channel_id=1, source_target_pairs={{0,8},{8,16},{1,9},{9,17},{2,10},{10,18},{3,11},{11,19},{4,12},{12... | collective-permute-start | bytes 1572872 | tf_op jit(solution)/shard_map/ppermute | solution.py:381
  42.3 20.5 %collective-permute-start.4 = (bf16[16,32,512]{2,1,0:T(8,128)(2,1)S(1)}, bf16[16,32,512]{2,1,0:T(8,128)(2,1)S(1)}, u32[]{:S(2)}, u32[]{:S(2)}) collective-permute-start(bf16[16,32,512]{2,1,0:T(8,128)(2,1)S(1)} %get-tuple-element.94), channel_id=1, source_target_pairs={{24,16},{16,8},{25,17},{17,9},{26,18},{18,10},{27,19},{19,11},{28,... | collective-permute-start | bytes 1572872 | tf_op jit(solution)/shard_map/ppermute | solution.py:382
  50.7 26.5 %collective-permute-start.12 = (bf16[16,32,512]{2,1,0:T(8,128)(2,1)S(1)}, bf16[16,32,512]{2,1,0:T(8,128)(2,1)S(1)}, u32[]{:S(2)}, u32[]{:S(2)}) collective-permute-start(bf16[16,32,512]{2,1,0:T(8,128)(2,1)S(1)} %get-tuple-element.99.refs_4_), channel_id=1, source_target_pairs={{0,8},{8,16},{1,9},{9,17},{2,10},{10,18},{3,11},{11,19},{4,12},{12... | collective-permute-start | bytes 1572872 | tf_op jit(solution)/shard_map/ppermute | solution.py:381
  56.2 21.0 %collective-permute-start.13 = (bf16[16,32,512]{2,1,0:T(8,128)(2,1)S(1)}, bf16[16,32,512]{2,1,0:T(8,128)(2,1)S(1)}, u32[]{:S(2)}, u32[]{:S(2)}) collective-permute-start(bf16[16,32,512]{2,1,0:T(8,128)(2,1)S(1)} %get-tuple-element.105), channel_id=1, source_target_pairs={{24,16},{16,8},{25,17},{17,9},{26,18},{18,10},{27,19},{19,11},{28,... | collective-permute-start | bytes 1572872 | tf_op jit(solution)/shard_map/ppermute | solution.py:382
  64.5 21.3 %collective-permute-start.7 = (bf16[16,32,512]{2,0,1:T(8,128)(2,1)S(1)}, bf16[16,32,512]{2,0,1:T(8,128)(2,1)S(1)}, u32[]{:S(2)}, u32[]{:S(2)}) collective-permute-start(bf16[16,32,512]{2,0,1:T(8,128)(2,1)S(1)} %copy.116), channel_id=1, source_target_pairs={{0,8},{8,16},{16,24},{1,9},{9,17},{17,25},{2,10},{10,18},{18,26},{... | collective-permute-start | bytes 1572872 | tf_op jit(solution)/shard_map/ppermute | solution.py:381
  69.9 15.8 %collective-permute-start.8 = (bf16[16,32,512]{2,0,1:T(8,128)(2,1)S(1)}, bf16[16,32,512]{2,0,1:T(8,128)(2,1)S(1)}, u32[]{:S(2)}, u32[]{:S(2)}) collective-permute-start(bf16[16,32,512]{2,0,1:T(8,128)(2,1)S(1)} %copy.117), channel_id=1, source_target_pairs={{24,16},{16,8},{8,0},{25,17},{17,9},{9,1},{26,18},{18,10},{10,2},{... | collective-permute-start | bytes 1572872 | tf_op jit(solution)/shard_map/ppermute | solution.py:382
  78.9 14.4 %collective-permute-start.14 = (bf16[16,32,512]{2,0,1:T(8,128)(2,1)S(1)}, bf16[16,32,512]{2,0,1:T(8,128)(2,1)S(1)}, u32[]{:S(2)}, u32[]{:S(2)}) collective-permute-start(bf16[16,32,512]{2,0,1:T(8,128)(2,1)S(1)} %copy.119), channel_id=1, source_target_pairs={{0,8},{8,16},{16,24},{1,9},{9,17},{17,25},{2,10},{10,18},{18,26},{... | collective-permute-start | bytes 1572872 | tf_op jit(solution)/shard_map/ppermute | solution.py:381
  84.4 13.4 %collective-permute-start.15 = (bf16[16,32,512]{2,0,1:T(8,128)(2,1)S(1)}, bf16[16,32,512]{2,0,1:T(8,128)(2,1)S(1)}, u32[]{:S(2)}, u32[]{:S(2)}) collective-permute-start(bf16[16,32,512]{2,0,1:T(8,128)(2,1)S(1)} %copy.120), channel_id=1, source_target_pairs={{24,16},{16,8},{8,0},{25,17},{17,9},{9,1},{26,18},{18,10},{10,2},{... | collective-permute-start | bytes 1572872 | tf_op jit(solution)/shard_map/ppermute | solution.py:382
  86.2 13.6 %collective-permute-start.10 = (bf16[8,16,512]{2,1,0:T(8,128)(2,1)S(1)}, bf16[8,16,512]{2,1,0:T(8,128)(2,1)S(1)}, u32[]{:S(2)}, u32[]{:S(2)}) collective-permute-start(bf16[8,16,512]{2,1,0:T(8,128)(2,1)S(1)} %get-tuple-element.209), channel_id=1, source_target_pairs={{0,4},{2,6},{4,0},{6,2},{1,5},{3,7},{5,1},{7,3},{8,12},{10,14},{12... | collective-permute-start | bytes 393224 | tf_op jit(solution)/shard_map/ppermute | solution.py:402
  87.8 13.6 %collective-permute-start.11 = (bf16[8,16,512]{2,1,0:T(8,128)(2,1)S(1)}, bf16[8,16,512]{2,1,0:T(8,128)(2,1)S(1)}, u32[]{:S(2)}, u32[]{:S(2)}) collective-permute-start(bf16[8,16,512]{2,1,0:T(8,128)(2,1)S(1)} %get-tuple-element.208), channel_id=1, source_target_pairs={{0,6},{2,4},{4,2},{6,0},{1,7},{3,5},{5,3},{7,1},{8,14},{10,12},{12... | collective-permute-start | bytes 393224 | tf_op jit(solution)/shard_map/ppermute | solution.py:402
  98.3 12.9 %collective-permute-start.16 = (bf16[8,16,512]{2,1,0:T(8,128)(2,1)S(1)}, bf16[8,16,512]{2,1,0:T(8,128)(2,1)S(1)}, u32[]{:S(2)}, u32[]{:S(2)}) collective-permute-start(bf16[8,16,512]{2,1,0:T(8,128)(2,1)S(1)} %get-tuple-element.204), channel_id=1, source_target_pairs={{0,2},{2,0},{4,6},{6,4},{1,3},{3,1},{5,7},{7,5},{8,10},{10,8},{12,... | collective-permute-start | bytes 393224 | tf_op jit(solution)/shard_map/ppermute | solution.py:402
  99.9 11.3 %collective-permute-start.17 = (bf16[8,16,512]{2,1,0:T(8,128)(2,1)S(1)}, bf16[8,16,512]{2,1,0:T(8,128)(2,1)S(1)}, u32[]{:S(2)}, u32[]{:S(2)}) collective-permute-start(bf16[8,16,512]{2,1,0:T(8,128)(2,1)S(1)} %get-tuple-element.203), channel_id=1, source_target_pairs={{0,4},{2,6},{4,0},{6,2},{1,5},{3,7},{5,1},{7,3},{8,12},{10,14},{12... | collective-permute-start | bytes 393224 | tf_op jit(solution)/shard_map/ppermute | solution.py:402
  101.4 9.8 %collective-permute-start.18 = (bf16[8,16,512]{2,1,0:T(8,128)(2,1)S(1)}, bf16[8,16,512]{2,1,0:T(8,128)(2,1)}, u32[]{:S(2)}, u32[]{:S(2)}) collective-permute-start(bf16[8,16,512]{2,1,0:T(8,128)(2,1)S(1)} %get-tuple-element.202), channel_id=1, source_target_pairs={{0,6},{2,4},{4,2},{6,0},{1,7},{3,5},{5,3},{7,1},{8,14},{10,12},{12... | collective-permute-start | bytes 393224 | tf_op jit(solution)/shard_map/ppermute | solution.py:402
  113.2 10.4 %collective-permute-start.19 = (bf16[4,8,16,512]{3,1,2,0:T(8,128)(2,1)S(1)}, bf16[4,8,16,512]{3,1,2,0:T(8,128)(2,1)S(1)}, u32[]{:S(2)}, u32[]{:S(2)}) collective-permute-start(bf16[4,8,16,512]{3,1,2,0:T(8,128)(2,1)S(1)} %copy.122), channel_id=1, source_target_pairs={{0,1},{1,0},{2,3},{3,2},{4,5},{5,4},{6,7},{7,6},{8,9},{9,8},{10,11... | collective-permute-start | bytes 1572872 | tf_op jit(solution)/shard_map/ppermute | solution.py:406
  140.0 31.1 %collective-permute-start.27 = (bf16[16,64,512]{2,1,0:T(8,128)(2,1)}, bf16[16,64,512]{2,1,0:T(8,128)(2,1)}, u32[]{:S(2)}, u32[]{:S(2)}) collective-permute-start(bf16[16,64,512]{2,1,0:T(8,128)(2,1)} %bitcast.16.refs_3_.refs_4_.refs_6_), channel_id=1, source_target_pairs={{0,8},{8,16},{16,24},{1,9},{9,17},{17,25},{2,10},{10,18},{18,26},{... | collective-permute-start | bytes 3145736 | tf_op jit(solution)/shard_map/ppermute | solution.py:394
  144.6 25.2 %collective-permute-start.30 = (bf16[16,64,512]{2,1,0:T(8,128)(2,1)}, bf16[16,64,512]{2,1,0:T(8,128)(2,1)}, u32[]{:S(2)}, u32[]{:S(2)}) collective-permute-start(bf16[16,64,512]{2,1,0:T(8,128)(2,1)} %bitcast.16.refs_3_.refs_4_.refs_6_), channel_id=1, source_target_pairs={{24,16},{16,8},{8,0},{25,17},{17,9},{9,1},{26,18},{18,10},{10,2},{... | collective-permute-start | bytes 3145736 | tf_op jit(solution)/shard_map/ppermute | solution.py:395
  169.8 25.7 %collective-permute-start.31 = (bf16[16,64,512]{2,1,0:T(8,128)(2,1)}, bf16[16,64,512]{2,1,0:T(8,128)(2,1)}, u32[]{:S(2)}, u32[]{:S(2)}) collective-permute-start(bf16[16,64,512]{2,1,0:T(8,128)(2,1)} %shard_map.121.refs_10_), channel_id=1, source_target_pairs={{16,8},{8,0},{17,9},{9,1},{18,10},{10,2},{19,11},{11,3},{20,12},{1... | collective-permute-start | bytes 3145736 | tf_op jit(solution)/shard_map/ppermute | solution.py:395
  171.1 25.7 %collective-permute-start.28 = (bf16[16,64,512]{2,1,0:T(8,128)(2,1)}, bf16[16,64,512]{2,1,0:T(8,128)(2,1)}, u32[]{:S(2)}, u32[]{:S(2)}) collective-permute-start(bf16[16,64,512]{2,1,0:T(8,128)(2,1)} %shard_map.117.refs_3_.refs_4_.refs_7_), channel_id=1, source_target_pairs={{8,16},{16,24},{9,17},{17,25},{10,18},{18,26},{11,19},{19,27},{12,... | collective-permute-start | bytes 3145736 | tf_op jit(solution)/shard_map/ppermute | solution.py:394
  195.5 24.3 %collective-permute-start.32 = (bf16[16,64,512]{2,1,0:T(8,128)(2,1)}, bf16[16,64,512]{2,1,0:T(8,128)(2,1)}, u32[]{:S(2)}, u32[]{:S(2)}) collective-permute-start(bf16[16,64,512]{2,1,0:T(8,128)(2,1)} %shard_map.122.refs_11_), channel_id=1, source_target_pairs={{8,0},{9,1},{10,2},{11,3},{12,4},{13,5},{14,6},{15,7}} | collective-permute-start | bytes 3145736 | tf_op jit(solution)/shard_map/ppermute | solution.py:395
  196.9 23.0 %collective-permute-start.29 = (bf16[16,64,512]{2,1,0:T(8,128)(2,1)}, bf16[16,64,512]{2,1,0:T(8,128)(2,1)}, u32[]{:S(2)}, u32[]{:S(2)}) collective-permute-start(bf16[16,64,512]{2,1,0:T(8,128)(2,1)} %shard_map.120.refs_4_.refs_8_), channel_id=1, source_target_pairs={{16,24},{17,25},{18,26},{19,27},{20,28},{21,29},{22,30},{23,31}} | collective-permute-start | bytes 3145736 | tf_op jit(solution)/shard_map/ppermute | solution.py:394
  247.4 20.9 %collective-permute-start.35 = (bf16[16,32,512]{2,1,0:T(8,128)(2,1)}, bf16[16,32,512]{2,1,0:T(8,128)(2,1)S(1)}, u32[]{:S(2)}, u32[]{:S(2)}) collective-permute-start(bf16[16,32,512]{2,1,0:T(8,128)(2,1)} %get-tuple-element.136.refs_2_), channel_id=1, source_target_pairs={{0,8},{1,9},{2,10},{3,11},{4,12},{5,13},{6,14},{7,15}} | collective-permute-start | bytes 1572872 | tf_op jit(solution)/shard_map/ppermute | solution.py:381
  248.9 19.4 %collective-permute-start.36 = (bf16[16,32,512]{2,1,0:T(8,128)(2,1)}, bf16[16,32,512]{2,1,0:T(8,128)(2,1)S(1)}, u32[]{:S(2)}, u32[]{:S(2)}) collective-permute-start(bf16[16,32,512]{2,1,0:T(8,128)(2,1)} %get-tuple-element.137.refs_0_), channel_id=1, source_target_pairs={{24,16},{25,17},{26,18},{27,19},{28,20},{29,21},{30,22},{31,23}} | collective-permute-start | bytes 1572872 | tf_op jit(solution)/shard_map/ppermute | solution.py:382
  249.6 26.3 %collective-permute-start.33 = (bf16[16,32,512]{2,1,0:T(8,128)(2,1)}, bf16[16,32,512]{2,1,0:T(8,128)(2,1)S(1)}, u32[]{:S(2)}, u32[]{:S(2)}) collective-permute-start(bf16[16,32,512]{2,1,0:T(8,128)(2,1)} %get-tuple-element.127.refs_6_.refs_8_.refs_2_), channel_id=1, source_target_pairs={{0,8},{1,9},{2,10},{3,11},{4,12},{5,13},{6,14},{7,15}} | collective-permute-start | bytes 1572872 | tf_op jit(solution)/shard_map/ppermute | solution.py:381
  250.9 24.9 %collective-permute-start.34 = (bf16[16,32,512]{2,1,0:T(8,128)(2,1)}, bf16[16,32,512]{2,1,0:T(8,128)(2,1)S(1)}, u32[]{:S(2)}, u32[]{:S(2)}) collective-permute-start(bf16[16,32,512]{2,1,0:T(8,128)(2,1)} %get-tuple-element.125.refs_0_), channel_id=1, source_target_pairs={{24,16},{25,17},{26,18},{27,19},{28,20},{29,21},{30,22},{31,23}} | collective-permute-start | bytes 1572872 | tf_op jit(solution)/shard_map/ppermute | solution.py:382
  268.7 20.5 %collective-permute-start.39 = (bf16[16,32,512]{2,1,0:T(8,128)(2,1)S(1)}, bf16[16,32,512]{2,1,0:T(8,128)(2,1)S(1)}, u32[]{:S(2)}, u32[]{:S(2)}) collective-permute-start(bf16[16,32,512]{2,1,0:T(8,128)(2,1)S(1)} %get-tuple-element.138.refs_8_), channel_id=1, source_target_pairs={{0,8},{8,16},{1,9},{9,17},{2,10},{10,18},{3,11},{11,19},{4,12},{12... | collective-permute-start | bytes 1572872 | tf_op jit(solution)/shard_map/ppermute | solution.py:381
  270.0 19.2 %collective-permute-start.40 = (bf16[16,32,512]{2,1,0:T(8,128)(2,1)S(1)}, bf16[16,32,512]{2,1,0:T(8,128)(2,1)S(1)}, u32[]{:S(2)}, u32[]{:S(2)}) collective-permute-start(bf16[16,32,512]{2,1,0:T(8,128)(2,1)S(1)} %get-tuple-element.145), channel_id=1, source_target_pairs={{24,16},{16,8},{25,17},{17,9},{26,18},{18,10},{27,19},{19,11},{28,... | collective-permute-start | bytes 1572872 | tf_op jit(solution)/shard_map/ppermute | solution.py:382
  276.2 19.3 %collective-permute-start.37 = (bf16[16,32,512]{2,1,0:T(8,128)(2,1)S(1)}, bf16[16,32,512]{2,1,0:T(8,128)(2,1)S(1)}, u32[]{:S(2)}, u32[]{:S(2)}) collective-permute-start(bf16[16,32,512]{2,1,0:T(8,128)(2,1)S(1)} %get-tuple-element.140.refs_8_), channel_id=1, source_target_pairs={{0,8},{8,16},{1,9},{9,17},{2,10},{10,18},{3,11},{11,19},{4,12},{12... | collective-permute-start | bytes 1572872 | tf_op jit(solution)/shard_map/ppermute | solution.py:381
  283.0 12.5 %collective-permute-start.38 = (bf16[16,32,512]{2,1,0:T(8,128)(2,1)S(1)}, bf16[16,32,512]{2,1,0:T(8,128)(2,1)S(1)}, u32[]{:S(2)}, u32[]{:S(2)}) collective-permute-start(bf16[16,32,512]{2,1,0:T(8,128)(2,1)S(1)} %get-tuple-element.141), channel_id=1, source_target_pairs={{24,16},{16,8},{25,17},{17,9},{26,18},{18,10},{27,19},{19,11},{28,... | collective-permute-start | bytes 1572872 | tf_op jit(solution)/shard_map/ppermute | solution.py:382
  296.1 16.9 %collective-permute-start.41 = (bf16[16,32,512]{2,0,1:T(8,128)(2,1)S(1)}, bf16[16,32,512]{2,0,1:T(8,128)(2,1)S(1)}, u32[]{:S(2)}, u32[]{:S(2)}) collective-permute-start(bf16[16,32,512]{2,0,1:T(8,128)(2,1)S(1)} %copy.127), channel_id=1, source_target_pairs={{0,8},{8,16},{16,24},{1,9},{9,17},{17,25},{2,10},{10,18},{18,26},{... | collective-permute-start | bytes 1572872 | tf_op jit(solution)/shard_map/ppermute | solution.py:381
  301.6 17.0 %collective-permute-start.42 = (bf16[16,32,512]{2,0,1:T(8,128)(2,1)S(1)}, bf16[16,32,512]{2,0,1:T(8,128)(2,1)S(1)}, u32[]{:S(2)}, u32[]{:S(2)}) collective-permute-start(bf16[16,32,512]{2,0,1:T(8,128)(2,1)S(1)} %copy.128), channel_id=1, source_target_pairs={{24,16},{16,8},{8,0},{25,17},{17,9},{9,1},{26,18},{18,10},{10,2},{... | collective-permute-start | bytes 1572872 | tf_op jit(solution)/shard_map/ppermute | solution.py:382
  303.2 19.5 %collective-permute-start.47 = (bf16[16,32,512]{2,0,1:T(8,128)(2,1)S(1)}, bf16[16,32,512]{2,0,1:T(8,128)(2,1)S(1)}, u32[]{:S(2)}, u32[]{:S(2)}) collective-permute-start(bf16[16,32,512]{2,0,1:T(8,128)(2,1)S(1)} %copy.130), channel_id=1, source_target_pairs={{0,8},{8,16},{16,24},{1,9},{9,17},{17,25},{2,10},{10,18},{18,26},{... | collective-permute-start | bytes 1572872 | tf_op jit(solution)/shard_map/ppermute | solution.py:381
  308.7 15.5 %collective-permute-start.48 = (bf16[16,32,512]{2,0,1:T(8,128)(2,1)S(1)}, bf16[16,32,512]{2,0,1:T(8,128)(2,1)S(1)}, u32[]{:S(2)}, u32[]{:S(2)}) collective-permute-start(bf16[16,32,512]{2,0,1:T(8,128)(2,1)S(1)} %copy.131), channel_id=1, source_target_pairs={{24,16},{16,8},{8,0},{25,17},{17,9},{9,1},{26,18},{18,10},{10,2},{... | collective-permute-start | bytes 1572872 | tf_op jit(solution)/shard_map/ppermute | solution.py:382
  319.2 9.1 %collective-permute-start.44 = (bf16[8,16,512]{2,1,0:T(8,128)(2,1)S(1)}, bf16[8,16,512]{2,1,0:T(8,128)(2,1)S(1)}, u32[]{:S(2)}, u32[]{:S(2)}) collective-permute-start(bf16[8,16,512]{2,1,0:T(8,128)(2,1)S(1)} %get-tuple-element.196), channel_id=1, source_target_pairs={{0,4},{2,6},{4,0},{6,2},{1,5},{3,7},{5,1},{7,3},{8,12},{10,14},{12... | collective-permute-start | bytes 393224 | tf_op jit(solution)/shard_map/ppermute | solution.py:402
  319.7 8.6 %collective-permute-start.45 = (bf16[8,16,512]{2,1,0:T(8,128)(2,1)S(1)}, bf16[8,16,512]{2,1,0:T(8,128)(2,1)S(1)}, u32[]{:S(2)}, u32[]{:S(2)}) collective-permute-start(bf16[8,16,512]{2,1,0:T(8,128)(2,1)S(1)} %get-tuple-element.195), channel_id=1, source_target_pairs={{0,6},{2,4},{4,2},{6,0},{1,7},{3,5},{5,3},{7,1},{8,14},{10,12},{12... | collective-permute-start | bytes 393224 | tf_op jit(solution)/shard_map/ppermute | solution.py:402
  331.5 8.6 %collective-permute-start.52 = (bf16[4,8,16,512]{3,2,1,0:T(8,128)(2,1)S(1)}, bf16[4,8,16,512]{3,2,1,0:T(8,128)(2,1)S(1)}, u32[]{:S(2)}, u32[]{:S(2)}) collective-permute-start(bf16[4,8,16,512]{3,2,1,0:T(8,128)(2,1)S(1)} %pad_maximum_fusion.1), channel_id=1, source_target_pairs={{0,1},{1,0},{2,3},{3,2},{4,5},{5,4},{6,7},{7,6},{8,9},{9,8},{10,11... | collective-permute-start | bytes 1572872 | tf_op jit(solution)/shard_map/ppermute | solution.py:406
  352.8 8.8 %collective-permute-start.56 = (bf16[8,16,512]{2,0,1:T(8,128)(2,1)S(1)}, bf16[8,16,512]{2,0,1:T(8,128)(2,1)S(1)}, u32[]{:S(2)}, u32[]{:S(2)}) collective-permute-start(bf16[8,16,512]{2,0,1:T(8,128)(2,1)S(1)} %bitcast.123), channel_id=1, source_target_pairs={{0,2},{2,0},{4,6},{6,4},{1,3},{3,1},{5,7},{7,5},{8,10},{10,8},{12,... | collective-permute-start | bytes 393224 | tf_op jit(solution)/shard_map/ppermute | solution.py:402
  354.7 10.1 %collective-permute-start.57 = (bf16[8,16,512]{2,0,1:T(8,128)(2,1)S(1)}, bf16[8,16,512]{2,0,1:T(8,128)(2,1)S(1)}, u32[]{:S(2)}, u32[]{:S(2)}) collective-permute-start(bf16[8,16,512]{2,0,1:T(8,128)(2,1)S(1)} %bitcast.122), channel_id=1, source_target_pairs={{0,4},{2,6},{4,0},{6,2},{1,5},{3,7},{5,1},{7,3},{8,12},{10,14},{12... | collective-permute-start | bytes 393224 | tf_op jit(solution)/shard_map/ppermute | solution.py:402
  364.8 27.1 %collective-permute-start.60 = (bf16[16,64,512]{2,1,0:T(8,128)(2,1)S(1)}, bf16[16,64,512]{2,1,0:T(8,128)(2,1)S(1)}, u32[]{:S(2)}, u32[]{:S(2)}) collective-permute-start(bf16[16,64,512]{2,1,0:T(8,128)(2,1)S(1)} %bitcast.104), channel_id=1, source_target_pairs={{24,16},{16,8},{8,0},{25,17},{17,9},{9,1},{26,18},{18,10},{10,2},{... | collective-permute-start | bytes 3145736 | tf_op jit(solution)/shard_map/ppermute | solution.py:395
  366.1 28.1 %collective-permute-start.59 = (bf16[16,64,512]{2,1,0:T(8,128)(2,1)S(1)}, bf16[16,64,512]{2,1,0:T(8,128)(2,1)}, u32[]{:S(2)}, u32[]{:S(2)}) collective-permute-start(bf16[16,64,512]{2,1,0:T(8,128)(2,1)S(1)} %bitcast.105), channel_id=1, source_target_pairs={{0,8},{8,16},{16,24},{1,9},{9,17},{17,25},{2,10},{10,18},{18,26},{... | collective-permute-start | bytes 3145736 | tf_op jit(solution)/shard_map/ppermute | solution.py:394
  393.0 26.6 %collective-permute-start.62 = (bf16[16,64,512]{2,1,0:T(8,128)(2,1)}, bf16[16,64,512]{2,1,0:T(8,128)(2,1)}, u32[]{:S(2)}, u32[]{:S(2)}) collective-permute-start(bf16[16,64,512]{2,1,0:T(8,128)(2,1)} %shard_map.143.refs_2_), channel_id=1, source_target_pairs={{16,8},{8,0},{17,9},{9,1},{18,10},{10,2},{19,11},{11,3},{20,12},{1... | collective-permute-start | bytes 3145736 | tf_op jit(solution)/shard_map/ppermute | solution.py:395
  394.3 26.7 %collective-permute-start.61 = (bf16[16,64,512]{2,1,0:T(8,128)(2,1)}, bf16[16,64,512]{2,1,0:T(8,128)(2,1)}, u32[]{:S(2)}, u32[]{:S(2)}) collective-permute-start(bf16[16,64,512]{2,1,0:T(8,128)(2,1)} %shard_map.140.refs_8_.refs_1_), channel_id=1, source_target_pairs={{8,16},{16,24},{9,17},{17,25},{10,18},{18,26},{11,19},{19,27},{12,... | collective-permute-start | bytes 3145736 | tf_op jit(solution)/shard_map/ppermute | solution.py:394
  419.5 25.8 %collective-permute-start.64 = (bf16[16,64,512]{2,1,0:T(8,128)(2,1)}, bf16[16,64,512]{2,1,0:T(8,128)(2,1)}, u32[]{:S(2)}, u32[]{:S(2)}) collective-permute-start(bf16[16,64,512]{2,1,0:T(8,128)(2,1)} %shard_map.146.refs_1_), channel_id=1, source_target_pairs={{8,0},{9,1},{10,2},{11,3},{12,4},{13,5},{14,6},{15,7}} | collective-permute-start | bytes 3145736 | tf_op jit(solution)/shard_map/ppermute | solution.py:395
  421.0 24.3 %collective-permute-start.63 = (bf16[16,64,512]{2,1,0:T(8,128)(2,1)}, bf16[16,64,512]{2,1,0:T(8,128)(2,1)}, u32[]{:S(2)}, u32[]{:S(2)}) collective-permute-start(bf16[16,64,512]{2,1,0:T(8,128)(2,1)} %shard_map.144.refs_6_.refs_0_.refs_4_), channel_id=1, source_target_pairs={{16,24},{17,25},{18,26},{19,27},{20,28},{21,29},{22,30},{23,31}} | collective-permute-start | bytes 3145736 | tf_op jit(solution)/shard_map/ppermute | solution.py:394
  (87 other events, 874.9 us)

commit v6 on v5

--- a/solution.py
+++ b/solution.py
@@ -596,9 +596,9 @@
     fill = [local_piece(i, min(count, steps - i)) for i in range(0, steps, count)]
     below, above = [], []
     later = slope_fill[turns:]
-    fill = [together(a, *later[i : i + 1]) for i, a in enumerate(fill)]
-    fill.append(together(*later[len(fill) : len(fill) + 1]))
-    later = later[len(fill) :]
+    fill[-1] = together(fill[-1], *later[:1])
+    fill.append(together(*later[1:3]))
+    later = later[3:]
     tokens = chain_gather(out_modes, blocks, below, above, fill)
     while fill:
         tokens = tokens + run_next(fill, out_modes)
@@ -741,8 +741,8 @@
         return lambda source: pairs(([(0, back_modes)] if t == 0 else []) + arrived(t), [source])
 
     fill = [
-        together(*[weight_piece(part) for part in range(CHUNKS)], *later),
-        together(*back_fill[turns + 2 :]),
+        together(*[weight_piece(part) for part in range(CHUNKS)]),
+        together(*back_fill[turns + 2 :], *later),
         together(*[pair_piece(t) for t in range(min(2, blocks - 2))]),
     ]
     fill += [pair_piece(t) for t in range(2, blocks - 2)]

time: 480 us -> 476 us (level)
  waiting for transfers between devices: 69.4 us -> 59.9 us
  local copies, waits for them, and re-layouts: 43.7 us -> 49.9 us
    ppermute x6, waiting for transfers between devices: 31.2 us -> 24.3 us  [chain_gather(): lax.ppermute(down, 'blk', [(blocks - 1 - z, blocks - 2 - z) for z in rang...]
    unnamed x148 -> x150, local copies, waits for them, and re-layouts: 26.7 us -> 32.1 us
  transfers between devices with their start and end apart: 72 -> 72, of which waited for: 27 -> 28; matrix products, arithmetic and copies ran while one was open for 6% -> 7% of each run, Pallas kernels for 35% -> 35%
where the time goes in v6:
time: 476 us; the launch traced here: 466 us
  Pallas kernels  218 us (46%)
  starting transfers between devices  127 us (27%)
  waiting for transfers between devices  59.9 us (13%)
  local copies, waits for them, and re-layouts  49.9 us (10%)
  other arithmetic  9.15 us (2%)
    pallas_call x37, Pallas kernels, call(): pl.pallas_call(kernel, grid_spec=pltpu.PrefetchScalarGridSpec(num_scalar_...  218 us
    ppermute x12, starting transfers between devices, chain_sums(): below = lax.ppermute(up, 'blk', [(z, z + 1) for z in range(t + 1)])  47.7 us
    unnamed x150, local copies, waits for them, and re-layouts  32.1 us
    ppermute x24, starting transfers between devices, swap_samples(): lax.ppermute(pieces[j], 'dp', [(i, i ^ j) for i in range(n)])  30.5 us
    ppermute x6, waiting for transfers between devices, chain_gather(): lax.ppermute(down, 'blk', [(blocks - 1 - z, blocks - 2 - z) for z in rang...  24.3 us
    ppermute x6, starting transfers between devices, chain_gather(): lax.ppermute(up, 'blk', [(z, z + 1) for z in range(t, blocks - 1)])  17.4 us
    ppermute x12, starting transfers between devices, chain_sums(): lax.ppermute(down, 'blk', [(blocks - 1 - z, blocks - 2 - z) for z in rang...  13.6 us
    ppermute x6, waiting for transfers between devices, all_sum(): lax.ppermute(value, axis, [(i, i ^ j) for i in range(n)])  9.9 us
  transfers between devices with their start and end apart: 72, of which 28 were waited for; matrix products, arithmetic and copies ran while one was open for 7% of the time, Pallas kernels for 35%

profile of v6, /device:TPU:0, one launch (start us, length us, event | category | flops | bytes accessed | tf_op | source)
XLA Modules:
  0.0 466.3 jit_solution(4046597047653740500)
XLA Ops:
  2.7 13.1 %shard_map.103 = (bf16[16,256,1024]{2,1,0:T(8,128)(2,1)}, bf16[16,32,512]{2,1,0:T(8,128)(2,1)S(1)}, bf16[16,32,512]{2,1,0:T(8,128)(2,1)}, bf16[16,32,512]{2,1,0:...) custom-call(s32[2]{0:T(128)S(1)} %pad_add_fusion.refs_0_, ...), custom_call_target="tpu_custom_call" | custom-call | flops 6442450944 | bytes 19398912 | tf_op jit(solution)/shard_map/pallas_call | solution.py:317
  19.5 5.3 %collective-permute-start.1 = (bf16[16,32,512]{2,1,0:T(8,128)(2,1)}, bf16[16,32,512]{2,1,0:T(8,128)(2,1)}, u32[]{:S(2)}, u32[]{:S(2)}) collective-permute-start(bf16[16,32,512]{2,1,0:T(8,128)(2,1)} %get-tuple-element.90.refs_2_), channel_id=1, source_target_pairs={{0,8},{1,9},{2,10},{3,11},{4,12},{5,13},{6,14},{7,15}} | collective-permute-start | bytes 1572872 | tf_op jit(solution)/shard_map/ppermute | solution.py:381
  31.6 5.7 %shard_map.104 = (bf16[4,16,4,64,512]{4,3,2,1,0:T(8,128)(2,1)}, f32[8,128]{1,0:T(8,128)S(1)}) custom-call(f32[4,16]{1,0:T(4,128)S(1)} %get-tuple-element.221.refs_1_.refs_0_, bf16[4,256,1024]{2,1,0:T(8,128)(2,1)S(1)} %bitcast.88, bf16[1024,512]{1,0:T(8,128)(2,1)S(1)} %copy-done.2, bf16[512,256]{1,0:T(8,128)(2,1)S(1)} %get-tuple-element.179.refs_3_.refs_4_, ...), custom_call_target="tpu_custom_call" | custom-call | flops 3221225472 | bytes 5509376 | tf_op jit(solution)/shard_map/pallas_call | solution.py:317
  38.7 3.6 collective-permute-start.3
  43.2 5.7 %shard_map.106 = (bf16[4,16,4,64,512]{4,3,2,1,0:T(8,128)(2,1)}, f32[8,128]{1,0:T(8,128)S(1)}) custom-call(f32[4,16]{1,0:T(4,128)S(1)} %get-tuple-element.221.refs_1_.refs_0_, bf16[4,256,1024]{2,1,0:T(8,128)(2,1)S(1)} %bitcast.89, bf16[1024,512]{1,0:T(8,128)(2,1)S(1)} %copy-done.2, ...), custom_call_target="tpu_custom_call", output_to_operand_aliasing={{0}: (5, {})} | custom-call | flops 3221225472 | bytes 5509376 | tf_op jit(solution)/shard_map/pallas_call | solution.py:317
  50.4 5.5 %collective-permute-start.12 = (bf16[16,32,512]{2,1,0:T(8,128)(2,1)S(1)}, bf16[16,32,512]{2,1,0:T(8,128)(2,1)S(1)}, u32[]{:S(2)}, u32[]{:S(2)}) collective-permute-start(bf16[16,32,512]{2,1,0:T(8,128)(2,1)S(1)} %get-tuple-element.99.refs_4_), channel_id=1, source_target_pairs={{0,8},{8,16},{1,9},{9,17},{2,10},{10,18},{3,11},{11,19},{4,12},{12... | collective-permute-start | bytes 1572872 | tf_op jit(solution)/shard_map/ppermute | solution.py:381
  56.7 5.8 %shard_map.108 = (bf16[4,16,4,64,512]{4,3,2,1,0:T(8,128)(2,1)}, f32[8,128]{1,0:T(8,128)S(1)}) custom-call(f32[4,16]{1,0:T(4,128)S(1)} %get-tuple-element.221.refs_1_.refs_0_, bf16[4,256,1024]{2,1,0:T(8,128)(2,1)S(1)} %bitcast.90, bf16[1024,512]{1,0:T(8,128)(2,1)S(1)} %copy-done.2, ...), custom_call_target="tpu_custom_call", output_to_operand_aliasing={{0}: (5, {})} | custom-call | flops 3221225472 | bytes 5509376 | tf_op jit(solution)/shard_map/pallas_call | solution.py:317
  64.1 5.2 %collective-permute-start.7 = (bf16[16,32,512]{2,0,1:T(8,128)(2,1)S(1)}, bf16[16,32,512]{2,0,1:T(8,128)(2,1)S(1)}, u32[]{:S(2)}, u32[]{:S(2)}) collective-permute-start(bf16[16,32,512]{2,0,1:T(8,128)(2,1)S(1)} %copy.116), channel_id=1, source_target_pairs={{0,8},{8,16},{16,24},{1,9},{9,17},{17,25},{2,10},{10,18},{18,26},{... | collective-permute-start | bytes 1572872 | tf_op jit(solution)/shard_map/ppermute | solution.py:381
  71.4 5.8 %shard_map.110 = (bf16[4,16,4,64,512]{4,3,2,1,0:T(8,128)(2,1)}, f32[8,128]{1,0:T(8,128)S(1)}) custom-call(f32[4,16]{1,0:T(4,128)S(1)} %get-tuple-element.221.refs_1_.refs_0_, bf16[4,256,1024]{2,1,0:T(8,128)(2,1)S(1)} %bitcast.91, bf16[1024,512]{1,0:T(8,128)(2,1)S(1)} %copy-done.2, ...), custom_call_target="tpu_custom_call", output_to_operand_aliasing={{0}: (5, {})} | custom-call | flops 3221225472 | bytes 5509376 | tf_op jit(solution)/shard_map/pallas_call | solution.py:317
  78.9 5.2 %collective-permute-start.14 = (bf16[16,32,512]{2,0,1:T(8,128)(2,1)S(1)}, bf16[16,32,512]{2,0,1:T(8,128)(2,1)S(1)}, u32[]{:S(2)}, u32[]{:S(2)}) collective-permute-start(bf16[16,32,512]{2,0,1:T(8,128)(2,1)S(1)} %copy.119), channel_id=1, source_target_pairs={{0,8},{8,16},{16,24},{1,9},{9,17},{17,25},{2,10},{10,18},{18,26},{... | collective-permute-start | bytes 1572872 | tf_op jit(solution)/shard_map/ppermute | solution.py:381
  89.2 4.1 collective-permute-done.14
  101.8 7.6 %shard_map.112 = (bf16[4,8,16,512]{3,2,1,0:T(8,128)(2,1)S(1)}, bf16[4,8,16,512]{3,2,1,0:T(8,128)(2,1)S(1)}) custom-call(s32[1]{0:T(128)} %bitcast.refs_0_, bf16[2,16,16,32,256]{4,3,2,1,0:T(8,128)(2,1)} %refs_2_.16, bf16[2,16,16,32,256]{4,3,2,1,0:T(8,128)(2,1)} %refs_2_.16, bf16[8,16,512]{2,1,0:T(8,128)(2,1)S(1)} %get-tuple-element.211.refs_3_.refs_2_, ...), custom_call_target="tpu_custom_call" | custom-call | flops 33554432 | bytes 5767168 | tf_op jit(solution)/shard_map/pallas_call | solution.py:317
  115.1 7.7 %shard_map.114 = (bf16[4,8,16,512]{3,2,1,0:T(8,128)(2,1)S(1)}, bf16[4,8,16,512]{3,2,1,0:T(8,128)(2,1)S(1)}) custom-call(s32[1]{0:T(128)} %bitcast.refs_0_, bf16[2,16,16,32,256]{4,3,2,1,0:T(8,128)(2,1)} %refs_2_.16, bf16[2,16,16,32,256]{4,3,2,1,0:T(8,128)(2,1)} %refs_2_.16, bf16[8,16,512]{2,1,0:T(8,128)(2,1)S(1)} %get-tuple-element.201.refs_3_.refs_2_, ...), custom_call_target="tpu_custom_call" | custom-call | flops 33554432 | bytes 5767168 | tf_op jit(solution)/shard_map/pallas_call | solution.py:317
  141.2 5.6 %collective-permute-start.27 = (bf16[16,64,512]{2,1,0:T(8,128)(2,1)}, bf16[16,64,512]{2,1,0:T(8,128)(2,1)}, u32[]{:S(2)}, u32[]{:S(2)}) collective-permute-start(bf16[16,64,512]{2,1,0:T(8,128)(2,1)} %bitcast.16.refs_3_.refs_6_), channel_id=1, source_target_pairs={{0,8},{8,16},{16,24},{1,9},{9,17},{17,25},{2,10},{10,18},{18,26},{... | collective-permute-start | bytes 3145736 | tf_op jit(solution)/shard_map/ppermute | solution.py:394
  153.6 10.3 %shard_map.115 = (f32[16,256,1024]{2,1,0:T(8,128)}, f32[8,128]{1,0:T(8,128)S(1)}) custom-call(bf16[256,512]{1,0:T(8,128)(2,1)S(1)} %bitcast.104, bf16[16,256,1024]{2,1,0:T(8,128)(2,1)} %get-tuple-element.86.refs_1_.refs_3_, bf16[16,256,1024]{2,1,0:T(8,128)(2,1)} %collective-permute-done.refs_2_.refs_4_, bf16[16,64,512]{2,1,0:T(8,128)(2,1)} %bitcast.16.refs_3_.refs_6_), custom_call_target="tpu_custom_call" | custom-call | flops 2147483648 | bytes 18907136 | tf_op jit(solution)/shard_map/pallas_call | solution.py:317
  169.4 10.4 %shard_map.117 = (f32[16,256,1024]{2,1,0:T(8,128)}, f32[8,128]{1,0:T(8,128)S(1)}) custom-call(bf16[256,512]{1,0:T(8,128)(2,1)S(1)} %bitcast.105, bf16[16,256,1024]{2,1,0:T(8,128)(2,1)} %get-tuple-element.86.refs_1_.refs_3_, bf16[16,256,1024]{2,1,0:T(8,128)(2,1)} %collective-permute-done.refs_2_.refs_4_, ...), custom_call_target="tpu_custom_call", output_to_operand_aliasing={{0}: (4, {})} | custom-call | flops 2147483648 | bytes 18907136 | tf_op jit(solution)/shard_map/pallas_call | solution.py:317
  179.8 5.8 %shard_map.118 = (bf16[4,16,4,64,512]{4,3,2,1,0:T(8,128)(2,1)}, f32[8,128]{1,0:T(8,128)S(1)}) custom-call(f32[4,16]{1,0:T(4,128)S(1)} %get-tuple-element.221.refs_1_.refs_0_, bf16[4,256,1024]{2,1,0:T(8,128)(2,1)S(1)} %bitcast.92, bf16[1024,512]{1,0:T(8,128)(2,1)S(1)} %copy-done.2, bf16[512,256]{1,0:T(8,128)(2,1)S(1)} %copy-done.8, ...), custom_call_target="tpu_custom_call", output_to_operand_aliasing={{0}: (5, {})} | custom-call | flops 3221225472 | bytes 5509376 | tf_op jit(solution)/shard_map/pallas_call | solution.py:317
  186.2 3.9 collective-permute-done.31.refs_0_
  196.0 5.7 %shard_map.122 = (bf16[4,16,4,64,512]{4,3,2,1,0:T(8,128)(2,1)}, f32[8,128]{1,0:T(8,128)S(1)}) custom-call(f32[4,16]{1,0:T(4,128)S(1)} %get-tuple-element.221.refs_1_.refs_0_, bf16[4,256,1024]{2,1,0:T(8,128)(2,1)S(1)} %bitcast.93, bf16[1024,512]{1,0:T(8,128)(2,1)S(1)} %copy-done.2, bf16[512,256]{1,0:T(8,128)(2,1)S(1)} %copy-done.9, ...), custom_call_target="tpu_custom_call", output_to_operand_aliasing={{0}: (5, {})} | custom-call | flops 3221225472 | bytes 5509376 | tf_op jit(solution)/shard_map/pallas_call | solution.py:317
  202.3 5.7 %shard_map.123 = (bf16[4,16,4,64,512]{4,3,2,1,0:T(8,128)(2,1)}, f32[8,128]{1,0:T(8,128)S(1)}) custom-call(f32[4,16]{1,0:T(4,128)S(1)} %get-tuple-element.221.refs_1_.refs_0_, bf16[4,256,1024]{2,1,0:T(8,128)(2,1)S(1)} %bitcast.94, bf16[1024,512]{1,0:T(8,128)(2,1)S(1)} %copy-done.2, bf16[512,256]{1,0:T(8,128)(2,1)S(1)} %copy-done.9, ...), custom_call_target="tpu_custom_call", output_to_operand_aliasing={{0}: (5, {})} | custom-call | flops 3221225472 | bytes 5509376 | tf_op jit(solution)/shard_map/pallas_call | solution.py:317
  208.6 5.8 %collective-permute-done.32.refs_12_ = bf16[16,64,512]{2,1,0:T(8,128)(2,1)} collective-permute-done((bf16[16,64,512]{2,1,0:T(8,128)(2,1)}, bf16[16,64,512]{2,1,0:T(8,128)(2,1)}, u32[]{:S(2)}, u32[]{:S(2)}) %collective-permute-start.32) | collective-permute-done | bytes 1048608 | tf_op jit(solution)/shard_map/ppermute | solution.py:395
  214.4 27.6 %shard_map.124 = (bf16[16,256,1024]{2,1,0:T(8,128)(2,1)}, bf16[16,32,512]{2,1,0:T(8,128)(2,1)}, bf16[16,32,512]{2,1,0:T(8,128)(2,1)}, bf16[16,32,512]{2,1,0:T(8,...) custom-call(f32[16,256,1024]{2,1,0:T(8,128)} %get-tuple-element.116., ...), custom_call_target="tpu_custom_call" | custom-call | flops 12884901888 | bytes 55574528 | tf_op jit(solution)/shard_map/pallas_call | solution.py:317
  247.6 5.1 %shard_map.125 = (f32[2,256,256]{2,1,0:T(8,128)S(1)}, f32[32,4,8,128]{3,2,1,0:T(8,128)S(1)}) custom-call(f32[4,32]{1,0:T(4,128)S(1)} %pad_maximum_fusion.4.refs_0_, bf16[512,256]{1,0:T(8,128)(2,1)S(1)} %mul.58.refs_1_, bf16[4,256,1024]{2,1,0:T(8,128)(2,1)S(1)} %bitcast.95, bf16[16,256,1024]{2,1,0:T(8,128)(2,1)} %get-tuple-element.86.refs_1_.refs_3_, ...), custom_call_target="tpu_custom_call" | custom-call | flops 1073741824 | bytes 6029824 | tf_op jit(solution)/shard_map/pallas_call | solution.py:317
  252.7 5.1 %shard_map.126 = (f32[2,256,256]{2,1,0:T(8,128)S(1)}, f32[32,4,8,128]{3,2,1,0:T(8,128)S(1)}) custom-call(f32[4,32]{1,0:T(4,128)S(1)} %pad_maximum_fusion.4.refs_0_, bf16[512,256]{1,0:T(8,128)(2,1)S(1)} %mul.58.refs_1_, bf16[4,256,1024]{2,1,0:T(8,128)(2,1)S(1)} %bitcast.96, bf16[16,256,1024]{2,1,0:T(8,128)(2,1)} %get-tuple-element.86.refs_1_.refs_3_, ...), custom_call_target="tpu_custom_call" | custom-call | flops 1073741824 | bytes 8126976 | tf_op jit(solution)/shard_map/pallas_call | solution.py:317
  257.8 5.2 %shard_map.127 = (f32[2,256,256]{2,1,0:T(8,128)S(1)}, f32[32,4,8,128]{3,2,1,0:T(8,128)S(1)}) custom-call(f32[4,32]{1,0:T(4,128)S(1)} %pad_maximum_fusion.4.refs_0_, bf16[512,256]{1,0:T(8,128)(2,1)S(1)} %mul.58.refs_1_, bf16[4,256,1024]{2,1,0:T(8,128)(2,1)S(1)} %bitcast.97, bf16[16,256,1024]{2,1,0:T(8,128)(2,1)} %get-tuple-element.86.refs_1_.refs_3_, ...), custom_call_target="tpu_custom_call" | custom-call | flops 1073741824 | bytes 8126976 | tf_op jit(solution)/shard_map/pallas_call | solution.py:317
  265.4 5.2 %shard_map.129 = (f32[2,256,256]{2,1,0:T(8,128)S(1)}, f32[32,4,8,128]{3,2,1,0:T(8,128)S(1)}) custom-call(f32[4,32]{1,0:T(4,128)S(1)} %pad_maximum_fusion.4.refs_0_, bf16[512,256]{1,0:T(8,128)(2,1)S(1)} %mul.58.refs_1_, bf16[4,256,1024]{2,1,0:T(8,128)(2,1)S(1)} %bitcast.98, bf16[16,256,1024]{2,1,0:T(8,128)(2,1)} %get-tuple-element.86.refs_1_.refs_3_, ...), custom_call_target="tpu_custom_call" | custom-call | flops 1073741824 | bytes 8126976 | tf_op jit(solution)/shard_map/pallas_call | solution.py:317
  270.9 6.4 %collective-permute-start.37 = (bf16[16,32,512]{2,1,0:T(8,128)(2,1)S(1)}, bf16[16,32,512]{2,1,0:T(8,128)(2,1)S(1)}, u32[]{:S(2)}, u32[]{:S(2)}) collective-permute-start(bf16[16,32,512]{2,1,0:T(8,128)(2,1)S(1)} %get-tuple-element.140.refs_8_), channel_id=1, source_target_pairs={{0,8},{8,16},{1,9},{9,17},{2,10},{10,18},{3,11},{11,19},{4,12},{12... | collective-permute-start | bytes 1572872 | tf_op jit(solution)/shard_map/ppermute | solution.py:381
  278.4 5.2 %shard_map.131 = (f32[2,256,256]{2,1,0:T(8,128)S(1)}, f32[32,4,8,128]{3,2,1,0:T(8,128)S(1)}) custom-call(f32[4,32]{1,0:T(4,128)S(1)} %pad_maximum_fusion.4.refs_0_, bf16[512,256]{1,0:T(8,128)(2,1)S(1)} %mul.58.refs_1_, bf16[4,256,1024]{2,1,0:T(8,128)(2,1)S(1)} %bitcast.99, bf16[16,256,1024]{2,1,0:T(8,128)(2,1)} %get-tuple-element.86.refs_1_.refs_3_, ...), custom_call_target="tpu_custom_call" | custom-call | flops 1073741824 | bytes 8126976 | tf_op jit(solution)/shard_map/pallas_call | solution.py:317
  284.0 5.2 %shard_map.133 = (f32[2,256,256]{2,1,0:T(8,128)S(1)}, f32[32,4,8,128]{3,2,1,0:T(8,128)S(1)}) custom-call(f32[4,32]{1,0:T(4,128)S(1)} %pad_maximum_fusion.4.refs_0_, bf16[512,256]{1,0:T(8,128)(2,1)S(1)} %mul.58.refs_1_, bf16[4,256,1024]{2,1,0:T(8,128)(2,1)S(1)} %bitcast.100, bf16[16,256,1024]{2,1,0:T(8,128)(2,1)} %get-tuple-element.86.refs_1_.refs_3_, ...), custom_call_target="tpu_custom_call" | custom-call | flops 1073741824 | bytes 8126976 | tf_op jit(solution)/shard_map/pallas_call | solution.py:317
  290.7 5.1 %collective-permute-start.41 = (bf16[16,32,512]{2,0,1:T(8,128)(2,1)S(1)}, bf16[16,32,512]{2,0,1:T(8,128)(2,1)S(1)}, u32[]{:S(2)}, u32[]{:S(2)}) collective-permute-start(bf16[16,32,512]{2,0,1:T(8,128)(2,1)S(1)} %copy.127), channel_id=1, source_target_pairs={{0,8},{8,16},{16,24},{1,9},{9,17},{17,25},{2,10},{10,18},{18,26},{... | collective-permute-start | bytes 1572872 | tf_op jit(solution)/shard_map/ppermute | solution.py:381
  297.7 5.2 %collective-permute-start.47 = (bf16[16,32,512]{2,0,1:T(8,128)(2,1)S(1)}, bf16[16,32,512]{2,0,1:T(8,128)(2,1)S(1)}, u32[]{:S(2)}, u32[]{:S(2)}) collective-permute-start(bf16[16,32,512]{2,0,1:T(8,128)(2,1)S(1)} %copy.130), channel_id=1, source_target_pairs={{0,8},{8,16},{16,24},{1,9},{9,17},{17,25},{2,10},{10,18},{18,26},{... | collective-permute-start | bytes 1572872 | tf_op jit(solution)/shard_map/ppermute | solution.py:381
  307.8 4.9 %collective-permute-done.42 = bf16[16,32,512]{2,0,1:T(8,128)(2,1)S(1)} collective-permute-done((bf16[16,32,512]{2,0,1:T(8,128)(2,1)S(1)}, bf16[16,32,512]{2,0,1:T(8,128)(2,1)S(1)}, u32[]{:S(2)}, u32[]{:S(2)}) %collective-permute-start.42) | collective-permute-done | bytes 524320 | tf_op jit(solution)/shard_map/ppermute | solution.py:382
  325.7 8.4 %shard_map.136 = bf16[4,8,16,512]{3,2,1,0:T(8,128)(2,1)S(1)} custom-call(s32[1]{0:T(128)} %bitcast.refs_0_, bf16[2,16,16,32,256]{4,3,2,1,0:T(8,128)(2,1)} %refs_2_.16, bf16[2,16,16,32,256]{4,3,2,1,0:T(8,128)(2,1)} %refs_2_.16, bf16[4,8,16,512]{3,2,1,0:T(8,128)(2,1)S(1)} %collective-permute-done.46.refs_3_.refs_1_, ...), custom_call_target="tpu_custom_call" | custom-call | flops 33554432 | bytes 5767168 | tf_op jit(solution)/shard_map/pallas_call | solution.py:317
  334.3 8.5 %shard_map.135 = bf16[4,8,16,512]{3,2,1,0:T(8,128)(2,1)S(1)} custom-call(s32[1]{0:T(128)} %bitcast.refs_0_, bf16[2,16,16,32,256]{4,3,2,1,0:T(8,128)(2,1)} %refs_2_.16, bf16[2,16,16,32,256]{4,3,2,1,0:T(8,128)(2,1)} %refs_2_.16, bf16[4,8,16,512]{3,2,1,0:T(8,128)(2,1)S(1)} %collective-permute-done.52.refs_3_.refs_1_, ...), custom_call_target="tpu_custom_call" | custom-call | flops 33554432 | bytes 5767168 | tf_op jit(solution)/shard_map/pallas_call | solution.py:317
  361.2 4.8 %collective-permute-start.59 = (bf16[16,64,512]{2,1,0:T(8,128)(2,1)}, bf16[16,64,512]{2,1,0:T(8,128)(2,1)S(1)}, u32[]{:S(2)}, u32[]{:S(2)}) collective-permute-start(bf16[16,64,512]{2,1,0:T(8,128)(2,1)} %bitcast.38.refs_10_.refs_0_), channel_id=1, source_target_pairs={{0,8},{8,16},{16,24},{1,9},{9,17},{17,25},{2,10},{10,18},{18,26},{... | collective-permute-start | bytes 3145736 | tf_op jit(solution)/shard_map/ppermute | solution.py:394
  366.0 6.4 %shard_map.137 = (bf16[2,16,16,32,256]{4,3,2,1,0:T(8,128)(2,1)}, f32[8,128]{1,0:T(8,128)S(1)}) custom-call(s32[1]{0:T(128)} %bitcast.refs_0_, bf16[4,8,16,512]{3,2,1,0:T(8,128)(2,1)S(1)} %collective-permute-done.52.refs_3_.refs_1_, bf16[8,16,512]{2,1,0:T(8,128)(2,1)S(1)} %copy-done.34, bf16[8,16,512]{2,1,0:T(8,128)(2,1)S(1)} %copy-done.40, ...), custom_call_target="tpu_custom_call" | custom-call | flops 33554432 | bytes 5799936 | tf_op jit(solution)/shard_map/pallas_call | solution.py:317
  372.4 7.2 %shard_map.138 = (bf16[2,16,16,32,256]{4,3,2,1,0:T(8,128)(2,1)}, f32[8,128]{1,0:T(8,128)S(1)}) custom-call(s32[1]{0:T(128)} %bitcast.refs_0_, bf16[4,8,16,512]{3,2,1,0:T(8,128)(2,1)S(1)} %collective-permute-done.46.refs_3_.refs_1_, bf16[8,16,512]{2,1,0:T(8,128)(2,1)S(1)} %get-tuple-element.201.refs_3_.refs_2_, ...), custom_call_target="tpu_custom_call", output_to_operand_aliasing={{0}: (11, {})} | custom-call | flops 33554432 | bytes 5799936 | tf_op jit(solution)/shard_map/pallas_call | solution.py:317
  380.2 5.9 %collective-permute-done.60.refs_0_ = bf16[16,64,512]{2,1,0:T(8,128)(2,1)} collective-permute-done((bf16[16,64,512]{2,1,0:T(8,128)(2,1)}, bf16[16,64,512]{2,1,0:T(8,128)(2,1)}, u32[]{:S(2)}, u32[]{:S(2)}) %collective-permute-start.60) | collective-permute-done | bytes 1048608 | tf_op jit(solution)/shard_map/ppermute | solution.py:395
  393.5 5.2 %shard_map.140 = (f32[2,256,256]{2,1,0:T(8,128)S(1)}, f32[32,4,8,128]{3,2,1,0:T(8,128)S(1)}) custom-call(f32[4,32]{1,0:T(4,128)S(1)} %pad_maximum_fusion.4.refs_0_, bf16[512,256]{1,0:T(8,128)(2,1)S(1)} %mul.58.refs_1_, bf16[4,256,1024]{2,1,0:T(8,128)(2,1)S(1)} %bitcast.101, bf16[16,256,1024]{2,1,0:T(8,128)(2,1)} %get-tuple-element.86.refs_1_.refs_3_, ...), custom_call_target="tpu_custom_call" | custom-call | flops 1073741824 | bytes 8126976 | tf_op jit(solution)/shard_map/pallas_call | solution.py:317
  398.7 5.3 %shard_map.141 = (f32[2,256,256]{2,1,0:T(8,128)S(1)}, f32[32,4,8,128]{3,2,1,0:T(8,128)S(1)}) custom-call(f32[4,32]{1,0:T(4,128)S(1)} %pad_maximum_fusion.4.refs_0_, bf16[512,256]{1,0:T(8,128)(2,1)S(1)} %mul.58.refs_1_, bf16[4,256,1024]{2,1,0:T(8,128)(2,1)S(1)} %bitcast.102, bf16[16,256,1024]{2,1,0:T(8,128)(2,1)} %get-tuple-element.86.refs_1_.refs_3_, ...), custom_call_target="tpu_custom_call" | custom-call | flops 1073741824 | bytes 8126976 | tf_op jit(solution)/shard_map/pallas_call | solution.py:317
  404.1 5.8 %shard_map.143 = (bf16[4,16,4,64,512]{4,3,2,1,0:T(8,128)(2,1)}, f32[8,128]{1,0:T(8,128)S(1)}) custom-call(f32[4,16]{1,0:T(4,128)S(1)} %get-tuple-element.221.refs_1_.refs_0_, bf16[4,256,1024]{2,1,0:T(8,128)(2,1)S(1)} %bitcast.103, bf16[1024,512]{1,0:T(8,128)(2,1)S(1)} %copy-done.3, bf16[512,256]{1,0:T(8,128)(2,1)S(1)} %copy-done.10, ...), custom_call_target="tpu_custom_call", output_to_operand_aliasing={{0}: (5, {})} | custom-call | flops 3221225472 | bytes 5509376 | tf_op jit(solution)/shard_map/pallas_call | solution.py:317
  414.8 3.7 reshape.60
  421.6 5.5 %shard_map.147 = (f32[16,4,8,128]{3,2,1,0:T(8,128)S(1)}, f32[8,128]{1,0:T(8,128)S(1)}) custom-call(bf16[16,64,512]{2,1,0:T(8,128)(2,1)} %shard_map.144.refs_6_.refs_0_.refs_4_, bf16[16,64,512]{2,1,0:T(8,128)(2,1)} %shard_map.146.refs_1_, bf16[4,16,4,64,512]{4,3,2,1,0:T(8,128)(2,1)} %get-tuple-element.161.refs_3_.refs_4_.refs_5_.refs_2_, ...), custom_call_target="tpu_custom_call" | custom-call | flops 16777216 | bytes 10764288 | tf_op jit(solution)/shard_map/pallas_call | solution.py:317
  427.1 5.8 %shard_map.145 = (f32[16,4,8,128]{3,2,1,0:T(8,128)S(1)}, f32[8,128]{1,0:T(8,128)S(1)}) custom-call(bf16[16,64,512]{2,1,0:T(8,128)(2,1)} %bitcast.38.refs_10_.refs_0_, bf16[16,64,512]{2,1,0:T(8,128)(2,1)S(1)} %copy-done.6, bf16[16,64,512]{2,1,0:T(8,128)(2,1)} %shard_map.142.refs_2_, ...), custom_call_target="tpu_custom_call" | custom-call | flops 25165824 | bytes 16007168 | tf_op jit(solution)/shard_map/pallas_call | solution.py:317
  433.0 6.6 %collective-permute-done.64.refs_1_ = bf16[16,64,512]{2,1,0:T(8,128)(2,1)} collective-permute-done((bf16[16,64,512]{2,1,0:T(8,128)(2,1)}, bf16[16,64,512]{2,1,0:T(8,128)(2,1)}, u32[]{:S(2)}, u32[]{:S(2)}) %collective-permute-start.64) | collective-permute-done | bytes 1048608 | tf_op jit(solution)/shard_map/ppermute | solution.py:395
  439.6 5.2 %shard_map.148 = (f32[16,4,8,128]{3,2,1,0:T(8,128)S(1)}, f32[8,128]{1,0:T(8,128)}) custom-call(bf16[16,64,512]{2,1,0:T(8,128)(2,1)} %collective-permute-done.63.refs_0_, bf16[16,64,512]{2,1,0:T(8,128)(2,1)} %collective-permute-done.64.refs_1_, bf16[4,16,4,64,512]{4,3,2,1,0:T(8,128)(2,1)} %get-tuple-element.161.refs_3_.refs_4_.refs_5_.refs_2_, ...), custom_call_target="tpu_custom_call" | custom-call | flops 16777216 | bytes 10764288 | tf_op jit(solution)/shard_map/pallas_call | solution.py:317
  454.2 4.5 collective-permute-start.69
  460.3 3.8 collective-permute-done.70
  (357 shorter events, 157.8 us)
Async XLA Ops:
  19.0 133.6 %collective-permute-start = (bf16[16,256,1024]{2,1,0:T(8,128)(2,1)}, bf16[16,256,1024]{2,1,0:T(8,128)(2,1)}, u32[]{:S(2)}, u32[]{:S(2)}) collective-permute-start(bf16[16,256,1024]{2,1,0:T(8,128)(2,1)} %get-tuple-element.86.refs_1_.refs_3_), channel_id=1, source_target_pairs={{0,1},{1,0},{2,3},{3,2},{4,5},{5,4},{6,7},{7,6},{8,9},{9,8},{10,11... | collective-permute-start | bytes 25165832 | tf_op jit(solution)/shard_map/ppermute | solution.py:406
  19.5 17.8 %collective-permute-start.1 = (bf16[16,32,512]{2,1,0:T(8,128)(2,1)}, bf16[16,32,512]{2,1,0:T(8,128)(2,1)}, u32[]{:S(2)}, u32[]{:S(2)}) collective-permute-start(bf16[16,32,512]{2,1,0:T(8,128)(2,1)} %get-tuple-element.90.refs_2_), channel_id=1, source_target_pairs={{0,8},{1,9},{2,10},{3,11},{4,12},{5,13},{6,14},{7,15}} | collective-permute-start | bytes 1572872 | tf_op jit(solution)/shard_map/ppermute | solution.py:381
  24.7 12.6 %collective-permute-start.2 = (bf16[16,32,512]{2,1,0:T(8,128)(2,1)}, bf16[16,32,512]{2,1,0:T(8,128)(2,1)}, u32[]{:S(2)}, u32[]{:S(2)}) collective-permute-start(bf16[16,32,512]{2,1,0:T(8,128)(2,1)} %get-tuple-element.88.refs_0_), channel_id=1, source_target_pairs={{24,16},{25,17},{26,18},{27,19},{28,20},{29,21},{30,22},{31,23}} | collective-permute-start | bytes 1572872 | tf_op jit(solution)/shard_map/ppermute | solution.py:382
  26.3 22.7 %collective-permute-start.5 = (bf16[16,32,512]{2,1,0:T(8,128)(2,1)}, bf16[16,32,512]{2,1,0:T(8,128)(2,1)}, u32[]{:S(2)}, u32[]{:S(2)}) collective-permute-start(bf16[16,32,512]{2,1,0:T(8,128)(2,1)} %get-tuple-element.91.refs_4_.refs_2_), channel_id=1, source_target_pairs={{0,8},{1,9},{2,10},{3,11},{4,12},{5,13},{6,14},{7,15}} | collective-permute-start | bytes 1572872 | tf_op jit(solution)/shard_map/ppermute | solution.py:381
  28.3 20.6 %collective-permute-start.6 = (bf16[16,32,512]{2,1,0:T(8,128)(2,1)}, bf16[16,32,512]{2,1,0:T(8,128)(2,1)}, u32[]{:S(2)}, u32[]{:S(2)}) collective-permute-start(bf16[16,32,512]{2,1,0:T(8,128)(2,1)} %get-tuple-element.96.refs_0_), channel_id=1, source_target_pairs={{24,16},{25,17},{26,18},{27,19},{28,20},{29,21},{30,22},{31,23}} | collective-permute-start | bytes 1572872 | tf_op jit(solution)/shard_map/ppermute | solution.py:382
  38.7 23.7 %collective-permute-start.3 = (bf16[16,32,512]{2,1,0:T(8,128)(2,1)S(1)}, bf16[16,32,512]{2,1,0:T(8,128)(2,1)S(1)}, u32[]{:S(2)}, u32[]{:S(2)}) collective-permute-start(bf16[16,32,512]{2,1,0:T(8,128)(2,1)S(1)} %get-tuple-element.93.refs_4_), channel_id=1, source_target_pairs={{0,8},{8,16},{1,9},{9,17},{2,10},{10,18},{3,11},{11,19},{4,12},{12... | collective-permute-start | bytes 1572872 | tf_op jit(solution)/shard_map/ppermute | solution.py:381
  42.3 20.1 %collective-permute-start.4 = (bf16[16,32,512]{2,1,0:T(8,128)(2,1)S(1)}, bf16[16,32,512]{2,1,0:T(8,128)(2,1)S(1)}, u32[]{:S(2)}, u32[]{:S(2)}) collective-permute-start(bf16[16,32,512]{2,1,0:T(8,128)(2,1)S(1)} %get-tuple-element.94), channel_id=1, source_target_pairs={{24,16},{16,8},{25,17},{17,9},{26,18},{18,10},{27,19},{19,11},{28,... | collective-permute-start | bytes 1572872 | tf_op jit(solution)/shard_map/ppermute | solution.py:382
  50.4 26.8 %collective-permute-start.12 = (bf16[16,32,512]{2,1,0:T(8,128)(2,1)S(1)}, bf16[16,32,512]{2,1,0:T(8,128)(2,1)S(1)}, u32[]{:S(2)}, u32[]{:S(2)}) collective-permute-start(bf16[16,32,512]{2,1,0:T(8,128)(2,1)S(1)} %get-tuple-element.99.refs_4_), channel_id=1, source_target_pairs={{0,8},{8,16},{1,9},{9,17},{2,10},{10,18},{3,11},{11,19},{4,12},{12... | collective-permute-start | bytes 1572872 | tf_op jit(solution)/shard_map/ppermute | solution.py:381
  56.0 21.3 %collective-permute-start.13 = (bf16[16,32,512]{2,1,0:T(8,128)(2,1)S(1)}, bf16[16,32,512]{2,1,0:T(8,128)(2,1)S(1)}, u32[]{:S(2)}, u32[]{:S(2)}) collective-permute-start(bf16[16,32,512]{2,1,0:T(8,128)(2,1)S(1)} %get-tuple-element.105), channel_id=1, source_target_pairs={{24,16},{16,8},{25,17},{17,9},{26,18},{18,10},{27,19},{19,11},{28,... | collective-permute-start | bytes 1572872 | tf_op jit(solution)/shard_map/ppermute | solution.py:382
  64.1 21.5 %collective-permute-start.7 = (bf16[16,32,512]{2,0,1:T(8,128)(2,1)S(1)}, bf16[16,32,512]{2,0,1:T(8,128)(2,1)S(1)}, u32[]{:S(2)}, u32[]{:S(2)}) collective-permute-start(bf16[16,32,512]{2,0,1:T(8,128)(2,1)S(1)} %copy.116), channel_id=1, source_target_pairs={{0,8},{8,16},{16,24},{1,9},{9,17},{17,25},{2,10},{10,18},{18,26},{... | collective-permute-start | bytes 1572872 | tf_op jit(solution)/shard_map/ppermute | solution.py:381
  69.6 16.1 %collective-permute-start.8 = (bf16[16,32,512]{2,0,1:T(8,128)(2,1)S(1)}, bf16[16,32,512]{2,0,1:T(8,128)(2,1)S(1)}, u32[]{:S(2)}, u32[]{:S(2)}) collective-permute-start(bf16[16,32,512]{2,0,1:T(8,128)(2,1)S(1)} %copy.117), channel_id=1, source_target_pairs={{24,16},{16,8},{8,0},{25,17},{17,9},{9,1},{26,18},{18,10},{10,2},{... | collective-permute-start | bytes 1572872 | tf_op jit(solution)/shard_map/ppermute | solution.py:382
  78.9 14.4 %collective-permute-start.14 = (bf16[16,32,512]{2,0,1:T(8,128)(2,1)S(1)}, bf16[16,32,512]{2,0,1:T(8,128)(2,1)S(1)}, u32[]{:S(2)}, u32[]{:S(2)}) collective-permute-start(bf16[16,32,512]{2,0,1:T(8,128)(2,1)S(1)} %copy.119), channel_id=1, source_target_pairs={{0,8},{8,16},{16,24},{1,9},{9,17},{17,25},{2,10},{10,18},{18,26},{... | collective-permute-start | bytes 1572872 | tf_op jit(solution)/shard_map/ppermute | solution.py:381
  84.4 13.4 %collective-permute-start.15 = (bf16[16,32,512]{2,0,1:T(8,128)(2,1)S(1)}, bf16[16,32,512]{2,0,1:T(8,128)(2,1)S(1)}, u32[]{:S(2)}, u32[]{:S(2)}) collective-permute-start(bf16[16,32,512]{2,0,1:T(8,128)(2,1)S(1)} %copy.120), channel_id=1, source_target_pairs={{24,16},{16,8},{8,0},{25,17},{17,9},{9,1},{26,18},{18,10},{10,2},{... | collective-permute-start | bytes 1572872 | tf_op jit(solution)/shard_map/ppermute | solution.py:382
  86.2 13.6 %collective-permute-start.10 = (bf16[8,16,512]{2,1,0:T(8,128)(2,1)S(1)}, bf16[8,16,512]{2,1,0:T(8,128)(2,1)S(1)}, u32[]{:S(2)}, u32[]{:S(2)}) collective-permute-start(bf16[8,16,512]{2,1,0:T(8,128)(2,1)S(1)} %get-tuple-element.209), channel_id=1, source_target_pairs={{0,4},{2,6},{4,0},{6,2},{1,5},{3,7},{5,1},{7,3},{8,12},{10,14},{12... | collective-permute-start | bytes 393224 | tf_op jit(solution)/shard_map/ppermute | solution.py:402
  87.8 13.5 %collective-permute-start.11 = (bf16[8,16,512]{2,1,0:T(8,128)(2,1)S(1)}, bf16[8,16,512]{2,1,0:T(8,128)(2,1)S(1)}, u32[]{:S(2)}, u32[]{:S(2)}) collective-permute-start(bf16[8,16,512]{2,1,0:T(8,128)(2,1)S(1)} %get-tuple-element.208), channel_id=1, source_target_pairs={{0,6},{2,4},{4,2},{6,0},{1,7},{3,5},{5,3},{7,1},{8,14},{10,12},{12... | collective-permute-start | bytes 393224 | tf_op jit(solution)/shard_map/ppermute | solution.py:402
  93.3 8.5 %collective-permute-start.9 = (bf16[8,16,512]{2,1,0:T(8,128)(2,1)S(1)}, bf16[8,16,512]{2,1,0:T(8,128)(2,1)S(1)}, u32[]{:S(2)}, u32[]{:S(2)}) collective-permute-start(bf16[8,16,512]{2,1,0:T(8,128)(2,1)S(1)} %get-tuple-element.210), channel_id=1, source_target_pairs={{0,2},{2,0},{4,6},{6,4},{1,3},{3,1},{5,7},{7,5},{8,10},{10,8},{12,... | collective-permute-start | bytes 393224 | tf_op jit(solution)/shard_map/ppermute | solution.py:402
  98.3 12.9 %collective-permute-start.16 = (bf16[8,16,512]{2,1,0:T(8,128)(2,1)S(1)}, bf16[8,16,512]{2,1,0:T(8,128)(2,1)S(1)}, u32[]{:S(2)}, u32[]{:S(2)}) collective-permute-start(bf16[8,16,512]{2,1,0:T(8,128)(2,1)S(1)} %get-tuple-element.204), channel_id=1, source_target_pairs={{0,2},{2,0},{4,6},{6,4},{1,3},{3,1},{5,7},{7,5},{8,10},{10,8},{12,... | collective-permute-start | bytes 393224 | tf_op jit(solution)/shard_map/ppermute | solution.py:402
  99.8 11.3 %collective-permute-start.17 = (bf16[8,16,512]{2,1,0:T(8,128)(2,1)S(1)}, bf16[8,16,512]{2,1,0:T(8,128)(2,1)S(1)}, u32[]{:S(2)}, u32[]{:S(2)}) collective-permute-start(bf16[8,16,512]{2,1,0:T(8,128)(2,1)S(1)} %get-tuple-element.203), channel_id=1, source_target_pairs={{0,4},{2,6},{4,0},{6,2},{1,5},{3,7},{5,1},{7,3},{8,12},{10,14},{12... | collective-permute-start | bytes 393224 | tf_op jit(solution)/shard_map/ppermute | solution.py:402
  101.3 9.8 %collective-permute-start.18 = (bf16[8,16,512]{2,1,0:T(8,128)(2,1)S(1)}, bf16[8,16,512]{2,1,0:T(8,128)(2,1)}, u32[]{:S(2)}, u32[]{:S(2)}) collective-permute-start(bf16[8,16,512]{2,1,0:T(8,128)(2,1)S(1)} %get-tuple-element.202), channel_id=1, source_target_pairs={{0,6},{2,4},{4,2},{6,0},{1,7},{3,5},{5,3},{7,1},{8,14},{10,12},{12... | collective-permute-start | bytes 393224 | tf_op jit(solution)/shard_map/ppermute | solution.py:402
  113.2 10.4 %collective-permute-start.19 = (bf16[4,8,16,512]{3,1,2,0:T(8,128)(2,1)S(1)}, bf16[4,8,16,512]{3,1,2,0:T(8,128)(2,1)S(1)}, u32[]{:S(2)}, u32[]{:S(2)}) collective-permute-start(bf16[4,8,16,512]{3,1,2,0:T(8,128)(2,1)S(1)} %copy.122), channel_id=1, source_target_pairs={{0,1},{1,0},{2,3},{3,2},{4,5},{5,4},{6,7},{7,6},{8,9},{9,8},{10,11... | collective-permute-start | bytes 1572872 | tf_op jit(solution)/shard_map/ppermute | solution.py:406
  139.9 25.6 %collective-permute-start.30 = (bf16[16,64,512]{2,1,0:T(8,128)(2,1)}, bf16[16,64,512]{2,1,0:T(8,128)(2,1)}, u32[]{:S(2)}, u32[]{:S(2)}) collective-permute-start(bf16[16,64,512]{2,1,0:T(8,128)(2,1)} %bitcast.16.refs_3_.refs_6_), channel_id=1, source_target_pairs={{24,16},{16,8},{8,0},{25,17},{17,9},{9,1},{26,18},{18,10},{10,2},{... | collective-permute-start | bytes 3145736 | tf_op jit(solution)/shard_map/ppermute | solution.py:395
  141.2 25.6 %collective-permute-start.27 = (bf16[16,64,512]{2,1,0:T(8,128)(2,1)}, bf16[16,64,512]{2,1,0:T(8,128)(2,1)}, u32[]{:S(2)}, u32[]{:S(2)}) collective-permute-start(bf16[16,64,512]{2,1,0:T(8,128)(2,1)} %bitcast.16.refs_3_.refs_6_), channel_id=1, source_target_pairs={{0,8},{8,16},{16,24},{1,9},{9,17},{17,25},{2,10},{10,18},{18,26},{... | collective-permute-start | bytes 3145736 | tf_op jit(solution)/shard_map/ppermute | solution.py:394
  165.5 24.6 %collective-permute-start.31 = (bf16[16,64,512]{2,1,0:T(8,128)(2,1)}, bf16[16,64,512]{2,1,0:T(8,128)(2,1)}, u32[]{:S(2)}, u32[]{:S(2)}) collective-permute-start(bf16[16,64,512]{2,1,0:T(8,128)(2,1)} %shard_map.120.refs_10_), channel_id=1, source_target_pairs={{16,8},{8,0},{17,9},{9,1},{18,10},{10,2},{19,11},{11,3},{20,12},{1... | collective-permute-start | bytes 3145736 | tf_op jit(solution)/shard_map/ppermute | solution.py:395
  166.8 24.6 %collective-permute-start.28 = (bf16[16,64,512]{2,1,0:T(8,128)(2,1)}, bf16[16,64,512]{2,1,0:T(8,128)(2,1)}, u32[]{:S(2)}, u32[]{:S(2)}) collective-permute-start(bf16[16,64,512]{2,1,0:T(8,128)(2,1)} %shard_map.116.refs_3_.refs_4_.refs_7_), channel_id=1, source_target_pairs={{8,16},{16,24},{9,17},{17,25},{10,18},{18,26},{11,19},{19,27},{12,... | collective-permute-start | bytes 3145736 | tf_op jit(solution)/shard_map/ppermute | solution.py:394
  190.1 24.4 %collective-permute-start.32 = (bf16[16,64,512]{2,1,0:T(8,128)(2,1)}, bf16[16,64,512]{2,1,0:T(8,128)(2,1)}, u32[]{:S(2)}, u32[]{:S(2)}) collective-permute-start(bf16[16,64,512]{2,1,0:T(8,128)(2,1)} %shard_map.121.refs_11_), channel_id=1, source_target_pairs={{8,0},{9,1},{10,2},{11,3},{12,4},{13,5},{14,6},{15,7}} | collective-permute-start | bytes 3145736 | tf_op jit(solution)/shard_map/ppermute | solution.py:395
  191.4 23.0 %collective-permute-start.29 = (bf16[16,64,512]{2,1,0:T(8,128)(2,1)}, bf16[16,64,512]{2,1,0:T(8,128)(2,1)}, u32[]{:S(2)}, u32[]{:S(2)}) collective-permute-start(bf16[16,64,512]{2,1,0:T(8,128)(2,1)} %shard_map.119.refs_4_.refs_8_), channel_id=1, source_target_pairs={{16,24},{17,25},{18,26},{19,27},{20,28},{21,29},{22,30},{23,31}} | collective-permute-start | bytes 3145736 | tf_op jit(solution)/shard_map/ppermute | solution.py:394
  242.1 20.9 %collective-permute-start.35 = (bf16[16,32,512]{2,1,0:T(8,128)(2,1)}, bf16[16,32,512]{2,1,0:T(8,128)(2,1)S(1)}, u32[]{:S(2)}, u32[]{:S(2)}) collective-permute-start(bf16[16,32,512]{2,1,0:T(8,128)(2,1)} %get-tuple-element.136.refs_2_), channel_id=1, source_target_pairs={{0,8},{1,9},{2,10},{3,11},{4,12},{5,13},{6,14},{7,15}} | collective-permute-start | bytes 1572872 | tf_op jit(solution)/shard_map/ppermute | solution.py:381
  243.6 19.5 %collective-permute-start.36 = (bf16[16,32,512]{2,1,0:T(8,128)(2,1)}, bf16[16,32,512]{2,1,0:T(8,128)(2,1)S(1)}, u32[]{:S(2)}, u32[]{:S(2)}) collective-permute-start(bf16[16,32,512]{2,1,0:T(8,128)(2,1)} %get-tuple-element.137.refs_0_), channel_id=1, source_target_pairs={{24,16},{25,17},{26,18},{27,19},{28,20},{29,21},{30,22},{31,23}} | collective-permute-start | bytes 1572872 | tf_op jit(solution)/shard_map/ppermute | solution.py:382
  244.3 26.3 %collective-permute-start.33 = (bf16[16,32,512]{2,1,0:T(8,128)(2,1)}, bf16[16,32,512]{2,1,0:T(8,128)(2,1)S(1)}, u32[]{:S(2)}, u32[]{:S(2)}) collective-permute-start(bf16[16,32,512]{2,1,0:T(8,128)(2,1)} %get-tuple-element.127.refs_6_.refs_8_.refs_2_), channel_id=1, source_target_pairs={{0,8},{1,9},{2,10},{3,11},{4,12},{5,13},{6,14},{7,15}} | collective-permute-start | bytes 1572872 | tf_op jit(solution)/shard_map/ppermute | solution.py:381
  245.6 25.0 %collective-permute-start.34 = (bf16[16,32,512]{2,1,0:T(8,128)(2,1)}, bf16[16,32,512]{2,1,0:T(8,128)(2,1)S(1)}, u32[]{:S(2)}, u32[]{:S(2)}) collective-permute-start(bf16[16,32,512]{2,1,0:T(8,128)(2,1)} %get-tuple-element.125.refs_0_), channel_id=1, source_target_pairs={{24,16},{25,17},{26,18},{27,19},{28,20},{29,21},{30,22},{31,23}} | collective-permute-start | bytes 1572872 | tf_op jit(solution)/shard_map/ppermute | solution.py:382
  263.3 20.3 %collective-permute-start.39 = (bf16[16,32,512]{2,1,0:T(8,128)(2,1)S(1)}, bf16[16,32,512]{2,1,0:T(8,128)(2,1)S(1)}, u32[]{:S(2)}, u32[]{:S(2)}) collective-permute-start(bf16[16,32,512]{2,1,0:T(8,128)(2,1)S(1)} %get-tuple-element.138.refs_8_), channel_id=1, source_target_pairs={{0,8},{8,16},{1,9},{9,17},{2,10},{10,18},{3,11},{11,19},{4,12},{12... | collective-permute-start | bytes 1572872 | tf_op jit(solution)/shard_map/ppermute | solution.py:381
  264.7 19.0 %collective-permute-start.40 = (bf16[16,32,512]{2,1,0:T(8,128)(2,1)S(1)}, bf16[16,32,512]{2,1,0:T(8,128)(2,1)S(1)}, u32[]{:S(2)}, u32[]{:S(2)}) collective-permute-start(bf16[16,32,512]{2,1,0:T(8,128)(2,1)S(1)} %get-tuple-element.145), channel_id=1, source_target_pairs={{24,16},{16,8},{25,17},{17,9},{26,18},{18,10},{27,19},{19,11},{28,... | collective-permute-start | bytes 1572872 | tf_op jit(solution)/shard_map/ppermute | solution.py:382
  270.9 19.2 %collective-permute-start.37 = (bf16[16,32,512]{2,1,0:T(8,128)(2,1)S(1)}, bf16[16,32,512]{2,1,0:T(8,128)(2,1)S(1)}, u32[]{:S(2)}, u32[]{:S(2)}) collective-permute-start(bf16[16,32,512]{2,1,0:T(8,128)(2,1)S(1)} %get-tuple-element.140.refs_8_), channel_id=1, source_target_pairs={{0,8},{8,16},{1,9},{9,17},{2,10},{10,18},{3,11},{11,19},{4,12},{12... | collective-permute-start | bytes 1572872 | tf_op jit(solution)/shard_map/ppermute | solution.py:381
  277.3 12.8 %collective-permute-start.38 = (bf16[16,32,512]{2,1,0:T(8,128)(2,1)S(1)}, bf16[16,32,512]{2,1,0:T(8,128)(2,1)S(1)}, u32[]{:S(2)}, u32[]{:S(2)}) collective-permute-start(bf16[16,32,512]{2,1,0:T(8,128)(2,1)S(1)} %get-tuple-element.141), channel_id=1, source_target_pairs={{24,16},{16,8},{25,17},{17,9},{26,18},{18,10},{27,19},{19,11},{28,... | collective-permute-start | bytes 1572872 | tf_op jit(solution)/shard_map/ppermute | solution.py:382
  290.7 17.2 %collective-permute-start.41 = (bf16[16,32,512]{2,0,1:T(8,128)(2,1)S(1)}, bf16[16,32,512]{2,0,1:T(8,128)(2,1)S(1)}, u32[]{:S(2)}, u32[]{:S(2)}) collective-permute-start(bf16[16,32,512]{2,0,1:T(8,128)(2,1)S(1)} %copy.127), channel_id=1, source_target_pairs={{0,8},{8,16},{16,24},{1,9},{9,17},{17,25},{2,10},{10,18},{18,26},{... | collective-permute-start | bytes 1572872 | tf_op jit(solution)/shard_map/ppermute | solution.py:381
  296.1 16.7 %collective-permute-start.42 = (bf16[16,32,512]{2,0,1:T(8,128)(2,1)S(1)}, bf16[16,32,512]{2,0,1:T(8,128)(2,1)S(1)}, u32[]{:S(2)}, u32[]{:S(2)}) collective-permute-start(bf16[16,32,512]{2,0,1:T(8,128)(2,1)S(1)} %copy.128), channel_id=1, source_target_pairs={{24,16},{16,8},{8,0},{25,17},{17,9},{9,1},{26,18},{18,10},{10,2},{... | collective-permute-start | bytes 1572872 | tf_op jit(solution)/shard_map/ppermute | solution.py:382
  297.7 19.1 %collective-permute-start.47 = (bf16[16,32,512]{2,0,1:T(8,128)(2,1)S(1)}, bf16[16,32,512]{2,0,1:T(8,128)(2,1)S(1)}, u32[]{:S(2)}, u32[]{:S(2)}) collective-permute-start(bf16[16,32,512]{2,0,1:T(8,128)(2,1)S(1)} %copy.130), channel_id=1, source_target_pairs={{0,8},{8,16},{16,24},{1,9},{9,17},{17,25},{2,10},{10,18},{18,26},{... | collective-permute-start | bytes 1572872 | tf_op jit(solution)/shard_map/ppermute | solution.py:381
  303.2 15.2 %collective-permute-start.48 = (bf16[16,32,512]{2,0,1:T(8,128)(2,1)S(1)}, bf16[16,32,512]{2,0,1:T(8,128)(2,1)S(1)}, u32[]{:S(2)}, u32[]{:S(2)}) collective-permute-start(bf16[16,32,512]{2,0,1:T(8,128)(2,1)S(1)} %copy.131), channel_id=1, source_target_pairs={{24,16},{16,8},{8,0},{25,17},{17,9},{9,1},{26,18},{18,10},{10,2},{... | collective-permute-start | bytes 1572872 | tf_op jit(solution)/shard_map/ppermute | solution.py:382
  313.4 9.1 %collective-permute-start.44 = (bf16[8,16,512]{2,1,0:T(8,128)(2,1)S(1)}, bf16[8,16,512]{2,1,0:T(8,128)(2,1)S(1)}, u32[]{:S(2)}, u32[]{:S(2)}) collective-permute-start(bf16[8,16,512]{2,1,0:T(8,128)(2,1)S(1)} %get-tuple-element.196), channel_id=1, source_target_pairs={{0,4},{2,6},{4,0},{6,2},{1,5},{3,7},{5,1},{7,3},{8,12},{10,14},{12... | collective-permute-start | bytes 393224 | tf_op jit(solution)/shard_map/ppermute | solution.py:402
  313.5 9.0 %collective-permute-start.45 = (bf16[8,16,512]{2,1,0:T(8,128)(2,1)S(1)}, bf16[8,16,512]{2,1,0:T(8,128)(2,1)S(1)}, u32[]{:S(2)}, u32[]{:S(2)}) collective-permute-start(bf16[8,16,512]{2,1,0:T(8,128)(2,1)S(1)} %get-tuple-element.195), channel_id=1, source_target_pairs={{0,6},{2,4},{4,2},{6,0},{1,7},{3,5},{5,3},{7,1},{8,14},{10,12},{12... | collective-permute-start | bytes 393224 | tf_op jit(solution)/shard_map/ppermute | solution.py:402
  325.6 8.6 %collective-permute-start.52 = (bf16[4,8,16,512]{3,2,1,0:T(8,128)(2,1)S(1)}, bf16[4,8,16,512]{3,2,1,0:T(8,128)(2,1)S(1)}, u32[]{:S(2)}, u32[]{:S(2)}) collective-permute-start(bf16[4,8,16,512]{3,2,1,0:T(8,128)(2,1)S(1)} %pad_maximum_fusion.1), channel_id=1, source_target_pairs={{0,1},{1,0},{2,3},{3,2},{4,5},{5,4},{6,7},{7,6},{8,9},{9,8},{10,11... | collective-permute-start | bytes 1572872 | tf_op jit(solution)/shard_map/ppermute | solution.py:406
  347.6 8.9 %collective-permute-start.56 = (bf16[8,16,512]{2,0,1:T(8,128)(2,1)S(1)}, bf16[8,16,512]{2,0,1:T(8,128)(2,1)S(1)}, u32[]{:S(2)}, u32[]{:S(2)}) collective-permute-start(bf16[8,16,512]{2,0,1:T(8,128)(2,1)S(1)} %bitcast.117), channel_id=1, source_target_pairs={{0,2},{2,0},{4,6},{6,4},{1,3},{3,1},{5,7},{7,5},{8,10},{10,8},{12,... | collective-permute-start | bytes 393224 | tf_op jit(solution)/shard_map/ppermute | solution.py:402
  359.9 26.3 %collective-permute-start.60 = (bf16[16,64,512]{2,1,0:T(8,128)(2,1)}, bf16[16,64,512]{2,1,0:T(8,128)(2,1)}, u32[]{:S(2)}, u32[]{:S(2)}) collective-permute-start(bf16[16,64,512]{2,1,0:T(8,128)(2,1)} %bitcast.38.refs_10_.refs_0_), channel_id=1, source_target_pairs={{24,16},{16,8},{8,0},{25,17},{17,9},{9,1},{26,18},{18,10},{10,2},{... | collective-permute-start | bytes 3145736 | tf_op jit(solution)/shard_map/ppermute | solution.py:395
  361.2 26.3 %collective-permute-start.59 = (bf16[16,64,512]{2,1,0:T(8,128)(2,1)}, bf16[16,64,512]{2,1,0:T(8,128)(2,1)S(1)}, u32[]{:S(2)}, u32[]{:S(2)}) collective-permute-start(bf16[16,64,512]{2,1,0:T(8,128)(2,1)} %bitcast.38.refs_10_.refs_0_), channel_id=1, source_target_pairs={{0,8},{8,16},{16,24},{1,9},{9,17},{17,25},{2,10},{10,18},{18,26},{... | collective-permute-start | bytes 3145736 | tf_op jit(solution)/shard_map/ppermute | solution.py:394
  386.2 25.4 %collective-permute-start.62 = (bf16[16,64,512]{2,1,0:T(8,128)(2,1)}, bf16[16,64,512]{2,1,0:T(8,128)(2,1)}, u32[]{:S(2)}, u32[]{:S(2)}) collective-permute-start(bf16[16,64,512]{2,1,0:T(8,128)(2,1)} %shard_map.142.refs_2_), channel_id=1, source_target_pairs={{16,8},{8,0},{17,9},{9,1},{18,10},{10,2},{19,11},{11,3},{20,12},{1... | collective-permute-start | bytes 3145736 | tf_op jit(solution)/shard_map/ppermute | solution.py:395
  388.4 24.5 %collective-permute-start.61 = (bf16[16,64,512]{2,1,0:T(8,128)(2,1)}, bf16[16,64,512]{2,1,0:T(8,128)(2,1)}, u32[]{:S(2)}, u32[]{:S(2)}) collective-permute-start(bf16[16,64,512]{2,1,0:T(8,128)(2,1)} %shard_map.139.refs_8_.refs_4_.refs_1_), channel_id=1, source_target_pairs={{8,16},{16,24},{9,17},{17,25},{10,18},{18,26},{11,19},{19,27},{12,... | collective-permute-start | bytes 3145736 | tf_op jit(solution)/shard_map/ppermute | solution.py:394
  411.6 28.0 %collective-permute-start.64 = (bf16[16,64,512]{2,1,0:T(8,128)(2,1)}, bf16[16,64,512]{2,1,0:T(8,128)(2,1)}, u32[]{:S(2)}, u32[]{:S(2)}) collective-permute-start(bf16[16,64,512]{2,1,0:T(8,128)(2,1)} %shard_map.146.refs_1_), channel_id=1, source_target_pairs={{8,0},{9,1},{10,2},{11,3},{12,4},{13,5},{14,6},{15,7}} | collective-permute-start | bytes 3145736 | tf_op jit(solution)/shard_map/ppermute | solution.py:395
  413.0 26.6 %collective-permute-start.63 = (bf16[16,64,512]{2,1,0:T(8,128)(2,1)}, bf16[16,64,512]{2,1,0:T(8,128)(2,1)}, u32[]{:S(2)}, u32[]{:S(2)}) collective-permute-start(bf16[16,64,512]{2,1,0:T(8,128)(2,1)} %shard_map.144.refs_6_.refs_0_.refs_4_), channel_id=1, source_target_pairs={{16,24},{17,25},{18,26},{19,27},{20,28},{21,29},{22,30},{23,31}} | collective-permute-start | bytes 3145736 | tf_op jit(solution)/shard_map/ppermute | solution.py:394
  (88 other events, 807.6 us)
